TPU v7x, 32 devices: a whole 2x2x4 slice. The times are simulated.
32 devices in a mesh: seq: 4 (over y, x), ctx: 4 (over z), wt: 2 (over core).
Axes of the slice: x: 2, y: 2, z: 4, core: 2. Of those that a mesh axis runs over, the one named last changes fastest.
Arguments:
- layer_input: bfloat16 [4, 1024, 1536], P('seq', 'ctx'), may hold values from -6 to 6
- pairs: int32 [4, 4], P('seq'), may hold values from 0 to 3, each once within a row
- gain_attn: bfloat16 [1536], replicated, may hold values from 0.5 to 1.5
- w_q: bfloat16 [1536, 1536], P(('seq', 'ctx'), 'wt'), may hold values from -0.15625 to 0.15625
- b_q: bfloat16 [1536], P('wt'), may hold values from -3 to 3
- w_k: bfloat16 [1536, 256], P(('seq', 'ctx'), 'wt'), may hold values from -0.15625 to 0.15625
- b_k: bfloat16 [256], P('wt'), may hold values from -3 to 3
- w_v: bfloat16 [1536, 256], P(('seq', 'ctx'), 'wt'), may hold values from -0.15625 to 0.15625
- b_v: bfloat16 [256], P('wt'), may hold values from -3 to 3
- w_o: bfloat16 [1536, 1536], P(('seq', 'ctx'), 'wt'), may hold values from -0.875 to 0.875
- gain_mlp: bfloat16 [1536], replicated, may hold values from 0.5 to 1.5
- w_gate: bfloat16 [1536, 8960], P(('seq', 'ctx'), 'wt'), may hold values from -0.15625 to 0.15625
- w_up: bfloat16 [1536, 8960], P(('seq', 'ctx'), 'wt'), may hold values from -0.15625 to 0.15625
- w_down: bfloat16 [1536, 8960], P(('seq', 'ctx'), 'wt'), may hold values from -0.0625 to 0.0625
- out_grad: bfloat16 [4, 1024, 1536], P('seq', 'ctx'), may hold values from -6 to 6
Outputs:
- layer_output: bfloat16 [4, 1024, 1536], P('seq', 'ctx')
- grad_input: bfloat16 [4, 1024, 1536], P('seq', 'ctx')
- grad_gain_attn: float32 [1536], replicated
- grad_w_q: float32 [1536, 1536], P(('seq', 'ctx'), 'wt')
- grad_b_q: float32 [1536], P('wt')
- grad_w_k: float32 [1536, 256], P(('seq', 'ctx'), 'wt')
- grad_b_k: float32 [256], P('wt')
- grad_w_v: float32 [1536, 256], P(('seq', 'ctx'), 'wt')
- grad_b_v: float32 [256], P('wt')
- grad_w_o: float32 [1536, 1536], P(('seq', 'ctx'), 'wt')
- grad_gain_mlp: float32 [1536], replicated
- grad_w_gate: float32 [1536, 8960], P(('seq', 'ctx'), 'wt')
- grad_w_up: float32 [1536, 8960], P(('seq', 'ctx'), 'wt')
- grad_w_down: float32 [1536, 8960], P(('seq', 'ctx'), 'wt')
Inputs may be any that keep to these rules, and one draw needn't show every extreme that they name: Each row of pairs holds every number below 4 once.
All inputs are finite; a program needn't handle non-finite values.
Results may differ from a plain program's by a relative error of at most 0.017.
Values may be sent and summed in bfloat16 or wider, within the bound.
No kernel may reach another device: no remote copies, remote signals or barrier semaphores. Data moves between devices by JAX's collectives and lax.ppermute only.
A program may use at most 192 MiB of HBM per device.

v0:
```python
import jax
import jax.numpy as jnp
from jax import lax
from jax.sharding import PartitionSpec as P

HD = 128


EPSILON = 1e-06
THETA_BASE = 1000000.0
NEGATIVE = -1e30


def rotate(values):
    middle = values.shape[-1] // 2
    return jnp.concatenate([-values[..., middle:], values[..., :middle]], -1)


def rope_tables(positions):
    freqs = THETA_BASE ** (-(jnp.arange(HD // 2, dtype=jnp.float32) * 2.0) / HD)
    angles = positions.astype(jnp.float32)[:, None] * freqs[None, :]
    cosines = jnp.cos(angles)
    sines = jnp.sin(angles)
    return (jnp.concatenate([cosines, cosines], -1), jnp.concatenate([sines, sines], -1))


def column_slice(matrix, count):
    return lax.slice_in_dim(matrix, 0, count, axis=1)


def matmul(left, right):
    return jnp.dot(left, right, preferred_element_type=jnp.float32)


def times_transposed(left, right):
    return lax.dot_general(
        left, right, (((1,), (1,)), ((), ())), preferred_element_type=jnp.float32
    )


def inner_rows(left, right):
    return lax.dot_general(
        left, right, (((0,), (0,)), ((), ())), preferred_element_type=jnp.float32
    )


def wt_total(partial_sum):
    return lax.psum(partial_sum, "wt")


def norm_back(grad_normed, inputs, inverse_rms, gain):
    weighted = grad_normed * gain
    back = inverse_rms * weighted - inputs * inverse_rms**3 * jnp.mean(
        weighted * inputs, -1, keepdims=True
    )
    gain_grad = jnp.sum(grad_normed * inputs * inverse_rms, 0)
    return (back, gain_grad)


def pick_pair(query_seq, first_head):
    return (
        query_seq[:, first_head : first_head + 2]
        .transpose(1, 0, 2)
        .reshape(2 * query_seq.shape[0], HD)
    )


def on_device(
    layer_input,
    pairs,
    gain_attn,
    w_q,
    b_q,
    w_k,
    b_k,
    w_v,
    b_v,
    w_o,
    gain_mlp,
    w_gate,
    w_up,
    w_down,
    out_grad,
):
    seq_count, span_rows, model_width = layer_input.shape
    row_count = seq_count * span_rows
    half_rows = span_rows // 2
    heads_here = w_q.shape[1] // HD
    kv_here = w_k.shape[1] // HD
    group_size = heads_here // kv_here
    ctx_size = lax.axis_size("ctx")
    ctx_index = lax.axis_index("ctx")
    scale = HD ** (-0.5)
    pair_rows = jnp.repeat(pairs, span_rows, axis=1)
    within = jnp.arange(ctx_size * span_rows, dtype=jnp.int32) % span_rows
    key_positions = jnp.where(
        within < half_rows,
        pair_rows * half_rows + within,
        (2 * ctx_size - 1 - pair_rows) * half_rows + within - half_rows,
    )
    query_positions = lax.dynamic_slice_in_dim(key_positions, ctx_index * span_rows, span_rows, 1)
    cosines, sines = rope_tables(query_positions.reshape(row_count))

    def rope_rows(values):
        return values * cosines[:, None, :] + rotate(values) * sines[:, None, :]

    def unrope_rows(grads):
        return grads * cosines[:, None, :] - rotate(grads * sines[:, None, :])

    input_rows = layer_input.reshape(row_count, model_width).astype(jnp.float32)
    gain_one = gain_attn.astype(jnp.float32)
    gain_two = gain_mlp.astype(jnp.float32)
    rms_attn = lax.rsqrt(jnp.mean(input_rows * input_rows, -1, keepdims=True) + EPSILON)
    normed_attn = (input_rows * rms_attn * gain_one).astype(jnp.bfloat16)
    query_all, key_all, value_all, output_all = (
        lax.all_gather(w_q, ("seq", "ctx"), axis=0, tiled=True),
        lax.all_gather(w_k, ("seq", "ctx"), axis=0, tiled=True),
        lax.all_gather(w_v, ("seq", "ctx"), axis=0, tiled=True),
        lax.all_gather(w_o, ("seq", "ctx"), axis=0, tiled=True),
    )
    query_lin = (matmul(normed_attn, query_all) + b_q.astype(jnp.float32)).reshape(
        row_count, heads_here, HD
    )
    key_lin = (matmul(normed_attn, key_all) + b_k.astype(jnp.float32)).reshape(
        row_count, kv_here, HD
    )
    value_rows = (matmul(normed_attn, value_all) + b_v.astype(jnp.float32)).astype(jnp.bfloat16)
    query_rot = rope_rows(query_lin).astype(jnp.bfloat16)
    key_rot = rope_rows(key_lin).astype(jnp.bfloat16)
    keys_seq, values_seq = (
        lax.all_gather(
            key_rot.reshape(seq_count, span_rows, kv_here * HD), "ctx", axis=1, tiled=True
        ),
        lax.all_gather(
            value_rows.reshape(seq_count, span_rows, kv_here * HD), "ctx", axis=1, tiled=True
        ),
    )
    query_seqs = query_rot.reshape(seq_count, span_rows, heads_here, HD)

    def masked_scores(query_block, key_head, visible_two):
        scores = times_transposed(query_block, key_head) * scale
        return jnp.where(visible_two, scores, NEGATIVE)

    def attend(inputs):
        query_seq, key_seq, value_seq, query_pos, key_pos = inputs
        visible = key_pos[None, :] <= query_pos[:, None]
        visible_two = jnp.concatenate([visible, visible], 0)
        outputs = []
        log_sums = []
        for pair_index in range(group_size // 2):
            first_head = 2 * pair_index
            scores = masked_scores(pick_pair(query_seq, first_head), key_seq, visible_two)
            highest = jnp.max(scores, -1, keepdims=True)
            weights = jnp.exp(scores - highest)
            totals = jnp.sum(weights, -1, keepdims=True)
            block_out = matmul((weights / totals).astype(jnp.bfloat16), value_seq)
            outputs.append(block_out.reshape(2, span_rows, HD))
            log_sums.append((highest + jnp.log(totals)).reshape(2, span_rows))
        return (jnp.concatenate(outputs, 0), jnp.concatenate(log_sums, 0))

    heads_out, log_sum = lax.map(
        attend, (query_seqs, keys_seq, values_seq, query_positions, key_positions)
    )
    attn_heads = (
        heads_out.transpose(0, 2, 1, 3).reshape(row_count, heads_here * HD).astype(jnp.bfloat16)
    )
    hidden = input_rows + wt_total(times_transposed(attn_heads, output_all))
    rms_mlp = lax.rsqrt(jnp.mean(hidden * hidden, -1, keepdims=True) + EPSILON)
    normed_mlp = (hidden * rms_mlp * gain_two).astype(jnp.bfloat16)
    units_here = w_gate.shape[1]
    empty_units = jnp.zeros((row_count, units_here), jnp.float32)
    totals = (empty_units, empty_units)
    pieces = (
        lax.all_gather(w_gate, ("seq", "ctx"), axis=0, tiled=True),
        lax.all_gather(w_up, ("seq", "ctx"), axis=0, tiled=True),
    )
    columns = column_slice(normed_mlp, pieces[0].shape[0])
    gate = totals[0] + matmul(columns, pieces[0])
    up_proj = totals[1] + matmul(columns, pieces[1])
    sigmoid_gate = jax.nn.sigmoid(gate)
    silu_gate = gate * sigmoid_gate
    act = (silu_gate * up_proj).astype(jnp.bfloat16)
    mlp_out = wt_total(
        times_transposed(act, lax.all_gather(w_down, ("seq", "ctx"), axis=0, tiled=True))
    )
    layer_output = (
        (hidden + mlp_out).astype(jnp.bfloat16).reshape(seq_count, span_rows, model_width)
    )
    grad_out = out_grad.reshape(row_count, model_width)
    pieces = lax.all_gather(w_down, ("seq", "ctx"), axis=0, tiled=True)
    g_act = matmul(column_slice(grad_out, pieces.shape[0]), pieces)
    silu_slope = sigmoid_gate * (1.0 + gate * (1.0 - sigmoid_gate))
    g_gate = (g_act * up_proj * silu_slope).astype(jnp.bfloat16)
    g_up = (g_act * silu_gate).astype(jnp.bfloat16)
    own_rows = w_q.shape[0]
    pieces = lax.all_gather((w_gate, w_up), ("seq", "ctx"), axis=0, tiled=True)
    g_normed_mlp = wt_total(times_transposed(g_gate, pieces[0]) + times_transposed(g_up, pieces[1]))
    back_mlp, grad_gain_mlp = norm_back(g_normed_mlp, hidden, rms_mlp, gain_two)
    g_hidden = grad_out.astype(jnp.float32) + back_mlp
    g_branch = g_hidden.astype(jnp.bfloat16)
    g_heads = (
        matmul(g_branch, output_all)
        .astype(jnp.bfloat16)
        .reshape(seq_count, span_rows, heads_here, HD)
    )

    def attend_back(inputs):
        query_seq, key_seq, value_seq, grad_seq, log_seq, query_pos, key_pos = inputs
        visible = key_pos[None, :] <= query_pos[:, None]
        visible_two = jnp.concatenate([visible, visible], 0)
        query_grads = []
        key_total = jnp.zeros(key_seq.shape, jnp.float32)
        value_total = jnp.zeros(value_seq.shape, jnp.float32)
        for pair_index in range(group_size // 2):
            first_head = 2 * pair_index
            query_block = pick_pair(query_seq, first_head)
            grad_block = pick_pair(grad_seq, first_head)
            log_block = log_seq[first_head : first_head + 2].reshape(2 * span_rows, 1)
            probs = jnp.exp(masked_scores(query_block, key_seq, visible_two) - log_block)
            g_probs = times_transposed(grad_block, value_seq)
            delta = jnp.sum(probs * g_probs, -1, keepdims=True)
            g_scores = (probs * (g_probs - delta)).astype(jnp.bfloat16)
            query_grads.append((matmul(g_scores, key_seq) * scale).reshape(2, span_rows, HD))
            key_total = key_total + inner_rows(g_scores, query_block) * scale
            value_total = value_total + inner_rows(probs.astype(jnp.bfloat16), grad_block)
        key_grads = [key_total]
        value_grads = [value_total]
        return (
            jnp.concatenate(query_grads, 0),
            jnp.concatenate(key_grads, 1),
            jnp.concatenate(value_grads, 1),
        )

    g_query, g_key_all, g_value_all = lax.map(
        attend_back,
        (query_seqs, keys_seq, values_seq, g_heads, log_sum, query_positions, key_positions),
    )
    g_key, g_value = (
        lax.psum_scatter(g_key_all, "ctx", scatter_dimension=1, tiled=True),
        lax.psum_scatter(g_value_all, "ctx", scatter_dimension=1, tiled=True),
    )
    g_query_lin = (
        unrope_rows(g_query.transpose(0, 2, 1, 3).reshape(row_count, heads_here, HD))
        .reshape(row_count, heads_here * HD)
        .astype(jnp.bfloat16)
    )
    g_key_lin = (
        unrope_rows(g_key.reshape(row_count, kv_here, HD))
        .reshape(row_count, kv_here * HD)
        .astype(jnp.bfloat16)
    )
    g_value_lin = g_value.reshape(row_count, kv_here * HD).astype(jnp.bfloat16)
    g_normed_attn = wt_total(
        times_transposed(g_query_lin, query_all)
        + times_transposed(g_key_lin, key_all)
        + times_transposed(g_value_lin, value_all)
    )
    back_attn, grad_gain_attn = norm_back(g_normed_attn, input_rows, rms_attn, gain_one)
    grad_input = (
        (g_hidden + back_attn).astype(jnp.bfloat16).reshape(seq_count, span_rows, model_width)
    )
    small_sums = lax.psum(
        (
            grad_gain_attn,
            grad_gain_mlp,
            jnp.sum(g_query_lin.astype(jnp.float32), 0),
            jnp.sum(g_key_lin.astype(jnp.float32), 0),
            jnp.sum(g_value_lin.astype(jnp.float32), 0),
        ),
        ("seq", "ctx"),
    )
    projected = jnp.concatenate([g_query_lin, g_key_lin, g_value_lin], 1)
    qkv_sums, grad_w_o = (
        lax.psum_scatter(
            inner_rows(normed_attn, projected), ("seq", "ctx"), scatter_dimension=0, tiled=True
        ),
        lax.psum_scatter(
            inner_rows(g_branch, attn_heads), ("seq", "ctx"), scatter_dimension=0, tiled=True
        ),
    )
    lefts = jnp.stack([normed_mlp, normed_mlp, grad_out])
    rights = jnp.stack([g_gate, g_up, act])
    blocks_per = 5
    block_width = units_here // blocks_per

    def one_block(index):
        which = index // blocks_per
        start = index % blocks_per * block_width
        left = lax.dynamic_index_in_dim(lefts, which, 0, False)
        right = lax.dynamic_slice(rights, (which, 0, start), (1, row_count, block_width))[0]
        return lax.psum_scatter(
            inner_rows(left, right), ("seq", "ctx"), scatter_dimension=0, tiled=True
        )

    summed = lax.map(one_block, jnp.arange(3 * blocks_per, dtype=jnp.int32))
    mlp_sums = (
        summed.reshape(3, blocks_per, own_rows, block_width)
        .transpose(0, 2, 1, 3)
        .reshape(3, own_rows, units_here)
    )
    query_cols = heads_here * HD
    key_cols = kv_here * HD
    grad_w_q = qkv_sums[:, :query_cols]
    grad_w_k = qkv_sums[:, query_cols : query_cols + key_cols]
    grad_w_v = qkv_sums[:, query_cols + key_cols :]
    return (
        layer_output,
        grad_input,
        small_sums[0],
        grad_w_q,
        small_sums[2],
        grad_w_k,
        small_sums[3],
        grad_w_v,
        small_sums[4],
        grad_w_o,
        small_sums[1],
        mlp_sums[0],
        mlp_sums[1],
        mlp_sums[2],
    )


def solution(mesh):
    placed = (
        P("seq", "ctx", None),
        P("seq", None),
        P(),
        P(("seq", "ctx"), "wt"),
        P("wt"),
        P(("seq", "ctx"), "wt"),
        P("wt"),
        P(("seq", "ctx"), "wt"),
        P("wt"),
        P(("seq", "ctx"), "wt"),
        P(),
        P(("seq", "ctx"), "wt"),
        P(("seq", "ctx"), "wt"),
        P(("seq", "ctx"), "wt"),
        P("seq", "ctx", None),
    )
    return jax.shard_map(
        on_device,
        mesh=mesh,
        in_specs=placed,
        out_specs=(
            P("seq", "ctx", None),
            P("seq", "ctx", None),
            P(),
            P(("seq", "ctx"), "wt"),
            P("wt"),
            P(("seq", "ctx"), "wt"),
            P("wt"),
            P(("seq", "ctx"), "wt"),
            P("wt"),
            P(("seq", "ctx"), "wt"),
            P(),
            P(("seq", "ctx"), "wt"),
            P(("seq", "ctx"), "wt"),
            P(("seq", "ctx"), "wt"),
        ),
        check_vma=False,
    )
```

profile of v0, /device:TPU:0, one launch (start us, length us, event | category | flops | bytes accessed | tf_op | source)
XLA Modules:
  0.0 3380.7 jit_solution(7304573719213360956)
XLA Ops:
  12.1 48.0 %all_gather.31 = bf16[1536,128]{1,0:T(8,128)(2,1)S(1)} all-gather(bf16[96,128]{1,0:T(8,128)(2,1)} %param.22), channel_id=1, replica_groups=mesh['seq'=4,'ctx'=4,'wt'=2] {'seq','ctx'}, dimensions={0}, use_global_device_ids=true | all-gather | bytes 417792 | tf_op jit(solution)/shard_map/all_gather | solution.py:117
  63.6 15.5 all-gather
  80.0 41.6 %all_gather.33 = bf16[1536,128]{1,0:T(8,128)(2,1)S(1)} all-gather(bf16[96,128]{1,0:T(8,128)(2,1)S(1)} %copy-done.55), channel_id=1, replica_groups=mesh['seq'=4,'ctx'=4,'wt'=2] {'seq','ctx'}, dimensions={0}, use_global_device_ids=true | all-gather | bytes 417792 | tf_op jit(solution)/shard_map/all_gather | solution.py:118
  122.8 15.4 all-gather.1
  138.2 2.5 convolution_add_fusion.3
  151.6 3.8 fusion.78
  161.9 12.4 all-reduce.6.cloned.1.call-done
  179.4 162.3 %all-gather.12.cloned.1.call-done = bf16[1536,4480]{1,0:T(8,128)(2,1)} async-done(((bf16[96,4480]{1,0:T(8,128)(2,1)}), bf16[1536,4480]{1,0:T(8,128)(2,1)}) %all-gather.12.cloned.1.call-update) | async-done | bytes 13762576 | tf_op jit(solution)/shard_map/all_gather | solution.py:174
  341.7 11.3 fusion.79
  353.0 153.0 %all-gather.14.cloned.1.call-done = bf16[1536,4480]{1,0:T(8,128)(2,1)} async-done(((bf16[96,4480]{1,0:T(8,128)(2,1)}), bf16[1536,4480]{1,0:T(8,128)(2,1)}) %all-gather.14.cloned.1.call-update) | async-done | bytes 13762576 | tf_op jit(solution)/shard_map/all_gather | solution.py:175
  506.1 11.4 fusion.80
  517.4 153.0 %all-gather.16.cloned.1.call-done = bf16[1536,4480]{1,0:T(8,128)(2,1)} async-done(((bf16[96,4480]{1,0:T(8,128)(2,1)}), bf16[1536,4480]{1,0:T(8,128)(2,1)}) %all-gather.16.cloned.1.call-update) | async-done | bytes 13762576 | tf_op jit(solution)/shard_map/all_gather | solution.py:184
  670.4 14.0 multiply_convert_fusion
  684.4 8.7 fusion.82
  693.1 8.5 convolution_add_fusion.2
  701.7 6.8 pad_maximum_fusion
  708.6 8.3 fusion.81
  716.9 3.5 all-reduce.8.cloned.1.call-done
  720.4 3.0 multiply_reduce_fusion.3
  768.0 3.8 fusion.83
  771.7 12.8 reduce-scatter.6.cloned.1.call-done
  788.3 19.0 reduce-scatter.8.cloned.1.call-done
  810.8 2240.9 %while.8 = (s32[]{:T(128)}, f32[15,96,896]{2,1,0:T(8,128)}, s32[15]{0:T(128)S(1)}, bf16[3,256,1536]{2,1,0:T(8,128)(2,1)}, bf16[3,256,4480]{2,1,0:T(8,128)(2,1)},...) while((s32[]{:T(128)}, f32[15,96,896]{2,1,0:T(8,128)}, ...), condition=%wide.region_33.34_spmd, body=%wide.region_31.33_spmd.sunk | while | flops 704643072 | bytes 24987528 | solution.py:295
  813.4 4.7 fusion.145
  818.1 139.5 %reduce-scatter.14.cloned.1.call-done = f32[96,896]{1,0:T(8,128)} async-done(((f32[1536,896]{1,0:T(8,128)}), f32[96,896]{1,0:T(8,128)}) %reduce-scatter.14.cloned.1.call-update) | async-done | bytes 344080 | tf_op jit(solution)/shard_map/while/body/eval_jaxpr/reduce_scatter | solution.py:291
  962.0 4.7 fusion.145
  966.7 140.3 %reduce-scatter.14.cloned.1.call-done = f32[96,896]{1,0:T(8,128)} async-done(((f32[1536,896]{1,0:T(8,128)}), f32[96,896]{1,0:T(8,128)}) %reduce-scatter.14.cloned.1.call-update) | async-done | bytes 344080 | tf_op jit(solution)/shard_map/while/body/eval_jaxpr/reduce_scatter | solution.py:291
  1111.3 4.7 fusion.145
  1116.0 140.5 %reduce-scatter.14.cloned.1.call-done = f32[96,896]{1,0:T(8,128)} async-done(((f32[1536,896]{1,0:T(8,128)}), f32[96,896]{1,0:T(8,128)}) %reduce-scatter.14.cloned.1.call-update) | async-done | bytes 344080 | tf_op jit(solution)/shard_map/while/body/eval_jaxpr/reduce_scatter | solution.py:291
  1260.8 4.7 fusion.145
  1265.5 140.9 %reduce-scatter.14.cloned.1.call-done = f32[96,896]{1,0:T(8,128)} async-done(((f32[1536,896]{1,0:T(8,128)}), f32[96,896]{1,0:T(8,128)}) %reduce-scatter.14.cloned.1.call-update) | async-done | bytes 344080 | tf_op jit(solution)/shard_map/while/body/eval_jaxpr/reduce_scatter | solution.py:291
  1410.7 4.7 fusion.145
  1415.5 140.3 %reduce-scatter.14.cloned.1.call-done = f32[96,896]{1,0:T(8,128)} async-done(((f32[1536,896]{1,0:T(8,128)}), f32[96,896]{1,0:T(8,128)}) %reduce-scatter.14.cloned.1.call-update) | async-done | bytes 344080 | tf_op jit(solution)/shard_map/while/body/eval_jaxpr/reduce_scatter | solution.py:291
  1560.1 4.7 fusion.145
  1564.9 140.5 %reduce-scatter.14.cloned.1.call-done = f32[96,896]{1,0:T(8,128)} async-done(((f32[1536,896]{1,0:T(8,128)}), f32[96,896]{1,0:T(8,128)}) %reduce-scatter.14.cloned.1.call-update) | async-done | bytes 344080 | tf_op jit(solution)/shard_map/while/body/eval_jaxpr/reduce_scatter | solution.py:291
  1709.7 4.7 fusion.145
  1714.4 140.3 %reduce-scatter.14.cloned.1.call-done = f32[96,896]{1,0:T(8,128)} async-done(((f32[1536,896]{1,0:T(8,128)}), f32[96,896]{1,0:T(8,128)}) %reduce-scatter.14.cloned.1.call-update) | async-done | bytes 344080 | tf_op jit(solution)/shard_map/while/body/eval_jaxpr/reduce_scatter | solution.py:291
  1859.0 4.7 fusion.145
  1863.8 140.4 %reduce-scatter.14.cloned.1.call-done = f32[96,896]{1,0:T(8,128)} async-done(((f32[1536,896]{1,0:T(8,128)}), f32[96,896]{1,0:T(8,128)}) %reduce-scatter.14.cloned.1.call-update) | async-done | bytes 344080 | tf_op jit(solution)/shard_map/while/body/eval_jaxpr/reduce_scatter | solution.py:291
  2008.4 4.7 fusion.145
  2013.1 140.3 %reduce-scatter.14.cloned.1.call-done = f32[96,896]{1,0:T(8,128)} async-done(((f32[1536,896]{1,0:T(8,128)}), f32[96,896]{1,0:T(8,128)}) %reduce-scatter.14.cloned.1.call-update) | async-done | bytes 344080 | tf_op jit(solution)/shard_map/while/body/eval_jaxpr/reduce_scatter | solution.py:291
  2157.7 4.7 fusion.145
  2162.5 140.5 %reduce-scatter.14.cloned.1.call-done = f32[96,896]{1,0:T(8,128)} async-done(((f32[1536,896]{1,0:T(8,128)}), f32[96,896]{1,0:T(8,128)}) %reduce-scatter.14.cloned.1.call-update) | async-done | bytes 344080 | tf_op jit(solution)/shard_map/while/body/eval_jaxpr/reduce_scatter | solution.py:291
  2307.2 4.7 fusion.145
  2311.9 140.3 %reduce-scatter.14.cloned.1.call-done = f32[96,896]{1,0:T(8,128)} async-done(((f32[1536,896]{1,0:T(8,128)}), f32[96,896]{1,0:T(8,128)}) %reduce-scatter.14.cloned.1.call-update) | async-done | bytes 344080 | tf_op jit(solution)/shard_map/while/body/eval_jaxpr/reduce_scatter | solution.py:291
  2456.5 4.7 fusion.145
  2461.2 140.6 %reduce-scatter.14.cloned.1.call-done = f32[96,896]{1,0:T(8,128)} async-done(((f32[1536,896]{1,0:T(8,128)}), f32[96,896]{1,0:T(8,128)}) %reduce-scatter.14.cloned.1.call-update) | async-done | bytes 344080 | tf_op jit(solution)/shard_map/while/body/eval_jaxpr/reduce_scatter | solution.py:291
  2606.1 4.7 fusion.145
  2610.8 140.3 %reduce-scatter.14.cloned.1.call-done = f32[96,896]{1,0:T(8,128)} async-done(((f32[1536,896]{1,0:T(8,128)}), f32[96,896]{1,0:T(8,128)}) %reduce-scatter.14.cloned.1.call-update) | async-done | bytes 344080 | tf_op jit(solution)/shard_map/while/body/eval_jaxpr/reduce_scatter | solution.py:291
  2755.5 4.7 fusion.145
  2760.2 140.3 %reduce-scatter.14.cloned.1.call-done = f32[96,896]{1,0:T(8,128)} async-done(((f32[1536,896]{1,0:T(8,128)}), f32[96,896]{1,0:T(8,128)}) %reduce-scatter.14.cloned.1.call-update) | async-done | bytes 344080 | tf_op jit(solution)/shard_map/while/body/eval_jaxpr/reduce_scatter | solution.py:291
  2904.8 4.7 fusion.145
  2909.6 140.5 %reduce-scatter.14.cloned.1.call-done = f32[96,896]{1,0:T(8,128)} async-done(((f32[1536,896]{1,0:T(8,128)}), f32[96,896]{1,0:T(8,128)}) %reduce-scatter.14.cloned.1.call-update) | async-done | bytes 344080 | tf_op jit(solution)/shard_map/while/body/eval_jaxpr/reduce_scatter | solution.py:291
  3052.7 3.8 fusion.44
  3058.0 3.4 fusion.50
  3061.4 7.7 copy.60
  3069.1 6.6 fusion.73
  3075.7 2.9 copy.61
  3078.7 2.9 copy.62
  3081.6 2.9 copy.63
  3086.7 75.7 %all-reduce = (f32[1536]{0:T(1024)}, f32[768]{0:T(1024)}, f32[128]{0:T(128)}, f32[128]{0:T(128)}, f32[1536]{0:T(1024)}) all-reduce(f32[1536]{0:T(1024)S(1)} %get-tuple-element.156, f32[768]{0:T(1024)S(1)} %bitcast.251, f32[128]{0:T(128)S(1)} %get-tuple-element.177, ...), channel_id=1, replica_groups=mesh['seq'=4,'ctx'=4,'wt'=2] {'seq','ctx'}, use_global_device_ids=true, to_apply=%region_20.21 | all-reduce | flops 4096 | bytes 32768 | tf_op jit(solution)/shard_map/psum | solution.py:262
  3162.4 2.7 fusion.34
  3166.4 64.6 %reduce-scatter.10.cloned.1.call-done = f32[96,1024]{1,0:T(8,128)} async-done(((f32[1536,1024]{1,0:T(8,128)}), f32[96,1024]{1,0:T(8,128)}) %reduce-scatter.10.cloned.1.call-update) | async-done | bytes 393232 | tf_op jit(solution)/shard_map/reduce_scatter | solution.py:274
  3234.1 139.3 %reduce-scatter.12.cloned.1.call-done = f32[96,768]{1,0:T(8,128)} async-done(((f32[1536,768]{1,0:T(8,128)}), f32[96,768]{1,0:T(8,128)}) %reduce-scatter.12.cloned.1.call-update) | async-done | bytes 294928 | tf_op jit(solution)/shard_map/reduce_scatter | solution.py:277
  (321 shorter events, 128.2 us)
Async XLA Ops:
  7.2 55.3 %copy-start.67 = (s32[1,4]{1,0:T(1,128)S(1)}, s32[1,4]{1,0:T(1,128)}, u32[]{:S(2)}) copy-start(s32[1,4]{1,0:T(1,128)} %param.18) | copy-start | bytes 52
  7.2 131.0 %all-gather.8.cloned.1.call-start = ((), (), s32[]{:S(2)}) async-start(), calls=%async_computation.5 | async-start | bytes 2506752 | tf_op jit(solution)/shard_map/all_gather | solution.py:116
  7.9 143.6 %all-gather.10.cloned.1.call-start = ((), (), s32[]{:S(2)}) async-start(), calls=%async_computation.6 | async-start | bytes 2506752 | tf_op jit(solution)/shard_map/all_gather | solution.py:119
  8.7 165.7 %all-reduce.6.cloned.1.call-start = ((), (), s32[]{:S(2)}) async-start(), calls=%async_computation.7 | async-start | bytes 3145728 | tf_op jit(solution)/shard_map/psum | solution.py:48
  11.5 68.5 %copy-start.55 = (bf16[96,128]{1,0:T(8,128)(2,1)S(1)}, bf16[96,128]{1,0:T(8,128)(2,1)}, u32[]{:S(2)}) copy-start(bf16[96,128]{1,0:T(8,128)(2,1)} %param.24) | copy-start | bytes 73732
  12.1 126.1 %copy-start.53 = (f32[256]{0:T(256)}, f32[256]{0:T(256)S(1)}, u32[]{:S(2)}) copy-start(f32[256]{0:T(256)S(1)} %get-tuple-element.212) | copy-start | bytes 3076
  60.1 61.5 %copy-start.68 = (bf16[128]{0:T(256)(128)(2,1)S(1)}, bf16[128]{0:T(256)(128)(2,1)}, u32[]{:S(2)}) copy-start(bf16[128]{0:T(256)(128)(2,1)} %param.25) | copy-start | bytes 772
  60.1 62.3 %copy-start.11 = (bf16[1,256,1536]{2,1,0:T(8,128)(2,1)S(1)}, bf16[1,256,1536]{2,1,0:T(8,128)(2,1)}, u32[]{:S(2)}) copy-start(bf16[1,256,1536]{2,1,0:T(8,128)(2,1)} %param.17) | copy-start | bytes 2359300
  63.6 58.0 %copy-start.39 = (f32[256,64]{0,1:T(8,128)}, f32[256,64]{0,1:T(8,128)S(1)}, u32[]{:S(2)}) copy-start(f32[256,64]{0,1:T(8,128)S(1)} %get-tuple-element.210) | copy-start | bytes 196612
  63.6 77.4 %copy-start.35 = (f32[256,128]{0,1:T(8,128)}, f32[256,128]{0,1:T(8,128)S(1)}, u32[]{:S(2)}) copy-start(f32[256,128]{0,1:T(8,128)S(1)} %get-tuple-element.206) | copy-start | bytes 393220
  79.1 656.2 %copy-start.23 = (bf16[1024,128]{0,1:T(8,128)(2,1)}, bf16[1024,128]{0,1:T(8,128)(2,1)S(1)}, u32[]{:S(2)}) copy-start(bf16[1024,128]{0,1:T(8,128)(2,1)S(1)} %all-gather) | copy-start | bytes 786436
  145.2 2.7 copy-start.56
  146.3 2.6 copy-start
  146.3 2.6 copy-start.58
  147.4 2.4 copy-start.3
  147.4 2.4 copy-start.60
  155.4 186.3 %all-gather.12.cloned.1.call-start = ((), (), s32[]{:S(2)}) async-start(), calls=%async_computation.8 | async-start | bytes 14622720 | tf_op jit(solution)/shard_map/all_gather | solution.py:174
  156.0 350.1 %all-gather.14.cloned.1.call-start = ((), (), s32[]{:S(2)}) async-start(), calls=%async_computation.9 | async-start | bytes 14622720 | tf_op jit(solution)/shard_map/all_gather | solution.py:175
  156.5 513.9 %all-gather.16.cloned.1.call-start = ((), (), s32[]{:S(2)}) async-start(), calls=%async_computation.10 | async-start | bytes 14622720 | tf_op jit(solution)/shard_map/all_gather | solution.py:184
  157.1 563.3 %all-reduce.8.cloned.1.call-start = ((), (), s32[]{:S(2)}) async-start(), calls=%async_computation.11 | async-start | bytes 3145728 | tf_op jit(solution)/shard_map/psum | solution.py:48
  684.4 8.7 copy-start.31
  684.4 8.7 copy-start.30
  701.7 82.9 %reduce-scatter.6.cloned.1.call-start = ((), (), s32[]{:S(2)}) async-start(), calls=%async_computation.12 | async-start | bytes 655360 | tf_op jit(solution)/shard_map/reduce_scatter | solution.py:239
  701.7 6.9 copy-start.29
  720.4 3.0 copy-start.7
  720.4 3.0 copy-start.21
  720.4 3.0 copy-start.64
  720.4 3.0 copy-start.66
  723.5 2.9 copy-start.13
  726.4 6.9 copy-start.50
  736.2 3.9 copy-start.51
  740.1 2.4 copy-start.1
  744.0 4.6 copy-start.48
  752.4 2.9 copy-start.22
  755.3 3.2 copy-start.19
  755.3 3.2 copy-start.45
  757.3 2.5 copy-start.17
  757.3 2.5 copy-start.43
  761.6 45.8 %reduce-scatter.8.cloned.1.call-start = ((), (), s32[]{:S(2)}) async-start(), calls=%async_computation.13 | async-start | bytes 655360 | tf_op jit(solution)/shard_map/reduce_scatter | solution.py:240
  767.9 16.6 copy-start.46
  768.0 17.5 copy-start.40
  768.0 18.6 copy-start.33
  810.8 146.8 %reduce-scatter.14.cloned.1.call-start = ((), (), s32[]{:S(2)}) async-start(), calls=%async_computation.17 | async-start | bytes 5849088 | tf_op jit(solution)/shard_map/while/body/eval_jaxpr/reduce_scatter | solution.py:291
  959.4 147.6 %reduce-scatter.14.cloned.1.call-start = ((), (), s32[]{:S(2)}) async-start(), calls=%async_computation.17 | async-start | bytes 5849088 | tf_op jit(solution)/shard_map/while/body/eval_jaxpr/reduce_scatter | solution.py:291
  1108.8 147.8 %reduce-scatter.14.cloned.1.call-start = ((), (), s32[]{:S(2)}) async-start(), calls=%async_computation.17 | async-start | bytes 5849088 | tf_op jit(solution)/shard_map/while/body/eval_jaxpr/reduce_scatter | solution.py:291
  1258.3 148.2 %reduce-scatter.14.cloned.1.call-start = ((), (), s32[]{:S(2)}) async-start(), calls=%async_computation.17 | async-start | bytes 5849088 | tf_op jit(solution)/shard_map/while/body/eval_jaxpr/reduce_scatter | solution.py:291
  1408.2 147.6 %reduce-scatter.14.cloned.1.call-start = ((), (), s32[]{:S(2)}) async-start(), calls=%async_computation.17 | async-start | bytes 5849088 | tf_op jit(solution)/shard_map/while/body/eval_jaxpr/reduce_scatter | solution.py:291
  1557.6 147.8 %reduce-scatter.14.cloned.1.call-start = ((), (), s32[]{:S(2)}) async-start(), calls=%async_computation.17 | async-start | bytes 5849088 | tf_op jit(solution)/shard_map/while/body/eval_jaxpr/reduce_scatter | solution.py:291
  1707.1 147.6 %reduce-scatter.14.cloned.1.call-start = ((), (), s32[]{:S(2)}) async-start(), calls=%async_computation.17 | async-start | bytes 5849088 | tf_op jit(solution)/shard_map/while/body/eval_jaxpr/reduce_scatter | solution.py:291
  1856.5 147.7 %reduce-scatter.14.cloned.1.call-start = ((), (), s32[]{:S(2)}) async-start(), calls=%async_computation.17 | async-start | bytes 5849088 | tf_op jit(solution)/shard_map/while/body/eval_jaxpr/reduce_scatter | solution.py:291
  2005.9 147.6 %reduce-scatter.14.cloned.1.call-start = ((), (), s32[]{:S(2)}) async-start(), calls=%async_computation.17 | async-start | bytes 5849088 | tf_op jit(solution)/shard_map/while/body/eval_jaxpr/reduce_scatter | solution.py:291
  2155.2 147.7 %reduce-scatter.14.cloned.1.call-start = ((), (), s32[]{:S(2)}) async-start(), calls=%async_computation.17 | async-start | bytes 5849088 | tf_op jit(solution)/shard_map/while/body/eval_jaxpr/reduce_scatter | solution.py:291
  2304.7 147.6 %reduce-scatter.14.cloned.1.call-start = ((), (), s32[]{:S(2)}) async-start(), calls=%async_computation.17 | async-start | bytes 5849088 | tf_op jit(solution)/shard_map/while/body/eval_jaxpr/reduce_scatter | solution.py:291
  2454.0 147.9 %reduce-scatter.14.cloned.1.call-start = ((), (), s32[]{:S(2)}) async-start(), calls=%async_computation.17 | async-start | bytes 5849088 | tf_op jit(solution)/shard_map/while/body/eval_jaxpr/reduce_scatter | solution.py:291
  2603.5 147.6 %reduce-scatter.14.cloned.1.call-start = ((), (), s32[]{:S(2)}) async-start(), calls=%async_computation.17 | async-start | bytes 5849088 | tf_op jit(solution)/shard_map/while/body/eval_jaxpr/reduce_scatter | solution.py:291
  2752.9 147.6 %reduce-scatter.14.cloned.1.call-start = ((), (), s32[]{:S(2)}) async-start(), calls=%async_computation.17 | async-start | bytes 5849088 | tf_op jit(solution)/shard_map/while/body/eval_jaxpr/reduce_scatter | solution.py:291
  2902.3 147.7 %reduce-scatter.14.cloned.1.call-start = ((), (), s32[]{:S(2)}) async-start(), calls=%async_computation.17 | async-start | bytes 5849088 | tf_op jit(solution)/shard_map/while/body/eval_jaxpr/reduce_scatter | solution.py:291
  3051.8 32.7 all-reduce.10.cloned.1.call-start
  3052.5 178.5 %reduce-scatter.10.cloned.1.call-start = ((), (), s32[]{:S(2)}) async-start(), calls=%async_computation.14 | async-start | bytes 6684672 | tf_op jit(solution)/shard_map/reduce_scatter | solution.py:274
  3056.5 316.8 %reduce-scatter.12.cloned.1.call-start = ((), (), s32[]{:S(2)}) async-start(), calls=%async_computation.15 | async-start | bytes 5013504 | tf_op jit(solution)/shard_map/reduce_scatter | solution.py:277
  3084.5 77.9 %copy-start.8 = (f32[256,1536]{1,0:T(8,128)S(1)}, f32[256,1536]{1,0:T(8,128)}, u32[]{:S(2)}) copy-start(f32[256,1536]{1,0:T(8,128)} %copy-done.6) | copy-start | bytes 4718596
  3086.6 78.4 %copy-start.65 = (f32[256]{0:T(256)S(1)}, f32[256]{0:T(256)}, u32[]{:S(2)}) copy-start(f32[256]{0:T(256)} %get-tuple-element.211) | copy-start | bytes 3076
  3162.4 2.7 copy-start.12
  3162.4 2.7 copy-start.20
  (32 other events, 49.7 us)
Sparse Core Ops, SparseCore 0:
  10.8 68.5 all-gather.7
  82.1 61.2 all-gather.9
  155.5 18.7 all-reduce.5
  177.3 164.3 all-gather.11
  344.7 161.3 all-gather.13
  509.1 161.3 all-gather.15
  701.8 18.5 all-reduce.7
  761.7 22.8 reduce-scatter.5
  787.4 19.9 reduce-scatter.7
  818.2 139.3 reduce-scatter.13
  966.8 140.1 reduce-scatter.13
  1116.2 140.3 reduce-scatter.13
  1265.7 140.7 reduce-scatter.13
  1415.6 140.1 reduce-scatter.13
  1565.0 140.3 reduce-scatter.13
  1714.5 140.1 reduce-scatter.13
  1863.9 140.2 reduce-scatter.13
  2013.3 140.1 reduce-scatter.13
  2162.6 140.2 reduce-scatter.13
  2312.1 140.1 reduce-scatter.13
  2461.4 140.4 reduce-scatter.13
  2610.9 140.1 reduce-scatter.13
  2760.3 140.1 reduce-scatter.13
  2909.7 140.2 reduce-scatter.13
  3055.0 22.1 all-reduce.9
  3083.1 147.7 reduce-scatter.9
  3237.4 135.9 reduce-scatter.11
where the time goes:
time: 3390 us; the launch traced here: 3380 us
  waiting for transfers between devices  2830 us (83%)
  blocking collectives  196 us (6%)
  matrix products  176 us (5%)
  local copies, waits for them, and re-layouts  85.5 us (3%)
  other arithmetic  47 us (1%)
    reduce_scatter x15, waiting for transfers between devices, one_block(): lax.psum_scatter(inner_rows(left, right), ('seq', 'ctx'), scatter_dimensi...  2110 us
    all_gather x1, waiting for transfers between devices, on_device(): lax.all_gather(w_gate, ('seq', 'ctx'), axis=0, tiled=True)  162 us
    all_gather x1, waiting for transfers between devices, on_device(): lax.all_gather(w_down, ('seq', 'ctx'), axis=0, tiled=True)  153 us
    all_gather x1, waiting for transfers between devices, on_device(): lax.all_gather(w_up, ('seq', 'ctx'), axis=0, tiled=True)  153 us
    reduce_scatter x1, waiting for transfers between devices, on_device(): lax.psum_scatter(inner_rows(g_branch, attn_heads), ('seq', 'ctx'), scatte...  139 us
    dot_general x23, matrix products, inner_rows(): lax.dot_general(left, right, (((0,), (0,)), ((), ())), preferred_element_...  82.3 us
    psum x1, blocking collectives, on_device(): lax.psum((grad_gain_attn, grad_gain_mlp, jnp.sum(g_query_lin.astype(jnp.f...  75.7 us
  transfers between devices with their start and end apart: 27, of which 24 were waited for; matrix products, arithmetic and copies ran while one was open for 4% of the time, Pallas kernels for 0%

commit v1 on v0

v1 whole, which is shorter than its diff:
```python
import jax
import jax.numpy as jnp
from jax import lax
from jax.sharding import PartitionSpec as P

HD = 128
LANES = 128


EPSILON = 1e-06
THETA_BASE = 1000000.0
NEGATIVE = -1e30


def rotate(values):
    middle = values.shape[-1] // 2
    return jnp.concatenate([-values[..., middle:], values[..., :middle]], -1)


def rope_tables(positions):
    freqs = THETA_BASE ** (-(jnp.arange(HD // 2, dtype=jnp.float32) * 2.0) / HD)
    angles = positions.astype(jnp.float32)[:, None] * freqs[None, :]
    cosines = jnp.cos(angles)
    sines = jnp.sin(angles)
    return (jnp.concatenate([cosines, cosines], -1), jnp.concatenate([sines, sines], -1))


def matmul(left, right):
    return jnp.dot(left, right, preferred_element_type=jnp.float32)


def times_transposed(left, right):
    return lax.dot_general(
        left, right, (((1,), (1,)), ((), ())), preferred_element_type=jnp.float32
    )


def inner_rows(left, right):
    return lax.dot_general(
        left, right, (((0,), (0,)), ((), ())), preferred_element_type=jnp.float32
    )


def swap(values, axis, offset):
    size = lax.axis_size(axis)
    return lax.ppermute(values, axis, [(i, i ^ offset) for i in range(size)])


def rows_at(values, index, count):
    return lax.dynamic_slice_in_dim(values, index * count, count, 0)


def place_rows(parts, indices, rows):
    whole = jnp.zeros((rows,) + parts[0].shape[1:], parts[0].dtype)
    for part, index in zip(parts, indices):
        whole = lax.dynamic_update_slice_in_dim(whole, part, index * part.shape[0], 0)
    return whole


def gather_ctx(block):
    size = lax.axis_size("ctx")
    return [block] + [swap(block, "ctx", k) for k in range(1, size)]


def exchange_ctx(pieces):
    return [pieces[0]] + [swap(pieces[k], "ctx", k) for k in range(1, len(pieces))]


def gather_seq(shard):
    size = lax.axis_size("seq")
    if size != 4:
        return lax.all_gather(shard, "seq", axis=0, tiled=True)
    me = lax.axis_index("seq")
    half = shard.shape[0] // 2
    from_x = swap(shard, "seq", 1)
    from_y = swap(shard, "seq", 2)
    far_top = swap(from_y[:half], "seq", 1)
    far_bottom = swap(from_x[half:], "seq", 2)
    far = jnp.concatenate([far_top, far_bottom], 0)
    return place_rows(
        [shard, from_x, from_y, far], [me, me ^ 1, me ^ 2, me ^ 3], size * shard.shape[0]
    )


def scatter_seq(partial_sum):
    size = lax.axis_size("seq")
    if size != 4:
        return lax.psum_scatter(
            partial_sum.astype(jnp.float32), "seq", scatter_dimension=0, tiled=True
        )
    me = lax.axis_index("seq")
    rows = partial_sum.shape[0] // size
    half = rows // 2
    own = rows_at(partial_sum, me, rows)
    for_x = rows_at(partial_sum, me ^ 1, rows)
    for_y = rows_at(partial_sum, me ^ 2, rows)
    for_far = rows_at(partial_sum, me ^ 3, rows)
    got_x = swap(jnp.concatenate([for_far[half:], for_x[half:]], 0), "seq", 1)
    got_y = swap(jnp.concatenate([for_far[:half], for_y[:half]], 0), "seq", 2)
    on_x = (for_x[:half].astype(jnp.float32) + got_y[:half].astype(jnp.float32)).astype(
        jnp.bfloat16
    )
    on_y = (for_y[half:].astype(jnp.float32) + got_x[:half].astype(jnp.float32)).astype(
        jnp.bfloat16
    )
    last_x = swap(on_x, "seq", 1)
    last_y = swap(on_y, "seq", 2)
    top = (
        own[:half].astype(jnp.float32)
        + got_y[half:].astype(jnp.float32)
        + last_x.astype(jnp.float32)
    )
    bottom = (
        own[half:].astype(jnp.float32)
        + got_x[half:].astype(jnp.float32)
        + last_y.astype(jnp.float32)
    )
    return jnp.concatenate([top, bottom], 0)


def add_up(parts):
    total = parts[0].astype(jnp.float32)
    for part in parts[1:]:
        total = total + part.astype(jnp.float32)
    return total


def gather_weight(shard):
    ctx = lax.axis_index("ctx")
    parts = gather_ctx(shard)
    rows = len(parts) * shard.shape[0]
    own = place_rows(parts, [ctx ^ k for k in range(len(parts))], rows)
    return gather_seq(own)


def units_per(units):
    size = lax.axis_size("ctx")
    return -(-units // (size * LANES)) * LANES


def spread_units(shard):
    size = lax.axis_size("ctx")
    ctx = lax.axis_index("ctx")
    width = units_per(shard.shape[1])
    padded = jnp.pad(shard, ((0, 0), (0, size * width - shard.shape[1])))
    pieces = [lax.dynamic_slice_in_dim(padded, (ctx ^ k) * width, width, 1) for k in range(size)]
    parts = exchange_ctx(pieces)
    own = place_rows(parts, [ctx ^ k for k in range(size)], size * shard.shape[0])
    return gather_seq(own)


def collect_units(partial_sum, units):
    size = lax.axis_size("ctx")
    ctx = lax.axis_index("ctx")
    summed = scatter_seq(partial_sum.astype(jnp.bfloat16)).astype(jnp.bfloat16)
    rows, width = summed.shape[0] // size, summed.shape[1]
    parts = exchange_ctx([rows_at(summed, ctx ^ k, rows) for k in range(size)])
    whole = jnp.zeros((rows, size * width), jnp.float32)
    for k in range(size):
        whole = lax.dynamic_update_slice_in_dim(
            whole, parts[k].astype(jnp.float32), (ctx ^ k) * width, 1
        )
    return whole[:, :units]


def scatter_weight(partial_sum):
    size = lax.axis_size("ctx")
    ctx = lax.axis_index("ctx")
    summed = scatter_seq(partial_sum.astype(jnp.bfloat16))
    rows = summed.shape[0] // size
    pieces = [rows_at(summed, ctx ^ k, rows) for k in range(size)]
    return add_up(exchange_ctx([pieces[0]] + [piece.astype(jnp.bfloat16) for piece in pieces[1:]]))


def gather_tokens(half):
    mine = jnp.concatenate(gather_ctx(half), 0)
    return jnp.concatenate([mine, swap(mine, "wt", 1)], 0)


def scatter_tokens(partial_sum):
    size = lax.axis_size("ctx")
    middle = partial_sum.shape[0] // 2
    other = swap(partial_sum[middle:].astype(jnp.bfloat16), "wt", 1)
    chip = partial_sum[:middle] + other.astype(jnp.float32)
    pieces = jnp.split(chip, size, 0)
    return add_up(exchange_ctx([pieces[0]] + [piece.astype(jnp.bfloat16) for piece in pieces[1:]]))


def add_all(values, axes):
    for axis in axes:
        offset = 1
        while offset < lax.axis_size(axis):
            values = values + swap(values, axis, offset)
            offset *= 2
    return values


def norm_back(grad_normed, inputs, inverse_rms, gain):
    weighted = grad_normed * gain
    back = inverse_rms * weighted - inputs * inverse_rms**3 * jnp.mean(
        weighted * inputs, -1, keepdims=True
    )
    gain_grad = jnp.sum(grad_normed * inputs * inverse_rms, 0)
    return (back, gain_grad)


def on_device(
    layer_input,
    pairs,
    gain_attn,
    w_q,
    b_q,
    w_k,
    b_k,
    w_v,
    b_v,
    w_o,
    gain_mlp,
    w_gate,
    w_up,
    w_down,
    out_grad,
):
    _, span_rows, model_width = layer_input.shape
    half_rows = span_rows // 2
    query_cols = w_q.shape[1]
    key_cols = w_k.shape[1]
    heads_here = query_cols // HD
    units_here = w_gate.shape[1]
    ctx_size = lax.axis_size("ctx")
    ctx = lax.axis_index("ctx")
    core = lax.axis_index("wt")
    scale = HD ** (-0.5)

    def own_half(values):
        return rows_at(values, core, half_rows)

    def join_halves(mine):
        other = swap(mine, "wt", 1)
        return jnp.where(
            core == 0, jnp.concatenate([mine, other], 0), jnp.concatenate([other, mine], 0)
        )

    def sum_half(partial_sum):
        return own_half(partial_sum) + swap(rows_at(partial_sum, 1 - core, half_rows), "wt", 1)

    within = jnp.arange(half_rows, dtype=jnp.int32)

    def positions_at(index):
        early = lax.dynamic_index_in_dim(pairs[0], index, 0, False)
        return jnp.concatenate(
            [early * half_rows + within, (2 * ctx_size - 1 - early) * half_rows + within]
        )

    query_positions = positions_at(ctx)
    key_positions = jnp.concatenate([positions_at(ctx ^ k) for k in range(ctx_size)])
    visible = key_positions[None, :] <= query_positions[:, None]
    cosines, sines = rope_tables(query_positions)

    def rope_rows(values):
        return values * cosines[:, None, :] + rotate(values) * sines[:, None, :]

    def unrope_rows(grads):
        return grads * cosines[:, None, :] - rotate(grads * sines[:, None, :])

    input_rows = layer_input.reshape(span_rows, model_width).astype(jnp.float32)
    grad_out = out_grad.reshape(span_rows, model_width)
    gain_one = gain_attn.astype(jnp.float32)
    gain_two = gain_mlp.astype(jnp.float32)

    w_qkv = gather_weight(jnp.concatenate([w_q, w_k, w_v], 1))
    w_out = gather_weight(w_o)
    gate_here = spread_units(w_gate)
    up_here = spread_units(w_up)
    down_here = spread_units(w_down)
    grad_half = own_half(grad_out)
    grad_seq = gather_tokens(grad_half)

    rms_attn = lax.rsqrt(jnp.mean(input_rows * input_rows, -1, keepdims=True) + EPSILON)
    normed_attn = (input_rows * rms_attn * gain_one).astype(jnp.bfloat16)
    bias = jnp.concatenate([b_q, b_k, b_v]).astype(jnp.float32)
    qkv = matmul(normed_attn, w_qkv) + bias
    query = rope_rows(qkv[:, :query_cols].reshape(span_rows, heads_here, HD)).astype(jnp.bfloat16)
    key = rope_rows(qkv[:, query_cols : query_cols + key_cols].reshape(span_rows, 1, HD))
    key_value = jnp.concatenate(
        [key.reshape(span_rows, HD), qkv[:, query_cols + key_cols :]], 1
    ).astype(jnp.bfloat16)
    keys_values = jnp.concatenate(gather_ctx(key_value), 0)
    keys, values = keys_values[:, :HD], keys_values[:, HD:]

    def masked_scores(query_block):
        return jnp.where(visible, times_transposed(query_block, keys) * scale, NEGATIVE)

    heads_out, log_sums = [], []
    for head in range(heads_here):
        scores = masked_scores(query[:, head])
        highest = jnp.max(scores, -1, keepdims=True)
        weights = jnp.exp(scores - highest)
        totals = jnp.sum(weights, -1, keepdims=True)
        heads_out.append(matmul((weights / totals).astype(jnp.bfloat16), values))
        log_sums.append(highest + jnp.log(totals))
    attn_heads = jnp.concatenate(heads_out, 1).astype(jnp.bfloat16)

    input_half = own_half(input_rows)
    hidden = input_half + sum_half(times_transposed(attn_heads, w_out))
    rms_mlp = lax.rsqrt(jnp.mean(hidden * hidden, -1, keepdims=True) + EPSILON)
    normed_half = (hidden * rms_mlp * gain_two).astype(jnp.bfloat16)
    normed_seq = gather_tokens(normed_half)

    gate = matmul(normed_seq, gate_here)
    up = matmul(normed_seq, up_here)
    g_act = matmul(grad_seq, down_here)
    sigmoid_gate = jax.nn.sigmoid(gate)
    silu_gate = gate * sigmoid_gate
    act = (silu_gate * up).astype(jnp.bfloat16)
    g_gate = (g_act * up * sigmoid_gate * (1.0 + gate * (1.0 - sigmoid_gate))).astype(jnp.bfloat16)
    g_up = (g_act * silu_gate).astype(jnp.bfloat16)

    g_normed_mlp = scatter_tokens(
        times_transposed(g_gate, gate_here) + times_transposed(g_up, up_here)
    )
    mlp_out = scatter_tokens(times_transposed(act, down_here))
    layer_output = join_halves((hidden + mlp_out).astype(jnp.bfloat16))
    grad_w_gate = collect_units(inner_rows(normed_seq, g_gate), units_here)
    grad_w_up = collect_units(inner_rows(normed_seq, g_up), units_here)
    grad_w_down = collect_units(inner_rows(grad_seq, act), units_here)

    back_mlp, grad_gain_mlp = norm_back(g_normed_mlp, hidden, rms_mlp, gain_two)
    g_hidden = grad_half.astype(jnp.float32) + back_mlp
    g_branch = join_halves(g_hidden.astype(jnp.bfloat16))
    g_heads = matmul(g_branch, w_out).astype(jnp.bfloat16)

    g_query_parts = []
    g_keys = jnp.zeros(keys.shape, jnp.float32)
    g_values = jnp.zeros(values.shape, jnp.float32)
    for head in range(heads_here):
        grad_block = g_heads[:, head * HD : (head + 1) * HD]
        probs = jnp.exp(masked_scores(query[:, head]) - log_sums[head])
        g_probs = times_transposed(grad_block, values)
        delta = jnp.sum(probs * g_probs, -1, keepdims=True)
        g_scores = (probs * (g_probs - delta)).astype(jnp.bfloat16)
        g_query_parts.append(matmul(g_scores, keys) * scale)
        g_keys = g_keys + inner_rows(g_scores, query[:, head]) * scale
        g_values = g_values + inner_rows(probs.astype(jnp.bfloat16), grad_block)
    g_query = jnp.stack(g_query_parts, 1)
    g_blocks = jnp.split(jnp.concatenate([g_keys, g_values], 1), ctx_size, 0)
    g_key_value = add_up(
        exchange_ctx([g_blocks[0]] + [block.astype(jnp.bfloat16) for block in g_blocks[1:]])
    )
    g_query_lin = unrope_rows(g_query).reshape(span_rows, query_cols)
    g_key_lin = unrope_rows(g_key_value[:, :HD].reshape(span_rows, 1, HD)).reshape(span_rows, HD)
    projected = jnp.concatenate([g_query_lin, g_key_lin, g_key_value[:, HD:]], 1).astype(
        jnp.bfloat16
    )

    g_normed_attn = sum_half(times_transposed(projected, w_qkv))
    back_attn, grad_gain_attn = norm_back(
        g_normed_attn, input_half, own_half(rms_attn), gain_one
    )
    grad_input = join_halves((g_hidden + back_attn).astype(jnp.bfloat16))

    grad_w_o = scatter_weight(inner_rows(g_branch, attn_heads))
    grad_w_qkv = scatter_weight(inner_rows(normed_attn, projected))

    gains = jnp.concatenate([grad_gain_attn, grad_gain_mlp])
    small = jnp.concatenate([gains, jnp.sum(projected.astype(jnp.float32), 0)])
    small = add_all(small.reshape(-1, LANES), ("seq", "ctx")).reshape(-1)
    gains = add_all(small[: 2 * model_width].reshape(-1, LANES), ("wt",)).reshape(-1)
    grad_bias = small[2 * model_width :]
    return (
        layer_output[None],
        grad_input[None],
        gains[:model_width],
        grad_w_qkv[:, :query_cols],
        grad_bias[:query_cols],
        grad_w_qkv[:, query_cols : query_cols + key_cols],
        grad_bias[query_cols : query_cols + key_cols],
        grad_w_qkv[:, query_cols + key_cols :],
        grad_bias[query_cols + key_cols :],
        grad_w_o,
        gains[model_width:],
        grad_w_gate,
        grad_w_up,
        grad_w_down,
    )


def solution(mesh):
    tokens = P("seq", "ctx", None)
    weight = P(("seq", "ctx"), "wt")
    return jax.shard_map(
        on_device,
        mesh=mesh,
        in_specs=(
            tokens,
            P("seq", None),
            P(),
            weight,
            P("wt"),
            weight,
            P("wt"),
            weight,
            P("wt"),
            weight,
            P(),
            weight,
            weight,
            weight,
            tokens,
        ),
        out_specs=(
            tokens,
            tokens,
            P(),
            weight,
            P("wt"),
            weight,
            P("wt"),
            weight,
            P("wt"),
            weight,
            P(),
            weight,
            weight,
            weight,
        ),
        check_vma=False,
    )
```

time: 3390 us -> 709 us (0.21)
  waiting for transfers between devices: 2830 us -> 303 us
  blocking collectives: 196 us -> 0 us
  starting transfers between devices: 0.91 us -> 181 us
  matrix products: 176 us -> 98.5 us
    reduce_scatter x19 -> x0, waiting for transfers between devices: 2340 us -> none  [the longest x15 2110 us: one_block(): lax.psum_scatter(inner_rows(left, right), ('seq', 'ctx'), scatter_dimensi...]
    all_gather x5 -> x0, waiting for transfers between devices: 468 us -> none  [the longest x1 162 us: on_device(): lax.all_gather(w_gate, ('seq', 'ctx'), axis=0, tiled=True)]
    ppermute x0 -> x102, waiting for transfers between devices: none -> 303 us  [swap(): return lax.ppermute(values, axis, [(i, i ^ offset) for i in range(size)])]
    ppermute x0 -> x102, starting transfers between devices: none -> 181 us  [swap(): return lax.ppermute(values, axis, [(i, i ^ offset) for i in range(size)])]
    all_gather x4 -> x0, blocking collectives: 120 us -> none  [the longest x1 48 us: on_device(): lax.all_gather(w_k, ('seq', 'ctx'), axis=0, tiled=True)]
    psum x1 -> x0, blocking collectives: 75.7 us -> none  [on_device(): lax.psum((grad_gain_attn, grad_gain_mlp, jnp.sum(g_query_lin.astype(jnp.f...]
    dot_general x23 -> x17, matrix products: 82.3 us -> 34.5 us  [inner_rows(): lax.dot_general(left, right, (((0,), (0,)), ((), ())), preferred_element_...]
  transfers between devices with their start and end apart: 27 -> 102, of which waited for: 24 -> 39; matrix products, arithmetic and copies ran while one was open for 4% -> 21% of each run, Pallas kernels for 0% -> 0%
where the time goes in v1:
time: 709 us; the launch traced here: 699 us
  waiting for transfers between devices  303 us (43%)
  starting transfers between devices  181 us (26%)
  matrix products  98.5 us (14%)
  local copies, waits for them, and re-layouts  54.1 us (8%)
  other arithmetic  53.4 us (8%)
  between operations  8.71 us (1%)
    ppermute x102, waiting for transfers between devices, swap(): return lax.ppermute(values, axis, [(i, i ^ offset) for i in range(size)])  303 us
    ppermute x102, starting transfers between devices, swap(): return lax.ppermute(values, axis, [(i, i ^ offset) for i in range(size)])  181 us
    dot_general x17, matrix products, inner_rows(): lax.dot_general(left, right, (((0,), (0,)), ((), ())), preferred_element_...  34.5 us
    dot_general x17, matrix products, times_transposed(): lax.dot_general(left, right, (((1,), (1,)), ((), ())), preferred_element_...  33.9 us
    dot_general x17, matrix products, matmul(): return jnp.dot(left, right, preferred_element_type=jnp.float32)  30.1 us
  transfers between devices with their start and end apart: 102, of which 39 were waited for; matrix products, arithmetic and copies ran while one was open for 21% of the time, Pallas kernels for 0%

profile of v1, /device:TPU:0, one launch (start us, length us, event | category | flops | bytes accessed | tf_op | source)
XLA Modules:
  0.0 698.6 jit_solution(1411386143532415324)
XLA Ops:
  5.0 3.0 collective-permute-start
  8.0 2.6 collective-permute-start.1
  11.5 3.5 collective-permute-start.11
  26.5 2.2 pad_dynamic-slice_fusion.44
  28.8 2.1 pad_dynamic-slice_fusion.40
  38.1 6.4 collective-permute-done.12
  46.6 2.8 collective-permute-start.29
  52.8 17.5 %collective-permute-done.29 = bf16[96,1152]{1,0:T(8,128)(2,1)S(1)} collective-permute-done((bf16[96,1152]{1,0:T(8,128)(2,1)S(1)}, bf16[96,1152]{1,0:T(8,128)(2,1)S(1)}, u32[]{:S(2)}, u32[]{:S(2)}) %collective-permute-start.29) | collective-permute-done | bytes 221216 | tf_op jit(solution)/shard_map/ppermute | solution.py:46
  70.3 3.8 collective-permute-start.31
  74.1 21.8 %collective-permute-done.30 = bf16[96,1152]{1,0:T(8,128)(2,1)S(1)} collective-permute-done((bf16[96,1152]{1,0:T(8,128)(2,1)S(1)}, bf16[96,1152]{1,0:T(8,128)(2,1)S(1)}, u32[]{:S(2)}, u32[]{:S(2)}) %collective-permute-start.30) | collective-permute-done | bytes 221216 | tf_op jit(solution)/shard_map/ppermute | solution.py:46
  96.0 8.9 %collective-permute-start.37 = (bf16[96,1152]{1,0:T(8,128)(2,1)S(1)}, bf16[96,1152]{1,0:T(8,128)(2,1)S(1)}, u32[]{:S(2)}, u32[]{:S(2)}) collective-permute-start(bf16[96,1152]{1,0:T(8,128)(2,1)S(1)} %copy-done.40), channel_id=1, source_target_pairs={{0,4},{2,6},{4,0},{6,2},{1,5},{3,7},{5,1},{7,3},{8,12},{10,14},{12... | collective-permute-start | bytes 663560 | tf_op jit(solution)/shard_map/ppermute | solution.py:46
  105.9 3.3 collective-permute-start.38
  109.3 11.0 %collective-permute-done.37 = bf16[96,1152]{1,0:T(8,128)(2,1)S(1)} collective-permute-done((bf16[96,1152]{1,0:T(8,128)(2,1)S(1)}, bf16[96,1152]{1,0:T(8,128)(2,1)S(1)}, u32[]{:S(2)}, u32[]{:S(2)}) %collective-permute-start.37) | collective-permute-done | bytes 221216 | tf_op jit(solution)/shard_map/ppermute | solution.py:46
  121.1 6.6 collective-permute-start.23
  128.6 3.5 collective-permute-start.24
  146.4 6.3 collective-permute-done.14
  155.9 12.2 %collective-permute-done.4 = bf16[384,1024]{1,0:T(8,128)(2,1)S(1)} collective-permute-done((bf16[384,1024]{1,0:T(8,128)(2,1)S(1)}, bf16[384,1024]{1,0:T(8,128)(2,1)S(1)}, u32[]{:S(2)}, u32[]{:S(2)}) %collective-permute-start.4) | collective-permute-done | bytes 786464 | tf_op jit(solution)/shard_map/ppermute | solution.py:46
  170.0 22.3 %collective-permute-done.15 = bf16[192,768]{1,0:T(8,128)(2,1)S(1)} collective-permute-done((bf16[192,768]{1,0:T(8,128)(2,1)S(1)}, bf16[192,768]{1,0:T(8,128)(2,1)S(1)}, u32[]{:S(2)}, u32[]{:S(2)}) %collective-permute-start.15) | collective-permute-done | bytes 294944 | tf_op jit(solution)/shard_map/ppermute | solution.py:46
  199.5 11.8 %collective-permute-done.39 = bf16[384,1152]{1,0:T(8,128)(2,1)S(1)} collective-permute-done((bf16[384,1152]{1,0:T(8,128)(2,1)S(1)}, bf16[384,1152]{1,0:T(8,128)(2,1)S(1)}, u32[]{:S(2)}, u32[]{:S(2)}) %collective-permute-start.39) | collective-permute-done | bytes 884768 | tf_op jit(solution)/shard_map/ppermute | solution.py:46
  216.6 8.6 %collective-permute-done.25 = bf16[384,1152]{1,0:T(8,128)(2,1)S(1)} collective-permute-done((bf16[384,1152]{1,0:T(8,128)(2,1)}, bf16[384,1152]{1,0:T(8,128)(2,1)S(1)}, u32[]{:S(2)}, u32[]{:S(2)}) %collective-permute-start.25) | collective-permute-done | bytes 884768 | tf_op jit(solution)/shard_map/ppermute | solution.py:46
  235.6 3.3 collective-permute-start.7
  247.1 2.5 collective-permute-start.41
  273.0 5.4 collective-permute-done.27
  278.3 2.3 collective-permute-start.20
  280.9 7.2 %collective-permute-done.18 = bf16[128,1536]{1,0:T(8,128)(2,1)S(1)} collective-permute-done((bf16[128,1536]{1,0:T(8,128)(2,1)S(1)}, bf16[128,1536]{1,0:T(8,128)(2,1)S(1)}, u32[]{:S(2)}, u32[]{:S(2)}) %collective-permute-start.18) | collective-permute-done | bytes 393248 | tf_op jit(solution)/shard_map/ppermute | solution.py:46
  288.1 13.6 %collective-permute-done.19 = bf16[128,1536]{1,0:T(8,128)(2,1)S(1)} collective-permute-done((bf16[128,1536]{1,0:T(8,128)(2,1)S(1)}, bf16[128,1536]{1,0:T(8,128)(2,1)S(1)}, u32[]{:S(2)}, u32[]{:S(2)}) %collective-permute-start.19) | collective-permute-done | bytes 393248 | tf_op jit(solution)/shard_map/ppermute | solution.py:46
  301.8 5.9 fusion.176
  309.6 5.9 fusion.174
  315.4 12.0 %multiply_convert_fusion.1 = (bf16[1024,1152]{1,0:T(8,128)(2,1)}, bf16[1024,1152]{1,0:T(8,128)(2,1)}, bf16[1024,1152]{1,0:T(8,128)(2,1)}) fusion(f32[1024,1152]{1,0:T(8,128)} %fusion.176, f32[1024,1152]{1,0:T(8,128)} %fusion.174, bf16[1024,1536]{1,0:T(8,128)(2,1)} %copy-done.53, bf16[1536,1152]{1,0:T(8,128)(2,1)S(1)} %maximum_dynamic-update-slice_fusion), kind=kOutput, calls=%fused_computation.4 | convolution fusion | flops 3641573376 | bytes 23199744 | tf_op jit(solution)/shard_map/dot_general | solution.py:29
  327.4 7.0 %convolution_convert_fusion.1 = bf16[1536,1152]{1,0:T(8,128)(2,1)S(1)} fusion(bf16[1024,1536]{1,0:T(8,128)(2,1)} %copy-done.53, bf16[1024,1152]{1,0:T(8,128)(2,1)} %get-tuple-element.34), kind=kOutput, calls=%fused_computation.1 | convolution fusion | flops 3625648128 | bytes 9043968 | tf_op jit(solution)/shard_map/dot_general | solution.py:39
  334.5 6.3 fusion.177
  340.8 16.2 %convolution_convert_fusion = bf16[1536,1152]{1,0:T(8,128)(2,1)S(1)} fusion(bf16[1024,1536]{1,0:T(8,128)(2,1)S(1)} %constant_dynamic-update-slice_fusion.9, bf16[1024,1152]{1,0:T(8,128)(2,1)S(1)} %copy-done.74), kind=kOutput, calls=%fused_computation | convolution fusion | flops 3625648128 | bytes 9043968 | tf_op jit(solution)/shard_map/dot_general | solution.py:39
  364.8 4.5 convolution_convert_fusion.2
  370.9 8.9 %convolution_add_fusion = f32[1024,1536]{1,0:T(8,128)} fusion(f32[1024,1536]{1,0:T(8,128)} %fusion.177, bf16[1024,1152]{1,0:T(8,128)(2,1)} %get-tuple-element.33, bf16[1536,1152]{1,0:T(8,128)(2,1)S(1)} %maximum_dynamic-update-slice_fusion), kind=kOutput, calls=%fused_computation.8 | convolution fusion | flops 3625451520 | bytes 18481152 | tf_op jit(solution)/shard_map/dot_general | solution.py:33
  379.8 9.8 %fusion.175 = f32[1024,1536]{1,0:T(8,128)} fusion(bf16[1024,1152]{1,0:T(8,128)(2,1)} %get-tuple-element.35, bf16[1536,1152]{1,0:T(8,128)(2,1)} %copy-done.12), kind=kOutput, calls=%fused_computation.500 | convolution fusion | flops 3623878656 | bytes 12189696 | tf_op jit(solution)/shard_map/dot_general | solution.py:33
  389.6 2.1 slice.704
  394.6 6.8 collective-permute-done.90
  402.5 17.1 %collective-permute-done.83 = bf16[384,1152]{1,0:T(8,128)(2,1)S(1)} collective-permute-done((bf16[384,1152]{1,0:T(8,128)(2,1)S(1)}, bf16[384,1152]{1,0:T(8,128)(2,1)S(1)}, u32[]{:S(2)}, u32[]{:S(2)}) %collective-permute-start.83) | collective-permute-done | bytes 884768 | tf_op jit(solution)/shard_map/ppermute | solution.py:46
  421.6 9.6 %collective-permute-done.98 = bf16[192,1152]{1,0:T(8,128)(2,1)S(1)} collective-permute-done((bf16[192,1152]{1,0:T(8,128)(2,1)S(1)}, bf16[192,1152]{1,0:T(8,128)(2,1)S(1)}, u32[]{:S(2)}, u32[]{:S(2)}) %collective-permute-start.98) | collective-permute-done | bytes 442400 | tf_op jit(solution)/shard_map/ppermute | solution.py:46
  432.8 2.2 add_convert_fusion
  435.4 8.9 %collective-permute-done.91 = bf16[192,1152]{1,0:T(8,128)(2,1)S(1)} collective-permute-done((bf16[192,1152]{1,0:T(8,128)(2,1)S(1)}, bf16[192,1152]{1,0:T(8,128)(2,1)S(1)}, u32[]{:S(2)}, u32[]{:S(2)}) %collective-permute-start.91) | collective-permute-done | bytes 442400 | tf_op jit(solution)/shard_map/ppermute | solution.py:46
  447.8 3.5 collective-permute-done.84
  453.4 2.5 fusion.162
  456.0 7.4 %collective-permute-start.44 = (bf16[128,1536]{1,0:T(8,128)(2,1)S(1)}, bf16[128,1536]{1,0:T(8,128)(2,1)S(1)}, u32[]{:S(2)}, u32[]{:S(2)}) collective-permute-start(bf16[128,1536]{1,0:T(8,128)(2,1)S(1)} %get-tuple-element.72), channel_id=1, source_target_pairs={{0,2},{2,0},{4,6},{6,4},{1,3},{3,1},{5,7},{7,5},{8,10},{10,8},{12,... | collective-permute-start | bytes 1179656 | tf_op jit(solution)/shard_map/ppermute | solution.py:46
  470.1 3.8 collective-permute-start.54
  480.0 13.9 %collective-permute-done.53 = bf16[128,1536]{1,0:T(8,128)(2,1)S(1)} collective-permute-done((bf16[128,1536]{1,0:T(8,128)(2,1)S(1)}, bf16[128,1536]{1,0:T(8,128)(2,1)S(1)}, u32[]{:S(2)}, u32[]{:S(2)}) %collective-permute-start.53) | collective-permute-done | bytes 393248 | tf_op jit(solution)/shard_map/ppermute | solution.py:46
  494.0 2.1 collective-permute-start.46
  496.0 21.4 %collective-permute-done.54 = bf16[128,1536]{1,0:T(8,128)(2,1)S(1)} collective-permute-done((bf16[128,1536]{1,0:T(8,128)(2,1)S(1)}, bf16[128,1536]{1,0:T(8,128)(2,1)S(1)}, u32[]{:S(2)}, u32[]{:S(2)}) %collective-permute-start.54) | collective-permute-done | bytes 393248 | tf_op jit(solution)/shard_map/ppermute | solution.py:46
  518.1 15.1 %collective-permute-start.100 = (bf16[96,1152]{1,0:T(8,128)(2,1)S(1)}, bf16[96,1152]{1,0:T(8,128)(2,1)S(1)}, u32[]{:S(2)}, u32[]{:S(2)}) collective-permute-start(bf16[96,1152]{1,0:T(8,128)(2,1)S(1)} %get-tuple-element.80), channel_id=1, source_target_pairs={{0,4},{2,6},{4,0},{6,2},{1,5},{3,7},{5,1},{7,3},{8,12},{10,14},{12... | collective-permute-start | bytes 663560 | tf_op jit(solution)/shard_map/ppermute | solution.py:46
  534.7 16.4 %collective-permute-start.93 = (bf16[96,1152]{1,0:T(8,128)(2,1)S(1)}, bf16[96,1152]{1,0:T(8,128)(2,1)S(1)}, u32[]{:S(2)}, u32[]{:S(2)}) collective-permute-start(bf16[96,1152]{1,0:T(8,128)(2,1)S(1)} %get-tuple-element.83), channel_id=1, source_target_pairs={{0,4},{2,6},{4,0},{6,2},{1,5},{3,7},{5,1},{7,3},{8,12},{10,14},{12... | collective-permute-start | bytes 663560 | tf_op jit(solution)/shard_map/ppermute | solution.py:46
  552.1 10.6 %collective-permute-done.100 = bf16[96,1152]{1,0:T(8,128)(2,1)S(1)} collective-permute-done((bf16[96,1152]{1,0:T(8,128)(2,1)S(1)}, bf16[96,1152]{1,0:T(8,128)(2,1)S(1)}, u32[]{:S(2)}, u32[]{:S(2)}) %collective-permute-start.100) | collective-permute-done | bytes 221216 | tf_op jit(solution)/shard_map/ppermute | solution.py:46
  562.8 7.3 %collective-permute-start.86 = (bf16[96,1152]{1,0:T(8,128)(2,1)S(1)}, bf16[96,1152]{1,0:T(8,128)(2,1)S(1)}, u32[]{:S(2)}, u32[]{:S(2)}) collective-permute-start(bf16[96,1152]{1,0:T(8,128)(2,1)S(1)} %get-tuple-element.86), channel_id=1, source_target_pairs={{0,4},{2,6},{4,0},{6,2},{1,5},{3,7},{5,1},{7,3},{8,12},{10,14},{12... | collective-permute-start | bytes 663560 | tf_op jit(solution)/shard_map/ppermute | solution.py:46
  570.7 3.9 collective-permute-done.93
  575.5 10.4 %collective-permute-done.86 = bf16[96,1152]{1,0:T(8,128)(2,1)S(1)} collective-permute-done((bf16[96,1152]{1,0:T(8,128)(2,1)S(1)}, bf16[96,1152]{1,0:T(8,128)(2,1)S(1)}, u32[]{:S(2)}, u32[]{:S(2)}) %collective-permute-start.86) | collective-permute-done | bytes 221216 | tf_op jit(solution)/shard_map/ppermute | solution.py:46
  606.9 2.7 collective-permute-start.58
  613.4 3.5 collective-permute-done.58
  617.9 3.0 fusion.158
  628.4 6.5 collective-permute-done.77
  636.8 6.3 collective-permute-done.62
  645.4 6.7 collective-permute-done.63
  655.9 3.0 collective-permute-start.65
  670.4 4.0 collective-permute-done.68
  681.7 3.8 collective-permute-done.71
  685.5 11.1 %collective-permute-done.72 = bf16[96,1024]{1,0:T(8,128)(2,1)S(1)} collective-permute-done((bf16[96,1024]{1,0:T(8,128)(2,1)S(1)}, bf16[96,1024]{1,0:T(8,128)(2,1)S(1)}, u32[]{:S(2)}, u32[]{:S(2)}) %collective-permute-start.72) | collective-permute-done | bytes 196640 | tf_op jit(solution)/shard_map/ppermute | solution.py:46
  (567 shorter events, 203.3 us)
Async XLA Ops:
  5.0 39.8 %collective-permute-start = (bf16[96,1024]{1,0:T(8,128)(2,1)}, bf16[96,1024]{1,0:T(8,128)(2,1)}, u32[]{:S(2)}, u32[]{:S(2)}) collective-permute-start(bf16[96,1024]{1,0:T(8,128)(2,1)} %constant_dynamic-update-slice_fusion.1), channel_id=1, source_target_pairs={{0,2},{2,0},{4,6},{6,4},{1,3},{3,1},{5,7},{7,5},{8,10},{10,8},{12,... | collective-permute-start | bytes 589832 | tf_op jit(solution)/shard_map/ppermute | solution.py:46
  8.0 38.6 %collective-permute-start.1 = (bf16[96,1024]{1,0:T(8,128)(2,1)}, bf16[96,1024]{1,0:T(8,128)(2,1)}, u32[]{:S(2)}, u32[]{:S(2)}) collective-permute-start(bf16[96,1024]{1,0:T(8,128)(2,1)} %constant_dynamic-update-slice_fusion.1), channel_id=1, source_target_pairs={{0,4},{2,6},{4,0},{6,2},{1,5},{3,7},{5,1},{7,3},{8,12},{10,14},{12... | collective-permute-start | bytes 589832 | tf_op jit(solution)/shard_map/ppermute | solution.py:46
  10.6 39.7 %collective-permute-start.2 = (bf16[96,1024]{1,0:T(8,128)(2,1)}, bf16[96,1024]{1,0:T(8,128)(2,1)}, u32[]{:S(2)}, u32[]{:S(2)}) collective-permute-start(bf16[96,1024]{1,0:T(8,128)(2,1)} %constant_dynamic-update-slice_fusion.1), channel_id=1, source_target_pairs={{0,6},{2,4},{4,2},{6,0},{1,7},{3,5},{5,3},{7,1},{8,14},{10,12},{12... | collective-permute-start | bytes 589832 | tf_op jit(solution)/shard_map/ppermute | solution.py:46
  10.6 25.0 %collective-permute-start.10 = (bf16[96,768]{1,0:T(8,128)(2,1)}, bf16[96,768]{1,0:T(8,128)(2,1)}, u32[]{:S(2)}, u32[]{:S(2)}) collective-permute-start(bf16[96,768]{1,0:T(8,128)(2,1)} %param.24), channel_id=1, source_target_pairs={{0,2},{2,0},{4,6},{6,4},{1,3},{3,1},{5,7},{7,5},{8,10},{10,8},{12,... | collective-permute-start | bytes 442376 | tf_op jit(solution)/shard_map/ppermute | solution.py:46
  11.5 25.2 %collective-permute-start.11 = (bf16[96,768]{1,0:T(8,128)(2,1)}, bf16[96,768]{1,0:T(8,128)(2,1)}, u32[]{:S(2)}, u32[]{:S(2)}) collective-permute-start(bf16[96,768]{1,0:T(8,128)(2,1)} %param.24), channel_id=1, source_target_pairs={{0,4},{2,6},{4,0},{6,2},{1,5},{3,7},{5,1},{7,3},{8,12},{10,14},{12... | collective-permute-start | bytes 442376 | tf_op jit(solution)/shard_map/ppermute | solution.py:46
  36.7 103.6 %collective-permute-start.48 = (bf16[128,1536]{1,0:T(8,128)(2,1)S(1)}, bf16[128,1536]{1,0:T(8,128)(2,1)S(1)}, u32[]{:S(2)}, u32[]{:S(2)}) collective-permute-start(bf16[128,1536]{1,0:T(8,128)(2,1)S(1)} %get-tuple-element.26), channel_id=1, source_target_pairs={{0,2},{2,0},{4,6},{6,4},{1,3},{3,1},{5,7},{7,5},{8,10},{10,8},{12,... | collective-permute-start | bytes 1179656 | tf_op jit(solution)/shard_map/ppermute | solution.py:46
  44.6 97.3 %collective-permute-start.49 = (bf16[128,1536]{1,0:T(8,128)(2,1)S(1)}, bf16[128,1536]{1,0:T(8,128)(2,1)S(1)}, u32[]{:S(2)}, u32[]{:S(2)}) collective-permute-start(bf16[128,1536]{1,0:T(8,128)(2,1)S(1)} %get-tuple-element.26), channel_id=1, source_target_pairs={{0,4},{2,6},{4,0},{6,2},{1,5},{3,7},{5,1},{7,3},{8,12},{10,14},{12... | collective-permute-start | bytes 1179656 | tf_op jit(solution)/shard_map/ppermute | solution.py:46
  44.8 97.6 %collective-permute-start.50 = (bf16[128,1536]{1,0:T(8,128)(2,1)S(1)}, bf16[128,1536]{1,0:T(8,128)(2,1)S(1)}, u32[]{:S(2)}, u32[]{:S(2)}) collective-permute-start(bf16[128,1536]{1,0:T(8,128)(2,1)S(1)} %get-tuple-element.26), channel_id=1, source_target_pairs={{0,6},{2,4},{4,2},{6,0},{1,7},{3,5},{5,3},{7,1},{8,14},{10,12},{12... | collective-permute-start | bytes 1179656 | tf_op jit(solution)/shard_map/ppermute | solution.py:46
  46.6 23.7 %collective-permute-start.29 = (bf16[96,1152]{1,0:T(8,128)(2,1)S(1)}, bf16[96,1152]{1,0:T(8,128)(2,1)S(1)}, u32[]{:S(2)}, u32[]{:S(2)}) collective-permute-start(bf16[96,1152]{1,0:T(8,128)(2,1)S(1)} %copy-done.44), channel_id=1, source_target_pairs={{0,2},{2,0},{4,6},{6,4},{1,3},{3,1},{5,7},{7,5},{8,10},{10,8},{12,... | collective-permute-start | bytes 663560 | tf_op jit(solution)/shard_map/ppermute | solution.py:46
  50.4 45.6 %collective-permute-start.30 = (bf16[96,1152]{1,0:T(8,128)(2,1)S(1)}, bf16[96,1152]{1,0:T(8,128)(2,1)S(1)}, u32[]{:S(2)}, u32[]{:S(2)}) collective-permute-start(bf16[96,1152]{1,0:T(8,128)(2,1)S(1)} %copy-done.43), channel_id=1, source_target_pairs={{0,4},{2,6},{4,0},{6,2},{1,5},{3,7},{5,1},{7,3},{8,12},{10,14},{12... | collective-permute-start | bytes 663560 | tf_op jit(solution)/shard_map/ppermute | solution.py:46
  70.3 25.7 %collective-permute-start.31 = (bf16[96,1152]{1,0:T(8,128)(2,1)S(1)}, bf16[96,1152]{1,0:T(8,128)(2,1)S(1)}, u32[]{:S(2)}, u32[]{:S(2)}) collective-permute-start(bf16[96,1152]{1,0:T(8,128)(2,1)S(1)} %copy-done.42), channel_id=1, source_target_pairs={{0,6},{2,4},{4,2},{6,0},{1,7},{3,5},{5,3},{7,1},{8,14},{10,12},{12... | collective-permute-start | bytes 663560 | tf_op jit(solution)/shard_map/ppermute | solution.py:46
  96.0 24.3 %collective-permute-start.37 = (bf16[96,1152]{1,0:T(8,128)(2,1)S(1)}, bf16[96,1152]{1,0:T(8,128)(2,1)S(1)}, u32[]{:S(2)}, u32[]{:S(2)}) collective-permute-start(bf16[96,1152]{1,0:T(8,128)(2,1)S(1)} %copy-done.40), channel_id=1, source_target_pairs={{0,4},{2,6},{4,0},{6,2},{1,5},{3,7},{5,1},{7,3},{8,12},{10,14},{12... | collective-permute-start | bytes 663560 | tf_op jit(solution)/shard_map/ppermute | solution.py:46
  134.0 20.3 %collective-permute-start.13 = (bf16[384,768]{1,0:T(8,128)(2,1)S(1)}, bf16[384,768]{1,0:T(8,128)(2,1)S(1)}, u32[]{:S(2)}, u32[]{:S(2)}) collective-permute-start(bf16[384,768]{1,0:T(8,128)(2,1)S(1)} %constant_dynamic-update-slice_fusion.35), channel_id=1, source_target_pairs={{0,8},{8,0},{16,24},{24,16},{1,9},{9,1},{17,25},{25,17},{2,10},{10... | collective-permute-start | bytes 1769480 | tf_op jit(solution)/shard_map/ppermute | solution.py:46
  140.3 29.5 %collective-permute-start.3 = (bf16[384,1024]{1,0:T(8,128)(2,1)S(1)}, bf16[384,1024]{1,0:T(8,128)(2,1)S(1)}, u32[]{:S(2)}, u32[]{:S(2)}) collective-permute-start(bf16[384,1024]{1,0:T(8,128)(2,1)S(1)} %constant_dynamic-update-slice_fusion.42), channel_id=1, source_target_pairs={{0,8},{8,0},{16,24},{24,16},{1,9},{9,1},{17,25},{25,17},{2,10},{10... | collective-permute-start | bytes 2359304 | tf_op jit(solution)/shard_map/ppermute | solution.py:46
  141.9 26.3 %collective-permute-start.4 = (bf16[384,1024]{1,0:T(8,128)(2,1)S(1)}, bf16[384,1024]{1,0:T(8,128)(2,1)S(1)}, u32[]{:S(2)}, u32[]{:S(2)}) collective-permute-start(bf16[384,1024]{1,0:T(8,128)(2,1)S(1)} %constant_dynamic-update-slice_fusion.42), channel_id=1, source_target_pairs={{0,16},{8,24},{16,0},{24,8},{1,17},{9,25},{17,1},{25,9},{2,18},{10... | collective-permute-start | bytes 2359304 | tf_op jit(solution)/shard_map/ppermute | solution.py:46
  142.4 53.1 %collective-permute-start.32 = (bf16[384,1152]{1,0:T(8,128)(2,1)S(1)}, bf16[384,1152]{1,0:T(8,128)(2,1)S(1)}, u32[]{:S(2)}, u32[]{:S(2)}) collective-permute-start(bf16[384,1152]{1,0:T(8,128)(2,1)S(1)} %constant_dynamic-update-slice_fusion.23), channel_id=1, source_target_pairs={{0,8},{8,0},{16,24},{24,16},{1,9},{9,1},{17,25},{25,17},{2,10},{10... | collective-permute-start | bytes 2654216 | tf_op jit(solution)/shard_map/ppermute | solution.py:46
  152.7 43.4 %collective-permute-start.33 = (bf16[384,1152]{1,0:T(8,128)(2,1)S(1)}, bf16[384,1152]{1,0:T(8,128)(2,1)S(1)}, u32[]{:S(2)}, u32[]{:S(2)}) collective-permute-start(bf16[384,1152]{1,0:T(8,128)(2,1)S(1)} %constant_dynamic-update-slice_fusion.23), channel_id=1, source_target_pairs={{0,16},{8,24},{16,0},{24,8},{1,17},{9,25},{17,1},{25,9},{2,18},{10... | collective-permute-start | bytes 2654216 | tf_op jit(solution)/shard_map/ppermute | solution.py:46
  154.3 38.1 %collective-permute-start.15 = (bf16[192,768]{1,0:T(8,128)(2,1)S(1)}, bf16[192,768]{1,0:T(8,128)(2,1)S(1)}, u32[]{:S(2)}, u32[]{:S(2)}) collective-permute-start(bf16[192,768]{1,0:T(8,128)(2,1)S(1)} %slice.511), channel_id=1, source_target_pairs={{0,8},{8,0},{16,24},{24,16},{1,9},{9,1},{17,25},{25,17},{2,10},{10... | collective-permute-start | bytes 884744 | tf_op jit(solution)/shard_map/ppermute | solution.py:46
  168.1 25.7 %collective-permute-start.16 = (bf16[192,768]{1,0:T(8,128)(2,1)S(1)}, bf16[192,768]{1,0:T(8,128)(2,1)S(1)}, u32[]{:S(2)}, u32[]{:S(2)}) collective-permute-start(bf16[192,768]{1,0:T(8,128)(2,1)S(1)} %slice.512), channel_id=1, source_target_pairs={{0,16},{8,24},{16,0},{24,8},{1,17},{9,25},{17,1},{25,9},{2,18},{10... | collective-permute-start | bytes 884744 | tf_op jit(solution)/shard_map/ppermute | solution.py:46
  169.7 41.6 %collective-permute-start.39 = (bf16[384,1152]{1,0:T(8,128)(2,1)S(1)}, bf16[384,1152]{1,0:T(8,128)(2,1)S(1)}, u32[]{:S(2)}, u32[]{:S(2)}) collective-permute-start(bf16[384,1152]{1,0:T(8,128)(2,1)S(1)} %constant_dynamic-update-slice_fusion.17), channel_id=1, source_target_pairs={{0,8},{8,0},{16,24},{24,16},{1,9},{9,1},{17,25},{25,17},{2,10},{10... | collective-permute-start | bytes 2654216 | tf_op jit(solution)/shard_map/ppermute | solution.py:46
  192.4 22.6 %collective-permute-start.40 = (bf16[384,1152]{1,0:T(8,128)(2,1)S(1)}, bf16[384,1152]{1,0:T(8,128)(2,1)S(1)}, u32[]{:S(2)}, u32[]{:S(2)}) collective-permute-start(bf16[384,1152]{1,0:T(8,128)(2,1)S(1)} %constant_dynamic-update-slice_fusion.17), channel_id=1, source_target_pairs={{0,16},{8,24},{16,0},{24,8},{1,17},{9,25},{17,1},{25,9},{2,18},{10... | collective-permute-start | bytes 2654216 | tf_op jit(solution)/shard_map/ppermute | solution.py:46
  193.9 31.3 %collective-permute-start.25 = (bf16[384,1152]{1,0:T(8,128)(2,1)}, bf16[384,1152]{1,0:T(8,128)(2,1)S(1)}, u32[]{:S(2)}, u32[]{:S(2)}) collective-permute-start(bf16[384,1152]{1,0:T(8,128)(2,1)} %constant_dynamic-update-slice_fusion.29), channel_id=1, source_target_pairs={{0,8},{8,0},{16,24},{24,16},{1,9},{9,1},{17,25},{25,17},{2,10},{10... | collective-permute-start | bytes 2654216 | tf_op jit(solution)/shard_map/ppermute | solution.py:46
  195.4 33.7 %collective-permute-start.26 = (bf16[384,1152]{1,0:T(8,128)(2,1)}, bf16[384,1152]{1,0:T(8,128)(2,1)S(1)}, u32[]{:S(2)}, u32[]{:S(2)}) collective-permute-start(bf16[384,1152]{1,0:T(8,128)(2,1)} %constant_dynamic-update-slice_fusion.29), channel_id=1, source_target_pairs={{0,16},{8,24},{16,0},{24,8},{1,17},{9,25},{17,1},{25,9},{2,18},{10... | collective-permute-start | bytes 2654216 | tf_op jit(solution)/shard_map/ppermute | solution.py:46
  196.1 34.0 %collective-permute-start.5 = (bf16[192,1024]{1,0:T(8,128)(2,1)S(1)}, bf16[192,1024]{1,0:T(8,128)(2,1)S(1)}, u32[]{:S(2)}, u32[]{:S(2)}) collective-permute-start(bf16[192,1024]{1,0:T(8,128)(2,1)S(1)} %slice.494), channel_id=1, source_target_pairs={{0,8},{8,0},{16,24},{24,16},{1,9},{9,1},{17,25},{25,17},{2,10},{10... | collective-permute-start | bytes 1179656 | tf_op jit(solution)/shard_map/ppermute | solution.py:46
  211.3 20.0 %collective-permute-start.6 = (bf16[192,1024]{1,0:T(8,128)(2,1)S(1)}, bf16[192,1024]{1,0:T(8,128)(2,1)S(1)}, u32[]{:S(2)}, u32[]{:S(2)}) collective-permute-start(bf16[192,1024]{1,0:T(8,128)(2,1)S(1)} %slice.495), channel_id=1, source_target_pairs={{0,16},{8,24},{16,0},{24,8},{1,17},{9,25},{17,1},{25,9},{2,18},{10... | collective-permute-start | bytes 1179656 | tf_op jit(solution)/shard_map/ppermute | solution.py:46
  214.9 50.7 %collective-permute-start.34 = (bf16[192,1152]{1,0:T(8,128)(2,1)}, bf16[192,1152]{1,0:T(8,128)(2,1)}, u32[]{:S(2)}, u32[]{:S(2)}) collective-permute-start(bf16[192,1152]{1,0:T(8,128)(2,1)} %slice.515), channel_id=1, source_target_pairs={{0,8},{8,0},{16,24},{24,16},{1,9},{9,1},{17,25},{25,17},{2,10},{10... | collective-permute-start | bytes 1327112 | tf_op jit(solution)/shard_map/ppermute | solution.py:46
  225.1 41.0 %collective-permute-start.35 = (bf16[192,1152]{1,0:T(8,128)(2,1)}, bf16[192,1152]{1,0:T(8,128)(2,1)}, u32[]{:S(2)}, u32[]{:S(2)}) collective-permute-start(bf16[192,1152]{1,0:T(8,128)(2,1)} %slice.516), channel_id=1, source_target_pairs={{0,16},{8,24},{16,0},{24,8},{1,17},{9,25},{17,1},{25,9},{2,18},{10... | collective-permute-start | bytes 1327112 | tf_op jit(solution)/shard_map/ppermute | solution.py:46
  247.1 20.5 %collective-permute-start.41 = (bf16[192,1152]{1,0:T(8,128)(2,1)}, bf16[192,1152]{1,0:T(8,128)(2,1)S(1)}, u32[]{:S(2)}, u32[]{:S(2)}) collective-permute-start(bf16[192,1152]{1,0:T(8,128)(2,1)} %slice.517), channel_id=1, source_target_pairs={{0,8},{8,0},{16,24},{24,16},{1,9},{9,1},{17,25},{25,17},{2,10},{10... | collective-permute-start | bytes 1327112 | tf_op jit(solution)/shard_map/ppermute | solution.py:46
  249.6 19.2 %collective-permute-start.42 = (bf16[192,1152]{1,0:T(8,128)(2,1)}, bf16[192,1152]{1,0:T(8,128)(2,1)S(1)}, u32[]{:S(2)}, u32[]{:S(2)}) collective-permute-start(bf16[192,1152]{1,0:T(8,128)(2,1)} %slice.518), channel_id=1, source_target_pairs={{0,16},{8,24},{16,0},{24,8},{1,17},{9,25},{17,1},{25,9},{2,18},{10... | collective-permute-start | bytes 1327112 | tf_op jit(solution)/shard_map/ppermute | solution.py:46
  271.8 29.8 %collective-permute-start.19 = (bf16[128,1536]{1,0:T(8,128)(2,1)S(1)}, bf16[128,1536]{1,0:T(8,128)(2,1)S(1)}, u32[]{:S(2)}, u32[]{:S(2)}) collective-permute-start(bf16[128,1536]{1,0:T(8,128)(2,1)S(1)} %get-tuple-element.30), channel_id=1, source_target_pairs={{0,4},{2,6},{4,0},{6,2},{1,5},{3,7},{5,1},{7,3},{8,12},{10,14},{12... | collective-permute-start | bytes 1179656 | tf_op jit(solution)/shard_map/ppermute | solution.py:46
  278.3 23.3 %collective-permute-start.20 = (bf16[128,1536]{1,0:T(8,128)(2,1)S(1)}, bf16[128,1536]{1,0:T(8,128)(2,1)S(1)}, u32[]{:S(2)}, u32[]{:S(2)}) collective-permute-start(bf16[128,1536]{1,0:T(8,128)(2,1)S(1)} %get-tuple-element.30), channel_id=1, source_target_pairs={{0,6},{2,4},{4,2},{6,0},{1,7},{3,5},{5,3},{7,1},{8,14},{10,12},{12... | collective-permute-start | bytes 1179656 | tf_op jit(solution)/shard_map/ppermute | solution.py:46
  358.5 63.0 %collective-permute-start.95 = (bf16[384,1152]{1,0:T(8,128)(2,1)}, bf16[384,1152]{1,0:T(8,128)(2,1)}, u32[]{:S(2)}, u32[]{:S(2)}) collective-permute-start(bf16[384,1152]{1,0:T(8,128)(2,1)} %pad_maximum_fusion.7), channel_id=1, source_target_pairs={{0,16},{8,24},{16,0},{24,8},{1,17},{9,25},{17,1},{25,9},{2,18},{10... | collective-permute-start | bytes 2654216 | tf_op jit(solution)/shard_map/ppermute | solution.py:46
  359.6 32.3 %collective-permute-start.97 = (bf16[384,1152]{1,0:T(8,128)(2,1)}, bf16[384,1152]{1,0:T(8,128)(2,1)}, u32[]{:S(2)}, u32[]{:S(2)}) collective-permute-start(bf16[384,1152]{1,0:T(8,128)(2,1)} %pad_maximum_fusion.8), channel_id=1, source_target_pairs={{0,8},{8,0},{16,24},{24,16},{1,9},{9,1},{17,25},{25,17},{2,10},{10... | collective-permute-start | bytes 2654216 | tf_op jit(solution)/shard_map/ppermute | solution.py:46
  361.0 74.0 %collective-permute-start.88 = (bf16[384,1152]{1,0:T(8,128)(2,1)S(1)}, bf16[384,1152]{1,0:T(8,128)(2,1)}, u32[]{:S(2)}, u32[]{:S(2)}) collective-permute-start(bf16[384,1152]{1,0:T(8,128)(2,1)S(1)} %pad_maximum_fusion.5), channel_id=1, source_target_pairs={{0,16},{8,24},{16,0},{24,8},{1,17},{9,25},{17,1},{25,9},{2,18},{10... | collective-permute-start | bytes 2654216 | tf_op jit(solution)/shard_map/ppermute | solution.py:46
  362.8 38.6 %collective-permute-start.90 = (bf16[384,1152]{1,0:T(8,128)(2,1)}, bf16[384,1152]{1,0:T(8,128)(2,1)}, u32[]{:S(2)}, u32[]{:S(2)}) collective-permute-start(bf16[384,1152]{1,0:T(8,128)(2,1)} %pad_maximum_fusion.6), channel_id=1, source_target_pairs={{0,8},{8,0},{16,24},{24,16},{1,9},{9,1},{17,25},{25,17},{2,10},{10... | collective-permute-start | bytes 2654216 | tf_op jit(solution)/shard_map/ppermute | solution.py:46
  370.7 75.9 %collective-permute-start.81 = (bf16[384,1152]{1,0:T(8,128)(2,1)}, bf16[384,1152]{1,0:T(8,128)(2,1)}, u32[]{:S(2)}, u32[]{:S(2)}) collective-permute-start(bf16[384,1152]{1,0:T(8,128)(2,1)} %pad_maximum_fusion.3), channel_id=1, source_target_pairs={{0,16},{8,24},{16,0},{24,8},{1,17},{9,25},{17,1},{25,9},{2,18},{10... | collective-permute-start | bytes 2654216 | tf_op jit(solution)/shard_map/ppermute | solution.py:46
  391.9 27.7 %collective-permute-start.83 = (bf16[384,1152]{1,0:T(8,128)(2,1)S(1)}, bf16[384,1152]{1,0:T(8,128)(2,1)S(1)}, u32[]{:S(2)}, u32[]{:S(2)}) collective-permute-start(bf16[384,1152]{1,0:T(8,128)(2,1)S(1)} %pad_maximum_fusion.4), channel_id=1, source_target_pairs={{0,8},{8,0},{16,24},{24,16},{1,9},{9,1},{17,25},{25,17},{2,10},{10... | collective-permute-start | bytes 2654216 | tf_op jit(solution)/shard_map/ppermute | solution.py:46
  401.4 52.0 %collective-permute-start.43 = (bf16[512,1536]{1,0:T(8,128)(2,1)S(1)}, bf16[512,1536]{1,0:T(8,128)(2,1)S(1)}, u32[]{:S(2)}, u32[]{:S(2)}) collective-permute-start(bf16[512,1536]{1,0:T(8,128)(2,1)S(1)} %slice.704), channel_id=1, source_target_pairs={{0,1},{1,0},{2,3},{3,2},{4,5},{5,4},{6,7},{7,6},{8,9},{9,8},{10,11... | collective-permute-start | bytes 4718600 | tf_op jit(solution)/shard_map/ppermute | solution.py:46
  421.5 42.0 %collective-permute-start.52 = (bf16[512,1536]{1,0:T(8,128)(2,1)S(1)}, bf16[512,1536]{1,0:T(8,128)(2,1)S(1)}, u32[]{:S(2)}, u32[]{:S(2)}) collective-permute-start(bf16[512,1536]{1,0:T(8,128)(2,1)S(1)} %slice.703), channel_id=1, source_target_pairs={{0,1},{1,0},{2,3},{3,2},{4,5},{5,4},{6,7},{7,6},{8,9},{9,8},{10,11... | collective-permute-start | bytes 4718600 | tf_op jit(solution)/shard_map/ppermute | solution.py:46
  444.3 21.5 %collective-permute-start.96 = (bf16[192,1152]{1,0:T(8,128)(2,1)}, bf16[192,1152]{1,0:T(8,128)(2,1)S(1)}, u32[]{:S(2)}, u32[]{:S(2)}) collective-permute-start(bf16[192,1152]{1,0:T(8,128)(2,1)} %get-tuple-element.37), channel_id=1, source_target_pairs={{0,8},{8,0},{16,24},{24,16},{1,9},{9,1},{17,25},{25,17},{2,10},{10... | collective-permute-start | bytes 1327112 | tf_op jit(solution)/shard_map/ppermute | solution.py:46
  446.6 23.5 %collective-permute-start.89 = (bf16[192,1152]{1,0:T(8,128)(2,1)S(1)}, bf16[192,1152]{1,0:T(8,128)(2,1)S(1)}, u32[]{:S(2)}, u32[]{:S(2)}) collective-permute-start(bf16[192,1152]{1,0:T(8,128)(2,1)S(1)} %get-tuple-element.43), channel_id=1, source_target_pairs={{0,8},{8,0},{16,24},{24,16},{1,9},{9,1},{17,25},{25,17},{2,10},{10... | collective-permute-start | bytes 1327112 | tf_op jit(solution)/shard_map/ppermute | solution.py:46
  452.6 23.7 %collective-permute-start.82 = (bf16[192,1152]{1,0:T(8,128)(2,1)S(1)}, bf16[192,1152]{1,0:T(8,128)(2,1)S(1)}, u32[]{:S(2)}, u32[]{:S(2)}) collective-permute-start(bf16[192,1152]{1,0:T(8,128)(2,1)S(1)} %get-tuple-element.49), channel_id=1, source_target_pairs={{0,8},{8,0},{16,24},{24,16},{1,9},{9,1},{17,25},{25,17},{2,10},{10... | collective-permute-start | bytes 1327112 | tf_op jit(solution)/shard_map/ppermute | solution.py:46
  456.0 78.2 %collective-permute-start.44 = (bf16[128,1536]{1,0:T(8,128)(2,1)S(1)}, bf16[128,1536]{1,0:T(8,128)(2,1)S(1)}, u32[]{:S(2)}, u32[]{:S(2)}) collective-permute-start(bf16[128,1536]{1,0:T(8,128)(2,1)S(1)} %get-tuple-element.72), channel_id=1, source_target_pairs={{0,2},{2,0},{4,6},{6,4},{1,3},{3,1},{5,7},{7,5},{8,10},{10,8},{12,... | collective-permute-start | bytes 1179656 | tf_op jit(solution)/shard_map/ppermute | solution.py:46
  463.4 71.2 %collective-permute-start.45 = (bf16[128,1536]{1,0:T(8,128)(2,1)S(1)}, bf16[128,1536]{1,0:T(8,128)(2,1)S(1)}, u32[]{:S(2)}, u32[]{:S(2)}) collective-permute-start(bf16[128,1536]{1,0:T(8,128)(2,1)S(1)} %get-tuple-element.74), channel_id=1, source_target_pairs={{0,4},{2,6},{4,0},{6,2},{1,5},{3,7},{5,1},{7,3},{8,12},{10,14},{12... | collective-permute-start | bytes 1179656 | tf_op jit(solution)/shard_map/ppermute | solution.py:46
  465.7 28.2 %collective-permute-start.53 = (bf16[128,1536]{1,0:T(8,128)(2,1)S(1)}, bf16[128,1536]{1,0:T(8,128)(2,1)S(1)}, u32[]{:S(2)}, u32[]{:S(2)}) collective-permute-start(bf16[128,1536]{1,0:T(8,128)(2,1)S(1)} %get-tuple-element.69), channel_id=1, source_target_pairs={{0,2},{2,0},{4,6},{6,4},{1,3},{3,1},{5,7},{7,5},{8,10},{10,8},{12,... | collective-permute-start | bytes 1179656 | tf_op jit(solution)/shard_map/ppermute | solution.py:46
  470.1 47.3 %collective-permute-start.54 = (bf16[128,1536]{1,0:T(8,128)(2,1)S(1)}, bf16[128,1536]{1,0:T(8,128)(2,1)S(1)}, u32[]{:S(2)}, u32[]{:S(2)}) collective-permute-start(bf16[128,1536]{1,0:T(8,128)(2,1)S(1)} %get-tuple-element.71), channel_id=1, source_target_pairs={{0,4},{2,6},{4,0},{6,2},{1,5},{3,7},{5,1},{7,3},{8,12},{10,14},{12... | collective-permute-start | bytes 1179656 | tf_op jit(solution)/shard_map/ppermute | solution.py:46
  476.2 41.8 %collective-permute-start.55 = (bf16[128,1536]{1,0:T(8,128)(2,1)S(1)}, bf16[128,1536]{1,0:T(8,128)(2,1)S(1)}, u32[]{:S(2)}, u32[]{:S(2)}) collective-permute-start(bf16[128,1536]{1,0:T(8,128)(2,1)S(1)} %get-tuple-element.70), channel_id=1, source_target_pairs={{0,6},{2,4},{4,2},{6,0},{1,7},{3,5},{5,3},{7,1},{8,14},{10,12},{12... | collective-permute-start | bytes 1179656 | tf_op jit(solution)/shard_map/ppermute | solution.py:46
  494.0 40.8 %collective-permute-start.46 = (bf16[128,1536]{1,0:T(8,128)(2,1)S(1)}, bf16[128,1536]{1,0:T(8,128)(2,1)S(1)}, u32[]{:S(2)}, u32[]{:S(2)}) collective-permute-start(bf16[128,1536]{1,0:T(8,128)(2,1)S(1)} %get-tuple-element.73), channel_id=1, source_target_pairs={{0,6},{2,4},{4,2},{6,0},{1,7},{3,5},{5,3},{7,1},{8,14},{10,12},{12... | collective-permute-start | bytes 1179656 | tf_op jit(solution)/shard_map/ppermute | solution.py:46
  517.4 34.1 %collective-permute-start.99 = (bf16[96,1152]{1,0:T(8,128)(2,1)S(1)}, bf16[96,1152]{1,0:T(8,128)(2,1)S(1)}, u32[]{:S(2)}, u32[]{:S(2)}) collective-permute-start(bf16[96,1152]{1,0:T(8,128)(2,1)S(1)} %get-tuple-element.79), channel_id=1, source_target_pairs={{0,2},{2,0},{4,6},{6,4},{1,3},{3,1},{5,7},{7,5},{8,10},{10,8},{12,... | collective-permute-start | bytes 663560 | tf_op jit(solution)/shard_map/ppermute | solution.py:46
  518.1 44.7 %collective-permute-start.100 = (bf16[96,1152]{1,0:T(8,128)(2,1)S(1)}, bf16[96,1152]{1,0:T(8,128)(2,1)S(1)}, u32[]{:S(2)}, u32[]{:S(2)}) collective-permute-start(bf16[96,1152]{1,0:T(8,128)(2,1)S(1)} %get-tuple-element.80), channel_id=1, source_target_pairs={{0,4},{2,6},{4,0},{6,2},{1,5},{3,7},{5,1},{7,3},{8,12},{10,14},{12... | collective-permute-start | bytes 663560 | tf_op jit(solution)/shard_map/ppermute | solution.py:46
  534.2 28.6 %collective-permute-start.101 = (bf16[96,1152]{1,0:T(8,128)(2,1)S(1)}, bf16[96,1152]{1,0:T(8,128)(2,1)S(1)}, u32[]{:S(2)}, u32[]{:S(2)}) collective-permute-start(bf16[96,1152]{1,0:T(8,128)(2,1)S(1)} %get-tuple-element.78), channel_id=1, source_target_pairs={{0,6},{2,4},{4,2},{6,0},{1,7},{3,5},{5,3},{7,1},{8,14},{10,12},{12... | collective-permute-start | bytes 663560 | tf_op jit(solution)/shard_map/ppermute | solution.py:46
  534.6 35.6 %collective-permute-start.92 = (bf16[96,1152]{1,0:T(8,128)(2,1)S(1)}, bf16[96,1152]{1,0:T(8,128)(2,1)S(1)}, u32[]{:S(2)}, u32[]{:S(2)}) collective-permute-start(bf16[96,1152]{1,0:T(8,128)(2,1)S(1)} %get-tuple-element.82), channel_id=1, source_target_pairs={{0,2},{2,0},{4,6},{6,4},{1,3},{3,1},{5,7},{7,5},{8,10},{10,8},{12,... | collective-permute-start | bytes 663560 | tf_op jit(solution)/shard_map/ppermute | solution.py:46
  534.7 39.8 %collective-permute-start.93 = (bf16[96,1152]{1,0:T(8,128)(2,1)S(1)}, bf16[96,1152]{1,0:T(8,128)(2,1)S(1)}, u32[]{:S(2)}, u32[]{:S(2)}) collective-permute-start(bf16[96,1152]{1,0:T(8,128)(2,1)S(1)} %get-tuple-element.83), channel_id=1, source_target_pairs={{0,4},{2,6},{4,0},{6,2},{1,5},{3,7},{5,1},{7,3},{8,12},{10,14},{12... | collective-permute-start | bytes 663560 | tf_op jit(solution)/shard_map/ppermute | solution.py:46
  551.5 23.1 %collective-permute-start.94 = (bf16[96,1152]{1,0:T(8,128)(2,1)S(1)}, bf16[96,1152]{1,0:T(8,128)(2,1)S(1)}, u32[]{:S(2)}, u32[]{:S(2)}) collective-permute-start(bf16[96,1152]{1,0:T(8,128)(2,1)S(1)} %get-tuple-element.81), channel_id=1, source_target_pairs={{0,6},{2,4},{4,2},{6,0},{1,7},{3,5},{5,3},{7,1},{8,14},{10,12},{12... | collective-permute-start | bytes 663560 | tf_op jit(solution)/shard_map/ppermute | solution.py:46
  562.8 23.1 %collective-permute-start.86 = (bf16[96,1152]{1,0:T(8,128)(2,1)S(1)}, bf16[96,1152]{1,0:T(8,128)(2,1)S(1)}, u32[]{:S(2)}, u32[]{:S(2)}) collective-permute-start(bf16[96,1152]{1,0:T(8,128)(2,1)S(1)} %get-tuple-element.86), channel_id=1, source_target_pairs={{0,4},{2,6},{4,0},{6,2},{1,5},{3,7},{5,1},{7,3},{8,12},{10,14},{12... | collective-permute-start | bytes 663560 | tf_op jit(solution)/shard_map/ppermute | solution.py:46
  574.6 35.2 %collective-permute-start.47 = (bf16[128,1536]{1,0:T(8,128)(2,1)S(1)}, bf16[128,1536]{1,0:T(8,128)(2,1)S(1)}, u32[]{:S(2)}, u32[]{:S(2)}) collective-permute-start(bf16[128,1536]{1,0:T(8,128)(2,1)S(1)} %get-tuple-element.101), channel_id=1, source_target_pairs={{0,1},{1,0},{2,3},{3,2},{4,5},{5,4},{6,7},{7,6},{8,9},{9,8},{10,11... | collective-permute-start | bytes 1179656 | tf_op jit(solution)/shard_map/ppermute | solution.py:46
  593.6 34.8 %collective-permute-start.74 = (bf16[384,768]{1,0:T(8,128)(2,1)S(1)}, bf16[384,768]{1,0:T(8,128)(2,1)}, u32[]{:S(2)}, u32[]{:S(2)}) collective-permute-start(bf16[384,768]{1,0:T(8,128)(2,1)S(1)} %pad_maximum_fusion.11), channel_id=1, source_target_pairs={{0,16},{8,24},{16,0},{24,8},{1,17},{9,25},{17,1},{25,9},{2,18},{10... | collective-permute-start | bytes 1769480 | tf_op jit(solution)/shard_map/ppermute | solution.py:46
  595.5 27.5 %collective-permute-start.76 = (bf16[384,768]{1,0:T(8,128)(2,1)}, bf16[384,768]{1,0:T(8,128)(2,1)}, u32[]{:S(2)}, u32[]{:S(2)}) collective-permute-start(bf16[384,768]{1,0:T(8,128)(2,1)} %pad_maximum_fusion.12), channel_id=1, source_target_pairs={{0,8},{8,0},{16,24},{24,16},{1,9},{9,1},{17,25},{25,17},{2,10},{10... | collective-permute-start | bytes 1769480 | tf_op jit(solution)/shard_map/ppermute | solution.py:46
  622.4 21.5 %collective-permute-start.69 = (bf16[384,1024]{1,0:T(8,128)(2,1)S(1)}, bf16[384,1024]{1,0:T(8,128)(2,1)S(1)}, u32[]{:S(2)}, u32[]{:S(2)}) collective-permute-start(bf16[384,1024]{1,0:T(8,128)(2,1)S(1)} %pad_maximum_fusion.10), channel_id=1, source_target_pairs={{0,8},{8,0},{16,24},{24,16},{1,9},{9,1},{17,25},{25,17},{2,10},{10... | collective-permute-start | bytes 2359304 | tf_op jit(solution)/shard_map/ppermute | solution.py:46
  626.1 36.5 %collective-permute-start.67 = (bf16[384,1024]{1,0:T(8,128)(2,1)S(1)}, bf16[384,1024]{1,0:T(8,128)(2,1)S(1)}, u32[]{:S(2)}, u32[]{:S(2)}) collective-permute-start(bf16[384,1024]{1,0:T(8,128)(2,1)S(1)} %pad_maximum_fusion.9), channel_id=1, source_target_pairs={{0,16},{8,24},{16,0},{24,8},{1,17},{9,25},{17,1},{25,9},{2,18},{10... | collective-permute-start | bytes 2359304 | tf_op jit(solution)/shard_map/ppermute | solution.py:46
  636.2 27.4 %collective-permute-start.75 = (bf16[192,768]{1,0:T(8,128)(2,1)S(1)}, bf16[192,768]{1,0:T(8,128)(2,1)S(1)}, u32[]{:S(2)}, u32[]{:S(2)}) collective-permute-start(bf16[192,768]{1,0:T(8,128)(2,1)S(1)} %get-tuple-element.61), channel_id=1, source_target_pairs={{0,8},{8,0},{16,24},{24,16},{1,9},{9,1},{17,25},{25,17},{2,10},{10... | collective-permute-start | bytes 884744 | tf_op jit(solution)/shard_map/ppermute | solution.py:46
  644.1 18.5 %collective-permute-start.70 = (bf16[192,1024]{1,0:T(8,128)(2,1)S(1)}, bf16[192,1024]{1,0:T(8,128)(2,1)S(1)}, u32[]{:S(2)}, u32[]{:S(2)}) collective-permute-start(bf16[192,1024]{1,0:T(8,128)(2,1)S(1)} %add_convert_fusion.12), channel_id=1, source_target_pairs={{0,16},{8,24},{16,0},{24,8},{1,17},{9,25},{17,1},{25,9},{2,18},{10... | collective-permute-start | bytes 1179656 | tf_op jit(solution)/shard_map/ppermute | solution.py:46
  676.9 19.7 %collective-permute-start.72 = (bf16[96,1024]{1,0:T(8,128)(2,1)S(1)}, bf16[96,1024]{1,0:T(8,128)(2,1)S(1)}, u32[]{:S(2)}, u32[]{:S(2)}) collective-permute-start(bf16[96,1024]{1,0:T(8,128)(2,1)S(1)} %get-tuple-element.67), channel_id=1, source_target_pairs={{0,4},{2,6},{4,0},{6,2},{1,5},{3,7},{5,1},{7,3},{8,12},{10,14},{12... | collective-permute-start | bytes 589832 | tf_op jit(solution)/shard_map/ppermute | solution.py:46
  678.1 18.6 %collective-permute-start.73 = (bf16[96,1024]{1,0:T(8,128)(2,1)S(1)}, bf16[96,1024]{1,0:T(8,128)(2,1)S(1)}, u32[]{:S(2)}, u32[]{:S(2)}) collective-permute-start(bf16[96,1024]{1,0:T(8,128)(2,1)S(1)} %get-tuple-element.68), channel_id=1, source_target_pairs={{0,6},{2,4},{4,2},{6,0},{1,7},{3,5},{5,3},{7,1},{8,14},{10,12},{12... | collective-permute-start | bytes 589832 | tf_op jit(solution)/shard_map/ppermute | solution.py:46
  (114 other events, 1811.0 us)

commit v2 on v1

--- a/solution.py
+++ b/solution.py
@@ -50,13 +50,28 @@
     return lax.dynamic_slice_in_dim(values, index * count, count, 0)
 
 
-def place_rows(parts, indices, rows):
+def place_rows(parts, indices):
+    rows = len(parts) * parts[0].shape[0]
     whole = jnp.zeros((rows,) + parts[0].shape[1:], parts[0].dtype)
     for part, index in zip(parts, indices):
         whole = lax.dynamic_update_slice_in_dim(whole, part, index * part.shape[0], 0)
     return whole
 
 
+def after(values, *others):
+    return lax.optimization_barrier((values, others))[0]
+
+
+def relative(values):
+    me = lax.axis_index("seq")
+    width = values.shape[-1] // 4
+    blocks = [
+        lax.dynamic_slice_in_dim(values, (me ^ j) * width, width, values.ndim - 1)
+        for j in range(4)
+    ]
+    return jnp.concatenate(blocks, -1)
+
+
 def gather_ctx(block):
     size = lax.axis_size("ctx")
     return [block] + [swap(block, "ctx", k) for k in range(1, size)]
@@ -66,55 +81,37 @@
     return [pieces[0]] + [swap(pieces[k], "ctx", k) for k in range(1, len(pieces))]
 
 
-def gather_seq(shard):
-    size = lax.axis_size("seq")
-    if size != 4:
-        return lax.all_gather(shard, "seq", axis=0, tiled=True)
-    me = lax.axis_index("seq")
-    half = shard.shape[0] // 2
-    from_x = swap(shard, "seq", 1)
-    from_y = swap(shard, "seq", 2)
-    far_top = swap(from_y[:half], "seq", 1)
-    far_bottom = swap(from_x[half:], "seq", 2)
-    far = jnp.concatenate([far_top, far_bottom], 0)
-    return place_rows(
-        [shard, from_x, from_y, far], [me, me ^ 1, me ^ 2, me ^ 3], size * shard.shape[0]
-    )
-
-
-def scatter_seq(partial_sum):
-    size = lax.axis_size("seq")
-    if size != 4:
-        return lax.psum_scatter(
-            partial_sum.astype(jnp.float32), "seq", scatter_dimension=0, tiled=True
-        )
-    me = lax.axis_index("seq")
-    rows = partial_sum.shape[0] // size
-    half = rows // 2
-    own = rows_at(partial_sum, me, rows)
-    for_x = rows_at(partial_sum, me ^ 1, rows)
-    for_y = rows_at(partial_sum, me ^ 2, rows)
-    for_far = rows_at(partial_sum, me ^ 3, rows)
+def near_seq(shard):
+    return swap(shard, "seq", 1), swap(shard, "seq", 2)
+
+
+def far_seq(from_x, from_y):
+    half = from_x.shape[0] // 2
+    return swap(from_y[:half], "seq", 1), swap(from_x[half:], "seq", 2)
+
+
+def lay_seq(shard, near, far):
+    return jnp.concatenate([shard, *near, *far], 0)
+
+
+def scatter_near(partial_sum):
+    own, for_x, for_y, for_far = jnp.split(partial_sum, 4, 0)
+    half = own.shape[0] // 2
     got_x = swap(jnp.concatenate([for_far[half:], for_x[half:]], 0), "seq", 1)
     got_y = swap(jnp.concatenate([for_far[:half], for_y[:half]], 0), "seq", 2)
-    on_x = (for_x[:half].astype(jnp.float32) + got_y[:half].astype(jnp.float32)).astype(
-        jnp.bfloat16
-    )
-    on_y = (for_y[half:].astype(jnp.float32) + got_x[:half].astype(jnp.float32)).astype(
-        jnp.bfloat16
-    )
+    return got_x, got_y
+
+
+def scatter_far(partial_sum, got_x, got_y):
+    own, for_x, for_y, _ = jnp.split(partial_sum, 4, 0)
+    half = own.shape[0] // 2
+    on_x = add_up([for_x[:half], got_y[:half]]).astype(jnp.bfloat16)
+    on_y = add_up([for_y[half:], got_x[:half]]).astype(jnp.bfloat16)
+    on_x, on_y = lax.optimization_barrier((on_x, on_y))
     last_x = swap(on_x, "seq", 1)
     last_y = swap(on_y, "seq", 2)
-    top = (
-        own[:half].astype(jnp.float32)
-        + got_y[half:].astype(jnp.float32)
-        + last_x.astype(jnp.float32)
-    )
-    bottom = (
-        own[half:].astype(jnp.float32)
-        + got_x[half:].astype(jnp.float32)
-        + last_y.astype(jnp.float32)
-    )
+    top = add_up([own[:half], got_y[half:], last_x])
+    bottom = add_up([own[half:], got_x[half:], last_y])
     return jnp.concatenate([top, bottom], 0)
 
 
@@ -125,65 +122,63 @@
     return total
 
 
-def gather_weight(shard):
-    ctx = lax.axis_index("ctx")
-    parts = gather_ctx(shard)
-    rows = len(parts) * shard.shape[0]
-    own = place_rows(parts, [ctx ^ k for k in range(len(parts))], rows)
-    return gather_seq(own)
-
-
 def units_per(units):
     size = lax.axis_size("ctx")
     return -(-units // (size * LANES)) * LANES
 
 
-def spread_units(shard):
+def unit_pieces(shards):
     size = lax.axis_size("ctx")
     ctx = lax.axis_index("ctx")
-    width = units_per(shard.shape[1])
-    padded = jnp.pad(shard, ((0, 0), (0, size * width - shard.shape[1])))
-    pieces = [lax.dynamic_slice_in_dim(padded, (ctx ^ k) * width, width, 1) for k in range(size)]
-    parts = exchange_ctx(pieces)
-    own = place_rows(parts, [ctx ^ k for k in range(size)], size * shard.shape[0])
-    return gather_seq(own)
-
-
-def collect_units(partial_sum, units):
+    width = units_per(shards[0].shape[1])
+    padded = [jnp.pad(w, ((0, 0), (0, size * width - w.shape[1]))) for w in shards]
+    return [
+        jnp.concatenate(
+            [lax.dynamic_slice_in_dim(w, (ctx ^ k) * width, width, 1) for w in padded], 1
+        )
+        for k in range(size)
+    ]
+
+
+def row_pieces(summed):
     size = lax.axis_size("ctx")
     ctx = lax.axis_index("ctx")
-    summed = scatter_seq(partial_sum.astype(jnp.bfloat16)).astype(jnp.bfloat16)
-    rows, width = summed.shape[0] // size, summed.shape[1]
-    parts = exchange_ctx([rows_at(summed, ctx ^ k, rows) for k in range(size)])
-    whole = jnp.zeros((rows, size * width), jnp.float32)
-    for k in range(size):
-        whole = lax.dynamic_update_slice_in_dim(
-            whole, parts[k].astype(jnp.float32), (ctx ^ k) * width, 1
-        )
-    return whole[:, :units]
-
-
-def scatter_weight(partial_sum):
+    rows = summed.shape[0] // size
+    return [rows_at(summed, ctx ^ k, rows) for k in range(size)]
+
+
+def place_ctx(parts):
+    ctx = lax.axis_index("ctx")
+    return place_rows(parts, [ctx ^ k for k in range(len(parts))])
+
+
+def place_units(parts, units):
     size = lax.axis_size("ctx")
     ctx = lax.axis_index("ctx")
-    summed = scatter_seq(partial_sum.astype(jnp.bfloat16))
-    rows = summed.shape[0] // size
-    pieces = [rows_at(summed, ctx ^ k, rows) for k in range(size)]
-    return add_up(exchange_ctx([pieces[0]] + [piece.astype(jnp.bfloat16) for piece in pieces[1:]]))
-
-
-def gather_tokens(half):
-    mine = jnp.concatenate(gather_ctx(half), 0)
+    width = units_per(units)
+    wholes = []
+    for start in range(0, parts[0].shape[1], width):
+        whole = jnp.zeros((parts[0].shape[0], size * width), jnp.float32)
+        for k in range(size):
+            part = parts[k][:, start : start + width].astype(jnp.float32)
+            whole = lax.dynamic_update_slice_in_dim(whole, part, (ctx ^ k) * width, 1)
+        wholes.append(whole[:, :units])
+    return wholes
+
+
+def narrow_others(pieces):
+    return [pieces[0]] + [piece.astype(jnp.bfloat16) for piece in pieces[1:]]
+
+
+def both_cores(mine):
     return jnp.concatenate([mine, swap(mine, "wt", 1)], 0)
 
 
-def scatter_tokens(partial_sum):
-    size = lax.axis_size("ctx")
+def chip_sum(partial_sum):
     middle = partial_sum.shape[0] // 2
     other = swap(partial_sum[middle:].astype(jnp.bfloat16), "wt", 1)
     chip = partial_sum[:middle] + other.astype(jnp.float32)
-    pieces = jnp.split(chip, size, 0)
-    return add_up(exchange_ctx([pieces[0]] + [piece.astype(jnp.bfloat16) for piece in pieces[1:]]))
+    return jnp.split(chip, lax.axis_size("ctx"), 0)
 
 
 def add_all(values, axes):
@@ -263,18 +258,27 @@
     def unrope_rows(grads):
         return grads * cosines[:, None, :] - rotate(grads * sines[:, None, :])
 
-    input_rows = layer_input.reshape(span_rows, model_width).astype(jnp.float32)
-    grad_out = out_grad.reshape(span_rows, model_width)
-    gain_one = gain_attn.astype(jnp.float32)
-    gain_two = gain_mlp.astype(jnp.float32)
-
-    w_qkv = gather_weight(jnp.concatenate([w_q, w_k, w_v], 1))
-    w_out = gather_weight(w_o)
-    gate_here = spread_units(w_gate)
-    up_here = spread_units(w_up)
-    down_here = spread_units(w_down)
+    input_rows = relative(layer_input.reshape(span_rows, model_width)).astype(jnp.float32)
+    grad_out = relative(out_grad.reshape(span_rows, model_width))
+    gain_one = relative(gain_attn.astype(jnp.float32))
+    gain_two = relative(gain_mlp.astype(jnp.float32))
+
+    attn_shard = place_ctx(gather_ctx(jnp.concatenate([w_q, w_k, w_v, w_o], 1)))
+    gate_up_pieces = unit_pieces([w_gate, w_up])
+    down_pieces = unit_pieces([w_down])
     grad_half = own_half(grad_out)
-    grad_seq = gather_tokens(grad_half)
+
+    attn_near = near_seq(attn_shard)
+    gate_up_parts = exchange_ctx(after(gate_up_pieces, attn_shard))
+    attn_near, gate_up_parts = lax.optimization_barrier((attn_near, gate_up_parts))
+    attn_far = far_seq(*attn_near)
+    down_parts = exchange_ctx(after(down_pieces, gate_up_parts))
+    attn_far, down_parts = lax.optimization_barrier((attn_far, down_parts))
+    w_attn = lay_seq(attn_shard, attn_near, attn_far)
+    w_qkv, w_out = w_attn[:, : query_cols + 2 * key_cols], w_attn[:, query_cols + 2 * key_cols :]
+    gate_up_shard = place_ctx(gate_up_parts)
+    down_shard = place_ctx(down_parts)
+    gate_up_near = near_seq(after(gate_up_shard, attn_far))
 
     rms_attn = lax.rsqrt(jnp.mean(input_rows * input_rows, -1, keepdims=True) + EPSILON)
     normed_attn = (input_rows * rms_attn * gain_one).astype(jnp.bfloat16)
@@ -286,6 +290,7 @@
         [key.reshape(span_rows, HD), qkv[:, query_cols + key_cols :]], 1
     ).astype(jnp.bfloat16)
     keys_values = jnp.concatenate(gather_ctx(key_value), 0)
+    grad_mine = jnp.concatenate(gather_ctx(after(grad_half, keys_values)), 0)
     keys, values = keys_values[:, :HD], keys_values[:, HD:]
 
     def masked_scores(query_block):
@@ -305,10 +310,23 @@
     hidden = input_half + sum_half(times_transposed(attn_heads, w_out))
     rms_mlp = lax.rsqrt(jnp.mean(hidden * hidden, -1, keepdims=True) + EPSILON)
     normed_half = (hidden * rms_mlp * gain_two).astype(jnp.bfloat16)
-    normed_seq = gather_tokens(normed_half)
+    normed_half, gate_up_near = lax.optimization_barrier((normed_half, gate_up_near))
+    normed_mine = jnp.concatenate(gather_ctx(normed_half), 0)
+    gate_up_far = far_seq(*gate_up_near)
+    down_near = near_seq(after(down_shard, gate_up_far))
+    normed_mine, down_near, grad_mine = lax.optimization_barrier(
+        (normed_mine, down_near, grad_mine)
+    )
+    down_far = far_seq(*down_near)
+    normed_seq = both_cores(normed_mine)
+    grad_seq = both_cores(grad_mine)
+    gate_up_here = lay_seq(gate_up_shard, gate_up_near, gate_up_far)
+    width = units_per(units_here)
+    gate_here, up_here = gate_up_here[:, :width], gate_up_here[:, width:]
 
     gate = matmul(normed_seq, gate_here)
     up = matmul(normed_seq, up_here)
+    down_here = lay_seq(down_shard, down_near, down_far)
     g_act = matmul(grad_seq, down_here)
     sigmoid_gate = jax.nn.sigmoid(gate)
     silu_gate = gate * sigmoid_gate
@@ -316,14 +334,28 @@
     g_gate = (g_act * up * sigmoid_gate * (1.0 + gate * (1.0 - sigmoid_gate))).astype(jnp.bfloat16)
     g_up = (g_act * silu_gate).astype(jnp.bfloat16)
 
-    g_normed_mlp = scatter_tokens(
-        times_transposed(g_gate, gate_here) + times_transposed(g_up, up_here)
-    )
-    mlp_out = scatter_tokens(times_transposed(act, down_here))
-    layer_output = join_halves((hidden + mlp_out).astype(jnp.bfloat16))
-    grad_w_gate = collect_units(inner_rows(normed_seq, g_gate), units_here)
-    grad_w_up = collect_units(inner_rows(normed_seq, g_up), units_here)
-    grad_w_down = collect_units(inner_rows(grad_seq, act), units_here)
+    g_normed_partial = times_transposed(g_gate, gate_here) + times_transposed(g_up, up_here)
+    act, g_gate, g_up, g_normed_partial = lax.optimization_barrier(
+        (act, g_gate, g_up, g_normed_partial)
+    )
+    g_normed_pieces = chip_sum(g_normed_partial)
+    g_down = inner_rows(grad_seq, act).astype(jnp.bfloat16)
+    act, g_gate, g_up, g_normed_pieces, g_down = lax.optimization_barrier(
+        (act, g_gate, g_up, g_normed_pieces, g_down)
+    )
+
+    g_normed_parts = exchange_ctx(narrow_others(g_normed_pieces))
+    down_got = scatter_near(g_down)
+    g_gate_up = inner_rows(normed_seq, jnp.concatenate([g_gate, g_up], 1)).astype(jnp.bfloat16)
+    mlp_pieces = chip_sum(after(times_transposed(act, down_here), down_got))
+    down_sum = scatter_far(g_down, *down_got).astype(jnp.bfloat16)
+    g_normed_parts, mlp_pieces, down_sum, g_gate_up = lax.optimization_barrier(
+        (g_normed_parts, mlp_pieces, down_sum, g_gate_up)
+    )
+
+    mlp_parts = exchange_ctx(narrow_others(mlp_pieces))
+    gate_up_got = scatter_near(g_gate_up)
+    g_normed_mlp = add_up(g_normed_parts)
 
     back_mlp, grad_gain_mlp = norm_back(g_normed_mlp, hidden, rms_mlp, gain_two)
     g_hidden = grad_half.astype(jnp.float32) + back_mlp
@@ -344,27 +376,46 @@
         g_values = g_values + inner_rows(probs.astype(jnp.bfloat16), grad_block)
     g_query = jnp.stack(g_query_parts, 1)
     g_blocks = jnp.split(jnp.concatenate([g_keys, g_values], 1), ctx_size, 0)
-    g_key_value = add_up(
-        exchange_ctx([g_blocks[0]] + [block.astype(jnp.bfloat16) for block in g_blocks[1:]])
-    )
+    g_out = inner_rows(g_branch, attn_heads).astype(jnp.bfloat16)
+    g_blocks, mlp_parts, gate_up_got, g_out = lax.optimization_barrier(
+        (g_blocks, mlp_parts, gate_up_got, g_out)
+    )
+
+    g_key_value_parts = exchange_ctx(narrow_others(g_blocks))
+    gate_up_sum = scatter_far(g_gate_up, *gate_up_got).astype(jnp.bfloat16)
+    layer_output = join_halves(relative((hidden + add_up(mlp_parts)).astype(jnp.bfloat16)))
+    g_key_value_parts, gate_up_sum = lax.optimization_barrier((g_key_value_parts, gate_up_sum))
+    g_key_value = add_up(g_key_value_parts)
     g_query_lin = unrope_rows(g_query).reshape(span_rows, query_cols)
     g_key_lin = unrope_rows(g_key_value[:, :HD].reshape(span_rows, 1, HD)).reshape(span_rows, HD)
     projected = jnp.concatenate([g_query_lin, g_key_lin, g_key_value[:, HD:]], 1).astype(
         jnp.bfloat16
     )
-
-    g_normed_attn = sum_half(times_transposed(projected, w_qkv))
+    g_qkv = inner_rows(normed_attn, projected).astype(jnp.bfloat16)
+    down_back = exchange_ctx(row_pieces(after(down_sum, g_key_value_parts)))
+    out_got = scatter_near(after(g_out, gate_up_sum))
+    down_back, out_got, g_qkv = lax.optimization_barrier((down_back, out_got, g_qkv))
+
+    gate_up_back = exchange_ctx(row_pieces(after(gate_up_sum, down_back)))
+    qkv_got = scatter_near(g_qkv)
+    g_normed_attn = sum_half(times_transposed(after(projected, g_qkv), w_qkv))
     back_attn, grad_gain_attn = norm_back(
         g_normed_attn, input_half, own_half(rms_attn), gain_one
     )
-    grad_input = join_halves((g_hidden + back_attn).astype(jnp.bfloat16))
-
-    grad_w_o = scatter_weight(inner_rows(g_branch, attn_heads))
-    grad_w_qkv = scatter_weight(inner_rows(normed_attn, projected))
-
-    gains = jnp.concatenate([grad_gain_attn, grad_gain_mlp])
+    grad_input = join_halves(relative((g_hidden + back_attn).astype(jnp.bfloat16)))
+    out_sum = scatter_far(g_out, *after(out_got, qkv_got))
+    qkv_sum = scatter_far(g_qkv, *qkv_got)
+    attn_sum = jnp.concatenate([qkv_sum, out_sum], 1)
+    attn_back = exchange_ctx(narrow_others(row_pieces(after(attn_sum, gate_up_back))))
+    grad_w_gate, grad_w_up = place_units(gate_up_back, units_here)
+    (grad_w_down,) = place_units(down_back, units_here)
+    grad_w_attn = add_up(attn_back)
+    grad_w_qkv = grad_w_attn[:, : query_cols + 2 * key_cols]
+    grad_w_o = grad_w_attn[:, query_cols + 2 * key_cols :]
+
+    gains = jnp.concatenate([relative(grad_gain_attn), relative(grad_gain_mlp)])
     small = jnp.concatenate([gains, jnp.sum(projected.astype(jnp.float32), 0)])
-    small = add_all(small.reshape(-1, LANES), ("seq", "ctx")).reshape(-1)
+    small = add_all(after(small, attn_sum).reshape(-1, LANES), ("seq", "ctx")).reshape(-1)
     gains = add_all(small[: 2 * model_width].reshape(-1, LANES), ("wt",)).reshape(-1)
     grad_bias = small[2 * model_width :]
     return (

time: 709 us -> 545 us (0.77)
  starting transfers between devices: 181 us -> 110 us
  waiting for transfers between devices: 303 us -> 242 us
  other arithmetic: 53.4 us -> 31.3 us
  matrix products: 98.5 us -> 82.6 us
  local copies, waits for them, and re-layouts: 54.1 us -> 61.9 us
    ppermute x102 -> x78, starting transfers between devices: 181 us -> 110 us  [swap(): return lax.ppermute(values, axis, [(i, i ^ offset) for i in range(size)])]
    ppermute x102 -> x78, waiting for transfers between devices: 303 us -> 242 us  [swap(): return lax.ppermute(values, axis, [(i, i ^ offset) for i in range(size)])]
    unnamed x161 -> x175, local copies, waits for them, and re-layouts: 12.6 us -> 22.8 us
    dot_general x17 -> x16, matrix products: 34.5 us -> 25.8 us  [inner_rows(): lax.dot_general(left, right, (((0,), (0,)), ((), ())), preferred_element_...]
    dot_general x17, matrix products: 33.9 us -> 25.5 us  [times_transposed(): lax.dot_general(left, right, (((1,), (1,)), ((), ())), preferred_element_...]
    another operation x12 -> x5, other arithmetic: 13.2 us -> 5.04 us
  transfers between devices with their start and end apart: 102 -> 78, of which waited for: 39 -> 33; matrix products, arithmetic and copies ran while one was open for 21% -> 22% of each run, Pallas kernels for 0% -> 0%
where the time goes in v2:
time: 545 us; the launch traced here: 536 us
  waiting for transfers between devices  242 us (44%)
  starting transfers between devices  110 us (20%)
  matrix products  82.6 us (15%)
  local copies, waits for them, and re-layouts  61.9 us (11%)
  other arithmetic  31.3 us (6%)
  between operations  8.43 us (2%)
    ppermute x78, waiting for transfers between devices, swap(): return lax.ppermute(values, axis, [(i, i ^ offset) for i in range(size)])  242 us
    ppermute x78, starting transfers between devices, swap(): return lax.ppermute(values, axis, [(i, i ^ offset) for i in range(size)])  110 us
    dot_general x17, matrix products, matmul(): return jnp.dot(left, right, preferred_element_type=jnp.float32)  31.3 us
    dot_general x16, matrix products, inner_rows(): lax.dot_general(left, right, (((0,), (0,)), ((), ())), preferred_element_...  25.8 us
    dot_general x17, matrix products, times_transposed(): lax.dot_general(left, right, (((1,), (1,)), ((), ())), preferred_element_...  25.5 us
    unnamed x175, local copies, waits for them, and re-layouts  22.8 us
  transfers between devices with their start and end apart: 78, of which 33 were waited for; matrix products, arithmetic and copies ran while one was open for 22% of the time, Pallas kernels for 0%

profile of v2, /device:TPU:0, one launch (start us, length us, event | category | flops | bytes accessed | tf_op | source)
XLA Modules:
  0.0 535.7 jit_solution(1496761413907519631)
XLA Ops:
  6.5 3.0 collective-permute-start
  9.5 2.6 collective-permute-start.1
  19.2 2.4 dynamic-slice_bitcast_fusion
  22.2 2.2 pad_dynamic-slice_fusion.4
  24.4 2.5 pad_dynamic-slice_fusion.8
  31.1 5.3 collective-permute-done.1
  41.8 5.5 %collective-permute-start.5 = (bf16[96,2304]{1,0:T(8,128)(2,1)S(1)}, bf16[96,2304]{1,0:T(8,128)(2,1)S(1)}, u32[]{:S(2)}, u32[]{:S(2)}) collective-permute-start(bf16[96,2304]{1,0:T(8,128)(2,1)S(1)} %copy-done.38), channel_id=1, source_target_pairs={{0,2},{2,0},{4,6},{6,4},{1,3},{3,1},{5,7},{7,5},{8,10},{10,8},{12,... | collective-permute-start | bytes 1327112 | tf_op jit(solution)/shard_map/ppermute | solution.py:46
  50.5 13.2 %collective-permute-done.5 = bf16[96,2304]{1,0:T(8,128)(2,1)S(1)} collective-permute-done((bf16[96,2304]{1,0:T(8,128)(2,1)S(1)}, bf16[96,2304]{1,0:T(8,128)(2,1)S(1)}, u32[]{:S(2)}, u32[]{:S(2)}) %collective-permute-start.5) | collective-permute-done | bytes 442400 | tf_op jit(solution)/shard_map/ppermute | solution.py:46
  63.7 16.6 %collective-permute-done.6 = bf16[96,2304]{1,0:T(8,128)(2,1)S(1)} collective-permute-done((bf16[96,2304]{1,0:T(8,128)(2,1)S(1)}, bf16[96,2304]{1,0:T(8,128)(2,1)S(1)}, u32[]{:S(2)}, u32[]{:S(2)}) %collective-permute-start.6) | collective-permute-done | bytes 442400 | tf_op jit(solution)/shard_map/ppermute | solution.py:46
  81.7 6.9 %collective-permute-start.10 = (bf16[96,1152]{1,0:T(8,128)(2,1)S(1)}, bf16[96,1152]{1,0:T(8,128)(2,1)S(1)}, u32[]{:S(2)}, u32[]{:S(2)}) collective-permute-start(bf16[96,1152]{1,0:T(8,128)(2,1)S(1)} %copy-done.50), channel_id=1, source_target_pairs={{0,2},{2,0},{4,6},{6,4},{1,3},{3,1},{5,7},{7,5},{8,10},{10,8},{12,... | collective-permute-start | bytes 663560 | tf_op jit(solution)/shard_map/ppermute | solution.py:46
  95.6 2.8 constant_dynamic-update-slice_fusion.16
  98.6 6.4 %collective-permute-done.11 = bf16[96,1152]{1,0:T(8,128)(2,1)S(1)} collective-permute-done((bf16[96,1152]{1,0:T(8,128)(2,1)S(1)}, bf16[96,1152]{1,0:T(8,128)(2,1)S(1)}, u32[]{:S(2)}, u32[]{:S(2)}) %collective-permute-start.11) | collective-permute-done | bytes 221216 | tf_op jit(solution)/shard_map/ppermute | solution.py:46
  109.4 2.1 collective-permute-start.15
  111.5 3.7 collective-permute-start.14
  118.6 1.7 copy.50
  120.2 1.7 copy.49
  132.1 2.8 fusion.17
  136.0 2.4 collective-permute-start.28
  140.9 11.6 %collective-permute-done.17 = bf16[384,2304]{1,0:T(8,128)(2,1)} collective-permute-done((bf16[384,2304]{1,0:T(8,128)(2,1)}, bf16[384,2304]{1,0:T(8,128)(2,1)}, u32[]{:S(2)}, u32[]{:S(2)}) %collective-permute-start.17) | collective-permute-done | bytes 1769504 | tf_op jit(solution)/shard_map/ppermute | solution.py:46
  156.9 1.7 collective-permute-start.23
  158.5 14.9 %collective-permute-done.27 = bf16[128,1536]{1,0:T(8,128)(2,1)S(1)} collective-permute-done((bf16[128,1536]{1,0:T(8,128)(2,1)S(1)}, bf16[128,1536]{1,0:T(8,128)(2,1)S(1)}, u32[]{:S(2)}, u32[]{:S(2)}) %collective-permute-start.27) | collective-permute-done | bytes 393248 | tf_op jit(solution)/shard_map/ppermute | solution.py:46
  173.5 2.5 collective-permute-start.21
  176.1 1.9 collective-permute-start.19
  182.5 5.0 collective-permute-done.21
  187.5 21.0 %collective-permute-done.20 = bf16[128,1536]{1,0:T(8,128)(2,1)S(1)} collective-permute-done((bf16[128,1536]{1,0:T(8,128)(2,1)S(1)}, bf16[128,1536]{1,0:T(8,128)(2,1)S(1)}, u32[]{:S(2)}, u32[]{:S(2)}) %collective-permute-start.20) | collective-permute-done | bytes 393248 | tf_op jit(solution)/shard_map/ppermute | solution.py:46
  210.7 11.0 %collective-permute-done.31 = bf16[192,1152]{1,0:T(8,128)(2,1)S(1)} collective-permute-done((bf16[192,1152]{1,0:T(8,128)(2,1)S(1)}, bf16[192,1152]{1,0:T(8,128)(2,1)S(1)}, u32[]{:S(2)}, u32[]{:S(2)}) %collective-permute-start.31) | collective-permute-done | bytes 442400 | tf_op jit(solution)/shard_map/ppermute | solution.py:46
  222.0 5.9 %fusion.9 = f32[1024,1152]{1,0:T(8,128)} fusion(bf16[1024,1536]{1,0:T(8,128)(2,1)S(1)} %constant_dynamic-update-slice_fusion.10, bf16[1536,2304]{1,0:T(8,128)(2,1)S(1)} %constant_dynamic-update-slice_fusion.12), kind=kOutput, calls=%fused_computation.22 | convolution fusion | flops 3623878656 | bytes 11403264 | tf_op jit(solution)/shard_map/dot_general | solution.py:29
  227.9 5.8 %fusion.6 = f32[1024,1152]{1,0:T(8,128)} fusion(bf16[1024,1536]{1,0:T(8,128)(2,1)S(1)} %constant_dynamic-update-slice_fusion.10, bf16[1536,2304]{1,0:T(8,128)(2,1)S(1)} %constant_dynamic-update-slice_fusion.12), kind=kOutput, calls=%fused_computation.19 | convolution fusion | flops 3623878656 | bytes 11403264 | tf_op jit(solution)/shard_map/dot_general | solution.py:29
  233.8 11.6 %multiply_convert_fusion = (bf16[1024,1152]{1,0:T(8,128)(2,1)S(1)}, bf16[1024,1152]{1,0:T(8,128)(2,1)}, bf16[1024,1152]{1,0:T(8,128)(2,1)}) fusion(f32[1024,1152]{1,0:T(8,128)} %fusion.9, f32[1024,1152]{1,0:T(8,128)} %fusion.6, bf16[1024,1536]{1,0:T(8,128)(2,1)S(1)} %constant_dynamic-update-slice_fusion.17, bf16[1536,1152]{1,0:T(8,128)(2,1)} %copy-done.40), kind=kOutput, calls=%fused_computation.5 | convolution fusion | flops 3641573376 | bytes 23199744 | tf_op jit(solution)/shard_map/dot_general | solution.py:29
  245.4 6.2 %fusion.4 = f32[1024,1536]{1,0:T(8,128)} fusion(bf16[1024,1152]{1,0:T(8,128)(2,1)S(1)} %get-tuple-element.150, bf16[1536,2304]{1,0:T(8,128)(2,1)S(1)} %constant_dynamic-update-slice_fusion.12), kind=kOutput, calls=%fused_computation.17 | convolution fusion | flops 3623878656 | bytes 12189696 | tf_op jit(solution)/shard_map/dot_general | solution.py:33
  251.6 6.4 %convolution_add_fusion = f32[1024,1536]{1,0:T(8,128)S(1)} fusion(f32[1024,1536]{1,0:T(8,128)} %fusion.4, bf16[1024,1152]{1,0:T(8,128)(2,1)S(1)} %copy-done.68, bf16[1536,2304]{1,0:T(8,128)(2,1)S(1)} %constant_dynamic-update-slice_fusion.12), kind=kOutput, calls=%fused_computation.10 | convolution fusion | flops 3625451520 | bytes 18481152 | tf_op jit(solution)/shard_map/dot_general | solution.py:33
  258.4 3.8 copy-done.29
  262.2 6.6 %convolution_convert_fusion.1 = bf16[1536,1152]{1,0:T(8,128)(2,1)S(1)} fusion(bf16[1024,1536]{1,0:T(8,128)(2,1)S(1)} %copy-done.29, bf16[1024,1152]{1,0:T(8,128)(2,1)} %get-tuple-element.144), kind=kOutput, calls=%fused_computation.1 | convolution fusion | flops 3625648128 | bytes 9043968 | tf_op jit(solution)/shard_map/dot_general | solution.py:39
  268.8 2.3 convert_add_fusion.1
  273.5 1.8 collective-permute-start.37
  275.7 2.0 collective-permute-start.35
  277.7 4.2 fusion.150
  282.0 12.2 %collective-permute-done.37 = bf16[384,1152]{1,0:T(8,128)(2,1)S(1)} collective-permute-done((bf16[384,1152]{1,0:T(8,128)(2,1)S(1)}, bf16[384,1152]{1,0:T(8,128)(2,1)S(1)}, u32[]{:S(2)}, u32[]{:S(2)}) %collective-permute-start.37) | collective-permute-done | bytes 884768 | tf_op jit(solution)/shard_map/ppermute | solution.py:46
  297.6 10.8 %convolution_convert_fusion = bf16[1536,2304]{1,0:T(8,128)(2,1)S(1)} fusion(bf16[1024,1536]{1,0:T(8,128)(2,1)} %copy-done.30, bf16[1024,1152]{1,0:T(8,128)(2,1)} %copy-done.69, bf16[1024,1152]{1,0:T(8,128)(2,1)} %get-tuple-element.149), kind=kOutput, calls=%fused_computation | convolution fusion | flops 7260733440 | bytes 14942208 | tf_op jit(solution)/shard_map/dot_general | solution.py:39
  313.3 2.3 convert_add_fusion
  317.3 5.1 collective-permute-done.36
  325.2 5.0 collective-permute-start.43
  333.9 1.7 collective-permute-start.47
  335.6 2.5 fusion.22
  349.6 2.5 convolution_convert_fusion.3
  352.1 7.8 %collective-permute-done.44 = bf16[128,1536]{1,0:T(8,128)(2,1)S(1)} collective-permute-done((bf16[128,1536]{1,0:T(8,128)(2,1)S(1)}, bf16[128,1536]{1,0:T(8,128)(2,1)S(1)}, u32[]{:S(2)}, u32[]{:S(2)}) %collective-permute-start.44) | collective-permute-done | bytes 393248 | tf_op jit(solution)/shard_map/ppermute | solution.py:46
  359.9 13.7 %collective-permute-done.46 = bf16[384,2304]{1,0:T(8,128)(2,1)S(1)} collective-permute-done((bf16[384,2304]{1,0:T(8,128)(2,1)S(1)}, bf16[384,2304]{1,0:T(8,128)(2,1)S(1)}, u32[]{:S(2)}, u32[]{:S(2)}) %collective-permute-start.46) | collective-permute-done | bytes 1769504 | tf_op jit(solution)/shard_map/ppermute | solution.py:46
  378.9 2.3 collective-permute-start.50
  383.7 11.6 %collective-permute-done.52 = bf16[192,2304]{1,0:T(8,128)(2,1)S(1)} collective-permute-done((bf16[192,2304]{1,0:T(8,128)(2,1)S(1)}, bf16[192,2304]{1,0:T(8,128)(2,1)S(1)}, u32[]{:S(2)}, u32[]{:S(2)}) %collective-permute-start.52) | collective-permute-done | bytes 884768 | tf_op jit(solution)/shard_map/ppermute | solution.py:46
  402.6 1.7 collective-permute-start.58
  404.8 2.6 collective-permute-start.55
  410.3 4.2 collective-permute-done.54
  414.5 7.0 %collective-permute-done.55 = bf16[96,1152]{1,0:T(8,128)(2,1)S(1)} collective-permute-done((bf16[96,1152]{1,0:T(8,128)(2,1)S(1)}, bf16[96,1152]{1,0:T(8,128)(2,1)S(1)}, u32[]{:S(2)}, u32[]{:S(2)}) %collective-permute-start.55) | collective-permute-done | bytes 221216 | tf_op jit(solution)/shard_map/ppermute | solution.py:46
  425.0 3.1 collective-permute-start.72
  431.2 16.5 %collective-permute-done.72 = bf16[96,2304]{1,0:T(8,128)(2,1)S(1)} collective-permute-done((bf16[96,2304]{1,0:T(8,128)(2,1)S(1)}, bf16[96,2304]{1,0:T(8,128)(2,1)S(1)}, u32[]{:S(2)}, u32[]{:S(2)}) %collective-permute-start.72) | collective-permute-done | bytes 442400 | tf_op jit(solution)/shard_map/ppermute | solution.py:46
  450.5 10.6 %collective-permute-done.74 = bf16[96,2304]{1,0:T(8,128)(2,1)S(1)} collective-permute-done((bf16[96,2304]{1,0:T(8,128)(2,1)S(1)}, bf16[96,2304]{1,0:T(8,128)(2,1)S(1)}, u32[]{:S(2)}, u32[]{:S(2)}) %collective-permute-start.74) | collective-permute-done | bytes 442400 | tf_op jit(solution)/shard_map/ppermute | solution.py:46
  466.3 1.6 collective-permute-start.66
  470.5 5.0 collective-permute-done.65
  476.5 5.0 collective-permute-done.63
  483.9 2.3 collective-permute-done.67
  488.0 2.0 collective-permute-done.68
  490.0 10.3 %collective-permute-start.69 = (f32[32,128]{1,0:T(8,128)S(1)}, f32[32,128]{1,0:T(8,128)S(1)}, u32[]{:S(2)}, u32[]{:S(2)}) collective-permute-start(f32[32,128]{1,0:T(8,128)S(1)} %fusion.178), channel_id=1, source_target_pairs={{0,2},{2,0},{4,6},{6,4},{1,3},{3,1},{5,7},{7,5},{8,10},{10,8},{12,... | collective-permute-start | bytes 49160 | tf_op jit(solution)/shard_map/ppermute | solution.py:46
  501.9 2.9 collective-permute-start.75
  506.0 25.3 %collective-permute-done.70 = f32[32,128]{1,0:T(8,128)S(1)} collective-permute-done((f32[32,128]{1,0:T(8,128)S(1)}, f32[32,128]{1,0:T(8,128)S(1)}, u32[]{:S(2)}, u32[]{:S(2)}) %collective-permute-start.70) | collective-permute-done | bytes 16416 | tf_op jit(solution)/shard_map/ppermute | solution.py:46
  (504 shorter events, 139.4 us)
Async XLA Ops:
  6.5 23.5 %collective-permute-start = (bf16[96,1792]{1,0:T(8,128)(2,1)}, bf16[96,1792]{1,0:T(8,128)(2,1)}, u32[]{:S(2)}, u32[]{:S(2)}) collective-permute-start(bf16[96,1792]{1,0:T(8,128)(2,1)} %constant_dynamic-update-slice_fusion.1), channel_id=1, source_target_pairs={{0,2},{2,0},{4,6},{6,4},{1,3},{3,1},{5,7},{7,5},{8,10},{10,8},{12,... | collective-permute-start | bytes 1032200 | tf_op jit(solution)/shard_map/ppermute | solution.py:46
  9.5 26.9 %collective-permute-start.1 = (bf16[96,1792]{1,0:T(8,128)(2,1)}, bf16[96,1792]{1,0:T(8,128)(2,1)}, u32[]{:S(2)}, u32[]{:S(2)}) collective-permute-start(bf16[96,1792]{1,0:T(8,128)(2,1)} %constant_dynamic-update-slice_fusion.1), channel_id=1, source_target_pairs={{0,4},{2,6},{4,0},{6,2},{1,5},{3,7},{5,1},{7,3},{8,12},{10,14},{12... | collective-permute-start | bytes 1032200 | tf_op jit(solution)/shard_map/ppermute | solution.py:46
  12.1 25.4 %collective-permute-start.2 = (bf16[96,1792]{1,0:T(8,128)(2,1)}, bf16[96,1792]{1,0:T(8,128)(2,1)}, u32[]{:S(2)}, u32[]{:S(2)}) collective-permute-start(bf16[96,1792]{1,0:T(8,128)(2,1)} %constant_dynamic-update-slice_fusion.1), channel_id=1, source_target_pairs={{0,6},{2,4},{4,2},{6,0},{1,7},{3,5},{5,3},{7,1},{8,14},{10,12},{12... | collective-permute-start | bytes 1032200 | tf_op jit(solution)/shard_map/ppermute | solution.py:46
  38.6 41.8 %collective-permute-start.3 = (bf16[384,1792]{1,0:T(8,128)(2,1)S(1)}, bf16[384,1792]{1,0:T(8,128)(2,1)S(1)}, u32[]{:S(2)}, u32[]{:S(2)}) collective-permute-start(bf16[384,1792]{1,0:T(8,128)(2,1)S(1)} %constant_dynamic-update-slice_fusion.33), channel_id=1, source_target_pairs={{0,8},{8,0},{16,24},{24,16},{1,9},{9,1},{17,25},{25,17},{2,10},{10... | collective-permute-start | bytes 4128776 | tf_op jit(solution)/shard_map/ppermute | solution.py:46
  40.1 40.2 %collective-permute-start.4 = (bf16[384,1792]{1,0:T(8,128)(2,1)S(1)}, bf16[384,1792]{1,0:T(8,128)(2,1)S(1)}, u32[]{:S(2)}, u32[]{:S(2)}) collective-permute-start(bf16[384,1792]{1,0:T(8,128)(2,1)S(1)} %constant_dynamic-update-slice_fusion.33), channel_id=1, source_target_pairs={{0,16},{8,24},{16,0},{24,8},{1,17},{9,25},{17,1},{25,9},{2,18},{10... | collective-permute-start | bytes 4128776 | tf_op jit(solution)/shard_map/ppermute | solution.py:46
  41.8 21.8 %collective-permute-start.5 = (bf16[96,2304]{1,0:T(8,128)(2,1)S(1)}, bf16[96,2304]{1,0:T(8,128)(2,1)S(1)}, u32[]{:S(2)}, u32[]{:S(2)}) collective-permute-start(bf16[96,2304]{1,0:T(8,128)(2,1)S(1)} %copy-done.38), channel_id=1, source_target_pairs={{0,2},{2,0},{4,6},{6,4},{1,3},{3,1},{5,7},{7,5},{8,10},{10,8},{12,... | collective-permute-start | bytes 1327112 | tf_op jit(solution)/shard_map/ppermute | solution.py:46
  47.4 33.0 %collective-permute-start.6 = (bf16[96,2304]{1,0:T(8,128)(2,1)S(1)}, bf16[96,2304]{1,0:T(8,128)(2,1)S(1)}, u32[]{:S(2)}, u32[]{:S(2)}) collective-permute-start(bf16[96,2304]{1,0:T(8,128)(2,1)S(1)} %pad_maximum_fusion.16), channel_id=1, source_target_pairs={{0,4},{2,6},{4,0},{6,2},{1,5},{3,7},{5,1},{7,3},{8,12},{10,14},{12... | collective-permute-start | bytes 1327112 | tf_op jit(solution)/shard_map/ppermute | solution.py:46
  48.4 31.9 %collective-permute-start.7 = (bf16[96,2304]{1,0:T(8,128)(2,1)S(1)}, bf16[96,2304]{1,0:T(8,128)(2,1)S(1)}, u32[]{:S(2)}, u32[]{:S(2)}) collective-permute-start(bf16[96,2304]{1,0:T(8,128)(2,1)S(1)} %pad_maximum_fusion.17), channel_id=1, source_target_pairs={{0,6},{2,4},{4,2},{6,0},{1,7},{3,5},{5,3},{7,1},{8,14},{10,12},{12... | collective-permute-start | bytes 1327112 | tf_op jit(solution)/shard_map/ppermute | solution.py:46
  80.6 24.5 %collective-permute-start.8 = (bf16[192,1792]{1,0:T(8,128)(2,1)S(1)}, bf16[192,1792]{1,0:T(8,128)(2,1)S(1)}, u32[]{:S(2)}, u32[]{:S(2)}) collective-permute-start(bf16[192,1792]{1,0:T(8,128)(2,1)S(1)} %slice.403), channel_id=1, source_target_pairs={{0,8},{8,0},{16,24},{24,16},{1,9},{9,1},{17,25},{25,17},{2,10},{10... | collective-permute-start | bytes 2064392 | tf_op jit(solution)/shard_map/ppermute | solution.py:46
  81.2 23.9 %collective-permute-start.9 = (bf16[192,1792]{1,0:T(8,128)(2,1)S(1)}, bf16[192,1792]{1,0:T(8,128)(2,1)S(1)}, u32[]{:S(2)}, u32[]{:S(2)}) collective-permute-start(bf16[192,1792]{1,0:T(8,128)(2,1)S(1)} %slice.404), channel_id=1, source_target_pairs={{0,16},{8,24},{16,0},{24,8},{1,17},{9,25},{17,1},{25,9},{2,18},{10... | collective-permute-start | bytes 2064392 | tf_op jit(solution)/shard_map/ppermute | solution.py:46
  81.7 16.9 %collective-permute-start.10 = (bf16[96,1152]{1,0:T(8,128)(2,1)S(1)}, bf16[96,1152]{1,0:T(8,128)(2,1)S(1)}, u32[]{:S(2)}, u32[]{:S(2)}) collective-permute-start(bf16[96,1152]{1,0:T(8,128)(2,1)S(1)} %copy-done.50), channel_id=1, source_target_pairs={{0,2},{2,0},{4,6},{6,4},{1,3},{3,1},{5,7},{7,5},{8,10},{10,8},{12,... | collective-permute-start | bytes 663560 | tf_op jit(solution)/shard_map/ppermute | solution.py:46
  88.6 16.4 %collective-permute-start.11 = (bf16[96,1152]{1,0:T(8,128)(2,1)S(1)}, bf16[96,1152]{1,0:T(8,128)(2,1)S(1)}, u32[]{:S(2)}, u32[]{:S(2)}) collective-permute-start(bf16[96,1152]{1,0:T(8,128)(2,1)S(1)} %copy-done.49), channel_id=1, source_target_pairs={{0,4},{2,6},{4,0},{6,2},{1,5},{3,7},{5,1},{7,3},{8,12},{10,14},{12... | collective-permute-start | bytes 663560 | tf_op jit(solution)/shard_map/ppermute | solution.py:46
  89.6 15.4 %collective-permute-start.12 = (bf16[96,1152]{1,0:T(8,128)(2,1)S(1)}, bf16[96,1152]{1,0:T(8,128)(2,1)S(1)}, u32[]{:S(2)}, u32[]{:S(2)}) collective-permute-start(bf16[96,1152]{1,0:T(8,128)(2,1)S(1)} %copy-done.48), channel_id=1, source_target_pairs={{0,6},{2,4},{4,2},{6,0},{1,7},{3,5},{5,3},{7,1},{8,14},{10,12},{12... | collective-permute-start | bytes 663560 | tf_op jit(solution)/shard_map/ppermute | solution.py:46
  109.4 13.8 %collective-permute-start.15 = (bf16[256,256]{1,0:T(8,128)(2,1)}, bf16[256,256]{1,0:T(8,128)(2,1)}, u32[]{:S(2)}, u32[]{:S(2)}) collective-permute-start(bf16[256,256]{1,0:T(8,128)(2,1)} %pad_maximum_fusion.23), channel_id=1, source_target_pairs={{0,6},{2,4},{4,2},{6,0},{1,7},{3,5},{5,3},{7,1},{8,14},{10,12},{12... | collective-permute-start | bytes 393224 | tf_op jit(solution)/shard_map/ppermute | solution.py:46
  115.4 37.1 %collective-permute-start.17 = (bf16[384,2304]{1,0:T(8,128)(2,1)}, bf16[384,2304]{1,0:T(8,128)(2,1)}, u32[]{:S(2)}, u32[]{:S(2)}) collective-permute-start(bf16[384,2304]{1,0:T(8,128)(2,1)} %constant_dynamic-update-slice_fusion.29), channel_id=1, source_target_pairs={{0,8},{8,0},{16,24},{24,16},{1,9},{9,1},{17,25},{25,17},{2,10},{10... | collective-permute-start | bytes 5308424 | tf_op jit(solution)/shard_map/ppermute | solution.py:46
  116.7 36.8 %collective-permute-start.18 = (bf16[384,2304]{1,0:T(8,128)(2,1)}, bf16[384,2304]{1,0:T(8,128)(2,1)}, u32[]{:S(2)}, u32[]{:S(2)}) collective-permute-start(bf16[384,2304]{1,0:T(8,128)(2,1)} %constant_dynamic-update-slice_fusion.29), channel_id=1, source_target_pairs={{0,16},{8,24},{16,0},{24,8},{1,17},{9,25},{17,1},{25,9},{2,18},{10... | collective-permute-start | bytes 5308424 | tf_op jit(solution)/shard_map/ppermute | solution.py:46
  136.0 22.5 %collective-permute-start.28 = (bf16[128,1536]{1,0:T(8,128)(2,1)S(1)}, bf16[128,1536]{1,0:T(8,128)(2,1)S(1)}, u32[]{:S(2)}, u32[]{:S(2)}) collective-permute-start(bf16[128,1536]{1,0:T(8,128)(2,1)S(1)} %fusion.74), channel_id=1, source_target_pairs={{0,6},{2,4},{4,2},{6,0},{1,7},{3,5},{5,3},{7,1},{8,14},{10,12},{12... | collective-permute-start | bytes 1179656 | tf_op jit(solution)/shard_map/ppermute | solution.py:46
  138.4 35.0 %collective-permute-start.27 = (bf16[128,1536]{1,0:T(8,128)(2,1)S(1)}, bf16[128,1536]{1,0:T(8,128)(2,1)S(1)}, u32[]{:S(2)}, u32[]{:S(2)}) collective-permute-start(bf16[128,1536]{1,0:T(8,128)(2,1)S(1)} %fusion.74), channel_id=1, source_target_pairs={{0,4},{2,6},{4,0},{6,2},{1,5},{3,7},{5,1},{7,3},{8,12},{10,14},{12... | collective-permute-start | bytes 1179656 | tf_op jit(solution)/shard_map/ppermute | solution.py:46
  139.4 34.0 %collective-permute-start.26 = (bf16[128,1536]{1,0:T(8,128)(2,1)S(1)}, bf16[128,1536]{1,0:T(8,128)(2,1)S(1)}, u32[]{:S(2)}, u32[]{:S(2)}) collective-permute-start(bf16[128,1536]{1,0:T(8,128)(2,1)S(1)} %fusion.74), channel_id=1, source_target_pairs={{0,2},{2,0},{4,6},{6,4},{1,3},{3,1},{5,7},{7,5},{8,10},{10,8},{12,... | collective-permute-start | bytes 1179656 | tf_op jit(solution)/shard_map/ppermute | solution.py:46
  154.7 24.9 %collective-permute-start.22 = (bf16[192,2304]{1,0:T(8,128)(2,1)S(1)}, bf16[192,2304]{1,0:T(8,128)(2,1)S(1)}, u32[]{:S(2)}, u32[]{:S(2)}) collective-permute-start(bf16[192,2304]{1,0:T(8,128)(2,1)S(1)} %slice.422), channel_id=1, source_target_pairs={{0,8},{8,0},{16,24},{24,16},{1,9},{9,1},{17,25},{25,17},{2,10},{10... | collective-permute-start | bytes 2654216 | tf_op jit(solution)/shard_map/ppermute | solution.py:46
  156.9 22.8 %collective-permute-start.23 = (bf16[192,2304]{1,0:T(8,128)(2,1)S(1)}, bf16[192,2304]{1,0:T(8,128)(2,1)S(1)}, u32[]{:S(2)}, u32[]{:S(2)}) collective-permute-start(bf16[192,2304]{1,0:T(8,128)(2,1)S(1)} %slice.423), channel_id=1, source_target_pairs={{0,16},{8,24},{16,0},{24,8},{1,17},{9,25},{17,1},{25,9},{2,18},{10... | collective-permute-start | bytes 2654216 | tf_op jit(solution)/shard_map/ppermute | solution.py:46
  173.5 14.0 %collective-permute-start.21 = (bf16[128,1536]{1,0:T(8,128)(2,1)S(1)}, bf16[128,1536]{1,0:T(8,128)(2,1)S(1)}, u32[]{:S(2)}, u32[]{:S(2)}) collective-permute-start(bf16[128,1536]{1,0:T(8,128)(2,1)S(1)} %multiply_convert_fusion.10), channel_id=1, source_target_pairs={{0,6},{2,4},{4,2},{6,0},{1,7},{3,5},{5,3},{7,1},{8,14},{10,12},{12... | collective-permute-start | bytes 1179656 | tf_op jit(solution)/shard_map/ppermute | solution.py:46
  176.1 32.5 %collective-permute-start.20 = (bf16[128,1536]{1,0:T(8,128)(2,1)S(1)}, bf16[128,1536]{1,0:T(8,128)(2,1)S(1)}, u32[]{:S(2)}, u32[]{:S(2)}) collective-permute-start(bf16[128,1536]{1,0:T(8,128)(2,1)S(1)} %multiply_convert_fusion.10), channel_id=1, source_target_pairs={{0,4},{2,6},{4,0},{6,2},{1,5},{3,7},{5,1},{7,3},{8,12},{10,14},{12... | collective-permute-start | bytes 1179656 | tf_op jit(solution)/shard_map/ppermute | solution.py:46
  176.1 32.5 %collective-permute-start.19 = (bf16[128,1536]{1,0:T(8,128)(2,1)S(1)}, bf16[128,1536]{1,0:T(8,128)(2,1)S(1)}, u32[]{:S(2)}, u32[]{:S(2)}) collective-permute-start(bf16[128,1536]{1,0:T(8,128)(2,1)S(1)} %multiply_convert_fusion.10), channel_id=1, source_target_pairs={{0,2},{2,0},{4,6},{6,4},{1,3},{3,1},{5,7},{7,5},{8,10},{10,8},{12,... | collective-permute-start | bytes 1179656 | tf_op jit(solution)/shard_map/ppermute | solution.py:46
  179.6 29.1 %collective-permute-start.24 = (bf16[384,1152]{1,0:T(8,128)(2,1)S(1)}, bf16[384,1152]{1,0:T(8,128)(2,1)S(1)}, u32[]{:S(2)}, u32[]{:S(2)}) collective-permute-start(bf16[384,1152]{1,0:T(8,128)(2,1)S(1)} %constant_dynamic-update-slice_fusion.25), channel_id=1, source_target_pairs={{0,8},{8,0},{16,24},{24,16},{1,9},{9,1},{17,25},{25,17},{2,10},{10... | collective-permute-start | bytes 2654216 | tf_op jit(solution)/shard_map/ppermute | solution.py:46
  180.2 28.5 %collective-permute-start.25 = (bf16[384,1152]{1,0:T(8,128)(2,1)S(1)}, bf16[384,1152]{1,0:T(8,128)(2,1)S(1)}, u32[]{:S(2)}, u32[]{:S(2)}) collective-permute-start(bf16[384,1152]{1,0:T(8,128)(2,1)S(1)} %constant_dynamic-update-slice_fusion.25), channel_id=1, source_target_pairs={{0,16},{8,24},{16,0},{24,8},{1,17},{9,25},{17,1},{25,9},{2,18},{10... | collective-permute-start | bytes 2654216 | tf_op jit(solution)/shard_map/ppermute | solution.py:46
  208.8 13.1 %collective-permute-start.29 = (bf16[512,1536]{1,0:T(8,128)(2,1)S(1)}, bf16[512,1536]{1,0:T(8,128)(2,1)S(1)}, u32[]{:S(2)}, u32[]{:S(2)}) collective-permute-start(bf16[512,1536]{1,0:T(8,128)(2,1)S(1)} %pad_maximum_fusion.3), channel_id=1, source_target_pairs={{0,1},{1,0},{2,3},{3,2},{4,5},{5,4},{6,7},{7,6},{8,9},{9,8},{10,11... | collective-permute-start | bytes 4718600 | tf_op jit(solution)/shard_map/ppermute | solution.py:46
  208.9 24.7 %collective-permute-start.30 = (bf16[512,1536]{1,0:T(8,128)(2,1)S(1)}, bf16[512,1536]{1,0:T(8,128)(2,1)S(1)}, u32[]{:S(2)}, u32[]{:S(2)}) collective-permute-start(bf16[512,1536]{1,0:T(8,128)(2,1)S(1)} %pad_maximum_fusion.4), channel_id=1, source_target_pairs={{0,1},{1,0},{2,3},{3,2},{4,5},{5,4},{6,7},{7,6},{8,9},{9,8},{10,11... | collective-permute-start | bytes 4718600 | tf_op jit(solution)/shard_map/ppermute | solution.py:46
  273.5 20.7 %collective-permute-start.37 = (bf16[384,1152]{1,0:T(8,128)(2,1)S(1)}, bf16[384,1152]{1,0:T(8,128)(2,1)S(1)}, u32[]{:S(2)}, u32[]{:S(2)}) collective-permute-start(bf16[384,1152]{1,0:T(8,128)(2,1)S(1)} %pad_maximum_fusion.5), channel_id=1, source_target_pairs={{0,8},{8,0},{16,24},{24,16},{1,9},{9,1},{17,25},{25,17},{2,10},{10... | collective-permute-start | bytes 2654216 | tf_op jit(solution)/shard_map/ppermute | solution.py:46
  275.3 20.2 %collective-permute-start.38 = (bf16[384,1152]{1,0:T(8,128)(2,1)S(1)}, bf16[384,1152]{1,0:T(8,128)(2,1)S(1)}, u32[]{:S(2)}, u32[]{:S(2)}) collective-permute-start(bf16[384,1152]{1,0:T(8,128)(2,1)S(1)} %pad_maximum_fusion.6), channel_id=1, source_target_pairs={{0,16},{8,24},{16,0},{24,8},{1,17},{9,25},{17,1},{25,9},{2,18},{10... | collective-permute-start | bytes 2654216 | tf_op jit(solution)/shard_map/ppermute | solution.py:46
  275.7 41.7 %collective-permute-start.34 = (bf16[128,1536]{1,0:T(8,128)(2,1)}, bf16[128,1536]{1,0:T(8,128)(2,1)}, u32[]{:S(2)}, u32[]{:S(2)}) collective-permute-start(bf16[128,1536]{1,0:T(8,128)(2,1)} %get-tuple-element.141), channel_id=1, source_target_pairs={{0,2},{2,0},{4,6},{6,4},{1,3},{3,1},{5,7},{7,5},{8,10},{10,8},{12,... | collective-permute-start | bytes 1179656 | tf_op jit(solution)/shard_map/ppermute | solution.py:46
  275.7 41.7 %collective-permute-start.35 = (bf16[128,1536]{1,0:T(8,128)(2,1)}, bf16[128,1536]{1,0:T(8,128)(2,1)}, u32[]{:S(2)}, u32[]{:S(2)}) collective-permute-start(bf16[128,1536]{1,0:T(8,128)(2,1)} %get-tuple-element.142), channel_id=1, source_target_pairs={{0,4},{2,6},{4,0},{6,2},{1,5},{3,7},{5,1},{7,3},{8,12},{10,14},{12... | collective-permute-start | bytes 1179656 | tf_op jit(solution)/shard_map/ppermute | solution.py:46
  295.7 17.6 %collective-permute-start.39 = (bf16[512,1536]{1,0:T(8,128)(2,1)S(1)}, bf16[512,1536]{1,0:T(8,128)(2,1)S(1)}, u32[]{:S(2)}, u32[]{:S(2)}) collective-permute-start(bf16[512,1536]{1,0:T(8,128)(2,1)S(1)} %slice.752), channel_id=1, source_target_pairs={{0,1},{1,0},{2,3},{3,2},{4,5},{5,4},{6,7},{7,6},{8,9},{9,8},{10,11... | collective-permute-start | bytes 4718600 | tf_op jit(solution)/shard_map/ppermute | solution.py:46
  296.8 12.8 %collective-permute-start.40 = (bf16[192,1152]{1,0:T(8,128)(2,1)}, bf16[192,1152]{1,0:T(8,128)(2,1)S(1)}, u32[]{:S(2)}, u32[]{:S(2)}) collective-permute-start(bf16[192,1152]{1,0:T(8,128)(2,1)} %get-tuple-element.147), channel_id=1, source_target_pairs={{0,8},{8,0},{16,24},{24,16},{1,9},{9,1},{17,25},{25,17},{2,10},{10... | collective-permute-start | bytes 1327112 | tf_op jit(solution)/shard_map/ppermute | solution.py:46
  297.3 13.5 %collective-permute-start.41 = (bf16[192,1152]{1,0:T(8,128)(2,1)S(1)}, bf16[192,1152]{1,0:T(8,128)(2,1)}, u32[]{:S(2)}, u32[]{:S(2)}) collective-permute-start(bf16[192,1152]{1,0:T(8,128)(2,1)S(1)} %get-tuple-element.148), channel_id=1, source_target_pairs={{0,16},{8,24},{16,0},{24,8},{1,17},{9,25},{17,1},{25,9},{2,18},{10... | collective-permute-start | bytes 1327112 | tf_op jit(solution)/shard_map/ppermute | solution.py:46
  309.5 13.0 %collective-permute-start.36 = (bf16[128,1536]{1,0:T(8,128)(2,1)}, bf16[128,1536]{1,0:T(8,128)(2,1)S(1)}, u32[]{:S(2)}, u32[]{:S(2)}) collective-permute-start(bf16[128,1536]{1,0:T(8,128)(2,1)} %get-tuple-element.143), channel_id=1, source_target_pairs={{0,6},{2,4},{4,2},{6,0},{1,7},{3,5},{5,3},{7,1},{8,14},{10,12},{12... | collective-permute-start | bytes 1179656 | tf_op jit(solution)/shard_map/ppermute | solution.py:46
  325.2 26.9 %collective-permute-start.43 = (bf16[128,1536]{1,0:T(8,128)(2,1)S(1)}, bf16[128,1536]{1,0:T(8,128)(2,1)S(1)}, u32[]{:S(2)}, u32[]{:S(2)}) collective-permute-start(bf16[128,1536]{1,0:T(8,128)(2,1)S(1)} %get-tuple-element.156), channel_id=1, source_target_pairs={{0,2},{2,0},{4,6},{6,4},{1,3},{3,1},{5,7},{7,5},{8,10},{10,8},{12,... | collective-permute-start | bytes 1179656 | tf_op jit(solution)/shard_map/ppermute | solution.py:46
  330.2 29.7 %collective-permute-start.44 = (bf16[128,1536]{1,0:T(8,128)(2,1)S(1)}, bf16[128,1536]{1,0:T(8,128)(2,1)S(1)}, u32[]{:S(2)}, u32[]{:S(2)}) collective-permute-start(bf16[128,1536]{1,0:T(8,128)(2,1)S(1)} %get-tuple-element.157), channel_id=1, source_target_pairs={{0,4},{2,6},{4,0},{6,2},{1,5},{3,7},{5,1},{7,3},{8,12},{10,14},{12... | collective-permute-start | bytes 1179656 | tf_op jit(solution)/shard_map/ppermute | solution.py:46
  331.2 28.7 %collective-permute-start.45 = (bf16[128,1536]{1,0:T(8,128)(2,1)S(1)}, bf16[128,1536]{1,0:T(8,128)(2,1)S(1)}, u32[]{:S(2)}, u32[]{:S(2)}) collective-permute-start(bf16[128,1536]{1,0:T(8,128)(2,1)S(1)} %get-tuple-element.158), channel_id=1, source_target_pairs={{0,6},{2,4},{4,2},{6,0},{1,7},{3,5},{5,3},{7,1},{8,14},{10,12},{12... | collective-permute-start | bytes 1179656 | tf_op jit(solution)/shard_map/ppermute | solution.py:46
  333.1 40.5 %collective-permute-start.46 = (bf16[384,2304]{1,0:T(8,128)(2,1)S(1)}, bf16[384,2304]{1,0:T(8,128)(2,1)S(1)}, u32[]{:S(2)}, u32[]{:S(2)}) collective-permute-start(bf16[384,2304]{1,0:T(8,128)(2,1)S(1)} %pad_maximum_fusion), channel_id=1, source_target_pairs={{0,8},{8,0},{16,24},{24,16},{1,9},{9,1},{17,25},{25,17},{2,10},{10... | collective-permute-start | bytes 5308424 | tf_op jit(solution)/shard_map/ppermute | solution.py:46
  333.9 40.2 %collective-permute-start.47 = (bf16[384,2304]{1,0:T(8,128)(2,1)S(1)}, bf16[384,2304]{1,0:T(8,128)(2,1)S(1)}, u32[]{:S(2)}, u32[]{:S(2)}) collective-permute-start(bf16[384,2304]{1,0:T(8,128)(2,1)S(1)} %pad_maximum_fusion.1), channel_id=1, source_target_pairs={{0,16},{8,24},{16,0},{24,8},{1,17},{9,25},{17,1},{25,9},{2,18},{10... | collective-permute-start | bytes 5308424 | tf_op jit(solution)/shard_map/ppermute | solution.py:46
  374.9 20.4 %collective-permute-start.52 = (bf16[192,2304]{1,0:T(8,128)(2,1)S(1)}, bf16[192,2304]{1,0:T(8,128)(2,1)S(1)}, u32[]{:S(2)}, u32[]{:S(2)}) collective-permute-start(bf16[192,2304]{1,0:T(8,128)(2,1)S(1)} %get-tuple-element.170), channel_id=1, source_target_pairs={{0,8},{8,0},{16,24},{24,16},{1,9},{9,1},{17,25},{25,17},{2,10},{10... | collective-permute-start | bytes 2654216 | tf_op jit(solution)/shard_map/ppermute | solution.py:46
  376.3 20.0 %collective-permute-start.53 = (bf16[192,2304]{1,0:T(8,128)(2,1)S(1)}, bf16[192,2304]{1,0:T(8,128)(2,1)S(1)}, u32[]{:S(2)}, u32[]{:S(2)}) collective-permute-start(bf16[192,2304]{1,0:T(8,128)(2,1)S(1)} %get-tuple-element.171), channel_id=1, source_target_pairs={{0,16},{8,24},{16,0},{24,8},{1,17},{9,25},{17,1},{25,9},{2,18},{10... | collective-permute-start | bytes 2654216 | tf_op jit(solution)/shard_map/ppermute | solution.py:46
  378.2 18.9 %collective-permute-start.49 = (bf16[256,256]{1,0:T(8,128)(2,1)S(1)}, bf16[256,256]{1,0:T(8,128)(2,1)S(1)}, u32[]{:S(2)}, u32[]{:S(2)}) collective-permute-start(bf16[256,256]{1,0:T(8,128)(2,1)S(1)} %get-tuple-element.165), channel_id=1, source_target_pairs={{0,2},{2,0},{4,6},{6,4},{1,3},{3,1},{5,7},{7,5},{8,10},{10,8},{12,... | collective-permute-start | bytes 393224 | tf_op jit(solution)/shard_map/ppermute | solution.py:46
  378.9 18.2 %collective-permute-start.50 = (bf16[256,256]{1,0:T(8,128)(2,1)S(1)}, bf16[256,256]{1,0:T(8,128)(2,1)S(1)}, u32[]{:S(2)}, u32[]{:S(2)}) collective-permute-start(bf16[256,256]{1,0:T(8,128)(2,1)S(1)} %get-tuple-element.166), channel_id=1, source_target_pairs={{0,4},{2,6},{4,0},{6,2},{1,5},{3,7},{5,1},{7,3},{8,12},{10,14},{12... | collective-permute-start | bytes 393224 | tf_op jit(solution)/shard_map/ppermute | solution.py:46
  381.2 16.0 %collective-permute-start.51 = (bf16[256,256]{1,0:T(8,128)(2,1)S(1)}, bf16[256,256]{1,0:T(8,128)(2,1)S(1)}, u32[]{:S(2)}, u32[]{:S(2)}) collective-permute-start(bf16[256,256]{1,0:T(8,128)(2,1)S(1)} %get-tuple-element.167), channel_id=1, source_target_pairs={{0,6},{2,4},{4,2},{6,0},{1,7},{3,5},{5,3},{7,1},{8,14},{10,12},{12... | collective-permute-start | bytes 393224 | tf_op jit(solution)/shard_map/ppermute | solution.py:46
  401.8 19.7 %collective-permute-start.57 = (bf16[384,768]{1,0:T(8,128)(2,1)S(1)}, bf16[384,768]{1,0:T(8,128)(2,1)S(1)}, u32[]{:S(2)}, u32[]{:S(2)}) collective-permute-start(bf16[384,768]{1,0:T(8,128)(2,1)S(1)} %pad_maximum_fusion.10), channel_id=1, source_target_pairs={{0,8},{8,0},{16,24},{24,16},{1,9},{9,1},{17,25},{25,17},{2,10},{10... | collective-permute-start | bytes 1769480 | tf_op jit(solution)/shard_map/ppermute | solution.py:46
  402.6 18.9 %collective-permute-start.58 = (bf16[384,768]{1,0:T(8,128)(2,1)S(1)}, bf16[384,768]{1,0:T(8,128)(2,1)S(1)}, u32[]{:S(2)}, u32[]{:S(2)}) collective-permute-start(bf16[384,768]{1,0:T(8,128)(2,1)S(1)} %pad_maximum_fusion.11), channel_id=1, source_target_pairs={{0,16},{8,24},{16,0},{24,8},{1,17},{9,25},{17,1},{25,9},{2,18},{10... | collective-permute-start | bytes 1769480 | tf_op jit(solution)/shard_map/ppermute | solution.py:46
  404.8 16.7 %collective-permute-start.55 = (bf16[96,1152]{1,0:T(8,128)(2,1)S(1)}, bf16[96,1152]{1,0:T(8,128)(2,1)S(1)}, u32[]{:S(2)}, u32[]{:S(2)}) collective-permute-start(bf16[96,1152]{1,0:T(8,128)(2,1)S(1)} %get-tuple-element.262), channel_id=1, source_target_pairs={{0,4},{2,6},{4,0},{6,2},{1,5},{3,7},{5,1},{7,3},{8,12},{10,14},{12... | collective-permute-start | bytes 663560 | tf_op jit(solution)/shard_map/ppermute | solution.py:46
  407.4 14.2 %collective-permute-start.56 = (bf16[96,1152]{1,0:T(8,128)(2,1)S(1)}, bf16[96,1152]{1,0:T(8,128)(2,1)S(1)}, u32[]{:S(2)}, u32[]{:S(2)}) collective-permute-start(bf16[96,1152]{1,0:T(8,128)(2,1)S(1)} %get-tuple-element.261), channel_id=1, source_target_pairs={{0,6},{2,4},{4,2},{6,0},{1,7},{3,5},{5,3},{7,1},{8,14},{10,12},{12... | collective-permute-start | bytes 663560 | tf_op jit(solution)/shard_map/ppermute | solution.py:46
  422.8 40.9 %collective-permute-start.59 = (f32[128,1536]{1,0:T(8,128)S(1)}, f32[128,1536]{1,0:T(8,128)S(1)}, u32[]{:S(2)}, u32[]{:S(2)}) collective-permute-start(f32[128,1536]{1,0:T(8,128)S(1)} %constant_dynamic-slice_fusion.8), channel_id=1, source_target_pairs={{0,1},{1,0},{2,3},{3,2},{4,5},{5,4},{6,7},{7,6},{8,9},{9,8},{10,11... | collective-permute-start | bytes 2359304 | tf_op jit(solution)/shard_map/ppermute | solution.py:46
  423.0 42.0 %collective-permute-start.62 = (bf16[384,1024]{1,0:T(8,128)(2,1)S(1)}, bf16[384,1024]{1,0:T(8,128)(2,1)S(1)}, u32[]{:S(2)}, u32[]{:S(2)}) collective-permute-start(bf16[384,1024]{1,0:T(8,128)(2,1)S(1)} %pad_maximum_fusion.9), channel_id=1, source_target_pairs={{0,8},{8,0},{16,24},{24,16},{1,9},{9,1},{17,25},{25,17},{2,10},{10... | collective-permute-start | bytes 2359304 | tf_op jit(solution)/shard_map/ppermute | solution.py:46
  423.6 41.3 %collective-permute-start.61 = (bf16[384,1024]{1,0:T(8,128)(2,1)S(1)}, bf16[384,1024]{1,0:T(8,128)(2,1)S(1)}, u32[]{:S(2)}, u32[]{:S(2)}) collective-permute-start(bf16[384,1024]{1,0:T(8,128)(2,1)S(1)} %pad_maximum_fusion.8), channel_id=1, source_target_pairs={{0,16},{8,24},{16,0},{24,8},{1,17},{9,25},{17,1},{25,9},{2,18},{10... | collective-permute-start | bytes 2359304 | tf_op jit(solution)/shard_map/ppermute | solution.py:46
  425.0 22.7 %collective-permute-start.72 = (bf16[96,2304]{1,0:T(8,128)(2,1)S(1)}, bf16[96,2304]{1,0:T(8,128)(2,1)S(1)}, u32[]{:S(2)}, u32[]{:S(2)}) collective-permute-start(bf16[96,2304]{1,0:T(8,128)(2,1)S(1)} %get-tuple-element.257), channel_id=1, source_target_pairs={{0,2},{2,0},{4,6},{6,4},{1,3},{3,1},{5,7},{7,5},{8,10},{10,8},{12,... | collective-permute-start | bytes 1327112 | tf_op jit(solution)/shard_map/ppermute | solution.py:46
  428.1 22.3 %collective-permute-start.73 = (bf16[96,2304]{1,0:T(8,128)(2,1)S(1)}, bf16[96,2304]{1,0:T(8,128)(2,1)S(1)}, u32[]{:S(2)}, u32[]{:S(2)}) collective-permute-start(bf16[96,2304]{1,0:T(8,128)(2,1)S(1)} %get-tuple-element.256), channel_id=1, source_target_pairs={{0,4},{2,6},{4,0},{6,2},{1,5},{3,7},{5,1},{7,3},{8,12},{10,14},{12... | collective-permute-start | bytes 1327112 | tf_op jit(solution)/shard_map/ppermute | solution.py:46
  447.7 13.4 %collective-permute-start.74 = (bf16[96,2304]{1,0:T(8,128)(2,1)S(1)}, bf16[96,2304]{1,0:T(8,128)(2,1)S(1)}, u32[]{:S(2)}, u32[]{:S(2)}) collective-permute-start(bf16[96,2304]{1,0:T(8,128)(2,1)S(1)} %get-tuple-element.255), channel_id=1, source_target_pairs={{0,6},{2,4},{4,2},{6,0},{1,7},{3,5},{5,3},{7,1},{8,14},{10,12},{12... | collective-permute-start | bytes 1327112 | tf_op jit(solution)/shard_map/ppermute | solution.py:46
  468.2 13.2 %collective-permute-start.63 = (bf16[192,1024]{1,0:T(8,128)(2,1)S(1)}, bf16[192,1024]{1,0:T(8,128)(2,1)S(1)}, u32[]{:S(2)}, u32[]{:S(2)}) collective-permute-start(bf16[192,1024]{1,0:T(8,128)(2,1)S(1)} %get-tuple-element.183), channel_id=1, source_target_pairs={{0,8},{8,0},{16,24},{24,16},{1,9},{9,1},{17,25},{25,17},{2,10},{10... | collective-permute-start | bytes 1179656 | tf_op jit(solution)/shard_map/ppermute | solution.py:46
  468.9 13.0 %collective-permute-start.64 = (bf16[192,1024]{1,0:T(8,128)(2,1)S(1)}, bf16[192,1024]{1,0:T(8,128)(2,1)S(1)}, u32[]{:S(2)}, u32[]{:S(2)}) collective-permute-start(bf16[192,1024]{1,0:T(8,128)(2,1)S(1)} %get-tuple-element.184), channel_id=1, source_target_pairs={{0,16},{8,24},{16,0},{24,8},{1,17},{9,25},{17,1},{25,9},{2,18},{10... | collective-permute-start | bytes 1179656 | tf_op jit(solution)/shard_map/ppermute | solution.py:46
  487.9 17.0 %collective-permute-start.60 = (bf16[128,1536]{1,0:T(8,128)(2,1)S(1)}, bf16[128,1536]{1,0:T(8,128)(2,1)S(1)}, u32[]{:S(2)}, u32[]{:S(2)}) collective-permute-start(bf16[128,1536]{1,0:T(8,128)(2,1)S(1)} %get-tuple-element.300), channel_id=1, source_target_pairs={{0,1},{1,0},{2,3},{3,2},{4,5},{5,4},{6,7},{7,6},{8,9},{9,8},{10,11... | collective-permute-start | bytes 1179656 | tf_op jit(solution)/shard_map/ppermute | solution.py:46
  490.0 14.9 %collective-permute-start.69 = (f32[32,128]{1,0:T(8,128)S(1)}, f32[32,128]{1,0:T(8,128)S(1)}, u32[]{:S(2)}, u32[]{:S(2)}) collective-permute-start(f32[32,128]{1,0:T(8,128)S(1)} %fusion.178), channel_id=1, source_target_pairs={{0,2},{2,0},{4,6},{6,4},{1,3},{3,1},{5,7},{7,5},{8,10},{10,8},{12,... | collective-permute-start | bytes 49160 | tf_op jit(solution)/shard_map/ppermute | solution.py:46
  500.4 33.3 %collective-permute-start.77 = (bf16[96,1792]{1,0:T(8,128)(2,1)S(1)}, bf16[96,1792]{1,0:T(8,128)(2,1)S(1)}, u32[]{:S(2)}, u32[]{:S(2)}) collective-permute-start(bf16[96,1792]{1,0:T(8,128)(2,1)S(1)} %get-tuple-element.245), channel_id=1, source_target_pairs={{0,6},{2,4},{4,2},{6,0},{1,7},{3,5},{5,3},{7,1},{8,14},{10,12},{12... | collective-permute-start | bytes 1032200 | tf_op jit(solution)/shard_map/ppermute | solution.py:46
  501.9 31.8 %collective-permute-start.76 = (bf16[96,1792]{1,0:T(8,128)(2,1)S(1)}, bf16[96,1792]{1,0:T(8,128)(2,1)S(1)}, u32[]{:S(2)}, u32[]{:S(2)}) collective-permute-start(bf16[96,1792]{1,0:T(8,128)(2,1)S(1)} %get-tuple-element.246), channel_id=1, source_target_pairs={{0,4},{2,6},{4,0},{6,2},{1,5},{3,7},{5,1},{7,3},{8,12},{10,14},{12... | collective-permute-start | bytes 1032200 | tf_op jit(solution)/shard_map/ppermute | solution.py:46
  501.9 31.8 %collective-permute-start.75 = (bf16[96,1792]{1,0:T(8,128)(2,1)S(1)}, bf16[96,1792]{1,0:T(8,128)(2,1)S(1)}, u32[]{:S(2)}, u32[]{:S(2)}) collective-permute-start(bf16[96,1792]{1,0:T(8,128)(2,1)S(1)} %get-tuple-element.244), channel_id=1, source_target_pairs={{0,2},{2,0},{4,6},{6,4},{1,3},{3,1},{5,7},{7,5},{8,10},{10,8},{12,... | collective-permute-start | bytes 1032200 | tf_op jit(solution)/shard_map/ppermute | solution.py:46
  504.8 26.4 %collective-permute-start.70 = (f32[32,128]{1,0:T(8,128)S(1)}, f32[32,128]{1,0:T(8,128)S(1)}, u32[]{:S(2)}, u32[]{:S(2)}) collective-permute-start(f32[32,128]{1,0:T(8,128)S(1)} %add.574), channel_id=1, source_target_pairs={{0,4},{2,6},{4,0},{6,2},{1,5},{3,7},{5,1},{7,3},{8,12},{10,14},{12... | collective-permute-start | bytes 49160 | tf_op jit(solution)/shard_map/ppermute | solution.py:46
  (91 other events, 1188.4 us)

commit v3 on v2

v3 whole, which is shorter than its diff:
```python
import functools

import jax
import jax.numpy as jnp
from jax import lax
from jax.experimental import pallas as pl
from jax.experimental.pallas import tpu as pltpu
from jax.sharding import PartitionSpec as P

HD = 128
LANES = 128


EPSILON = 1e-06
THETA_BASE = 1000000.0
NEGATIVE = -1e30


def rope_tables(positions):
    freqs = THETA_BASE ** (-(jnp.arange(HD // 2, dtype=jnp.float32) * 2.0) / HD)
    angles = positions.astype(jnp.float32)[:, None] * freqs[None, :]
    cosines = jnp.cos(angles)
    sines = jnp.sin(angles)
    return (jnp.concatenate([cosines, cosines], -1), jnp.concatenate([sines, sines], -1))


def matmul(left, right):
    return jnp.dot(left, right, preferred_element_type=jnp.float32)


def times_transposed(left, right):
    return lax.dot_general(
        left, right, (((1,), (1,)), ((), ())), preferred_element_type=jnp.float32
    )


def inner_rows(left, right):
    return lax.dot_general(
        left, right, (((0,), (0,)), ((), ())), preferred_element_type=jnp.float32
    )


def swap(values, axis, offset):
    size = lax.axis_size(axis)
    return lax.ppermute(values, axis, [(i, i ^ offset) for i in range(size)])


def rows_at(values, index, count):
    return lax.dynamic_slice_in_dim(values, index * count, count, 0)


def place_rows(parts, indices):
    rows = len(parts) * parts[0].shape[0]
    whole = jnp.zeros((rows,) + parts[0].shape[1:], parts[0].dtype)
    for part, index in zip(parts, indices):
        whole = lax.dynamic_update_slice_in_dim(whole, part, index * part.shape[0], 0)
    return whole


def together(*values):
    return lax.optimization_barrier(values)


def relative(values):
    me = lax.axis_index("seq")
    width = values.shape[-1] // 4
    blocks = [
        lax.dynamic_slice_in_dim(values, (me ^ j) * width, width, values.ndim - 1)
        for j in range(4)
    ]
    return jnp.concatenate(blocks, -1)


def gather_ctx(block):
    size = lax.axis_size("ctx")
    return [block] + [swap(block, "ctx", k) for k in range(1, size)]


def exchange_ctx(pieces):
    return [pieces[0]] + [swap(pieces[k], "ctx", k) for k in range(1, len(pieces))]


def near_seq(shard):
    return swap(shard, "seq", 1), swap(shard, "seq", 2)


def far_seq(from_x, from_y):
    half = from_x.shape[0] // 2
    return swap(from_y[:half], "seq", 1), swap(from_x[half:], "seq", 2)


def scatter_near(partial_sum):
    own, for_x, for_y, for_far = jnp.split(partial_sum, 4, 0)
    half = own.shape[0] // 2
    got_x = swap(jnp.concatenate([for_far[half:], for_x[half:]], 0), "seq", 1)
    got_y = swap(jnp.concatenate([for_far[:half], for_y[:half]], 0), "seq", 2)
    return got_x, got_y


def relay(partial_sum, got_x, got_y):
    _, for_x, for_y, _ = jnp.split(partial_sum, 4, 0)
    half = for_x.shape[0] // 2
    on_x = add_up([for_x[:half], got_y[:half]]).astype(jnp.bfloat16)
    on_y = add_up([for_y[half:], got_x[:half]]).astype(jnp.bfloat16)
    return together(on_x, on_y)


def scatter_end(partial_sum, got_x, got_y, last_x, last_y):
    own = partial_sum[: partial_sum.shape[0] // 4]
    half = own.shape[0] // 2
    top = add_up([own[:half], got_y[half:], last_x])
    bottom = add_up([own[half:], got_x[half:], last_y])
    return jnp.concatenate([top, bottom], 0)


def scatter_far(partial_sum, got_x, got_y):
    on_x, on_y = relay(partial_sum, got_x, got_y)
    return scatter_end(
        partial_sum, got_x, got_y, swap(on_x, "seq", 1), swap(on_y, "seq", 2)
    )


def add_up(parts):
    total = parts[0].astype(jnp.float32)
    for part in parts[1:]:
        total = total + part.astype(jnp.float32)
    return total


def units_per(units):
    size = lax.axis_size("ctx")
    return -(-units // (size * LANES)) * LANES


def unit_pieces(shards):
    size = lax.axis_size("ctx")
    ctx = lax.axis_index("ctx")
    width = units_per(shards[0].shape[1])
    padded = [jnp.pad(w, ((0, 0), (0, size * width - w.shape[1]))) for w in shards]
    return [
        jnp.concatenate(
            [lax.dynamic_slice_in_dim(w, (ctx ^ k) * width, width, 1) for w in padded], 1
        )
        for k in range(size)
    ]


def row_pieces(summed):
    size = lax.axis_size("ctx")
    ctx = lax.axis_index("ctx")
    rows = summed.shape[0] // size
    return [rows_at(summed, ctx ^ k, rows) for k in range(size)]


def place_units(parts, units):
    size = lax.axis_size("ctx")
    ctx = lax.axis_index("ctx")
    width = units_per(units)
    wholes = []
    for start in range(0, parts[0].shape[1], width):
        whole = jnp.zeros((parts[0].shape[0], size * width), jnp.float32)
        for k in range(size):
            part = parts[k][:, start : start + width].astype(jnp.float32)
            whole = lax.dynamic_update_slice_in_dim(whole, part, (ctx ^ k) * width, 1)
        wholes.append(whole[:, :units])
    return wholes


def narrow_others(pieces):
    return [pieces[0]] + [piece.astype(jnp.bfloat16) for piece in pieces[1:]]


VMEM_BYTES = 56 * 1024 * 1024
LITTLE = pl.CostEstimate(flops=1, bytes_accessed=1, transcendentals=0)


def mlp_tile(tiles_each, x_mine, x_other, o_mine, o_other, *refs):
    up_parts, gate_down_parts, far = refs[:3], refs[3:6], refs[6:8]
    outs, scratch = refs[8:14], refs[14:]
    both_ref, act_ref, back_mine, back_send, out_mine, out_send = outs
    gu, down, sems = scratch
    step = pl.program_id(0)
    width = down.shape[1]

    @pl.when(step == 0)
    def _():
        copies = []
        for to, parts, start, far_start in (
            (gu.at[:, pl.ds(0, width)], gate_down_parts, 0, width),
            (gu.at[:, pl.ds(width, width)], up_parts, 0, 0),
            (down, gate_down_parts, width, 2 * width),
        ):
            row = 0
            starts = [start] * len(parts) + [far_start] * len(far)
            for part, column in zip((*parts, *far), starts):
                copies.append(
                    pltpu.make_async_copy(
                        part.at[:, pl.ds(column, width)],
                        to.at[pl.ds(row, part.shape[0])],
                        sems.at[len(copies)],
                    )
                )
                row += part.shape[0]
        for copy in copies:
            copy.start()
        for copy in copies:
            copy.wait()

    own = step < tiles_each
    rows = jnp.where(own, x_mine[...], x_other[...])
    grads = jnp.where(own, o_mine[...], o_other[...])
    gate_up = matmul(rows, gu[...])
    g_act = matmul(grads, down[...])
    gate, up = gate_up[:, :width], gate_up[:, width:]
    sigmoid_gate = 1.0 / (1.0 + jnp.exp(-gate))
    silu_gate = gate * sigmoid_gate
    act = (silu_gate * up).astype(jnp.bfloat16)
    g_gate = (g_act * up * sigmoid_gate * (1.0 + gate * (1.0 - sigmoid_gate))).astype(jnp.bfloat16)
    g_up = (g_act * silu_gate).astype(jnp.bfloat16)
    act_ref[...] = act
    both_ref[:, :width] = g_gate
    both_ref[:, width:] = g_up
    back = times_transposed(g_gate, gu[:, :width]) + times_transposed(g_up, gu[:, width:])
    out = times_transposed(act, down[...])

    @pl.when(own)
    def _():
        back_mine[...] = back
        out_mine[...] = out

    @pl.when(jnp.logical_not(own))
    def _():
        back_send[...] = back.astype(jnp.bfloat16)
        out_send[...] = out.astype(jnp.bfloat16)


def mlp(x_mine, x_other, o_mine, o_other, up_parts, gate_down_parts, far):
    count, model_width = x_mine.shape
    width = up_parts[0].shape[1]
    tile = min(256, count)
    tiles_each = count // tile
    mine = pl.BlockSpec((tile, model_width), lambda i: (jnp.minimum(i, tiles_each - 1), 0))
    other = pl.BlockSpec((tile, model_width), lambda i: (jnp.maximum(i - tiles_each, 0), 0))
    left = pl.BlockSpec(memory_space=pl.ANY)
    return pl.pallas_call(
        functools.partial(mlp_tile, tiles_each),
        grid=(2 * tiles_each,),
        in_specs=[mine, other, mine, other] + [left] * 8,
        out_specs=[
            pl.BlockSpec((tile, 2 * width), lambda i: (i, 0)),
            pl.BlockSpec((tile, width), lambda i: (i, 0)),
            mine,
            other,
            mine,
            other,
        ],
        out_shape=[
            jax.ShapeDtypeStruct((2 * count, 2 * width), jnp.bfloat16),
            jax.ShapeDtypeStruct((2 * count, width), jnp.bfloat16),
            jax.ShapeDtypeStruct((count, model_width), jnp.float32),
            jax.ShapeDtypeStruct((count, model_width), jnp.bfloat16),
            jax.ShapeDtypeStruct((count, model_width), jnp.float32),
            jax.ShapeDtypeStruct((count, model_width), jnp.bfloat16),
        ],
        scratch_shapes=[
            pltpu.VMEM((model_width, 2 * width), jnp.bfloat16),
            pltpu.VMEM((model_width, width), jnp.bfloat16),
            pltpu.SemaphoreType.DMA((15,)),
        ],
        compiler_params=pltpu.CompilerParams(vmem_limit_bytes=VMEM_BYTES),
        cost_estimate=LITTLE,
        name="mlp",
    )(x_mine, x_other, o_mine, o_other, *up_parts, *gate_down_parts, *far)


def weight_tile(x_mine, x_other, grads, out):
    count = x_mine.shape[0]
    out[...] = (
        inner_rows(x_mine[...], grads[:count]) + inner_rows(x_other[...], grads[count:])
    ).astype(jnp.bfloat16)


def weight_grad(x_mine, x_other, grads):
    count, model_width = x_mine.shape
    tile = model_width // 4
    columns = pl.BlockSpec((count, tile), lambda i: (0, i))
    return pl.pallas_call(
        weight_tile,
        grid=(4,),
        in_specs=[columns, columns, pl.BlockSpec(grads.shape, lambda i: (0, 0))],
        out_specs=pl.BlockSpec((tile, grads.shape[1]), lambda i: (i, 0)),
        out_shape=jax.ShapeDtypeStruct((model_width, grads.shape[1]), jnp.bfloat16),
        compiler_params=pltpu.CompilerParams(vmem_limit_bytes=VMEM_BYTES),
        cost_estimate=LITTLE,
        name="weight_grad",
    )(x_mine, x_other, grads)


def call(body, outs, args, scratch=(), name=None, in_specs=None):
    whole = pl.BlockSpec(memory_space=pltpu.VMEM)
    return pl.pallas_call(
        body,
        in_specs=in_specs or [whole] * len(args),
        out_specs=[whole] * len(outs),
        out_shape=[jax.ShapeDtypeStruct(shape, dtype) for shape, dtype in outs],
        scratch_shapes=list(scratch),
        compiler_params=pltpu.CompilerParams(vmem_limit_bytes=VMEM_BYTES),
        cost_estimate=LITTLE,
        name=name,
    )(*args)


def beside_body(*refs):
    *parts, out = refs
    start = 0
    for part in parts:
        out[:, start : start + part.shape[1]] = part[...]
        start += part.shape[1]


def side_by_side(parts):
    cols = sum(part.shape[1] for part in parts)
    return call(
        beside_body, [((parts[0].shape[0], cols), parts[0].dtype)], parts, name="side_by_side"
    )[0]


def place_body(groups, ctx_ref, *refs):
    *parts, out = refs
    count = len(parts) // groups
    rows = parts[0].shape[0]
    start = 0
    for group in range(groups):
        cols = parts[group * count].shape[1]
        for k in range(count):
            here = pl.ds(pl.multiple_of((ctx_ref[0] ^ k) * rows, rows), rows)
            out[here, start : start + cols] = parts[group * count + k][...]
        start += cols


def place_ctx(*groups):
    ctx = lax.axis_index("ctx")
    count, rows = len(groups[0]), groups[0][0].shape[0]
    if rows % 16:
        order = [ctx ^ k for k in range(count)]
        return jnp.concatenate([place_rows(parts, order) for parts in groups], 1)
    cols = sum(parts[0].shape[1] for parts in groups)
    parts = [part for group in groups for part in group]
    return call(
        functools.partial(place_body, len(groups)),
        [((count * rows, cols), parts[0].dtype)],
        [ctx.astype(jnp.int32).reshape(1), *parts],
        name="place",
        in_specs=[pl.BlockSpec(memory_space=pltpu.SMEM)]
        + [pl.BlockSpec(memory_space=pltpu.VMEM)] * len(parts),
    )[0]


def turn(values, cosines, signed_sines):
    return values * cosines + pltpu.roll(values, HD // 2, 1) * signed_sines


def turn_back(grads, cosines, signed_sines):
    return grads * cosines + pltpu.roll(grads, HD // 2, 1) * (-signed_sines)


def project_body(query_cols, key_cols, x, bias, cosines, signed_sines, *refs):
    shard, from_x, from_y, far_top, far_bottom = refs[:5]
    query, key_value, w_qkv, w_out, sems = refs[5:]
    near = shard.shape[0]
    half = near // 2
    split = w_qkv.shape[1]
    copies = []
    for part, start in (
        (shard, 0),
        (from_x, near),
        (from_y, 2 * near),
        (far_top, 3 * near),
        (far_bottom, 3 * near + half),
    ):
        rows = pl.ds(start, part.shape[0])
        left, right = part.at[:, pl.ds(0, split)], part.at[:, pl.ds(split, w_out.shape[1])]
        for source, target in ((left, w_qkv.at[rows]), (right, w_out.at[rows])):
            copies.append(pltpu.make_async_copy(source, target, sems.at[len(copies)]))
    for copy in copies:
        copy.start()
    for copy in copies[::2]:
        copy.wait()
    lin = matmul(x[...], w_qkv[...]) + bias[...]
    for start in range(0, query_cols, HD):
        query[:, start : start + HD] = turn(
            lin[:, start : start + HD], cosines[...], signed_sines[...]
        ).astype(jnp.bfloat16)
    for start in range(0, key_cols, HD):
        key_value[:, start : start + HD] = turn(
            lin[:, query_cols + start : query_cols + start + HD], cosines[...], signed_sines[...]
        ).astype(jnp.bfloat16)
    key_value[:, key_cols:] = lin[:, query_cols + key_cols :].astype(jnp.bfloat16)
    for copy in copies[1::2]:
        copy.wait()


def attend_body(count, core_ref, query, query_pos, key_pos, w_out, *refs):
    parts, (heads, log_sums, mine, send, total) = refs[:count], refs[count:]
    keys = jnp.concatenate([part[:, :HD] for part in parts], 0)
    values = jnp.concatenate([part[:, HD:] for part in parts], 0)
    visible = key_pos[...] <= query_pos[...]
    for start in range(0, query.shape[1], HD):
        scores = jnp.where(
            visible, times_transposed(query[:, start : start + HD], keys) * HD**-0.5, NEGATIVE
        )
        highest = jnp.max(scores, -1, keepdims=True)
        weights = jnp.exp(scores - highest)
        totals = jnp.sum(weights, -1, keepdims=True)
        heads[:, start : start + HD] = matmul(
            (weights * (1.0 / totals)).astype(jnp.bfloat16), values
        ).astype(jnp.bfloat16)
        log_sums[:, start : start + HD] = jnp.broadcast_to(
            highest + jnp.log(totals), (query.shape[0], HD)
        )
    split_rows(core_ref, times_transposed(heads[...], w_out[...]), total, mine, send)


def split_rows(core_ref, values, total, mine, send):
    half = mine.shape[0]
    core = core_ref[0]
    total[...] = values
    mine[...] = total[pl.ds(pl.multiple_of(core * half, half), half)]
    send[...] = total[pl.ds(pl.multiple_of((1 - core) * half, half), half)]


def norm_body(mine, got, inputs, gain, hidden, inverse_rms, normed):
    values = inputs[...] + mine[...] + got[...]
    hidden[...] = values
    inverse = lax.rsqrt(jnp.mean(values * values, -1, keepdims=True) + EPSILON)
    inverse_rms[...] = inverse
    normed[...] = (values * inverse * gain[...]).astype(jnp.bfloat16)


def norm_back_body(count, base, inputs, inverse_rms, gain, *refs):
    parts, outs = refs[:count], refs[count:]
    grads = parts[0][...].astype(jnp.float32)
    for part in parts[1:]:
        grads = grads + part[...].astype(jnp.float32)
    inverse = inverse_rms[...]
    values = inputs[...]
    weighted = grads * gain[...]
    back = inverse * weighted - values * (inverse * inverse * inverse) * jnp.mean(
        weighted * values, -1, keepdims=True
    )
    result = base[...].astype(jnp.float32) + back
    outs[0][...] = jnp.sum(grads * values * inverse, 0, keepdims=True)
    outs[1][...] = result.astype(jnp.bfloat16)
    if len(outs) > 2:
        outs[2][...] = result


def attend_back_body(
    count,
    core_ref,
    branch_mine,
    branch_other,
    query,
    query_pos,
    key_pos,
    w_out,
    heads,
    log_sums,
    cosines,
    signed_sines,
    *refs,
):
    parts, (query_lin, g_out), g_parts = refs[:count], refs[count : count + 2], refs[count + 2 : -1]
    branch = refs[-1]
    half = branch_mine.shape[0]
    core = core_ref[0]
    branch[pl.ds(pl.multiple_of(core * half, half), half)] = branch_mine[...]
    branch[pl.ds(pl.multiple_of((1 - core) * half, half), half)] = branch_other[...]
    keys = jnp.concatenate([part[:, :HD] for part in parts], 0)
    values = jnp.concatenate([part[:, HD:] for part in parts], 0)
    visible = key_pos[...] <= query_pos[...]
    g_heads = matmul(branch[...], w_out[...]).astype(jnp.bfloat16)
    scale = HD**-0.5
    g_keys = jnp.zeros(keys.shape, jnp.float32)
    g_values = jnp.zeros(values.shape, jnp.float32)
    for start in range(0, query.shape[1], HD):
        head = query[:, start : start + HD]
        g_head = g_heads[:, start : start + HD]
        scores = jnp.where(visible, times_transposed(head, keys) * scale, NEGATIVE)
        probs = jnp.exp(scores - log_sums[:, start : start + 1])
        g_probs = times_transposed(g_head, values)
        delta = jnp.sum(probs * g_probs, -1, keepdims=True)
        g_scores = (probs * (g_probs - delta)).astype(jnp.bfloat16)
        query_lin[:, start : start + HD] = turn_back(
            matmul(g_scores, keys) * scale, cosines[...], signed_sines[...]
        ).astype(jnp.bfloat16)
        g_keys = g_keys + inner_rows(g_scores, head)
        g_values = g_values + inner_rows(probs.astype(jnp.bfloat16), g_head)
    g_keys = g_keys * scale
    g_out[...] = inner_rows(branch[...], heads[...]).astype(jnp.bfloat16)
    rows = parts[0].shape[0]
    for k, out in enumerate(g_parts):
        out[:, :HD] = g_keys[k * rows : (k + 1) * rows].astype(out.dtype)
        out[:, HD:] = g_values[k * rows : (k + 1) * rows].astype(out.dtype)


def project_back_body(
    count, core_ref, query_lin, normed, w_qkv, cosines, signed_sines, *refs
):
    parts, (g_qkv, g_bias, mine, send, lin, total) = refs[:count], refs[count:]
    g_parts = parts[0][...].astype(jnp.float32)
    for part in parts[1:]:
        g_parts = g_parts + part[...].astype(jnp.float32)
    cols = query_lin.shape[1]
    lin[:, :cols] = query_lin[...]
    lin[:, cols : cols + HD] = turn_back(
        g_parts[:, :HD], cosines[...], signed_sines[...]
    ).astype(jnp.bfloat16)
    lin[:, cols + HD :] = g_parts[:, HD:].astype(jnp.bfloat16)
    split_rows(core_ref, times_transposed(lin[...], w_qkv[...]), total, mine, send)
    g_qkv[...] = inner_rows(normed[...], lin[...]).astype(jnp.bfloat16)
    g_bias[...] = jnp.sum(lin[...].astype(jnp.float32), 0, keepdims=True)


def chip_sum(own, got):
    return jnp.split(own + got.astype(jnp.float32), lax.axis_size("ctx"), 0)


def add_tree(parts):
    while len(parts) > 1:
        parts = [parts[i] + parts[i + 1] for i in range(0, len(parts), 2)]
    return parts[0]


def with_rows(block, rows):
    return jnp.concatenate([block, jnp.pad(rows, ((0, 0), (0, block.shape[1] - rows.shape[1])))], 0)


def on_device(
    layer_input,
    pairs,
    gain_attn,
    w_q,
    b_q,
    w_k,
    b_k,
    w_v,
    b_v,
    w_o,
    gain_mlp,
    w_gate,
    w_up,
    w_down,
    out_grad,
):
    _, span_rows, model_width = layer_input.shape
    half_rows = span_rows // 2
    query_cols = w_q.shape[1]
    key_cols = w_k.shape[1]
    units_here = w_gate.shape[1]
    ctx_size = lax.axis_size("ctx")
    ctx = lax.axis_index("ctx")
    core = lax.axis_index("wt")

    def own_half(values):
        return rows_at(values, core, half_rows)

    def join_halves(mine):
        other = swap(mine, "wt", 1)
        return jnp.where(
            core == 0, jnp.concatenate([mine, other], 0), jnp.concatenate([other, mine], 0)
        )

    within = jnp.arange(half_rows, dtype=jnp.int32)

    def positions_at(index):
        early = lax.dynamic_index_in_dim(pairs[0], index, 0, False)
        return jnp.concatenate(
            [early * half_rows + within, (2 * ctx_size - 1 - early) * half_rows + within]
        )

    query_positions = positions_at(ctx)
    key_positions = jnp.concatenate([positions_at(ctx ^ k) for k in range(ctx_size)])[None]
    cosines, sines = rope_tables(query_positions)
    signed_sines = jnp.concatenate([-sines[:, : HD // 2], sines[:, HD // 2 :]], 1)
    query_positions = query_positions[:, None]
    core_index = core.astype(jnp.int32).reshape(1)
    scalar = pl.BlockSpec(memory_space=pltpu.SMEM)
    whole = pl.BlockSpec(memory_space=pltpu.VMEM)
    left = pl.BlockSpec(memory_space=pl.ANY)

    input_rows = relative(layer_input.reshape(span_rows, model_width)).astype(jnp.float32)
    grad_out = relative(out_grad.reshape(span_rows, model_width))
    gain_one = relative(gain_attn.astype(jnp.float32))[None]
    gain_two = relative(gain_mlp.astype(jnp.float32))[None]

    attn_parts = gather_ctx(side_by_side([w_q, w_k, w_v, w_o]))
    gate_up_pieces = unit_pieces([w_gate, w_up])
    down_pieces = unit_pieces([w_down])
    grad_half = own_half(grad_out)
    attn_shard = place_ctx(attn_parts)
    attn_shard, gate_up_pieces, down_pieces = together(attn_shard, gate_up_pieces, down_pieces)

    attn_near = near_seq(attn_shard)
    gate_up_parts = exchange_ctx(gate_up_pieces)
    attn_near, gate_up_parts, down_pieces = together(attn_near, gate_up_parts, down_pieces)
    attn_far = far_seq(*attn_near)
    down_parts = exchange_ctx(down_pieces)
    width = units_per(units_here)
    up_shard = place_ctx([part[:, width:] for part in gate_up_parts])
    attn_far, up_shard = together(attn_far, up_shard)
    up_near = near_seq(up_shard)

    rms_attn = lax.rsqrt(jnp.mean(input_rows * input_rows, -1, keepdims=True) + EPSILON)
    normed_attn = (input_rows * rms_attn * gain_one).astype(jnp.bfloat16)
    qkv_cols = query_cols + 2 * key_cols
    bias = jnp.concatenate([b_q, b_k, b_v]).astype(jnp.float32)[None]
    query, key_value, w_qkv, w_out = call(
        functools.partial(project_body, query_cols, key_cols),
        [
            ((span_rows, query_cols), jnp.bfloat16),
            ((span_rows, 2 * key_cols), jnp.bfloat16),
            ((model_width, qkv_cols), jnp.bfloat16),
            ((model_width, query_cols), jnp.bfloat16),
        ],
        [normed_attn, bias, cosines, signed_sines, attn_shard, *attn_near, *attn_far],
        [pltpu.SemaphoreType.DMA((10,))],
        "project",
        [whole] * 4 + [left] * 5,
    )
    key_value, down_parts = together(key_value, down_parts)

    keys_values = gather_ctx(key_value)
    half_f32 = ((half_rows, model_width), jnp.float32)
    half_bf16 = ((half_rows, model_width), jnp.bfloat16)
    row_f32 = ((1, model_width), jnp.float32)
    attn_heads, log_sums, attn_mine, attn_send = call(
        functools.partial(attend_body, ctx_size),
        [
            ((span_rows, query_cols), jnp.bfloat16),
            ((span_rows, query_cols), jnp.float32),
            half_f32,
            half_f32,
        ],
        [core_index, query, query_positions, key_positions, w_out, *keys_values],
        [pltpu.VMEM((span_rows, model_width), jnp.float32)],
        "attend",
        [scalar] + [whole] * (4 + ctx_size),
    )
    input_half = own_half(input_rows)
    hidden, rms_mlp, normed_half = call(
        norm_body,
        [half_f32, ((half_rows, 1), jnp.float32), half_bf16],
        [attn_mine, swap(attn_send, "wt", 1), input_half, gain_two],
        name="norm",
    )
    gate_down_shard = place_ctx([part[:, :width] for part in gate_up_parts], down_parts)
    normed_half, gate_down_shard, up_near = together(normed_half, gate_down_shard, up_near)

    gate_down_near = near_seq(gate_down_shard)
    normed_parts, gate_down_near, grad_half = together(
        gather_ctx(normed_half), gate_down_near, grad_half
    )

    mlp_far = far_seq(*(jnp.concatenate(pair, 1) for pair in zip(up_near, gate_down_near)))
    normed_mine = jnp.concatenate(normed_parts, 0)
    normed_other = swap(normed_mine, "wt", 1)
    grad_parts, mlp_far = together(gather_ctx(grad_half), mlp_far)
    grad_mine = jnp.concatenate(grad_parts, 0)
    grad_other = swap(grad_mine, "wt", 1)
    g_both, act, back_mine, back_send, out_mine, out_send = mlp(
        normed_mine,
        normed_other,
        grad_mine,
        grad_other,
        [up_shard, *up_near],
        [gate_down_shard, *gate_down_near],
        mlp_far,
    )
    back_got = swap(back_send, "wt", 1)
    out_got = swap(out_send, "wt", 1)
    g_down = weight_grad(grad_mine, grad_other, act)
    g_normed_pieces = narrow_others(chip_sum(back_mine, back_got))
    g_normed_pieces, g_down, out_got = together(g_normed_pieces, g_down, out_got)

    g_normed_parts = exchange_ctx(g_normed_pieces)
    down_got = scatter_near(g_down)
    down_got, g_both = together(down_got, g_both)
    g_gate_up = weight_grad(normed_mine, normed_other, g_both)
    mlp_pieces = chip_sum(out_mine, out_got)
    down_sum = scatter_far(g_down, *down_got).astype(jnp.bfloat16)
    g_normed_parts, down_sum, g_gate_up, mlp_pieces = together(
        g_normed_parts, down_sum, g_gate_up, mlp_pieces
    )

    mlp_parts = exchange_ctx(narrow_others(mlp_pieces))
    gate_up_got = scatter_near(g_gate_up)
    down_pieces = row_pieces(down_sum)
    grad_gain_mlp, branch_mine, g_hidden = call(
        functools.partial(norm_back_body, ctx_size),
        [row_f32, half_bf16, half_f32],
        [grad_half, hidden, rms_mlp, gain_two, *g_normed_parts],
        name="mlp_norm_back",
    )
    block = (span_rows, 2 * key_cols)
    query_lin, g_out, *g_blocks = call(
        functools.partial(attend_back_body, ctx_size),
        [
            ((span_rows, query_cols), jnp.bfloat16),
            ((model_width, query_cols), jnp.bfloat16),
            (block, jnp.float32),
        ]
        + [(block, jnp.bfloat16)] * (ctx_size - 1),
        [
            core_index,
            branch_mine,
            swap(branch_mine, "wt", 1),
            query,
            query_positions,
            key_positions,
            w_out,
            attn_heads,
            log_sums,
            cosines,
            signed_sines,
            *keys_values,
        ],
        [pltpu.VMEM((span_rows, model_width), jnp.bfloat16)],
        "attend_back",
        [scalar] + [whole] * (10 + ctx_size),
    )
    g_blocks, mlp_parts, gate_up_got, g_out, down_pieces = together(
        g_blocks, mlp_parts, gate_up_got, g_out, down_pieces
    )

    g_key_value_parts = exchange_ctx(g_blocks)
    on_x, on_y = relay(g_gate_up, *gate_up_got)
    g_key_value_parts, down_pieces, last_x, last_y = together(
        g_key_value_parts, down_pieces, swap(on_x, "seq", 1), swap(on_y, "seq", 2)
    )
    down_back = exchange_ctx(down_pieces)
    gate_up_sum = scatter_end(g_gate_up, *gate_up_got, last_x, last_y).astype(jnp.bfloat16)
    gate_up_pieces = row_pieces(gate_up_sum)
    g_qkv, g_bias, normed_mine_grad, normed_send_grad = call(
        functools.partial(project_back_body, ctx_size),
        [
            ((model_width, qkv_cols), jnp.bfloat16),
            ((1, qkv_cols), jnp.float32),
            half_f32,
            half_f32,
        ],
        [
            core_index,
            query_lin,
            normed_attn,
            w_qkv,
            cosines,
            signed_sines,
            *g_key_value_parts,
        ],
        [
            pltpu.VMEM((span_rows, qkv_cols), jnp.bfloat16),
            pltpu.VMEM((span_rows, model_width), jnp.float32),
        ],
        "project_back",
        [scalar] + [whole] * (5 + ctx_size),
    )
    normed_got_grad, g_out = together(swap(normed_send_grad, "wt", 1), g_out)
    out_got = scatter_near(g_out)
    grad_gain_attn, grad_input_half = call(
        functools.partial(norm_back_body, 2),
        [row_f32, half_bf16],
        [
            g_hidden,
            input_half,
            own_half(rms_attn),
            gain_one,
            normed_mine_grad,
            normed_got_grad,
        ],
        name="attn_norm_back",
    )
    grad_input_half = relative(grad_input_half)

    small = jnp.concatenate(
        [
            relative(grad_gain_attn)[0],
            relative(grad_gain_mlp)[0],
            g_bias[0],
        ]
    ).astype(jnp.bfloat16)
    small_size = small.shape[0]
    small_rows = -(-small_size // (qkv_cols * 16)) * 16
    small = jnp.pad(small, (0, small_rows * qkv_cols - small_size)).reshape(small_rows, qkv_cols)

    down_back, gate_up_pieces, out_got, g_qkv, small = together(
        down_back, gate_up_pieces, out_got, g_qkv, small
    )

    gate_up_back = exchange_ctx(gate_up_pieces)
    _, for_x, for_y, for_far = jnp.split(g_qkv, 4, 0)
    rows = for_x.shape[0]
    half = rows // 2
    got_x = swap(jnp.concatenate([for_far[half:], for_x[half:], small], 0), "seq", 1)
    got_y = swap(jnp.concatenate([for_far[:half], for_y[:half]], 0), "seq", 2)
    attn_got = tuple(jnp.concatenate(pair, 1) for pair in zip((got_x[:rows], got_y), out_got))
    small = add_up([small, got_x[rows:]]).astype(jnp.bfloat16)
    g_attn = jnp.concatenate([g_qkv, g_out], 1)
    on_x, on_y = relay(g_attn, *attn_got)
    last_x = swap(on_x, "seq", 1)
    last_y = swap(with_rows(on_y, small), "seq", 2)
    small = add_up([small, last_y[half:, :qkv_cols]]).astype(jnp.bfloat16)
    attn_sum = scatter_end(g_attn, *attn_got, last_x, last_y[:half])
    attn_pieces = row_pieces(attn_sum)
    attn_send = [with_rows(piece.astype(jnp.bfloat16), small) for piece in attn_pieces]
    attn_send, gate_up_back, grad_input_half, mlp_parts = together(
        attn_send, gate_up_back, grad_input_half, mlp_parts
    )
    attn_back = exchange_ctx(attn_send)
    grad_input = join_halves(grad_input_half)
    layer_output = join_halves(relative((hidden + add_up(mlp_parts)).astype(jnp.bfloat16)))
    attn_back = attn_pieces[:1] + attn_back[1:]
    rows = attn_pieces[0].shape[0]
    grad_w_gate, grad_w_up = place_units(gate_up_back, units_here)
    (grad_w_down,) = place_units(down_back, units_here)
    grad_w_attn = add_up([part[:rows] for part in attn_back])
    grad_w_qkv = grad_w_attn[:, :qkv_cols]
    grad_w_o = grad_w_attn[:, qkv_cols:]
    small = add_tree(
        [small.astype(jnp.float32)]
        + [part[rows:, :qkv_cols].astype(jnp.float32) for part in attn_back[1:]]
    ).reshape(-1)
    gains = small[: 2 * model_width].reshape(-1, LANES)
    gains = (gains + swap(gains, "wt", 1)).reshape(-1)
    grad_bias = small[2 * model_width : small_size]
    return (
        layer_output[None],
        grad_input[None],
        gains[:model_width],
        grad_w_qkv[:, :query_cols],
        grad_bias[:query_cols],
        grad_w_qkv[:, query_cols : query_cols + key_cols],
        grad_bias[query_cols : query_cols + key_cols],
        grad_w_qkv[:, query_cols + key_cols :],
        grad_bias[query_cols + key_cols :],
        grad_w_o,
        gains[model_width:],
        grad_w_gate,
        grad_w_up,
        grad_w_down,
    )


def solution(mesh):
    tokens = P("seq", "ctx", None)
    weight = P(("seq", "ctx"), "wt")
    return jax.shard_map(
        on_device,
        mesh=mesh,
        in_specs=(
            tokens,
            P("seq", None),
            P(),
            weight,
            P("wt"),
            weight,
            P("wt"),
            weight,
            P("wt"),
            weight,
            P(),
            weight,
            weight,
            weight,
            tokens,
        ),
        out_specs=(
            tokens,
            tokens,
            P(),
            weight,
            P("wt"),
            weight,
            P("wt"),
            weight,
            P("wt"),
            weight,
            P(),
            weight,
            weight,
            weight,
        ),
        check_vma=False,
    )
```

time: 545 us -> 521 us (0.956)
  Pallas kernels: 0 us -> 108 us
  matrix products: 82.6 us -> 0 us
  waiting for transfers between devices: 242 us -> 206 us
  local copies, waits for them, and re-layouts: 61.9 us -> 44.4 us
    pallas_call x0 -> x14, Pallas kernels: none -> 108 us  [the longest x11 52.4 us: call(): pl.pallas_call(body, in_specs=in_specs or [whole] * len(args), out_specs=...]
    dot_general x50 -> x0, matrix products: 82.6 us -> none  [the longest x17 31.3 us: matmul(): return jnp.dot(left, right, preferred_element_type=jnp.float32)]
    ppermute x78 -> x70, waiting for transfers between devices: 242 us -> 206 us  [swap(): return lax.ppermute(values, axis, [(i, i ^ offset) for i in range(size)])]
    unnamed x175 -> x136, local copies, waits for them, and re-layouts: 22.8 us -> 10.8 us
    dynamic_update_slice x12 -> x0, local copies, waits for them, and re-layouts: 7.63 us -> none  [place_rows(): lax.dynamic_update_slice_in_dim(whole, part, index * part.shape[0], 0)]
    ppermute x78 -> x70, starting transfers between devices: 110 us -> 112 us  [swap(): return lax.ppermute(values, axis, [(i, i ^ offset) for i in range(size)])]
  transfers between devices with their start and end apart: 78 -> 70, of which waited for: 33 -> 26; matrix products, arithmetic and copies ran while one was open for 22% -> 11% of each run, Pallas kernels for 0% -> 13%
where the time goes in v3:
time: 521 us; the launch traced here: 512 us
  waiting for transfers between devices  206 us (40%)
  starting transfers between devices  112 us (21%)
  Pallas kernels  108 us (21%)
  local copies, waits for them, and re-layouts  44.4 us (9%)
  other arithmetic  33.4 us (6%)
  between operations  7.5 us (1%)
    ppermute x70, waiting for transfers between devices, swap(): return lax.ppermute(values, axis, [(i, i ^ offset) for i in range(size)])  206 us
    ppermute x70, starting transfers between devices, swap(): return lax.ppermute(values, axis, [(i, i ^ offset) for i in range(size)])  112 us
    pallas_call x11, Pallas kernels, call(): pl.pallas_call(body, in_specs=in_specs or [whole] * len(args), out_specs=...  52.4 us
    pallas_call x1, Pallas kernels, mlp(): pl.pallas_call(functools.partial(mlp_tile, tiles_each), grid=(2 * tiles_e...  35.3 us
    pallas_call x2, Pallas kernels, weight_grad(): pl.pallas_call(weight_tile, grid=(4,), in_specs=[columns, columns, pl.Blo...  20.6 us
    unnamed x136, local copies, waits for them, and re-layouts  10.8 us
  transfers between devices with their start and end apart: 70, of which 26 were waited for; matrix products, arithmetic and copies ran while one was open for 11% of the time, Pallas kernels for 13%

profile of v3, /device:TPU:0, one launch (start us, length us, event | category | flops | bytes accessed | tf_op | source)
XLA Modules:
  0.0 511.8 jit_solution(7377493994035545480)
XLA Ops:
  0.6 1.8 side_by_side.1.refs_0_
  2.4 3.0 collective-permute-start
  5.4 2.6 collective-permute-start.1
  15.7 2.5 dynamic-slice_bitcast_fusion
  19.3 1.7 pad_dynamic-slice_fusion.24
  22.5 9.9 %collective-permute-done.1.refs_2_ = bf16[96,1792]{1,0:T(8,128)(2,1)} collective-permute-done((bf16[96,1792]{1,0:T(8,128)(2,1)}, bf16[96,1792]{1,0:T(8,128)(2,1)}, u32[]{:S(2)}, u32[]{:S(2)}) %collective-permute-start.1) | collective-permute-done | bytes 344096 | tf_op jit(solution)/shard_map/ppermute | solution.py:45
  32.4 2.5 place.3.refs_0_
  34.9 1.5 collective-permute-start.3
  36.4 1.5 collective-permute-start.4
  40.0 6.5 %collective-permute-start.5 = (bf16[96,2304]{1,0:T(8,128)(2,1)S(1)}, bf16[96,2304]{1,0:T(8,128)(2,1)S(1)}, u32[]{:S(2)}, u32[]{:S(2)}) collective-permute-start(bf16[96,2304]{1,0:T(8,128)(2,1)S(1)} %pad_maximum_fusion.13), channel_id=1, source_target_pairs={{0,2},{2,0},{4,6},{6,4},{1,3},{3,1},{5,7},{7,5},{8,10},{10,8},{12,... | collective-permute-start | bytes 1327112 | tf_op jit(solution)/shard_map/ppermute | solution.py:45
  50.1 12.7 %collective-permute-done.5 = bf16[96,2304]{1,0:T(8,128)(2,1)S(1)} collective-permute-done((bf16[96,2304]{1,0:T(8,128)(2,1)S(1)}, bf16[96,2304]{1,0:T(8,128)(2,1)S(1)}, u32[]{:S(2)}, u32[]{:S(2)}) %collective-permute-start.5) | collective-permute-done | bytes 442400 | tf_op jit(solution)/shard_map/ppermute | solution.py:45
  62.8 16.6 %collective-permute-done.6 = bf16[96,2304]{1,0:T(8,128)(2,1)S(1)} collective-permute-done((bf16[96,2304]{1,0:T(8,128)(2,1)S(1)}, bf16[96,2304]{1,0:T(8,128)(2,1)S(1)}, u32[]{:S(2)}, u32[]{:S(2)}) %collective-permute-start.6) | collective-permute-done | bytes 442400 | tf_op jit(solution)/shard_map/ppermute | solution.py:45
  83.2 6.9 %collective-permute-start.10 = (bf16[96,1152]{1,0:T(8,128)(2,1)}, bf16[96,1152]{1,0:T(8,128)(2,1)S(1)}, u32[]{:S(2)}, u32[]{:S(2)}) collective-permute-start(bf16[96,1152]{1,0:T(8,128)(2,1)} %get-tuple-element.187), channel_id=1, source_target_pairs={{0,2},{2,0},{4,6},{6,4},{1,3},{3,1},{5,7},{7,5},{8,10},{10,8},{12,... | collective-permute-start | bytes 663560 | tf_op jit(solution)/shard_map/ppermute | solution.py:45
  93.4 2.3 place.4.refs_0_
  97.4 7.3 %project.1 = (bf16[256,768]{1,0:T(8,128)(2,1)}, bf16[256,256]{1,0:T(8,128)(2,1)}, bf16[1536,1024]{1,0:T(8,128)(2,1)}, bf16[1536,768]{1,0:T(8,128)(2,1)}) custom-call(bf16[256,1536]{1,0:T(8,128)(2,1)} %multiply_convert_fusion.x.normed, f32[1,1024]{1,0:T(1,128)} %maximum_convert_fusion.1.bias, f32[256,128]{1,0:T(8,128)} %pad_maximum_fusion.18.cosines, ...), custom_call_target="tpu_custom_call" | custom-call | flops 1 | bytes 1 | tf_op jit(solution)/shard_map/project/pallas_call | solution.py:301
  104.8 1.9 collective-permute-done.11.refs_6_
  106.7 3.9 collective-permute-start.13
  111.7 1.5 collective-permute-start.15
  116.5 4.3 collective-permute-done.14.refs_2_
  121.5 7.9 %attend.1 = (bf16[256,768]{1,0:T(8,128)(2,1)}, f32[256,768]{1,0:T(8,128)}, f32[128,1536]{1,0:T(8,128)}, f32[128,1536]{1,0:T(8,128)}) custom-call(s32[1]{0:T(128)} %bitcast.core_ref, bf16[256,768]{1,0:T(8,128)(2,1)} %get-tuple-element.183.query, s32[256,1]{1,0:T(8,128)} %copy.30.query_pos, s32[1,1024]{1,0:T(1,128)} %bitcast.48, ...), custom_call_target="tpu_custom_call" | custom-call | flops 1 | bytes 1 | tf_op jit(solution)/shard_map/attend/pallas_call | solution.py:301
  132.0 2.9 place.5.refs_3_
  135.0 2.9 norm.1
  141.1 1.5 collective-permute-start.23
  145.1 1.9 collective-permute-start.21
  147.1 14.4 %collective-permute-done.19 = bf16[128,1536]{1,0:T(8,128)(2,1)S(1)} collective-permute-done((bf16[128,1536]{1,0:T(8,128)(2,1)}, bf16[128,1536]{1,0:T(8,128)(2,1)S(1)}, u32[]{:S(2)}, u32[]{:S(2)}) %collective-permute-start.19) | collective-permute-done | bytes 393248 | tf_op jit(solution)/shard_map/ppermute | solution.py:45
  161.6 12.5 %collective-permute-done.20 = bf16[128,1536]{1,0:T(8,128)(2,1)S(1)} collective-permute-done((bf16[128,1536]{1,0:T(8,128)(2,1)}, bf16[128,1536]{1,0:T(8,128)(2,1)S(1)}, u32[]{:S(2)}, u32[]{:S(2)}) %collective-permute-start.20) | collective-permute-done | bytes 393248 | tf_op jit(solution)/shard_map/ppermute | solution.py:45
  174.1 6.6 %collective-permute-done.22.refs_4_ = bf16[384,2304]{1,0:T(8,128)(2,1)S(1)} collective-permute-done((bf16[384,2304]{1,0:T(8,128)(2,1)S(1)}, bf16[384,2304]{1,0:T(8,128)(2,1)S(1)}, u32[]{:S(2)}, u32[]{:S(2)}) %collective-permute-start.22) | collective-permute-done | bytes 1769504 | tf_op jit(solution)/shard_map/ppermute | solution.py:45
  185.6 1.5 collective-permute-start.25
  188.1 1.9 collective-permute-start.27
  190.1 12.3 %collective-permute-done.25 = bf16[128,1536]{1,0:T(8,128)(2,1)S(1)} collective-permute-done((bf16[128,1536]{1,0:T(8,128)(2,1)S(1)}, bf16[128,1536]{1,0:T(8,128)(2,1)S(1)}, u32[]{:S(2)}, u32[]{:S(2)}) %collective-permute-start.25) | collective-permute-done | bytes 393248 | tf_op jit(solution)/shard_map/ppermute | solution.py:45
  202.4 14.4 %collective-permute-done.26 = bf16[128,1536]{1,0:T(8,128)(2,1)S(1)} collective-permute-done((bf16[128,1536]{1,0:T(8,128)(2,1)S(1)}, bf16[128,1536]{1,0:T(8,128)(2,1)S(1)}, u32[]{:S(2)}, u32[]{:S(2)}) %collective-permute-start.26) | collective-permute-done | bytes 393248 | tf_op jit(solution)/shard_map/ppermute | solution.py:45
  217.9 2.6 collective-permute-done.30.o_other.x_other
  221.8 35.3 %mlp.1 = (bf16[1024,2304]{1,0:T(8,128)(2,1)}, bf16[1024,1152]{1,0:T(8,128)(2,1)}, f32[512,1536]{1,0:T(8,128)}, bf16[512,1536]{1,0:T(8,128)(2,1)}, f32[512,1536]{1,0:T(8,128)}, /*index=5*/bf16[512,1536]{1,0:T(8,128)(2,1)}) custom-call(bf16[512,1536]{1,0:T(8,128)(2,1)} %copy-done.2, bf16[512,1536]{1,0:T(8,128)(2,1)} %copy-done.8, bf16[512,1536]{1,0:T(8,128)(2,1)} %copy-done.3, ...), custom_call_target="tpu_custom_call" | custom-call | flops 1 | bytes 1 | tf_op jit(solution)/shard_map/mlp/pallas_call | solution.py:245
  257.7 8.2 %weight_grad.2 = bf16[1536,1152]{1,0:T(8,128)(2,1)} custom-call(bf16[512,1536]{1,0:T(8,128)(2,1)} %copy-done.3, bf16[512,1536]{1,0:T(8,128)(2,1)} %copy-done.9, bf16[1024,1152]{1,0:T(8,128)(2,1)} %get-tuple-element.220.grads), custom_call_target="tpu_custom_call" | custom-call | flops 1 | bytes 1 | tf_op jit(solution)/shard_map/weight_grad/pallas_call | solution.py:287
  271.6 6.6 %collective-permute-start.33 = (bf16[128,1536]{1,0:T(8,128)(2,1)}, bf16[128,1536]{1,0:T(8,128)(2,1)}, u32[]{:S(2)}, u32[]{:S(2)}) collective-permute-start(bf16[128,1536]{1,0:T(8,128)(2,1)} %get-tuple-element.223), channel_id=1, source_target_pairs={{0,2},{2,0},{4,6},{6,4},{1,3},{3,1},{5,7},{7,5},{8,10},{10,8},{12,... | collective-permute-start | bytes 1179656 | tf_op jit(solution)/shard_map/ppermute | solution.py:45
  280.6 1.9 convert_add_fusion
  282.5 8.8 %collective-permute-done.36 = bf16[384,1152]{1,0:T(8,128)(2,1)S(1)} collective-permute-done((bf16[384,1152]{1,0:T(8,128)(2,1)S(1)}, bf16[384,1152]{1,0:T(8,128)(2,1)S(1)}, u32[]{:S(2)}, u32[]{:S(2)}) %collective-permute-start.36) | collective-permute-done | bytes 884768 | tf_op jit(solution)/shard_map/ppermute | solution.py:45
  296.2 12.4 %weight_grad.3 = bf16[1536,2304]{1,0:T(8,128)(2,1)} custom-call(bf16[512,1536]{1,0:T(8,128)(2,1)} %copy-done.2, bf16[512,1536]{1,0:T(8,128)(2,1)} %copy-done.8, bf16[1024,2304]{1,0:T(8,128)(2,1)} %get-tuple-element.232.grads), custom_call_target="tpu_custom_call" | custom-call | flops 1 | bytes 1 | tf_op jit(solution)/shard_map/weight_grad/pallas_call | solution.py:287
  309.4 1.5 add_convert_fusion.7
  311.0 2.2 fusion.41
  315.7 1.5 collective-permute-start.45
  317.2 3.4 mlp_norm_back.1
  320.7 6.6 %collective-permute-start.41 = (bf16[128,1536]{1,0:T(8,128)(2,1)}, bf16[128,1536]{1,0:T(8,128)(2,1)S(1)}, u32[]{:S(2)}, u32[]{:S(2)}) collective-permute-start(bf16[128,1536]{1,0:T(8,128)(2,1)} %get-tuple-element.247), channel_id=1, source_target_pairs={{0,2},{2,0},{4,6},{6,4},{1,3},{3,1},{5,7},{7,5},{8,10},{10,8},{12,... | collective-permute-start | bytes 1179656 | tf_op jit(solution)/shard_map/ppermute | solution.py:45
  330.6 11.8 %attend_back.1 = (bf16[256,768]{1,0:T(8,128)(2,1)}, bf16[1536,768]{1,0:T(8,128)(2,1)}, f32[256,256]{1,0:T(8,128)}, bf16[256,256]{1,0:T(8,128)(2,1)}, bf16[256,256]{1,0:T(8,128)(2,1)}, /*index=5*/bf16[256,256]{1,0:T(8,128)(2,1)}) custom-call(s32[1]{0:T(128)} %bitcast.core_ref, bf16[128,1536]{1,0:T(8,128)(2,1)} %get-tuple-element.239.branch_mine, ...), custom_call_target="tpu_custom_call" | custom-call | flops 1 | bytes 1 | tf_op jit(solution)/shard_map/attend_back/pallas_call | solution.py:301
  342.4 2.8 collective-permute-done.41
  345.2 12.0 %collective-permute-done.42 = bf16[128,1536]{1,0:T(8,128)(2,1)} collective-permute-done((bf16[128,1536]{1,0:T(8,128)(2,1)}, bf16[128,1536]{1,0:T(8,128)(2,1)}, u32[]{:S(2)}, u32[]{:S(2)}) %collective-permute-start.42) | collective-permute-done | bytes 393248 | tf_op jit(solution)/shard_map/ppermute | solution.py:45
  357.3 3.3 add_convert_fusion.2
  362.2 8.3 %collective-permute-start.46 = (bf16[256,256]{1,0:T(8,128)(2,1)}, bf16[256,256]{1,0:T(8,128)(2,1)S(1)}, u32[]{:S(2)}, u32[]{:S(2)}) collective-permute-start(bf16[256,256]{1,0:T(8,128)(2,1)} %get-tuple-element.254), channel_id=1, source_target_pairs={{0,2},{2,0},{4,6},{6,4},{1,3},{3,1},{5,7},{7,5},{8,10},{10,8},{12,... | collective-permute-start | bytes 393224 | tf_op jit(solution)/shard_map/ppermute | solution.py:45
  374.9 7.7 %collective-permute-done.47.refs_2_ = bf16[256,256]{1,0:T(8,128)(2,1)S(1)} collective-permute-done((bf16[256,256]{1,0:T(8,128)(2,1)}, bf16[256,256]{1,0:T(8,128)(2,1)S(1)}, u32[]{:S(2)}, u32[]{:S(2)}) %collective-permute-start.47) | collective-permute-done | bytes 131104 | tf_op jit(solution)/shard_map/ppermute | solution.py:45
  382.7 8.0 %collective-permute-start.51 = (bf16[96,1152]{1,0:T(8,128)(2,1)}, bf16[96,1152]{1,0:T(8,128)(2,1)}, u32[]{:S(2)}, u32[]{:S(2)}) collective-permute-start(bf16[96,1152]{1,0:T(8,128)(2,1)} %get-tuple-element.266), channel_id=1, source_target_pairs={{0,2},{2,0},{4,6},{6,4},{1,3},{3,1},{5,7},{7,5},{8,10},{10,8},{12,... | collective-permute-start | bytes 663560 | tf_op jit(solution)/shard_map/ppermute | solution.py:45
  393.2 6.3 %project_back.1 = (bf16[1536,1024]{1,0:T(8,128)(2,1)}, f32[1,1024]{1,0:T(1,128)}, f32[128,1536]{1,0:T(8,128)}, f32[128,1536]{1,0:T(8,128)}) custom-call(s32[1]{0:T(128)} %bitcast.core_ref, bf16[256,768]{1,0:T(8,128)(2,1)} %get-tuple-element.271.query_lin, bf16[256,1536]{1,0:T(8,128)(2,1)} %multiply_convert_fusion.x.normed, ...), custom_call_target="tpu_custom_call" | custom-call | flops 1 | bytes 1 | tf_op jit(solution)/shard_map/project_back/pallas_call | solution.py:301
  399.6 2.6 add_convert_fusion
  402.2 2.4 fusion.14
  408.1 3.2 attn_norm_back.1
  413.3 8.5 %collective-permute-done.55 = bf16[384,768]{1,0:T(8,128)(2,1)} collective-permute-done((bf16[384,768]{1,0:T(8,128)(2,1)}, bf16[384,768]{1,0:T(8,128)(2,1)}, u32[]{:S(2)}, u32[]{:S(2)}) %collective-permute-start.55) | collective-permute-done | bytes 589856 | tf_op jit(solution)/shard_map/ppermute | solution.py:45
  421.8 1.6 collective-permute-done.56
  426.9 1.9 collective-permute-start.62
  428.8 1.5 collective-permute-start.63
  431.5 12.8 %collective-permute-done.57 = bf16[384,1024]{1,0:T(8,128)(2,1)S(1)} collective-permute-done((bf16[384,1024]{1,0:T(8,128)(2,1)S(1)}, bf16[384,1024]{1,0:T(8,128)(2,1)S(1)}, u32[]{:S(2)}, u32[]{:S(2)}) %collective-permute-start.57) | collective-permute-done | bytes 786464 | tf_op jit(solution)/shard_map/ppermute | solution.py:45
  451.8 11.2 %collective-permute-done.59 = bf16[192,1792]{1,0:T(8,128)(2,1)S(1)} collective-permute-done((bf16[192,1792]{1,0:T(8,128)(2,1)S(1)}, bf16[192,1792]{1,0:T(8,128)(2,1)S(1)}, u32[]{:S(2)}, u32[]{:S(2)}) %collective-permute-start.59) | collective-permute-done | bytes 688160 | tf_op jit(solution)/shard_map/ppermute | solution.py:45
  469.6 2.3 collective-permute-start.68
  472.1 1.9 collective-permute-start.66
  479.5 4.3 collective-permute-done.68
  483.7 23.4 %collective-permute-done.67 = bf16[112,1792]{1,0:T(8,128)(2,1)S(1)} collective-permute-done((bf16[112,1792]{1,0:T(8,128)(2,1)S(1)}, bf16[112,1792]{1,0:T(8,128)(2,1)S(1)}, u32[]{:S(2)}, u32[]{:S(2)}) %collective-permute-start.67) | collective-permute-done | bytes 401440 | tf_op jit(solution)/shard_map/ppermute | solution.py:45
  (350 shorter events, 103.5 us)
Async XLA Ops:
  2.4 20.1 %collective-permute-start = (bf16[96,1792]{1,0:T(8,128)(2,1)}, bf16[96,1792]{1,0:T(8,128)(2,1)}, u32[]{:S(2)}, u32[]{:S(2)}) collective-permute-start(bf16[96,1792]{1,0:T(8,128)(2,1)} %side_by_side.1.refs_0_), channel_id=1, source_target_pairs={{0,2},{2,0},{4,6},{6,4},{1,3},{3,1},{5,7},{7,5},{8,10},{10,8},{12,... | collective-permute-start | bytes 1032200 | tf_op jit(solution)/shard_map/ppermute | solution.py:45
  5.4 26.9 %collective-permute-start.1 = (bf16[96,1792]{1,0:T(8,128)(2,1)}, bf16[96,1792]{1,0:T(8,128)(2,1)}, u32[]{:S(2)}, u32[]{:S(2)}) collective-permute-start(bf16[96,1792]{1,0:T(8,128)(2,1)} %side_by_side.1.refs_0_), channel_id=1, source_target_pairs={{0,4},{2,6},{4,0},{6,2},{1,5},{3,7},{5,1},{7,3},{8,12},{10,14},{12... | collective-permute-start | bytes 1032200 | tf_op jit(solution)/shard_map/ppermute | solution.py:45
  8.0 24.4 %collective-permute-start.2 = (bf16[96,1792]{1,0:T(8,128)(2,1)}, bf16[96,1792]{1,0:T(8,128)(2,1)}, u32[]{:S(2)}, u32[]{:S(2)}) collective-permute-start(bf16[96,1792]{1,0:T(8,128)(2,1)} %side_by_side.1.refs_0_), channel_id=1, source_target_pairs={{0,6},{2,4},{4,2},{6,0},{1,7},{3,5},{5,3},{7,1},{8,14},{10,12},{12... | collective-permute-start | bytes 1032200 | tf_op jit(solution)/shard_map/ppermute | solution.py:45
  34.9 44.6 %collective-permute-start.3 = (bf16[384,1792]{1,0:T(8,128)(2,1)}, bf16[384,1792]{1,0:T(8,128)(2,1)S(1)}, u32[]{:S(2)}, u32[]{:S(2)}) collective-permute-start(bf16[384,1792]{1,0:T(8,128)(2,1)} %place.3.refs_0_), channel_id=1, source_target_pairs={{0,8},{8,0},{16,24},{24,16},{1,9},{9,1},{17,25},{25,17},{2,10},{10... | collective-permute-start | bytes 4128776 | tf_op jit(solution)/shard_map/ppermute | solution.py:45
  36.4 43.1 %collective-permute-start.4 = (bf16[384,1792]{1,0:T(8,128)(2,1)}, bf16[384,1792]{1,0:T(8,128)(2,1)S(1)}, u32[]{:S(2)}, u32[]{:S(2)}) collective-permute-start(bf16[384,1792]{1,0:T(8,128)(2,1)} %place.3.refs_0_), channel_id=1, source_target_pairs={{0,16},{8,24},{16,0},{24,8},{1,17},{9,25},{17,1},{25,9},{2,18},{10... | collective-permute-start | bytes 4128776 | tf_op jit(solution)/shard_map/ppermute | solution.py:45
  40.0 22.8 %collective-permute-start.5 = (bf16[96,2304]{1,0:T(8,128)(2,1)S(1)}, bf16[96,2304]{1,0:T(8,128)(2,1)S(1)}, u32[]{:S(2)}, u32[]{:S(2)}) collective-permute-start(bf16[96,2304]{1,0:T(8,128)(2,1)S(1)} %pad_maximum_fusion.13), channel_id=1, source_target_pairs={{0,2},{2,0},{4,6},{6,4},{1,3},{3,1},{5,7},{7,5},{8,10},{10,8},{12,... | collective-permute-start | bytes 1327112 | tf_op jit(solution)/shard_map/ppermute | solution.py:45
  46.5 33.0 %collective-permute-start.6 = (bf16[96,2304]{1,0:T(8,128)(2,1)S(1)}, bf16[96,2304]{1,0:T(8,128)(2,1)S(1)}, u32[]{:S(2)}, u32[]{:S(2)}) collective-permute-start(bf16[96,2304]{1,0:T(8,128)(2,1)S(1)} %pad_maximum_fusion.14), channel_id=1, source_target_pairs={{0,4},{2,6},{4,0},{6,2},{1,5},{3,7},{5,1},{7,3},{8,12},{10,14},{12... | collective-permute-start | bytes 1327112 | tf_op jit(solution)/shard_map/ppermute | solution.py:45
  47.6 31.9 %collective-permute-start.7 = (bf16[96,2304]{1,0:T(8,128)(2,1)S(1)}, bf16[96,2304]{1,0:T(8,128)(2,1)S(1)}, u32[]{:S(2)}, u32[]{:S(2)}) collective-permute-start(bf16[96,2304]{1,0:T(8,128)(2,1)S(1)} %pad_maximum_fusion.15), channel_id=1, source_target_pairs={{0,6},{2,4},{4,2},{6,0},{1,7},{3,5},{5,3},{7,1},{8,14},{10,12},{12... | collective-permute-start | bytes 1327112 | tf_op jit(solution)/shard_map/ppermute | solution.py:45
  79.6 16.1 %collective-permute-start.8 = (bf16[192,1792]{1,0:T(8,128)(2,1)S(1)}, bf16[192,1792]{1,0:T(8,128)(2,1)S(1)}, u32[]{:S(2)}, u32[]{:S(2)}) collective-permute-start(bf16[192,1792]{1,0:T(8,128)(2,1)S(1)} %slice.305), channel_id=1, source_target_pairs={{0,8},{8,0},{16,24},{24,16},{1,9},{9,1},{17,25},{25,17},{2,10},{10... | collective-permute-start | bytes 2064392 | tf_op jit(solution)/shard_map/ppermute | solution.py:45
  80.2 15.5 %collective-permute-start.9 = (bf16[192,1792]{1,0:T(8,128)(2,1)S(1)}, bf16[192,1792]{1,0:T(8,128)(2,1)S(1)}, u32[]{:S(2)}, u32[]{:S(2)}) collective-permute-start(bf16[192,1792]{1,0:T(8,128)(2,1)S(1)} %slice.306), channel_id=1, source_target_pairs={{0,16},{8,24},{16,0},{24,8},{1,17},{9,25},{17,1},{25,9},{2,18},{10... | collective-permute-start | bytes 2064392 | tf_op jit(solution)/shard_map/ppermute | solution.py:45
  83.2 21.5 %collective-permute-start.10 = (bf16[96,1152]{1,0:T(8,128)(2,1)}, bf16[96,1152]{1,0:T(8,128)(2,1)S(1)}, u32[]{:S(2)}, u32[]{:S(2)}) collective-permute-start(bf16[96,1152]{1,0:T(8,128)(2,1)} %get-tuple-element.187), channel_id=1, source_target_pairs={{0,2},{2,0},{4,6},{6,4},{1,3},{3,1},{5,7},{7,5},{8,10},{10,8},{12,... | collective-permute-start | bytes 663560 | tf_op jit(solution)/shard_map/ppermute | solution.py:45
  90.1 16.5 %collective-permute-start.11 = (bf16[96,1152]{1,0:T(8,128)(2,1)}, bf16[96,1152]{1,0:T(8,128)(2,1)S(1)}, u32[]{:S(2)}, u32[]{:S(2)}) collective-permute-start(bf16[96,1152]{1,0:T(8,128)(2,1)} %get-tuple-element.188), channel_id=1, source_target_pairs={{0,4},{2,6},{4,0},{6,2},{1,5},{3,7},{5,1},{7,3},{8,12},{10,14},{12... | collective-permute-start | bytes 663560 | tf_op jit(solution)/shard_map/ppermute | solution.py:45
  91.1 15.6 %collective-permute-start.12 = (bf16[96,1152]{1,0:T(8,128)(2,1)S(1)}, bf16[96,1152]{1,0:T(8,128)(2,1)S(1)}, u32[]{:S(2)}, u32[]{:S(2)}) collective-permute-start(bf16[96,1152]{1,0:T(8,128)(2,1)S(1)} %copy-done.49), channel_id=1, source_target_pairs={{0,6},{2,4},{4,2},{6,0},{1,7},{3,5},{5,3},{7,1},{8,14},{10,12},{12... | collective-permute-start | bytes 663560 | tf_op jit(solution)/shard_map/ppermute | solution.py:45
  106.7 9.8 %collective-permute-start.13 = (bf16[256,256]{1,0:T(8,128)(2,1)}, bf16[256,256]{1,0:T(8,128)(2,1)S(1)}, u32[]{:S(2)}, u32[]{:S(2)}) collective-permute-start(bf16[256,256]{1,0:T(8,128)(2,1)} %get-tuple-element.190.refs_0_), channel_id=1, source_target_pairs={{0,2},{2,0},{4,6},{6,4},{1,3},{3,1},{5,7},{7,5},{8,10},{10,8},{12,... | collective-permute-start | bytes 393224 | tf_op jit(solution)/shard_map/ppermute | solution.py:45
  110.6 10.2 %collective-permute-start.14 = (bf16[256,256]{1,0:T(8,128)(2,1)}, bf16[256,256]{1,0:T(8,128)(2,1)S(1)}, u32[]{:S(2)}, u32[]{:S(2)}) collective-permute-start(bf16[256,256]{1,0:T(8,128)(2,1)} %get-tuple-element.190.refs_0_), channel_id=1, source_target_pairs={{0,4},{2,6},{4,0},{6,2},{1,5},{3,7},{5,1},{7,3},{8,12},{10,14},{12... | collective-permute-start | bytes 393224 | tf_op jit(solution)/shard_map/ppermute | solution.py:45
  111.7 9.2 %collective-permute-start.15 = (bf16[256,256]{1,0:T(8,128)(2,1)}, bf16[256,256]{1,0:T(8,128)(2,1)}, u32[]{:S(2)}, u32[]{:S(2)}) collective-permute-start(bf16[256,256]{1,0:T(8,128)(2,1)} %get-tuple-element.190.refs_0_), channel_id=1, source_target_pairs={{0,6},{2,4},{4,2},{6,0},{1,7},{3,5},{5,3},{7,1},{8,14},{10,12},{12... | collective-permute-start | bytes 393224 | tf_op jit(solution)/shard_map/ppermute | solution.py:45
  114.6 23.3 %collective-permute-start.17 = (bf16[384,1152]{1,0:T(8,128)(2,1)S(1)}, bf16[384,1152]{1,0:T(8,128)(2,1)S(1)}, u32[]{:S(2)}, u32[]{:S(2)}) collective-permute-start(bf16[384,1152]{1,0:T(8,128)(2,1)S(1)} %copy-done.13), channel_id=1, source_target_pairs={{0,8},{8,0},{16,24},{24,16},{1,9},{9,1},{17,25},{25,17},{2,10},{10... | collective-permute-start | bytes 2654216 | tf_op jit(solution)/shard_map/ppermute | solution.py:45
  115.6 22.2 %collective-permute-start.18 = (bf16[384,1152]{1,0:T(8,128)(2,1)S(1)}, bf16[384,1152]{1,0:T(8,128)(2,1)S(1)}, u32[]{:S(2)}, u32[]{:S(2)}) collective-permute-start(bf16[384,1152]{1,0:T(8,128)(2,1)S(1)} %copy-done.13), channel_id=1, source_target_pairs={{0,16},{8,24},{16,0},{24,8},{1,17},{9,25},{17,1},{25,9},{2,18},{10... | collective-permute-start | bytes 2654216 | tf_op jit(solution)/shard_map/ppermute | solution.py:45
  139.7 41.0 %collective-permute-start.22 = (bf16[384,2304]{1,0:T(8,128)(2,1)S(1)}, bf16[384,2304]{1,0:T(8,128)(2,1)S(1)}, u32[]{:S(2)}, u32[]{:S(2)}) collective-permute-start(bf16[384,2304]{1,0:T(8,128)(2,1)S(1)} %copy-done.4), channel_id=1, source_target_pairs={{0,8},{8,0},{16,24},{24,16},{1,9},{9,1},{17,25},{25,17},{2,10},{10... | collective-permute-start | bytes 5308424 | tf_op jit(solution)/shard_map/ppermute | solution.py:45
  141.1 40.7 %collective-permute-start.23 = (bf16[384,2304]{1,0:T(8,128)(2,1)S(1)}, bf16[384,2304]{1,0:T(8,128)(2,1)S(1)}, u32[]{:S(2)}, u32[]{:S(2)}) collective-permute-start(bf16[384,2304]{1,0:T(8,128)(2,1)S(1)} %copy-done.4), channel_id=1, source_target_pairs={{0,16},{8,24},{16,0},{24,8},{1,17},{9,25},{17,1},{25,9},{2,18},{10... | collective-permute-start | bytes 5308424 | tf_op jit(solution)/shard_map/ppermute | solution.py:45
  142.7 18.9 %collective-permute-start.19 = (bf16[128,1536]{1,0:T(8,128)(2,1)}, bf16[128,1536]{1,0:T(8,128)(2,1)S(1)}, u32[]{:S(2)}, u32[]{:S(2)}) collective-permute-start(bf16[128,1536]{1,0:T(8,128)(2,1)} %get-tuple-element.204), channel_id=1, source_target_pairs={{0,2},{2,0},{4,6},{6,4},{1,3},{3,1},{5,7},{7,5},{8,10},{10,8},{12,... | collective-permute-start | bytes 1179656 | tf_op jit(solution)/shard_map/ppermute | solution.py:45
  144.1 30.0 %collective-permute-start.20 = (bf16[128,1536]{1,0:T(8,128)(2,1)}, bf16[128,1536]{1,0:T(8,128)(2,1)S(1)}, u32[]{:S(2)}, u32[]{:S(2)}) collective-permute-start(bf16[128,1536]{1,0:T(8,128)(2,1)} %get-tuple-element.204), channel_id=1, source_target_pairs={{0,4},{2,6},{4,0},{6,2},{1,5},{3,7},{5,1},{7,3},{8,12},{10,14},{12... | collective-permute-start | bytes 1179656 | tf_op jit(solution)/shard_map/ppermute | solution.py:45
  145.1 29.0 %collective-permute-start.21 = (bf16[128,1536]{1,0:T(8,128)(2,1)}, bf16[128,1536]{1,0:T(8,128)(2,1)S(1)}, u32[]{:S(2)}, u32[]{:S(2)}) collective-permute-start(bf16[128,1536]{1,0:T(8,128)(2,1)} %get-tuple-element.204), channel_id=1, source_target_pairs={{0,6},{2,4},{4,2},{6,0},{1,7},{3,5},{5,3},{7,1},{8,14},{10,12},{12... | collective-permute-start | bytes 1179656 | tf_op jit(solution)/shard_map/ppermute | solution.py:45
  183.1 33.7 %collective-permute-start.28 = (bf16[192,3456]{1,0:T(8,128)(2,1)S(1)}, bf16[192,3456]{1,0:T(8,128)(2,1)S(1)}, u32[]{:S(2)}, u32[]{:S(2)}) collective-permute-start(bf16[192,3456]{1,0:T(8,128)(2,1)S(1)} %pad_maximum_fusion.3), channel_id=1, source_target_pairs={{0,8},{8,0},{16,24},{24,16},{1,9},{9,1},{17,25},{25,17},{2,10},{10... | collective-permute-start | bytes 3981320 | tf_op jit(solution)/shard_map/ppermute | solution.py:45
  184.1 32.7 %collective-permute-start.29 = (bf16[192,3456]{1,0:T(8,128)(2,1)S(1)}, bf16[192,3456]{1,0:T(8,128)(2,1)S(1)}, u32[]{:S(2)}, u32[]{:S(2)}) collective-permute-start(bf16[192,3456]{1,0:T(8,128)(2,1)S(1)} %pad_maximum_fusion.2), channel_id=1, source_target_pairs={{0,16},{8,24},{16,0},{24,8},{1,17},{9,25},{17,1},{25,9},{2,18},{10... | collective-permute-start | bytes 3981320 | tf_op jit(solution)/shard_map/ppermute | solution.py:45
  185.6 16.9 %collective-permute-start.25 = (bf16[128,1536]{1,0:T(8,128)(2,1)S(1)}, bf16[128,1536]{1,0:T(8,128)(2,1)S(1)}, u32[]{:S(2)}, u32[]{:S(2)}) collective-permute-start(bf16[128,1536]{1,0:T(8,128)(2,1)S(1)} %fusion.23.base), channel_id=1, source_target_pairs={{0,2},{2,0},{4,6},{6,4},{1,3},{3,1},{5,7},{7,5},{8,10},{10,8},{12,... | collective-permute-start | bytes 1179656 | tf_op jit(solution)/shard_map/ppermute | solution.py:45
  187.0 29.8 %collective-permute-start.26 = (bf16[128,1536]{1,0:T(8,128)(2,1)S(1)}, bf16[128,1536]{1,0:T(8,128)(2,1)S(1)}, u32[]{:S(2)}, u32[]{:S(2)}) collective-permute-start(bf16[128,1536]{1,0:T(8,128)(2,1)S(1)} %fusion.23.base), channel_id=1, source_target_pairs={{0,4},{2,6},{4,0},{6,2},{1,5},{3,7},{5,1},{7,3},{8,12},{10,14},{12... | collective-permute-start | bytes 1179656 | tf_op jit(solution)/shard_map/ppermute | solution.py:45
  188.1 28.8 %collective-permute-start.27 = (bf16[128,1536]{1,0:T(8,128)(2,1)S(1)}, bf16[128,1536]{1,0:T(8,128)(2,1)S(1)}, u32[]{:S(2)}, u32[]{:S(2)}) collective-permute-start(bf16[128,1536]{1,0:T(8,128)(2,1)S(1)} %fusion.23.base), channel_id=1, source_target_pairs={{0,6},{2,4},{4,2},{6,0},{1,7},{3,5},{5,3},{7,1},{8,14},{10,12},{12... | collective-permute-start | bytes 1179656 | tf_op jit(solution)/shard_map/ppermute | solution.py:45
  202.4 14.7 %collective-permute-start.24 = (bf16[512,1536]{1,0:T(8,128)(2,1)S(1)}, bf16[512,1536]{1,0:T(8,128)(2,1)S(1)}, u32[]{:S(2)}, u32[]{:S(2)}) collective-permute-start(bf16[512,1536]{1,0:T(8,128)(2,1)S(1)} %constant_dynamic-update-slice_fusion.1.x_mine), channel_id=1, source_target_pairs={{0,1},{1,0},{2,3},{3,2},{4,5},{5,4},{6,7},{7,6},{8,9},{9,8},{10,11... | collective-permute-start | bytes 4718600 | tf_op jit(solution)/shard_map/ppermute | solution.py:45
  257.1 8.8 %collective-permute-start.31 = (bf16[512,1536]{1,0:T(8,128)(2,1)}, bf16[512,1536]{1,0:T(8,128)(2,1)S(1)}, u32[]{:S(2)}, u32[]{:S(2)}) collective-permute-start(bf16[512,1536]{1,0:T(8,128)(2,1)} %get-tuple-element.219), channel_id=1, source_target_pairs={{0,1},{1,0},{2,3},{3,2},{4,5},{5,4},{6,7},{7,6},{8,9},{9,8},{10,11... | collective-permute-start | bytes 4718600 | tf_op jit(solution)/shard_map/ppermute | solution.py:45
  257.3 11.1 %collective-permute-start.32 = (bf16[512,1536]{1,0:T(8,128)(2,1)}, bf16[512,1536]{1,0:T(8,128)(2,1)S(1)}, u32[]{:S(2)}, u32[]{:S(2)}) collective-permute-start(bf16[512,1536]{1,0:T(8,128)(2,1)} %get-tuple-element.221), channel_id=1, source_target_pairs={{0,1},{1,0},{2,3},{3,2},{4,5},{5,4},{6,7},{7,6},{8,9},{9,8},{10,11... | collective-permute-start | bytes 4718600 | tf_op jit(solution)/shard_map/ppermute | solution.py:45
  269.6 21.7 %collective-permute-start.36 = (bf16[384,1152]{1,0:T(8,128)(2,1)S(1)}, bf16[384,1152]{1,0:T(8,128)(2,1)S(1)}, u32[]{:S(2)}, u32[]{:S(2)}) collective-permute-start(bf16[384,1152]{1,0:T(8,128)(2,1)S(1)} %pad_maximum_fusion.4), channel_id=1, source_target_pairs={{0,8},{8,0},{16,24},{24,16},{1,9},{9,1},{17,25},{25,17},{2,10},{10... | collective-permute-start | bytes 2654216 | tf_op jit(solution)/shard_map/ppermute | solution.py:45
  271.0 21.5 %collective-permute-start.37 = (bf16[384,1152]{1,0:T(8,128)(2,1)S(1)}, bf16[384,1152]{1,0:T(8,128)(2,1)S(1)}, u32[]{:S(2)}, u32[]{:S(2)}) collective-permute-start(bf16[384,1152]{1,0:T(8,128)(2,1)S(1)} %pad_maximum_fusion.5), channel_id=1, source_target_pairs={{0,16},{8,24},{16,0},{24,8},{1,17},{9,25},{17,1},{25,9},{2,18},{10... | collective-permute-start | bytes 2654216 | tf_op jit(solution)/shard_map/ppermute | solution.py:45
  271.6 39.4 %collective-permute-start.33 = (bf16[128,1536]{1,0:T(8,128)(2,1)}, bf16[128,1536]{1,0:T(8,128)(2,1)}, u32[]{:S(2)}, u32[]{:S(2)}) collective-permute-start(bf16[128,1536]{1,0:T(8,128)(2,1)} %get-tuple-element.223), channel_id=1, source_target_pairs={{0,2},{2,0},{4,6},{6,4},{1,3},{3,1},{5,7},{7,5},{8,10},{10,8},{12,... | collective-permute-start | bytes 1179656 | tf_op jit(solution)/shard_map/ppermute | solution.py:45
  278.1 32.8 %collective-permute-start.34 = (bf16[128,1536]{1,0:T(8,128)(2,1)}, bf16[128,1536]{1,0:T(8,128)(2,1)}, u32[]{:S(2)}, u32[]{:S(2)}) collective-permute-start(bf16[128,1536]{1,0:T(8,128)(2,1)} %get-tuple-element.224), channel_id=1, source_target_pairs={{0,4},{2,6},{4,0},{6,2},{1,5},{3,7},{5,1},{7,3},{8,12},{10,14},{12... | collective-permute-start | bytes 1179656 | tf_op jit(solution)/shard_map/ppermute | solution.py:45
  279.1 31.8 %collective-permute-start.35 = (bf16[128,1536]{1,0:T(8,128)(2,1)S(1)}, bf16[128,1536]{1,0:T(8,128)(2,1)}, u32[]{:S(2)}, u32[]{:S(2)}) collective-permute-start(bf16[128,1536]{1,0:T(8,128)(2,1)S(1)} %get-tuple-element.225), channel_id=1, source_target_pairs={{0,6},{2,4},{4,2},{6,0},{1,7},{3,5},{5,3},{7,1},{8,14},{10,12},{12... | collective-permute-start | bytes 1179656 | tf_op jit(solution)/shard_map/ppermute | solution.py:45
  293.5 15.1 %collective-permute-start.38 = (bf16[192,1152]{1,0:T(8,128)(2,1)}, bf16[192,1152]{1,0:T(8,128)(2,1)S(1)}, u32[]{:S(2)}, u32[]{:S(2)}) collective-permute-start(bf16[192,1152]{1,0:T(8,128)(2,1)} %get-tuple-element.230), channel_id=1, source_target_pairs={{0,8},{8,0},{16,24},{24,16},{1,9},{9,1},{17,25},{25,17},{2,10},{10... | collective-permute-start | bytes 1327112 | tf_op jit(solution)/shard_map/ppermute | solution.py:45
  294.6 14.8 %collective-permute-start.39 = (bf16[192,1152]{1,0:T(8,128)(2,1)S(1)}, bf16[192,1152]{1,0:T(8,128)(2,1)}, u32[]{:S(2)}, u32[]{:S(2)}) collective-permute-start(bf16[192,1152]{1,0:T(8,128)(2,1)S(1)} %get-tuple-element.231), channel_id=1, source_target_pairs={{0,16},{8,24},{16,0},{24,8},{1,17},{9,25},{17,1},{25,9},{2,18},{10... | collective-permute-start | bytes 1327112 | tf_op jit(solution)/shard_map/ppermute | solution.py:45
  313.3 44.0 %collective-permute-start.44 = (bf16[384,2304]{1,0:T(8,128)(2,1)S(1)}, bf16[384,2304]{1,0:T(8,128)(2,1)}, u32[]{:S(2)}, u32[]{:S(2)}) collective-permute-start(bf16[384,2304]{1,0:T(8,128)(2,1)S(1)} %pad_maximum_fusion), channel_id=1, source_target_pairs={{0,8},{8,0},{16,24},{24,16},{1,9},{9,1},{17,25},{25,17},{2,10},{10... | collective-permute-start | bytes 5308424 | tf_op jit(solution)/shard_map/ppermute | solution.py:45
  315.7 41.6 %collective-permute-start.45 = (bf16[384,2304]{1,0:T(8,128)(2,1)}, bf16[384,2304]{1,0:T(8,128)(2,1)}, u32[]{:S(2)}, u32[]{:S(2)}) collective-permute-start(bf16[384,2304]{1,0:T(8,128)(2,1)} %pad_maximum_fusion.1), channel_id=1, source_target_pairs={{0,16},{8,24},{16,0},{24,8},{1,17},{9,25},{17,1},{25,9},{2,18},{10... | collective-permute-start | bytes 5308424 | tf_op jit(solution)/shard_map/ppermute | solution.py:45
  320.7 24.6 %collective-permute-start.41 = (bf16[128,1536]{1,0:T(8,128)(2,1)}, bf16[128,1536]{1,0:T(8,128)(2,1)S(1)}, u32[]{:S(2)}, u32[]{:S(2)}) collective-permute-start(bf16[128,1536]{1,0:T(8,128)(2,1)} %get-tuple-element.247), channel_id=1, source_target_pairs={{0,2},{2,0},{4,6},{6,4},{1,3},{3,1},{5,7},{7,5},{8,10},{10,8},{12,... | collective-permute-start | bytes 1179656 | tf_op jit(solution)/shard_map/ppermute | solution.py:45
  327.2 30.1 %collective-permute-start.42 = (bf16[128,1536]{1,0:T(8,128)(2,1)}, bf16[128,1536]{1,0:T(8,128)(2,1)}, u32[]{:S(2)}, u32[]{:S(2)}) collective-permute-start(bf16[128,1536]{1,0:T(8,128)(2,1)} %get-tuple-element.248), channel_id=1, source_target_pairs={{0,4},{2,6},{4,0},{6,2},{1,5},{3,7},{5,1},{7,3},{8,12},{10,14},{12... | collective-permute-start | bytes 1179656 | tf_op jit(solution)/shard_map/ppermute | solution.py:45
  328.3 29.0 %collective-permute-start.43 = (bf16[128,1536]{1,0:T(8,128)(2,1)}, bf16[128,1536]{1,0:T(8,128)(2,1)}, u32[]{:S(2)}, u32[]{:S(2)}) collective-permute-start(bf16[128,1536]{1,0:T(8,128)(2,1)} %get-tuple-element.249), channel_id=1, source_target_pairs={{0,6},{2,4},{4,2},{6,0},{1,7},{3,5},{5,3},{7,1},{8,14},{10,12},{12... | collective-permute-start | bytes 1179656 | tf_op jit(solution)/shard_map/ppermute | solution.py:45
  360.7 22.0 %collective-permute-start.49 = (bf16[192,2304]{1,0:T(8,128)(2,1)}, bf16[192,2304]{1,0:T(8,128)(2,1)S(1)}, u32[]{:S(2)}, u32[]{:S(2)}) collective-permute-start(bf16[192,2304]{1,0:T(8,128)(2,1)} %get-tuple-element.263), channel_id=1, source_target_pairs={{0,8},{8,0},{16,24},{24,16},{1,9},{9,1},{17,25},{25,17},{2,10},{10... | collective-permute-start | bytes 2654216 | tf_op jit(solution)/shard_map/ppermute | solution.py:45
  361.7 21.0 %collective-permute-start.50 = (bf16[192,2304]{1,0:T(8,128)(2,1)S(1)}, bf16[192,2304]{1,0:T(8,128)(2,1)S(1)}, u32[]{:S(2)}, u32[]{:S(2)}) collective-permute-start(bf16[192,2304]{1,0:T(8,128)(2,1)S(1)} %get-tuple-element.264), channel_id=1, source_target_pairs={{0,16},{8,24},{16,0},{24,8},{1,17},{9,25},{17,1},{25,9},{2,18},{10... | collective-permute-start | bytes 2654216 | tf_op jit(solution)/shard_map/ppermute | solution.py:45
  362.2 12.7 %collective-permute-start.46 = (bf16[256,256]{1,0:T(8,128)(2,1)}, bf16[256,256]{1,0:T(8,128)(2,1)S(1)}, u32[]{:S(2)}, u32[]{:S(2)}) collective-permute-start(bf16[256,256]{1,0:T(8,128)(2,1)} %get-tuple-element.254), channel_id=1, source_target_pairs={{0,2},{2,0},{4,6},{6,4},{1,3},{3,1},{5,7},{7,5},{8,10},{10,8},{12,... | collective-permute-start | bytes 393224 | tf_op jit(solution)/shard_map/ppermute | solution.py:45
  370.5 12.1 %collective-permute-start.47 = (bf16[256,256]{1,0:T(8,128)(2,1)}, bf16[256,256]{1,0:T(8,128)(2,1)S(1)}, u32[]{:S(2)}, u32[]{:S(2)}) collective-permute-start(bf16[256,256]{1,0:T(8,128)(2,1)} %get-tuple-element.255), channel_id=1, source_target_pairs={{0,4},{2,6},{4,0},{6,2},{1,5},{3,7},{5,1},{7,3},{8,12},{10,14},{12... | collective-permute-start | bytes 393224 | tf_op jit(solution)/shard_map/ppermute | solution.py:45
  371.5 11.1 %collective-permute-start.48 = (bf16[256,256]{1,0:T(8,128)(2,1)S(1)}, bf16[256,256]{1,0:T(8,128)(2,1)S(1)}, u32[]{:S(2)}, u32[]{:S(2)}) collective-permute-start(bf16[256,256]{1,0:T(8,128)(2,1)S(1)} %copy-done.63), channel_id=1, source_target_pairs={{0,6},{2,4},{4,2},{6,0},{1,7},{3,5},{5,3},{7,1},{8,14},{10,12},{12... | collective-permute-start | bytes 393224 | tf_op jit(solution)/shard_map/ppermute | solution.py:45
  382.7 30.6 %collective-permute-start.51 = (bf16[96,1152]{1,0:T(8,128)(2,1)}, bf16[96,1152]{1,0:T(8,128)(2,1)}, u32[]{:S(2)}, u32[]{:S(2)}) collective-permute-start(bf16[96,1152]{1,0:T(8,128)(2,1)} %get-tuple-element.266), channel_id=1, source_target_pairs={{0,2},{2,0},{4,6},{6,4},{1,3},{3,1},{5,7},{7,5},{8,10},{10,8},{12,... | collective-permute-start | bytes 663560 | tf_op jit(solution)/shard_map/ppermute | solution.py:45
  390.7 22.6 %collective-permute-start.52 = (bf16[96,1152]{1,0:T(8,128)(2,1)}, bf16[96,1152]{1,0:T(8,128)(2,1)}, u32[]{:S(2)}, u32[]{:S(2)}) collective-permute-start(bf16[96,1152]{1,0:T(8,128)(2,1)} %get-tuple-element.267), channel_id=1, source_target_pairs={{0,4},{2,6},{4,0},{6,2},{1,5},{3,7},{5,1},{7,3},{8,12},{10,14},{12... | collective-permute-start | bytes 663560 | tf_op jit(solution)/shard_map/ppermute | solution.py:45
  391.7 21.6 %collective-permute-start.53 = (bf16[96,1152]{1,0:T(8,128)(2,1)}, bf16[96,1152]{1,0:T(8,128)(2,1)}, u32[]{:S(2)}, u32[]{:S(2)}) collective-permute-start(bf16[96,1152]{1,0:T(8,128)(2,1)} %get-tuple-element.268), channel_id=1, source_target_pairs={{0,6},{2,4},{4,2},{6,0},{1,7},{3,5},{5,3},{7,1},{8,14},{10,12},{12... | collective-permute-start | bytes 663560 | tf_op jit(solution)/shard_map/ppermute | solution.py:45
  405.7 16.0 %collective-permute-start.55 = (bf16[384,768]{1,0:T(8,128)(2,1)}, bf16[384,768]{1,0:T(8,128)(2,1)}, u32[]{:S(2)}, u32[]{:S(2)}) collective-permute-start(bf16[384,768]{1,0:T(8,128)(2,1)} %pad_maximum_fusion.10), channel_id=1, source_target_pairs={{0,8},{8,0},{16,24},{24,16},{1,9},{9,1},{17,25},{25,17},{2,10},{10... | collective-permute-start | bytes 1769480 | tf_op jit(solution)/shard_map/ppermute | solution.py:45
  407.6 15.8 %collective-permute-start.56 = (bf16[384,768]{1,0:T(8,128)(2,1)}, bf16[384,768]{1,0:T(8,128)(2,1)}, u32[]{:S(2)}, u32[]{:S(2)}) collective-permute-start(bf16[384,768]{1,0:T(8,128)(2,1)} %pad_maximum_fusion.11), channel_id=1, source_target_pairs={{0,16},{8,24},{16,0},{24,8},{1,17},{9,25},{17,1},{25,9},{2,18},{10... | collective-permute-start | bytes 1769480 | tf_op jit(solution)/shard_map/ppermute | solution.py:45
  423.9 21.5 %collective-permute-start.58 = (bf16[400,1024]{1,0:T(8,128)(2,1)S(1)}, bf16[400,1024]{1,0:T(8,128)(2,1)S(1)}, u32[]{:S(2)}, u32[]{:S(2)}) collective-permute-start(bf16[400,1024]{1,0:T(8,128)(2,1)S(1)} %pad_maximum_fusion.7), channel_id=1, source_target_pairs={{0,8},{8,0},{16,24},{24,16},{1,9},{9,1},{17,25},{25,17},{2,10},{10... | collective-permute-start | bytes 2457608 | tf_op jit(solution)/shard_map/ppermute | solution.py:45
  425.4 18.9 %collective-permute-start.57 = (bf16[384,1024]{1,0:T(8,128)(2,1)S(1)}, bf16[384,1024]{1,0:T(8,128)(2,1)S(1)}, u32[]{:S(2)}, u32[]{:S(2)}) collective-permute-start(bf16[384,1024]{1,0:T(8,128)(2,1)S(1)} %pad_maximum_fusion.8), channel_id=1, source_target_pairs={{0,16},{8,24},{16,0},{24,8},{1,17},{9,25},{17,1},{25,9},{2,18},{10... | collective-permute-start | bytes 2359304 | tf_op jit(solution)/shard_map/ppermute | solution.py:45
  425.9 40.3 %collective-permute-start.61 = (bf16[96,2304]{1,0:T(8,128)(2,1)S(1)}, bf16[96,2304]{1,0:T(8,128)(2,1)S(1)}, u32[]{:S(2)}, u32[]{:S(2)}) collective-permute-start(bf16[96,2304]{1,0:T(8,128)(2,1)S(1)} %copy-done.44), channel_id=1, source_target_pairs={{0,2},{2,0},{4,6},{6,4},{1,3},{3,1},{5,7},{7,5},{8,10},{10,8},{12,... | collective-permute-start | bytes 1327112 | tf_op jit(solution)/shard_map/ppermute | solution.py:45
  426.9 39.3 %collective-permute-start.62 = (bf16[96,2304]{1,0:T(8,128)(2,1)S(1)}, bf16[96,2304]{1,0:T(8,128)(2,1)S(1)}, u32[]{:S(2)}, u32[]{:S(2)}) collective-permute-start(bf16[96,2304]{1,0:T(8,128)(2,1)S(1)} %copy-done.43), channel_id=1, source_target_pairs={{0,4},{2,6},{4,0},{6,2},{1,5},{3,7},{5,1},{7,3},{8,12},{10,14},{12... | collective-permute-start | bytes 1327112 | tf_op jit(solution)/shard_map/ppermute | solution.py:45
  428.8 37.4 %collective-permute-start.63 = (bf16[96,2304]{1,0:T(8,128)(2,1)S(1)}, bf16[96,2304]{1,0:T(8,128)(2,1)S(1)}, u32[]{:S(2)}, u32[]{:S(2)}) collective-permute-start(bf16[96,2304]{1,0:T(8,128)(2,1)S(1)} %copy-done.42), channel_id=1, source_target_pairs={{0,6},{2,4},{4,2},{6,0},{1,7},{3,5},{5,3},{7,1},{8,14},{10,12},{12... | collective-permute-start | bytes 1327112 | tf_op jit(solution)/shard_map/ppermute | solution.py:45
  446.9 17.1 %collective-permute-start.60 = (bf16[208,1792]{1,0:T(8,128)(2,1)S(1)}, bf16[208,1792]{1,0:T(8,128)(2,1)S(1)}, u32[]{:S(2)}, u32[]{:S(2)}) collective-permute-start(bf16[208,1792]{1,0:T(8,128)(2,1)S(1)} %fusion.2), channel_id=1, source_target_pairs={{0,16},{8,24},{16,0},{24,8},{1,17},{9,25},{17,1},{25,9},{2,18},{10... | collective-permute-start | bytes 2236424 | tf_op jit(solution)/shard_map/ppermute | solution.py:45
  447.4 15.5 %collective-permute-start.59 = (bf16[192,1792]{1,0:T(8,128)(2,1)S(1)}, bf16[192,1792]{1,0:T(8,128)(2,1)S(1)}, u32[]{:S(2)}, u32[]{:S(2)}) collective-permute-start(bf16[192,1792]{1,0:T(8,128)(2,1)S(1)} %get-tuple-element.291), channel_id=1, source_target_pairs={{0,8},{8,0},{16,24},{24,16},{1,9},{9,1},{17,25},{25,17},{2,10},{10... | collective-permute-start | bytes 2064392 | tf_op jit(solution)/shard_map/ppermute | solution.py:45
  469.1 9.3 %collective-permute-start.65 = (bf16[128,1536]{1,0:T(8,128)(2,1)S(1)}, bf16[128,1536]{1,0:T(8,128)(2,1)S(1)}, u32[]{:S(2)}, u32[]{:S(2)}) collective-permute-start(bf16[128,1536]{1,0:T(8,128)(2,1)S(1)} %pad_maximum_fusion.16), channel_id=1, source_target_pairs={{0,1},{1,0},{2,3},{3,2},{4,5},{5,4},{6,7},{7,6},{8,9},{9,8},{10,11... | collective-permute-start | bytes 1179656 | tf_op jit(solution)/shard_map/ppermute | solution.py:45
  469.6 14.1 %collective-permute-start.68 = (bf16[112,1792]{1,0:T(8,128)(2,1)S(1)}, bf16[112,1792]{1,0:T(8,128)(2,1)S(1)}, u32[]{:S(2)}, u32[]{:S(2)}) collective-permute-start(bf16[112,1792]{1,0:T(8,128)(2,1)S(1)} %get-tuple-element.309), channel_id=1, source_target_pairs={{0,6},{2,4},{4,2},{6,0},{1,7},{3,5},{5,3},{7,1},{8,14},{10,12},{12... | collective-permute-start | bytes 1204232 | tf_op jit(solution)/shard_map/ppermute | solution.py:45
  472.0 35.2 %collective-permute-start.67 = (bf16[112,1792]{1,0:T(8,128)(2,1)S(1)}, bf16[112,1792]{1,0:T(8,128)(2,1)S(1)}, u32[]{:S(2)}, u32[]{:S(2)}) collective-permute-start(bf16[112,1792]{1,0:T(8,128)(2,1)S(1)} %get-tuple-element.308), channel_id=1, source_target_pairs={{0,4},{2,6},{4,0},{6,2},{1,5},{3,7},{5,1},{7,3},{8,12},{10,14},{12... | collective-permute-start | bytes 1204232 | tf_op jit(solution)/shard_map/ppermute | solution.py:45
  472.1 35.1 %collective-permute-start.66 = (bf16[112,1792]{1,0:T(8,128)(2,1)S(1)}, bf16[112,1792]{1,0:T(8,128)(2,1)S(1)}, u32[]{:S(2)}, u32[]{:S(2)}) collective-permute-start(bf16[112,1792]{1,0:T(8,128)(2,1)S(1)} %get-tuple-element.307), channel_id=1, source_target_pairs={{0,2},{2,0},{4,6},{6,4},{1,3},{3,1},{5,7},{7,5},{8,10},{10,8},{12,... | collective-permute-start | bytes 1204232 | tf_op jit(solution)/shard_map/ppermute | solution.py:45
  (71 other events, 641.0 us)

commit v4 on v3

--- a/solution.py
+++ b/solution.py
@@ -174,54 +174,92 @@
 LITTLE = pl.CostEstimate(flops=1, bytes_accessed=1, transcendentals=0)
 
 
-def mlp_tile(tiles_each, x_mine, x_other, o_mine, o_other, *refs):
-    up_parts, gate_down_parts, far = refs[:3], refs[3:6], refs[6:8]
-    outs, scratch = refs[8:14], refs[14:]
-    both_ref, act_ref, back_mine, back_send, out_mine, out_send = outs
-    gu, down, sems = scratch
+def stack_copies(targets, sems, used=0):
+    copies = []
+    for target, parts in targets:
+        row, cols = 0, target.shape[1]
+        group = []
+        for part, column in parts:
+            group.append(
+                pltpu.make_async_copy(
+                    part.at[:, pl.ds(column, cols)],
+                    target.at[pl.ds(row, part.shape[0])],
+                    sems.at[used + sum(map(len, copies)) + len(group)],
+                )
+            )
+            row += part.shape[0]
+        copies.append(group)
+    return copies
+
+
+def start_all(groups):
+    for group in groups:
+        for copy in group:
+            copy.start()
+
+
+def wait_all(groups):
+    for group in groups:
+        for copy in group:
+            copy.wait()
+
+
+def gate_up_copies(refs, gu, sems):
+    up, gate_down, far = refs[:3], refs[3:6], refs[6:8]
+    width = gu.shape[1] // 2
+    return [
+        (gu.at[:, pl.ds(0, width)], [(p, 0) for p in gate_down] + [(p, width) for p in far]),
+        (gu.at[:, pl.ds(width, width)], [(p, 0) for p in up] + [(p, 0) for p in far]),
+    ]
+
+
+def forward_tile(tiles_each, x_mine, x_other, *refs):
+    parts, (gate_up, gu, sems) = refs[:8], refs[8:]
     step = pl.program_id(0)
-    width = down.shape[1]
 
     @pl.when(step == 0)
     def _():
-        copies = []
-        for to, parts, start, far_start in (
-            (gu.at[:, pl.ds(0, width)], gate_down_parts, 0, width),
-            (gu.at[:, pl.ds(width, width)], up_parts, 0, 0),
-            (down, gate_down_parts, width, 2 * width),
-        ):
-            row = 0
-            starts = [start] * len(parts) + [far_start] * len(far)
-            for part, column in zip((*parts, *far), starts):
-                copies.append(
-                    pltpu.make_async_copy(
-                        part.at[:, pl.ds(column, width)],
-                        to.at[pl.ds(row, part.shape[0])],
-                        sems.at[len(copies)],
-                    )
-                )
-                row += part.shape[0]
-        for copy in copies:
-            copy.start()
-        for copy in copies:
-            copy.wait()
-
+        copies = stack_copies(gate_up_copies(parts, gu, sems), sems)
+        start_all(copies)
+        wait_all(copies)
+
+    rows = jnp.where(step < tiles_each, x_mine[...], x_other[...])
+    gate_up[...] = matmul(rows, gu[...])
+
+
+def backward_tile(tiles_each, gate_up, o_mine, o_other, *refs):
+    parts, refs = refs[:8], refs[8:]
+    both_ref, act_ref, back_mine, back_send, out_mine, out_send, gu, down, sems = refs
+    step = pl.program_id(0)
     own = step < tiles_each
-    rows = jnp.where(own, x_mine[...], x_other[...])
+    width = down.shape[1]
+
+    down_target = [(down, [(p, width) for p in parts[3:6]] + [(p, 2 * width) for p in parts[6:]])]
+
+    @pl.when(step == 0)
+    def _():
+        first = stack_copies(down_target, sems)
+        start_all(first)
+        start_all(stack_copies(gate_up_copies(parts, gu, sems), sems, 5))
+        wait_all(first)
+
     grads = jnp.where(own, o_mine[...], o_other[...])
-    gate_up = matmul(rows, gu[...])
     g_act = matmul(grads, down[...])
     gate, up = gate_up[:, :width], gate_up[:, width:]
     sigmoid_gate = 1.0 / (1.0 + jnp.exp(-gate))
     silu_gate = gate * sigmoid_gate
-    act = (silu_gate * up).astype(jnp.bfloat16)
-    g_gate = (g_act * up * sigmoid_gate * (1.0 + gate * (1.0 - sigmoid_gate))).astype(jnp.bfloat16)
-    g_up = (g_act * silu_gate).astype(jnp.bfloat16)
-    act_ref[...] = act
-    both_ref[:, :width] = g_gate
-    both_ref[:, width:] = g_up
-    back = times_transposed(g_gate, gu[:, :width]) + times_transposed(g_up, gu[:, width:])
-    out = times_transposed(act, down[...])
+    act_ref[...] = (silu_gate * up).astype(jnp.bfloat16)
+    both_ref[:, :width] = (
+        g_act * up * sigmoid_gate * (1.0 + gate * (1.0 - sigmoid_gate))
+    ).astype(jnp.bfloat16)
+    both_ref[:, width:] = (g_act * silu_gate).astype(jnp.bfloat16)
+
+    @pl.when(step == 0)
+    def _():
+        wait_all(stack_copies(gate_up_copies(parts, gu, sems), sems, 5))
+
+    back = times_transposed(both_ref[...], gu[...])
+    out = times_transposed(act_ref[...], down[...])
 
     @pl.when(own)
     def _():
@@ -234,43 +272,39 @@
         out_send[...] = out.astype(jnp.bfloat16)
 
 
-def mlp(x_mine, x_other, o_mine, o_other, up_parts, gate_down_parts, far):
-    count, model_width = x_mine.shape
-    width = up_parts[0].shape[1]
+def by_tiles(body, count, ins, halves, parts, outs, half_outs, scratch, name):
     tile = min(256, count)
     tiles_each = count // tile
-    mine = pl.BlockSpec((tile, model_width), lambda i: (jnp.minimum(i, tiles_each - 1), 0))
-    other = pl.BlockSpec((tile, model_width), lambda i: (jnp.maximum(i - tiles_each, 0), 0))
-    left = pl.BlockSpec(memory_space=pl.ANY)
+
+    def rows(cols):
+        return pl.BlockSpec((tile, cols), lambda i: (i, 0))
+
+    def mine(cols):
+        return pl.BlockSpec((tile, cols), lambda i: (jnp.minimum(i, tiles_each - 1), 0))
+
+    def other(cols):
+        return pl.BlockSpec((tile, cols), lambda i: (jnp.maximum(i - tiles_each, 0), 0))
+
     return pl.pallas_call(
-        functools.partial(mlp_tile, tiles_each),
+        functools.partial(body, tiles_each),
         grid=(2 * tiles_each,),
-        in_specs=[mine, other, mine, other] + [left] * 8,
-        out_specs=[
-            pl.BlockSpec((tile, 2 * width), lambda i: (i, 0)),
-            pl.BlockSpec((tile, width), lambda i: (i, 0)),
-            mine,
-            other,
-            mine,
-            other,
+        in_specs=[rows(x.shape[1]) for x in ins]
+        + [spec(x.shape[1]) for pair in halves for spec, x in zip((mine, other), pair)]
+        + [pl.BlockSpec(memory_space=pl.ANY)] * len(parts),
+        out_specs=[rows(cols) for cols, _ in outs]
+        + [spec(cols) for cols in half_outs for spec in (mine, other)],
+        out_shape=[jax.ShapeDtypeStruct((2 * count, cols), dtype) for cols, dtype in outs]
+        + [
+            jax.ShapeDtypeStruct((count, cols), dtype)
+            for cols in half_outs
+            for dtype in (jnp.float32, jnp.bfloat16)
         ],
-        out_shape=[
-            jax.ShapeDtypeStruct((2 * count, 2 * width), jnp.bfloat16),
-            jax.ShapeDtypeStruct((2 * count, width), jnp.bfloat16),
-            jax.ShapeDtypeStruct((count, model_width), jnp.float32),
-            jax.ShapeDtypeStruct((count, model_width), jnp.bfloat16),
-            jax.ShapeDtypeStruct((count, model_width), jnp.float32),
-            jax.ShapeDtypeStruct((count, model_width), jnp.bfloat16),
-        ],
-        scratch_shapes=[
-            pltpu.VMEM((model_width, 2 * width), jnp.bfloat16),
-            pltpu.VMEM((model_width, width), jnp.bfloat16),
-            pltpu.SemaphoreType.DMA((15,)),
-        ],
+        scratch_shapes=[pltpu.VMEM(shape, jnp.bfloat16) for shape in scratch]
+        + [pltpu.SemaphoreType.DMA((15,))],
         compiler_params=pltpu.CompilerParams(vmem_limit_bytes=VMEM_BYTES),
         cost_estimate=LITTLE,
-        name="mlp",
-    )(x_mine, x_other, o_mine, o_other, *up_parts, *gate_down_parts, *far)
+        name=name,
+    )(*ins, *(x for pair in halves for x in pair), *parts)
 
 
 def weight_tile(x_mine, x_other, grads, out):
@@ -504,10 +538,14 @@
         out[:, HD:] = g_values[k * rows : (k + 1) * rows].astype(out.dtype)
 
 
+def product_body(left, right, out):
+    out[...] = inner_rows(left[...], right[...]).astype(jnp.bfloat16)
+
+
 def project_back_body(
-    count, core_ref, query_lin, normed, w_qkv, cosines, signed_sines, *refs
+    count, core_ref, query_lin, w_qkv, cosines, signed_sines, inputs, inverse_rms, *refs
 ):
-    parts, (g_qkv, g_bias, mine, send, lin, total) = refs[:count], refs[count:]
+    parts, (lin, g_bias, g_gain, mine, send, total) = refs[:count], refs[count:]
     g_parts = parts[0][...].astype(jnp.float32)
     for part in parts[1:]:
         g_parts = g_parts + part[...].astype(jnp.float32)
@@ -518,7 +556,7 @@
     ).astype(jnp.bfloat16)
     lin[:, cols + HD :] = g_parts[:, HD:].astype(jnp.bfloat16)
     split_rows(core_ref, times_transposed(lin[...], w_qkv[...]), total, mine, send)
-    g_qkv[...] = inner_rows(normed[...], lin[...]).astype(jnp.bfloat16)
+    g_gain[...] = jnp.sum(total[...] * inputs[...] * inverse_rms[...], 0, keepdims=True)
     g_bias[...] = jnp.sum(lin[...].astype(jnp.float32), 0, keepdims=True)
 
 
@@ -630,7 +668,8 @@
     )
     key_value, down_parts = together(key_value, down_parts)
 
-    keys_values = gather_ctx(key_value)
+    gate_down_shard = place_ctx([part[:, :width] for part in gate_up_parts], down_parts)
+    keys_values, gate_down_shard = together(gather_ctx(key_value), gate_down_shard)
     half_f32 = ((half_rows, model_width), jnp.float32)
     half_bf16 = ((half_rows, model_width), jnp.bfloat16)
     row_f32 = ((1, model_width), jnp.float32)
@@ -654,7 +693,6 @@
         [attn_mine, swap(attn_send, "wt", 1), input_half, gain_two],
         name="norm",
     )
-    gate_down_shard = place_ctx([part[:, :width] for part in gate_up_parts], down_parts)
     normed_half, gate_down_shard, up_near = together(normed_half, gate_down_shard, up_near)
 
     gate_down_near = near_seq(gate_down_shard)
@@ -664,18 +702,33 @@
 
     mlp_far = far_seq(*(jnp.concatenate(pair, 1) for pair in zip(up_near, gate_down_near)))
     normed_mine = jnp.concatenate(normed_parts, 0)
-    normed_other = swap(normed_mine, "wt", 1)
-    grad_parts, mlp_far = together(gather_ctx(grad_half), mlp_far)
+    normed_other, grad_half = together(swap(normed_mine, "wt", 1), grad_half)
+    count = normed_mine.shape[0]
+    mlp_parts = [up_shard, *up_near, gate_down_shard, *gate_down_near, *mlp_far]
+    (gate_up,) = by_tiles(
+        forward_tile,
+        count,
+        [],
+        [(normed_mine, normed_other)],
+        mlp_parts,
+        [(2 * width, jnp.float32)],
+        [],
+        [(model_width, 2 * width)],
+        "gate_up",
+    )
+    grad_parts, gate_up = together(gather_ctx(grad_half), gate_up)
     grad_mine = jnp.concatenate(grad_parts, 0)
     grad_other = swap(grad_mine, "wt", 1)
-    g_both, act, back_mine, back_send, out_mine, out_send = mlp(
-        normed_mine,
-        normed_other,
-        grad_mine,
-        grad_other,
-        [up_shard, *up_near],
-        [gate_down_shard, *gate_down_near],
-        mlp_far,
+    g_both, act, back_mine, back_send, out_mine, out_send = by_tiles(
+        backward_tile,
+        count,
+        [gate_up],
+        [(grad_mine, grad_other)],
+        mlp_parts,
+        [(2 * width, jnp.bfloat16), (width, jnp.bfloat16)],
+        [model_width, model_width],
+        [(model_width, 2 * width), (model_width, width)],
+        "mlp_back",
     )
     back_got = swap(back_send, "wt", 1)
     out_got = swap(out_send, "wt", 1)
@@ -693,9 +746,10 @@
         g_normed_parts, down_sum, g_gate_up, mlp_pieces
     )
 
-    mlp_parts = exchange_ctx(narrow_others(mlp_pieces))
+    down_back = lax.all_to_all(
+        down_sum.reshape(ctx_size, -1, down_sum.shape[1]), "ctx", 0, 0, tiled=True
+    )
     gate_up_got = scatter_near(g_gate_up)
-    down_pieces = row_pieces(down_sum)
     grad_gain_mlp, branch_mine, g_hidden = call(
         functools.partial(norm_back_body, ctx_size),
         [row_f32, half_bf16, half_f32],
@@ -729,59 +783,46 @@
         "attend_back",
         [scalar] + [whole] * (10 + ctx_size),
     )
-    g_blocks, mlp_parts, gate_up_got, g_out, down_pieces = together(
-        g_blocks, mlp_parts, gate_up_got, g_out, down_pieces
-    )
-
-    g_key_value_parts = exchange_ctx(g_blocks)
+    g_blocks, down_back = together(g_blocks, down_back)
+    g_key_value_parts, gate_up_got, mlp_pieces = together(
+        exchange_ctx(g_blocks), gate_up_got, mlp_pieces
+    )
+
+    mlp_parts = exchange_ctx(narrow_others(mlp_pieces))
     on_x, on_y = relay(g_gate_up, *gate_up_got)
-    g_key_value_parts, down_pieces, last_x, last_y = together(
-        g_key_value_parts, down_pieces, swap(on_x, "seq", 1), swap(on_y, "seq", 2)
-    )
-    down_back = exchange_ctx(down_pieces)
+    last_x, last_y, g_out = together(swap(on_x, "seq", 1), swap(on_y, "seq", 2), g_out)
+    out_got = scatter_near(g_out)
     gate_up_sum = scatter_end(g_gate_up, *gate_up_got, last_x, last_y).astype(jnp.bfloat16)
-    gate_up_pieces = row_pieces(gate_up_sum)
-    g_qkv, g_bias, normed_mine_grad, normed_send_grad = call(
+    gate_up_blocks = gate_up_sum.reshape(ctx_size, -1, 2 * width)
+    g_lin, g_bias, grad_gain_attn, normed_mine_grad, normed_send_grad = call(
         functools.partial(project_back_body, ctx_size),
         [
-            ((model_width, qkv_cols), jnp.bfloat16),
+            ((span_rows, qkv_cols), jnp.bfloat16),
             ((1, qkv_cols), jnp.float32),
+            row_f32,
             half_f32,
             half_f32,
         ],
         [
             core_index,
             query_lin,
-            normed_attn,
             w_qkv,
             cosines,
             signed_sines,
+            input_rows,
+            rms_attn,
             *g_key_value_parts,
         ],
-        [
-            pltpu.VMEM((span_rows, qkv_cols), jnp.bfloat16),
-            pltpu.VMEM((span_rows, model_width), jnp.float32),
-        ],
+        [pltpu.VMEM((span_rows, model_width), jnp.float32)],
         "project_back",
-        [scalar] + [whole] * (5 + ctx_size),
-    )
-    normed_got_grad, g_out = together(swap(normed_send_grad, "wt", 1), g_out)
-    out_got = scatter_near(g_out)
-    grad_gain_attn, grad_input_half = call(
-        functools.partial(norm_back_body, 2),
-        [row_f32, half_bf16],
-        [
-            g_hidden,
-            input_half,
-            own_half(rms_attn),
-            gain_one,
-            normed_mine_grad,
-            normed_got_grad,
-        ],
-        name="attn_norm_back",
-    )
-    grad_input_half = relative(grad_input_half)
-
+        [scalar] + [whole] * (6 + ctx_size),
+    )
+    (g_qkv,) = call(
+        product_body,
+        [((model_width, qkv_cols), jnp.bfloat16)],
+        [normed_attn, g_lin],
+        name="qkv_grads",
+    )
     small = jnp.concatenate(
         [
             relative(grad_gain_attn)[0],
@@ -793,11 +834,11 @@
     small_rows = -(-small_size // (qkv_cols * 16)) * 16
     small = jnp.pad(small, (0, small_rows * qkv_cols - small_size)).reshape(small_rows, qkv_cols)
 
-    down_back, gate_up_pieces, out_got, g_qkv, small = together(
-        down_back, gate_up_pieces, out_got, g_qkv, small
-    )
-
-    gate_up_back = exchange_ctx(gate_up_pieces)
+    mlp_parts, gate_up_blocks, out_got, g_qkv, small = together(
+        mlp_parts, gate_up_blocks, out_got, g_qkv, small
+    )
+
+    gate_up_back = lax.all_to_all(gate_up_blocks, "ctx", 0, 0, tiled=True)
     _, for_x, for_y, for_far = jnp.split(g_qkv, 4, 0)
     rows = for_x.shape[0]
     half = rows // 2
@@ -812,23 +853,50 @@
     small = add_up([small, last_y[half:, :qkv_cols]]).astype(jnp.bfloat16)
     attn_sum = scatter_end(g_attn, *attn_got, last_x, last_y[:half])
     attn_pieces = row_pieces(attn_sum)
-    attn_send = [with_rows(piece.astype(jnp.bfloat16), small) for piece in attn_pieces]
-    attn_send, gate_up_back, grad_input_half, mlp_parts = together(
-        attn_send, gate_up_back, grad_input_half, mlp_parts
-    )
+    rows, attn_cols = attn_pieces[0].shape
+    small_cols = -(-small_size // (rows * LANES)) * LANES
+    small = jnp.pad(small.reshape(-1)[:small_size], (0, rows * small_cols - small_size))
+    small = small.reshape(rows, small_cols)
+    attn_send = [
+        jnp.concatenate([piece.astype(jnp.bfloat16), small], 1) for piece in attn_pieces
+    ]
+    attn_send, gate_up_back, down_back, normed_send_grad, mlp_parts = together(
+        attn_send, gate_up_back, down_back, normed_send_grad, mlp_parts
+    )
+
     attn_back = exchange_ctx(attn_send)
+    _, grad_input_half = call(
+        functools.partial(norm_back_body, 2),
+        [row_f32, half_bf16],
+        [
+            g_hidden,
+            input_half,
+            own_half(rms_attn),
+            gain_one,
+            normed_mine_grad,
+            swap(normed_send_grad, "wt", 1),
+        ],
+        name="attn_norm_back",
+    )
+    grad_input_half = relative(grad_input_half)
+
     grad_input = join_halves(grad_input_half)
     layer_output = join_halves(relative((hidden + add_up(mlp_parts)).astype(jnp.bfloat16)))
+    attn_back, grad_input, layer_output = together(attn_back, grad_input, layer_output)
     attn_back = attn_pieces[:1] + attn_back[1:]
-    rows = attn_pieces[0].shape[0]
-    grad_w_gate, grad_w_up = place_units(gate_up_back, units_here)
-    (grad_w_down,) = place_units(down_back, units_here)
-    grad_w_attn = add_up([part[:rows] for part in attn_back])
+    grad_w_gate, grad_w_up = (
+        jnp.concatenate([block[:, start : start + width] for block in gate_up_back], 1)[
+            :, :units_here
+        ].astype(jnp.float32)
+        for start in (0, width)
+    )
+    grad_w_down = jnp.concatenate(list(down_back), 1)[:, :units_here].astype(jnp.float32)
+    grad_w_attn = add_up([part[:, :attn_cols] for part in attn_back])
     grad_w_qkv = grad_w_attn[:, :qkv_cols]
     grad_w_o = grad_w_attn[:, qkv_cols:]
     small = add_tree(
         [small.astype(jnp.float32)]
-        + [part[rows:, :qkv_cols].astype(jnp.float32) for part in attn_back[1:]]
+        + [part[:, attn_cols:].astype(jnp.float32) for part in attn_back[1:]]
     ).reshape(-1)
     gains = small[: 2 * model_width].reshape(-1, LANES)
     gains = (gains + swap(gains, "wt", 1)).reshape(-1)

time: 521 us -> 494 us (0.948)
  the two profiles are of different devices: /device:TPU:0 before, /device:TPU:13 now
where the time goes in v4:
time: 494 us; the launch traced here: 485 us
  waiting for transfers between devices  213 us (43%)
  Pallas kernels  116 us (23%)
  starting transfers between devices  68.9 us (14%)
  local copies, waits for them, and re-layouts  44.2 us (9%)
  other arithmetic  35.9 us (7%)
  between operations  7.34 us (1%)
    ppermute x64, waiting for transfers between devices, swap(): return lax.ppermute(values, axis, [(i, i ^ offset) for i in range(size)])  212 us
    ppermute x64, starting transfers between devices, swap(): return lax.ppermute(values, axis, [(i, i ^ offset) for i in range(size)])  60.6 us
    pallas_call x12, Pallas kernels, call(): pl.pallas_call(body, in_specs=in_specs or [whole] * len(args), out_specs=...  55 us
    pallas_call x2, Pallas kernels, by_tiles(): pl.pallas_call(functools.partial(body, tiles_each), grid=(2 * tiles_each,...  40.6 us
    pallas_call x2, Pallas kernels, weight_grad(): pl.pallas_call(weight_tile, grid=(4,), in_specs=[columns, columns, pl.Blo...  20.3 us
    unnamed x115, local copies, waits for them, and re-layouts  14.8 us
  transfers between devices with their start and end apart: 66, of which 36 were waited for; matrix products, arithmetic and copies ran while one was open for 12% of the time, Pallas kernels for 18%

profile of v4, /device:TPU:13, one launch (start us, length us, event | category | flops | bytes accessed | tf_op | source)
XLA Modules:
  0.0 484.7 jit_solution(15431444001726021681)
XLA Ops:
  0.6 1.8 side_by_side.1.refs_0_
  2.6 2.3 collective-permute-start.1
  12.7 2.6 dynamic-slice_bitcast_fusion
  16.3 1.7 pad_dynamic-slice_fusion.16
  20.1 14.7 %collective-permute-done.2.refs_3_ = bf16[96,1792]{1,0:T(8,128)(2,1)} collective-permute-done((bf16[96,1792]{1,0:T(8,128)(2,1)}, bf16[96,1792]{1,0:T(8,128)(2,1)}, u32[]{:S(2)}, u32[]{:S(2)}) %collective-permute-start.2) | collective-permute-done | bytes 344096 | tf_op jit(solution)/shard_map/ppermute | solution.py:45
  34.8 2.5 place.3.refs_0_
  40.7 2.4 collective-permute-start.6
  44.5 11.3 %collective-permute-done.5 = bf16[96,2304]{1,0:T(8,128)(2,1)S(1)} collective-permute-done((bf16[96,2304]{1,0:T(8,128)(2,1)S(1)}, bf16[96,2304]{1,0:T(8,128)(2,1)S(1)}, u32[]{:S(2)}, u32[]{:S(2)}) %collective-permute-start.5) | collective-permute-done | bytes 442400 | tf_op jit(solution)/shard_map/ppermute | solution.py:45
  55.8 4.7 collective-permute-done.6
  60.5 18.9 %collective-permute-done.7 = bf16[96,2304]{1,0:T(8,128)(2,1)S(1)} collective-permute-done((bf16[96,2304]{1,0:T(8,128)(2,1)S(1)}, bf16[96,2304]{1,0:T(8,128)(2,1)S(1)}, u32[]{:S(2)}, u32[]{:S(2)}) %collective-permute-start.7) | collective-permute-done | bytes 442400 | tf_op jit(solution)/shard_map/ppermute | solution.py:45
  83.6 2.4 collective-permute-start.11
  87.1 2.2 place.4.refs_0_
  89.3 3.7 collective-permute-done.8.refs_3_
  94.7 7.3 %project.1 = (bf16[256,768]{1,0:T(8,128)(2,1)}, bf16[256,256]{1,0:T(8,128)(2,1)}, bf16[1536,1024]{1,0:T(8,128)(2,1)}, bf16[1536,768]{1,0:T(8,128)(2,1)}) custom-call(bf16[256,1536]{1,0:T(8,128)(2,1)} %multiply_convert_fusion.x.left, f32[1,1024]{1,0:T(1,128)} %maximum_convert_fusion.1.bias, f32[256,128]{1,0:T(8,128)} %pad_maximum_fusion.31.cosines, ...), custom_call_target="tpu_custom_call" | custom-call | flops 1 | bytes 1 | tf_op jit(solution)/shard_map/project/pallas_call | solution.py:335
  102.1 1.8 collective-permute-done.12.refs_7_
  104.0 3.3 collective-permute-start.14
  110.2 2.9 place.5.refs_3_
  113.1 2.3 collective-permute-done.14.refs_2_
  115.3 3.1 collective-permute-done.15.refs_3_
  119.1 7.9 %attend.1 = (bf16[256,768]{1,0:T(8,128)(2,1)}, f32[256,768]{1,0:T(8,128)}, f32[128,1536]{1,0:T(8,128)}, f32[128,1536]{1,0:T(8,128)}) custom-call(s32[1]{0:T(128)} %bitcast.core_ref, bf16[256,768]{1,0:T(8,128)(2,1)} %get-tuple-element.180.query, s32[256,1]{1,0:T(8,128)} %copy.30.query_pos, s32[1,1024]{1,0:T(1,128)} %bitcast.77, ...), custom_call_target="tpu_custom_call" | custom-call | flops 1 | bytes 1 | tf_op jit(solution)/shard_map/attend/pallas_call | solution.py:335
  126.9 1.9 collective-permute-start.16
  131.1 3.0 norm.1
  135.6 2.4 collective-permute-start.20
  138.2 1.7 fusion.18.base
  140.0 11.4 %collective-permute-done.19 = bf16[128,1536]{1,0:T(8,128)(2,1)S(1)} collective-permute-done((bf16[128,1536]{1,0:T(8,128)(2,1)}, bf16[128,1536]{1,0:T(8,128)(2,1)S(1)}, u32[]{:S(2)}, u32[]{:S(2)}) %collective-permute-start.19) | collective-permute-done | bytes 393248 | tf_op jit(solution)/shard_map/ppermute | solution.py:45
  151.4 3.7 collective-permute-done.20
  155.1 16.8 %collective-permute-done.21 = bf16[128,1536]{1,0:T(8,128)(2,1)S(1)} collective-permute-done((bf16[128,1536]{1,0:T(8,128)(2,1)}, bf16[128,1536]{1,0:T(8,128)(2,1)S(1)}, u32[]{:S(2)}, u32[]{:S(2)}) %collective-permute-start.21) | collective-permute-done | bytes 393248 | tf_op jit(solution)/shard_map/ppermute | solution.py:45
  171.9 2.2 collective-permute-done.22.refs_4_
  180.9 2.4 collective-permute-start.26
  183.5 25.9 %collective-permute-done.28.refs_6_ = bf16[192,3456]{1,0:T(8,128)(2,1)S(1)} collective-permute-done((bf16[192,3456]{1,0:T(8,128)(2,1)S(1)}, bf16[192,3456]{1,0:T(8,128)(2,1)S(1)}, u32[]{:S(2)}, u32[]{:S(2)}) %collective-permute-start.28) | collective-permute-done | bytes 1327136 | tf_op jit(solution)/shard_map/ppermute | solution.py:45
  211.7 14.3 %gate_up.1 = f32[1024,2304]{1,0:T(8,128)} custom-call(bf16[512,1536]{1,0:T(8,128)(2,1)} %copy-done.7, bf16[512,1536]{1,0:T(8,128)(2,1)} %copy-done.11, bf16[384,1152]{1,0:T(8,128)(2,1)} %place.4.refs_0_, bf16[384,1152]{1,0:T(8,128)(2,1)} %collective-permute-done.17.refs_1_, bf16[384,1152]{1,0:T(8,128)(2,1)} %collective-permute-done.18.refs_2_, ...), custom_call_target="tpu_custom_call" | custom-call | flops 1 | bytes 1 | tf_op jit(solution)/shard_map/gate_up/pallas_call | solution.py:288
  228.7 3.0 collective-permute-done.30.o_other.x_other
  232.9 26.3 %mlp_back.1 = (bf16[1024,2304]{1,0:T(8,128)(2,1)}, bf16[1024,1152]{1,0:T(8,128)(2,1)}, f32[512,1536]{1,0:T(8,128)}, bf16[512,1536]{1,0:T(8,128)(2,1)}, f32[512,1536]{1,0:T(8,128)}, /*index=5*/bf16[512,1536]{1,0:T(8,128)(2,1)}) custom-call(f32[1024,2304]{1,0:T(8,128)} %gate_up.1, bf16[512,1536]{1,0:T(8,128)(2,1)} %copy-done.8, bf16[512,1536]{1,0:T(8,128)(2,1)} %copy-done.12, ...), custom_call_target="tpu_custom_call" | custom-call | flops 1 | bytes 1 | tf_op jit(solution)/shard_map/mlp_back/pallas_call | solution.py:288
  259.8 8.2 %weight_grad.2 = bf16[1536,1152]{1,0:T(8,128)(2,1)} custom-call(bf16[512,1536]{1,0:T(8,128)(2,1)} %copy-done.8, bf16[512,1536]{1,0:T(8,128)(2,1)} %copy-done.12, bf16[1024,1152]{1,0:T(8,128)(2,1)} %get-tuple-element.223.grads), custom_call_target="tpu_custom_call" | custom-call | flops 1 | bytes 1 | tf_op jit(solution)/shard_map/weight_grad/pallas_call | solution.py:321
  273.1 2.4 collective-permute-start.34
  276.3 16.2 %collective-permute-done.36 = bf16[384,1152]{1,0:T(8,128)(2,1)S(1)} collective-permute-done((bf16[384,1152]{1,0:T(8,128)(2,1)S(1)}, bf16[384,1152]{1,0:T(8,128)(2,1)S(1)}, u32[]{:S(2)}, u32[]{:S(2)}) %collective-permute-start.36) | collective-permute-done | bytes 884768 | tf_op jit(solution)/shard_map/ppermute | solution.py:45
  295.5 12.1 %weight_grad.3 = bf16[1536,2304]{1,0:T(8,128)(2,1)} custom-call(bf16[512,1536]{1,0:T(8,128)(2,1)} %copy-done.7, bf16[512,1536]{1,0:T(8,128)(2,1)} %copy-done.11, bf16[1024,2304]{1,0:T(8,128)(2,1)} %get-tuple-element.235.grads), custom_call_target="tpu_custom_call" | custom-call | flops 1 | bytes 1 | tf_op jit(solution)/shard_map/weight_grad/pallas_call | solution.py:321
  309.3 2.2 fusion.36
  315.0 3.9 all-to-all-start
  318.8 3.5 mlp_norm_back.1
  322.3 3.1 collective-permute-start.40
  325.4 1.6 collective-permute-done.40.branch_other
  327.7 11.8 %attend_back.1 = (bf16[256,768]{1,0:T(8,128)(2,1)}, bf16[1536,768]{1,0:T(8,128)(2,1)}, f32[256,256]{1,0:T(8,128)}, bf16[256,256]{1,0:T(8,128)(2,1)}, bf16[256,256]{1,0:T(8,128)(2,1)}, /*index=5*/bf16[256,256]{1,0:T(8,128)(2,1)}) custom-call(s32[1]{0:T(128)} %bitcast.core_ref, bf16[128,1536]{1,0:T(8,128)(2,1)} %get-tuple-element.242.branch_mine, ...), custom_call_target="tpu_custom_call" | custom-call | flops 1 | bytes 1 | tf_op jit(solution)/shard_map/attend_back/pallas_call | solution.py:335
  340.4 1.6 collective-permute-start.42
  342.2 2.3 collective-permute-done.41.refs_1_
  344.5 3.8 collective-permute-done.42.refs_2_
  348.3 5.4 %collective-permute-done.43.refs_3_ = bf16[256,256]{1,0:T(8,128)(2,1)S(1)} collective-permute-done((bf16[256,256]{1,0:T(8,128)(2,1)}, bf16[256,256]{1,0:T(8,128)(2,1)S(1)}, u32[]{:S(2)}, u32[]{:S(2)}) %collective-permute-start.43) | collective-permute-done | bytes 131104 | tf_op jit(solution)/shard_map/ppermute | solution.py:45
  353.7 3.6 add_convert_fusion.2
  359.7 2.4 collective-permute-start.47
  362.3 5.0 %project_back.1 = (bf16[256,1024]{1,0:T(8,128)(2,1)}, f32[1,1024]{1,0:T(1,128)}, f32[1,1536]{1,0:T(1,128)}, f32[128,1536]{1,0:T(8,128)}, f32[128,1536]{1,0:T(8,128)}) custom-call(s32[1]{0:T(128)} %bitcast.core_ref, bf16[256,768]{1,0:T(8,128)(2,1)} %get-tuple-element.271.query_lin, bf16[1536,1024]{1,0:T(8,128)(2,1)} %get-tuple-element.272.w_qkv, ...), custom_call_target="tpu_custom_call" | custom-call | flops 1 | bytes 1 | tf_op jit(solution)/shard_map/project_back/pallas_call | solution.py:335
  367.4 4.1 qkv_grads.1
  371.6 5.7 %collective-permute-done.49 = bf16[192,2304]{1,0:T(8,128)(2,1)S(1)} collective-permute-done((bf16[192,2304]{1,0:T(8,128)(2,1)}, bf16[192,2304]{1,0:T(8,128)(2,1)S(1)}, u32[]{:S(2)}, u32[]{:S(2)}) %collective-permute-start.49) | collective-permute-done | bytes 884768 | tf_op jit(solution)/shard_map/ppermute | solution.py:45
  378.8 3.1 add_convert_fusion.1
  383.3 10.9 %collective-permute-done.48 = bf16[128,1536]{1,0:T(8,128)(2,1)} collective-permute-done((bf16[128,1536]{1,0:T(8,128)(2,1)}, bf16[128,1536]{1,0:T(8,128)(2,1)}, u32[]{:S(2)}, u32[]{:S(2)}) %collective-permute-start.48) | collective-permute-done | bytes 393248 | tf_op jit(solution)/shard_map/ppermute | solution.py:45
  396.2 1.8 collective-permute-start.53
  399.2 4.4 all-to-all-start.1
  405.5 7.0 %collective-permute-done.53 = bf16[384,1024]{1,0:T(8,128)(2,1)} collective-permute-done((bf16[384,1024]{1,0:T(8,128)(2,1)}, bf16[384,1024]{1,0:T(8,128)(2,1)}, u32[]{:S(2)}, u32[]{:S(2)}) %collective-permute-start.53) | collective-permute-done | bytes 786464 | tf_op jit(solution)/shard_map/ppermute | solution.py:45
  413.8 1.8 collective-permute-done.54
  420.4 11.9 %collective-permute-done.56 = bf16[208,1792]{1,0:T(8,128)(2,1)S(1)} collective-permute-done((bf16[208,1792]{1,0:T(8,128)(2,1)S(1)}, bf16[208,1792]{1,0:T(8,128)(2,1)S(1)}, u32[]{:S(2)}, u32[]{:S(2)}) %collective-permute-start.56) | collective-permute-done | bytes 745504 | tf_op jit(solution)/shard_map/ppermute | solution.py:45
  433.2 2.5 convert_add_fusion.2
  438.1 7.7 %collective-permute-start.57 = (bf16[96,1920]{1,0:T(8,128)(2,1)}, bf16[96,1920]{1,0:T(8,128)(2,1)S(1)}, u32[]{:S(2)}, u32[]{:S(2)}) collective-permute-start(bf16[96,1920]{1,0:T(8,128)(2,1)} %get-tuple-element.294), channel_id=1, source_target_pairs={{0,2},{2,0},{4,6},{6,4},{1,3},{3,1},{5,7},{7,5},{8,10},{10,8},{12,... | collective-permute-start | bytes 1105928 | tf_op jit(solution)/shard_map/ppermute | solution.py:45
  448.2 1.7 add_convert_fusion.10
  455.4 3.1 attn_norm_back.1
  463.5 15.5 %collective-permute-done.59 = bf16[96,1920]{1,0:T(8,128)(2,1)S(1)} collective-permute-done((bf16[96,1920]{1,0:T(8,128)(2,1)}, bf16[96,1920]{1,0:T(8,128)(2,1)S(1)}, u32[]{:S(2)}, u32[]{:S(2)}) %collective-permute-start.59) | collective-permute-done | bytes 368672 | tf_op jit(solution)/shard_map/ppermute | solution.py:45
  (318 shorter events, 92.2 us)
Async XLA Ops:
  2.4 17.1 %collective-permute-start = (bf16[96,1792]{1,0:T(8,128)(2,1)}, bf16[96,1792]{1,0:T(8,128)(2,1)}, u32[]{:S(2)}, u32[]{:S(2)}) collective-permute-start(bf16[96,1792]{1,0:T(8,128)(2,1)} %side_by_side.1.refs_0_), channel_id=1, source_target_pairs={{0,2},{2,0},{4,6},{6,4},{1,3},{3,1},{5,7},{7,5},{8,10},{10,8},{12,... | collective-permute-start | bytes 1032200 | tf_op jit(solution)/shard_map/ppermute | solution.py:45
  2.6 17.5 %collective-permute-start.1 = (bf16[96,1792]{1,0:T(8,128)(2,1)}, bf16[96,1792]{1,0:T(8,128)(2,1)}, u32[]{:S(2)}, u32[]{:S(2)}) collective-permute-start(bf16[96,1792]{1,0:T(8,128)(2,1)} %side_by_side.1.refs_0_), channel_id=1, source_target_pairs={{0,4},{2,6},{4,0},{6,2},{1,5},{3,7},{5,1},{7,3},{8,12},{10,14},{12... | collective-permute-start | bytes 1032200 | tf_op jit(solution)/shard_map/ppermute | solution.py:45
  4.9 29.9 %collective-permute-start.2 = (bf16[96,1792]{1,0:T(8,128)(2,1)}, bf16[96,1792]{1,0:T(8,128)(2,1)}, u32[]{:S(2)}, u32[]{:S(2)}) collective-permute-start(bf16[96,1792]{1,0:T(8,128)(2,1)} %side_by_side.1.refs_0_), channel_id=1, source_target_pairs={{0,6},{2,4},{4,2},{6,0},{1,7},{3,5},{5,3},{7,1},{8,14},{10,12},{12... | collective-permute-start | bytes 1032200 | tf_op jit(solution)/shard_map/ppermute | solution.py:45
  37.2 42.2 %collective-permute-start.3 = (bf16[384,1792]{1,0:T(8,128)(2,1)}, bf16[384,1792]{1,0:T(8,128)(2,1)S(1)}, u32[]{:S(2)}, u32[]{:S(2)}) collective-permute-start(bf16[384,1792]{1,0:T(8,128)(2,1)} %place.3.refs_0_), channel_id=1, source_target_pairs={{0,8},{8,0},{16,24},{24,16},{1,9},{9,1},{17,25},{25,17},{2,10},{10... | collective-permute-start | bytes 4128776 | tf_op jit(solution)/shard_map/ppermute | solution.py:45
  38.4 41.0 %collective-permute-start.4 = (bf16[384,1792]{1,0:T(8,128)(2,1)}, bf16[384,1792]{1,0:T(8,128)(2,1)S(1)}, u32[]{:S(2)}, u32[]{:S(2)}) collective-permute-start(bf16[384,1792]{1,0:T(8,128)(2,1)} %place.3.refs_0_), channel_id=1, source_target_pairs={{0,16},{8,24},{16,0},{24,8},{1,17},{9,25},{17,1},{25,9},{2,18},{10... | collective-permute-start | bytes 4128776 | tf_op jit(solution)/shard_map/ppermute | solution.py:45
  40.7 15.1 %collective-permute-start.5 = (bf16[96,2304]{1,0:T(8,128)(2,1)S(1)}, bf16[96,2304]{1,0:T(8,128)(2,1)S(1)}, u32[]{:S(2)}, u32[]{:S(2)}) collective-permute-start(bf16[96,2304]{1,0:T(8,128)(2,1)S(1)} %pad_maximum_fusion.26), channel_id=1, source_target_pairs={{0,2},{2,0},{4,6},{6,4},{1,3},{3,1},{5,7},{7,5},{8,10},{10,8},{12,... | collective-permute-start | bytes 1327112 | tf_op jit(solution)/shard_map/ppermute | solution.py:45
  40.7 19.8 %collective-permute-start.6 = (bf16[96,2304]{1,0:T(8,128)(2,1)S(1)}, bf16[96,2304]{1,0:T(8,128)(2,1)S(1)}, u32[]{:S(2)}, u32[]{:S(2)}) collective-permute-start(bf16[96,2304]{1,0:T(8,128)(2,1)S(1)} %pad_maximum_fusion.27), channel_id=1, source_target_pairs={{0,4},{2,6},{4,0},{6,2},{1,5},{3,7},{5,1},{7,3},{8,12},{10,14},{12... | collective-permute-start | bytes 1327112 | tf_op jit(solution)/shard_map/ppermute | solution.py:45
  43.2 36.3 %collective-permute-start.7 = (bf16[96,2304]{1,0:T(8,128)(2,1)S(1)}, bf16[96,2304]{1,0:T(8,128)(2,1)S(1)}, u32[]{:S(2)}, u32[]{:S(2)}) collective-permute-start(bf16[96,2304]{1,0:T(8,128)(2,1)S(1)} %pad_maximum_fusion.28), channel_id=1, source_target_pairs={{0,6},{2,4},{4,2},{6,0},{1,7},{3,5},{5,3},{7,1},{8,14},{10,12},{12... | collective-permute-start | bytes 1327112 | tf_op jit(solution)/shard_map/ppermute | solution.py:45
  79.6 13.5 %collective-permute-start.8 = (bf16[192,1792]{1,0:T(8,128)(2,1)S(1)}, bf16[192,1792]{1,0:T(8,128)(2,1)S(1)}, u32[]{:S(2)}, u32[]{:S(2)}) collective-permute-start(bf16[192,1792]{1,0:T(8,128)(2,1)S(1)} %slice.311), channel_id=1, source_target_pairs={{0,8},{8,0},{16,24},{24,16},{1,9},{9,1},{17,25},{25,17},{2,10},{10... | collective-permute-start | bytes 2064392 | tf_op jit(solution)/shard_map/ppermute | solution.py:45
  79.9 13.2 %collective-permute-start.9 = (bf16[192,1792]{1,0:T(8,128)(2,1)S(1)}, bf16[192,1792]{1,0:T(8,128)(2,1)S(1)}, u32[]{:S(2)}, u32[]{:S(2)}) collective-permute-start(bf16[192,1792]{1,0:T(8,128)(2,1)S(1)} %slice.312), channel_id=1, source_target_pairs={{0,16},{8,24},{16,0},{24,8},{1,17},{9,25},{17,1},{25,9},{2,18},{10... | collective-permute-start | bytes 2064392 | tf_op jit(solution)/shard_map/ppermute | solution.py:45
  83.6 18.4 %collective-permute-start.10 = (bf16[96,1152]{1,0:T(8,128)(2,1)}, bf16[96,1152]{1,0:T(8,128)(2,1)S(1)}, u32[]{:S(2)}, u32[]{:S(2)}) collective-permute-start(bf16[96,1152]{1,0:T(8,128)(2,1)} %get-tuple-element.184), channel_id=1, source_target_pairs={{0,2},{2,0},{4,6},{6,4},{1,3},{3,1},{5,7},{7,5},{8,10},{10,8},{12,... | collective-permute-start | bytes 663560 | tf_op jit(solution)/shard_map/ppermute | solution.py:45
  83.6 18.5 %collective-permute-start.11 = (bf16[96,1152]{1,0:T(8,128)(2,1)}, bf16[96,1152]{1,0:T(8,128)(2,1)S(1)}, u32[]{:S(2)}, u32[]{:S(2)}) collective-permute-start(bf16[96,1152]{1,0:T(8,128)(2,1)} %get-tuple-element.185), channel_id=1, source_target_pairs={{0,4},{2,6},{4,0},{6,2},{1,5},{3,7},{5,1},{7,3},{8,12},{10,14},{12... | collective-permute-start | bytes 663560 | tf_op jit(solution)/shard_map/ppermute | solution.py:45
  86.1 17.9 %collective-permute-start.12 = (bf16[96,1152]{1,0:T(8,128)(2,1)}, bf16[96,1152]{1,0:T(8,128)(2,1)S(1)}, u32[]{:S(2)}, u32[]{:S(2)}) collective-permute-start(bf16[96,1152]{1,0:T(8,128)(2,1)} %get-tuple-element.186), channel_id=1, source_target_pairs={{0,6},{2,4},{4,2},{6,0},{1,7},{3,5},{5,3},{7,1},{8,14},{10,12},{12... | collective-permute-start | bytes 663560 | tf_op jit(solution)/shard_map/ppermute | solution.py:45
  104.0 9.1 %collective-permute-start.13 = (bf16[256,256]{1,0:T(8,128)(2,1)}, bf16[256,256]{1,0:T(8,128)(2,1)S(1)}, u32[]{:S(2)}, u32[]{:S(2)}) collective-permute-start(bf16[256,256]{1,0:T(8,128)(2,1)} %get-tuple-element.192.refs_0_), channel_id=1, source_target_pairs={{0,2},{2,0},{4,6},{6,4},{1,3},{3,1},{5,7},{7,5},{8,10},{10,8},{12,... | collective-permute-start | bytes 393224 | tf_op jit(solution)/shard_map/ppermute | solution.py:45
  104.0 11.4 %collective-permute-start.14 = (bf16[256,256]{1,0:T(8,128)(2,1)}, bf16[256,256]{1,0:T(8,128)(2,1)S(1)}, u32[]{:S(2)}, u32[]{:S(2)}) collective-permute-start(bf16[256,256]{1,0:T(8,128)(2,1)} %get-tuple-element.192.refs_0_), channel_id=1, source_target_pairs={{0,4},{2,6},{4,0},{6,2},{1,5},{3,7},{5,1},{7,3},{8,12},{10,14},{12... | collective-permute-start | bytes 393224 | tf_op jit(solution)/shard_map/ppermute | solution.py:45
  107.2 11.2 %collective-permute-start.15 = (bf16[256,256]{1,0:T(8,128)(2,1)}, bf16[256,256]{1,0:T(8,128)(2,1)S(1)}, u32[]{:S(2)}, u32[]{:S(2)}) collective-permute-start(bf16[256,256]{1,0:T(8,128)(2,1)} %get-tuple-element.192.refs_0_), channel_id=1, source_target_pairs={{0,6},{2,4},{4,2},{6,0},{1,7},{3,5},{5,3},{7,1},{8,14},{10,12},{12... | collective-permute-start | bytes 393224 | tf_op jit(solution)/shard_map/ppermute | solution.py:45
  108.7 25.4 %collective-permute-start.17 = (bf16[384,1152]{1,0:T(8,128)(2,1)S(1)}, bf16[384,1152]{1,0:T(8,128)(2,1)}, u32[]{:S(2)}, u32[]{:S(2)}) collective-permute-start(bf16[384,1152]{1,0:T(8,128)(2,1)S(1)} %copy-done.9), channel_id=1, source_target_pairs={{0,8},{8,0},{16,24},{24,16},{1,9},{9,1},{17,25},{25,17},{2,10},{10... | collective-permute-start | bytes 2654216 | tf_op jit(solution)/shard_map/ppermute | solution.py:45
  109.9 24.2 %collective-permute-start.18 = (bf16[384,1152]{1,0:T(8,128)(2,1)S(1)}, bf16[384,1152]{1,0:T(8,128)(2,1)}, u32[]{:S(2)}, u32[]{:S(2)}) collective-permute-start(bf16[384,1152]{1,0:T(8,128)(2,1)S(1)} %copy-done.9), channel_id=1, source_target_pairs={{0,16},{8,24},{16,0},{24,8},{1,17},{9,25},{17,1},{25,9},{2,18},{10... | collective-permute-start | bytes 2654216 | tf_op jit(solution)/shard_map/ppermute | solution.py:45
  126.9 4.2 collective-permute-start.16
  134.1 40.1 %collective-permute-start.22 = (bf16[384,2304]{1,0:T(8,128)(2,1)S(1)}, bf16[384,2304]{1,0:T(8,128)(2,1)S(1)}, u32[]{:S(2)}, u32[]{:S(2)}) collective-permute-start(bf16[384,2304]{1,0:T(8,128)(2,1)S(1)} %copy-done.1), channel_id=1, source_target_pairs={{0,8},{8,0},{16,24},{24,16},{1,9},{9,1},{17,25},{25,17},{2,10},{10... | collective-permute-start | bytes 5308424 | tf_op jit(solution)/shard_map/ppermute | solution.py:45
  135.4 39.7 %collective-permute-start.23 = (bf16[384,2304]{1,0:T(8,128)(2,1)S(1)}, bf16[384,2304]{1,0:T(8,128)(2,1)S(1)}, u32[]{:S(2)}, u32[]{:S(2)}) collective-permute-start(bf16[384,2304]{1,0:T(8,128)(2,1)S(1)} %copy-done.1), channel_id=1, source_target_pairs={{0,16},{8,24},{16,0},{24,8},{1,17},{9,25},{17,1},{25,9},{2,18},{10... | collective-permute-start | bytes 5308424 | tf_op jit(solution)/shard_map/ppermute | solution.py:45
  135.6 15.8 %collective-permute-start.19 = (bf16[128,1536]{1,0:T(8,128)(2,1)}, bf16[128,1536]{1,0:T(8,128)(2,1)S(1)}, u32[]{:S(2)}, u32[]{:S(2)}) collective-permute-start(bf16[128,1536]{1,0:T(8,128)(2,1)} %get-tuple-element.203), channel_id=1, source_target_pairs={{0,2},{2,0},{4,6},{6,4},{1,3},{3,1},{5,7},{7,5},{8,10},{10,8},{12,... | collective-permute-start | bytes 1179656 | tf_op jit(solution)/shard_map/ppermute | solution.py:45
  135.6 19.5 %collective-permute-start.20 = (bf16[128,1536]{1,0:T(8,128)(2,1)}, bf16[128,1536]{1,0:T(8,128)(2,1)S(1)}, u32[]{:S(2)}, u32[]{:S(2)}) collective-permute-start(bf16[128,1536]{1,0:T(8,128)(2,1)} %get-tuple-element.203), channel_id=1, source_target_pairs={{0,4},{2,6},{4,0},{6,2},{1,5},{3,7},{5,1},{7,3},{8,12},{10,14},{12... | collective-permute-start | bytes 1179656 | tf_op jit(solution)/shard_map/ppermute | solution.py:45
  138.0 33.9 %collective-permute-start.21 = (bf16[128,1536]{1,0:T(8,128)(2,1)}, bf16[128,1536]{1,0:T(8,128)(2,1)S(1)}, u32[]{:S(2)}, u32[]{:S(2)}) collective-permute-start(bf16[128,1536]{1,0:T(8,128)(2,1)} %get-tuple-element.203), channel_id=1, source_target_pairs={{0,6},{2,4},{4,2},{6,0},{1,7},{3,5},{5,3},{7,1},{8,14},{10,12},{12... | collective-permute-start | bytes 1179656 | tf_op jit(solution)/shard_map/ppermute | solution.py:45
  176.5 4.4 collective-permute-start.24
  179.0 30.4 %collective-permute-start.28 = (bf16[192,3456]{1,0:T(8,128)(2,1)S(1)}, bf16[192,3456]{1,0:T(8,128)(2,1)S(1)}, u32[]{:S(2)}, u32[]{:S(2)}) collective-permute-start(bf16[192,3456]{1,0:T(8,128)(2,1)S(1)} %pad_maximum_fusion.4), channel_id=1, source_target_pairs={{0,8},{8,0},{16,24},{24,16},{1,9},{9,1},{17,25},{25,17},{2,10},{10... | collective-permute-start | bytes 3981320 | tf_op jit(solution)/shard_map/ppermute | solution.py:45
  180.5 30.1 %collective-permute-start.29 = (bf16[192,3456]{1,0:T(8,128)(2,1)S(1)}, bf16[192,3456]{1,0:T(8,128)(2,1)S(1)}, u32[]{:S(2)}, u32[]{:S(2)}) collective-permute-start(bf16[192,3456]{1,0:T(8,128)(2,1)S(1)} %pad_maximum_fusion.3), channel_id=1, source_target_pairs={{0,16},{8,24},{16,0},{24,8},{1,17},{9,25},{17,1},{25,9},{2,18},{10... | collective-permute-start | bytes 3981320 | tf_op jit(solution)/shard_map/ppermute | solution.py:45
  180.9 45.0 %collective-permute-start.25 = (bf16[128,1536]{1,0:T(8,128)(2,1)}, bf16[128,1536]{1,0:T(8,128)(2,1)S(1)}, u32[]{:S(2)}, u32[]{:S(2)}) collective-permute-start(bf16[128,1536]{1,0:T(8,128)(2,1)} %fusion.18.base), channel_id=1, source_target_pairs={{0,2},{2,0},{4,6},{6,4},{1,3},{3,1},{5,7},{7,5},{8,10},{10,8},{12,... | collective-permute-start | bytes 1179656 | tf_op jit(solution)/shard_map/ppermute | solution.py:45
  180.9 45.0 %collective-permute-start.26 = (bf16[128,1536]{1,0:T(8,128)(2,1)}, bf16[128,1536]{1,0:T(8,128)(2,1)S(1)}, u32[]{:S(2)}, u32[]{:S(2)}) collective-permute-start(bf16[128,1536]{1,0:T(8,128)(2,1)} %fusion.18.base), channel_id=1, source_target_pairs={{0,4},{2,6},{4,0},{6,2},{1,5},{3,7},{5,1},{7,3},{8,12},{10,14},{12... | collective-permute-start | bytes 1179656 | tf_op jit(solution)/shard_map/ppermute | solution.py:45
  183.3 42.6 %collective-permute-start.27 = (bf16[128,1536]{1,0:T(8,128)(2,1)}, bf16[128,1536]{1,0:T(8,128)(2,1)S(1)}, u32[]{:S(2)}, u32[]{:S(2)}) collective-permute-start(bf16[128,1536]{1,0:T(8,128)(2,1)} %fusion.18.base), channel_id=1, source_target_pairs={{0,6},{2,4},{4,2},{6,0},{1,7},{3,5},{5,3},{7,1},{8,14},{10,12},{12... | collective-permute-start | bytes 1179656 | tf_op jit(solution)/shard_map/ppermute | solution.py:45
  227.1 4.6 collective-permute-start.30
  259.2 8.8 %collective-permute-start.31 = (bf16[512,1536]{1,0:T(8,128)(2,1)}, bf16[512,1536]{1,0:T(8,128)(2,1)S(1)}, u32[]{:S(2)}, u32[]{:S(2)}) collective-permute-start(bf16[512,1536]{1,0:T(8,128)(2,1)} %get-tuple-element.222), channel_id=1, source_target_pairs={{0,1},{1,0},{2,3},{3,2},{4,5},{5,4},{6,7},{7,6},{8,9},{9,8},{10,11... | collective-permute-start | bytes 4718600 | tf_op jit(solution)/shard_map/ppermute | solution.py:45
  259.6 10.9 %collective-permute-start.32 = (bf16[512,1536]{1,0:T(8,128)(2,1)}, bf16[512,1536]{1,0:T(8,128)(2,1)S(1)}, u32[]{:S(2)}, u32[]{:S(2)}) collective-permute-start(bf16[512,1536]{1,0:T(8,128)(2,1)} %get-tuple-element.224), channel_id=1, source_target_pairs={{0,1},{1,0},{2,3},{3,2},{4,5},{5,4},{6,7},{7,6},{8,9},{9,8},{10,11... | collective-permute-start | bytes 4718600 | tf_op jit(solution)/shard_map/ppermute | solution.py:45
  271.5 21.0 %collective-permute-start.36 = (bf16[384,1152]{1,0:T(8,128)(2,1)S(1)}, bf16[384,1152]{1,0:T(8,128)(2,1)S(1)}, u32[]{:S(2)}, u32[]{:S(2)}) collective-permute-start(bf16[384,1152]{1,0:T(8,128)(2,1)S(1)} %pad_maximum_fusion.5), channel_id=1, source_target_pairs={{0,8},{8,0},{16,24},{24,16},{1,9},{9,1},{17,25},{25,17},{2,10},{10... | collective-permute-start | bytes 2654216 | tf_op jit(solution)/shard_map/ppermute | solution.py:45
  272.8 20.7 %collective-permute-start.37 = (bf16[384,1152]{1,0:T(8,128)(2,1)S(1)}, bf16[384,1152]{1,0:T(8,128)(2,1)S(1)}, u32[]{:S(2)}, u32[]{:S(2)}) collective-permute-start(bf16[384,1152]{1,0:T(8,128)(2,1)S(1)} %pad_maximum_fusion.6), channel_id=1, source_target_pairs={{0,16},{8,24},{16,0},{24,8},{1,17},{9,25},{17,1},{25,9},{2,18},{10... | collective-permute-start | bytes 2654216 | tf_op jit(solution)/shard_map/ppermute | solution.py:45
  273.1 35.8 %collective-permute-start.33 = (bf16[128,1536]{1,0:T(8,128)(2,1)}, bf16[128,1536]{1,0:T(8,128)(2,1)}, u32[]{:S(2)}, u32[]{:S(2)}) collective-permute-start(bf16[128,1536]{1,0:T(8,128)(2,1)} %get-tuple-element.226), channel_id=1, source_target_pairs={{0,2},{2,0},{4,6},{6,4},{1,3},{3,1},{5,7},{7,5},{8,10},{10,8},{12,... | collective-permute-start | bytes 1179656 | tf_op jit(solution)/shard_map/ppermute | solution.py:45
  273.1 35.8 %collective-permute-start.34 = (bf16[128,1536]{1,0:T(8,128)(2,1)}, bf16[128,1536]{1,0:T(8,128)(2,1)}, u32[]{:S(2)}, u32[]{:S(2)}) collective-permute-start(bf16[128,1536]{1,0:T(8,128)(2,1)} %get-tuple-element.227), channel_id=1, source_target_pairs={{0,4},{2,6},{4,0},{6,2},{1,5},{3,7},{5,1},{7,3},{8,12},{10,14},{12... | collective-permute-start | bytes 1179656 | tf_op jit(solution)/shard_map/ppermute | solution.py:45
  275.5 33.9 %collective-permute-start.35 = (bf16[128,1536]{1,0:T(8,128)(2,1)}, bf16[128,1536]{1,0:T(8,128)(2,1)}, u32[]{:S(2)}, u32[]{:S(2)}) collective-permute-start(bf16[128,1536]{1,0:T(8,128)(2,1)} %get-tuple-element.228), channel_id=1, source_target_pairs={{0,6},{2,4},{4,2},{6,0},{1,7},{3,5},{5,3},{7,1},{8,14},{10,12},{12... | collective-permute-start | bytes 1179656 | tf_op jit(solution)/shard_map/ppermute | solution.py:45
  293.7 13.9 %collective-permute-start.38 = (bf16[192,1152]{1,0:T(8,128)(2,1)S(1)}, bf16[192,1152]{1,0:T(8,128)(2,1)S(1)}, u32[]{:S(2)}, u32[]{:S(2)}) collective-permute-start(bf16[192,1152]{1,0:T(8,128)(2,1)S(1)} %get-tuple-element.233), channel_id=1, source_target_pairs={{0,8},{8,0},{16,24},{24,16},{1,9},{9,1},{17,25},{25,17},{2,10},{10... | collective-permute-start | bytes 1327112 | tf_op jit(solution)/shard_map/ppermute | solution.py:45
  294.1 13.5 %collective-permute-start.39 = (bf16[192,1152]{1,0:T(8,128)(2,1)S(1)}, bf16[192,1152]{1,0:T(8,128)(2,1)S(1)}, u32[]{:S(2)}, u32[]{:S(2)}) collective-permute-start(bf16[192,1152]{1,0:T(8,128)(2,1)S(1)} %get-tuple-element.234), channel_id=1, source_target_pairs={{0,16},{8,24},{16,0},{24,8},{1,17},{9,25},{17,1},{25,9},{2,18},{10... | collective-permute-start | bytes 1327112 | tf_op jit(solution)/shard_map/ppermute | solution.py:45
  311.7 42.1 %collective-permute-start.44 = (bf16[384,2304]{1,0:T(8,128)(2,1)S(1)}, bf16[384,2304]{1,0:T(8,128)(2,1)}, u32[]{:S(2)}, u32[]{:S(2)}) collective-permute-start(bf16[384,2304]{1,0:T(8,128)(2,1)S(1)} %pad_maximum_fusion), channel_id=1, source_target_pairs={{0,8},{8,0},{16,24},{24,16},{1,9},{9,1},{17,25},{25,17},{2,10},{10... | collective-permute-start | bytes 5308424 | tf_op jit(solution)/shard_map/ppermute | solution.py:45
  313.7 40.0 %collective-permute-start.45 = (bf16[384,2304]{1,0:T(8,128)(2,1)}, bf16[384,2304]{1,0:T(8,128)(2,1)}, u32[]{:S(2)}, u32[]{:S(2)}) collective-permute-start(bf16[384,2304]{1,0:T(8,128)(2,1)} %pad_maximum_fusion.1), channel_id=1, source_target_pairs={{0,16},{8,24},{16,0},{24,8},{1,17},{9,25},{17,1},{25,9},{2,18},{10... | collective-permute-start | bytes 5308424 | tf_op jit(solution)/shard_map/ppermute | solution.py:45
  315.0 24.6 %all-to-all-start = ((bf16[4,96,1152]{2,1,0:T(8,128)(2,1)}), bf16[4,96,1152]{2,1,0:T(8,128)(2,1)S(1)}, u32[]{:S(2)}, u32[]{:S(2)}) async-start(bf16[4,96,1152]{2,1,0:T(8,128)(2,1)} %bitcast.22), calls=%async_computation | async-start | bytes 1769472 | tf_op jit(solution)/shard_map/all_to_all | solution.py:749
  322.3 4.7 collective-permute-start.40
  339.5 5.0 %collective-permute-start.41 = (bf16[256,256]{1,0:T(8,128)(2,1)}, bf16[256,256]{1,0:T(8,128)(2,1)S(1)}, u32[]{:S(2)}, u32[]{:S(2)}) collective-permute-start(bf16[256,256]{1,0:T(8,128)(2,1)} %get-tuple-element.251), channel_id=1, source_target_pairs={{0,2},{2,0},{4,6},{6,4},{1,3},{3,1},{5,7},{7,5},{8,10},{10,8},{12,... | collective-permute-start | bytes 393224 | tf_op jit(solution)/shard_map/ppermute | solution.py:45
  340.4 7.9 %collective-permute-start.42 = (bf16[256,256]{1,0:T(8,128)(2,1)}, bf16[256,256]{1,0:T(8,128)(2,1)S(1)}, u32[]{:S(2)}, u32[]{:S(2)}) collective-permute-start(bf16[256,256]{1,0:T(8,128)(2,1)} %get-tuple-element.252), channel_id=1, source_target_pairs={{0,4},{2,6},{4,0},{6,2},{1,5},{3,7},{5,1},{7,3},{8,12},{10,14},{12... | collective-permute-start | bytes 393224 | tf_op jit(solution)/shard_map/ppermute | solution.py:45
  342.0 11.8 %collective-permute-start.43 = (bf16[256,256]{1,0:T(8,128)(2,1)}, bf16[256,256]{1,0:T(8,128)(2,1)S(1)}, u32[]{:S(2)}, u32[]{:S(2)}) collective-permute-start(bf16[256,256]{1,0:T(8,128)(2,1)} %get-tuple-element.253), channel_id=1, source_target_pairs={{0,6},{2,4},{4,2},{6,0},{1,7},{3,5},{5,3},{7,1},{8,14},{10,12},{12... | collective-permute-start | bytes 393224 | tf_op jit(solution)/shard_map/ppermute | solution.py:45
  357.4 19.9 %collective-permute-start.49 = (bf16[192,2304]{1,0:T(8,128)(2,1)}, bf16[192,2304]{1,0:T(8,128)(2,1)S(1)}, u32[]{:S(2)}, u32[]{:S(2)}) collective-permute-start(bf16[192,2304]{1,0:T(8,128)(2,1)} %get-tuple-element.265), channel_id=1, source_target_pairs={{0,8},{8,0},{16,24},{24,16},{1,9},{9,1},{17,25},{25,17},{2,10},{10... | collective-permute-start | bytes 2654216 | tf_op jit(solution)/shard_map/ppermute | solution.py:45
  358.5 19.7 %collective-permute-start.50 = (bf16[192,2304]{1,0:T(8,128)(2,1)}, bf16[192,2304]{1,0:T(8,128)(2,1)}, u32[]{:S(2)}, u32[]{:S(2)}) collective-permute-start(bf16[192,2304]{1,0:T(8,128)(2,1)} %get-tuple-element.266), channel_id=1, source_target_pairs={{0,16},{8,24},{16,0},{24,8},{1,17},{9,25},{17,1},{25,9},{2,18},{10... | collective-permute-start | bytes 2654216 | tf_op jit(solution)/shard_map/ppermute | solution.py:45
  359.6 23.7 %collective-permute-start.46 = (bf16[128,1536]{1,0:T(8,128)(2,1)}, bf16[128,1536]{1,0:T(8,128)(2,1)}, u32[]{:S(2)}, u32[]{:S(2)}) collective-permute-start(bf16[128,1536]{1,0:T(8,128)(2,1)} %get-tuple-element.260), channel_id=1, source_target_pairs={{0,2},{2,0},{4,6},{6,4},{1,3},{3,1},{5,7},{7,5},{8,10},{10,8},{12,... | collective-permute-start | bytes 1179656 | tf_op jit(solution)/shard_map/ppermute | solution.py:45
  359.7 23.7 %collective-permute-start.47 = (bf16[128,1536]{1,0:T(8,128)(2,1)}, bf16[128,1536]{1,0:T(8,128)(2,1)}, u32[]{:S(2)}, u32[]{:S(2)}) collective-permute-start(bf16[128,1536]{1,0:T(8,128)(2,1)} %get-tuple-element.261), channel_id=1, source_target_pairs={{0,4},{2,6},{4,0},{6,2},{1,5},{3,7},{5,1},{7,3},{8,12},{10,14},{12... | collective-permute-start | bytes 1179656 | tf_op jit(solution)/shard_map/ppermute | solution.py:45
  362.1 32.2 %collective-permute-start.48 = (bf16[128,1536]{1,0:T(8,128)(2,1)}, bf16[128,1536]{1,0:T(8,128)(2,1)}, u32[]{:S(2)}, u32[]{:S(2)}) collective-permute-start(bf16[128,1536]{1,0:T(8,128)(2,1)} %get-tuple-element.262), channel_id=1, source_target_pairs={{0,6},{2,4},{4,2},{6,0},{1,7},{3,5},{5,3},{7,1},{8,14},{10,12},{12... | collective-permute-start | bytes 1179656 | tf_op jit(solution)/shard_map/ppermute | solution.py:45
  378.4 15.9 %collective-permute-start.51 = (bf16[384,768]{1,0:T(8,128)(2,1)S(1)}, bf16[384,768]{1,0:T(8,128)(2,1)S(1)}, u32[]{:S(2)}, u32[]{:S(2)}) collective-permute-start(bf16[384,768]{1,0:T(8,128)(2,1)S(1)} %pad_maximum_fusion.23), channel_id=1, source_target_pairs={{0,8},{8,0},{16,24},{24,16},{1,9},{9,1},{17,25},{25,17},{2,10},{10... | collective-permute-start | bytes 1769480 | tf_op jit(solution)/shard_map/ppermute | solution.py:45
  378.8 15.5 %collective-permute-start.52 = (bf16[384,768]{1,0:T(8,128)(2,1)S(1)}, bf16[384,768]{1,0:T(8,128)(2,1)S(1)}, u32[]{:S(2)}, u32[]{:S(2)}) collective-permute-start(bf16[384,768]{1,0:T(8,128)(2,1)S(1)} %pad_maximum_fusion.24), channel_id=1, source_target_pairs={{0,16},{8,24},{16,0},{24,8},{1,17},{9,25},{17,1},{25,9},{2,18},{10... | collective-permute-start | bytes 1769480 | tf_op jit(solution)/shard_map/ppermute | solution.py:45
  396.2 16.3 %collective-permute-start.53 = (bf16[384,1024]{1,0:T(8,128)(2,1)}, bf16[384,1024]{1,0:T(8,128)(2,1)}, u32[]{:S(2)}, u32[]{:S(2)}) collective-permute-start(bf16[384,1024]{1,0:T(8,128)(2,1)} %pad_maximum_fusion.18), channel_id=1, source_target_pairs={{0,16},{8,24},{16,0},{24,8},{1,17},{9,25},{17,1},{25,9},{2,18},{10... | collective-permute-start | bytes 2359304 | tf_op jit(solution)/shard_map/ppermute | solution.py:45
  399.0 16.6 %collective-permute-start.54 = (bf16[400,1024]{1,0:T(8,128)(2,1)}, bf16[400,1024]{1,0:T(8,128)(2,1)}, u32[]{:S(2)}, u32[]{:S(2)}) collective-permute-start(bf16[400,1024]{1,0:T(8,128)(2,1)} %pad_maximum_fusion.17), channel_id=1, source_target_pairs={{0,8},{8,0},{16,24},{24,16},{1,9},{9,1},{17,25},{25,17},{2,10},{10... | collective-permute-start | bytes 2457608 | tf_op jit(solution)/shard_map/ppermute | solution.py:45
  399.2 38.9 %all-to-all-start.1 = ((bf16[4,96,2304]{2,1,0:T(8,128)(2,1)}), bf16[4,96,2304]{2,1,0:T(8,128)(2,1)}, u32[]{:S(2)}, u32[]{:S(2)}) async-start(bf16[4,96,2304]{2,1,0:T(8,128)(2,1)} %bitcast.72), calls=%async_computation.1 | async-start | bytes 3538944 | tf_op jit(solution)/shard_map/all_to_all | solution.py:841
  418.3 13.9 %collective-permute-start.56 = (bf16[208,1792]{1,0:T(8,128)(2,1)S(1)}, bf16[208,1792]{1,0:T(8,128)(2,1)S(1)}, u32[]{:S(2)}, u32[]{:S(2)}) collective-permute-start(bf16[208,1792]{1,0:T(8,128)(2,1)S(1)} %fusion.4), channel_id=1, source_target_pairs={{0,16},{8,24},{16,0},{24,8},{1,17},{9,25},{17,1},{25,9},{2,18},{10... | collective-permute-start | bytes 2236424 | tf_op jit(solution)/shard_map/ppermute | solution.py:45
  418.9 14.3 %collective-permute-start.55 = (bf16[192,1792]{1,0:T(8,128)(2,1)S(1)}, bf16[192,1792]{1,0:T(8,128)(2,1)}, u32[]{:S(2)}, u32[]{:S(2)}) collective-permute-start(bf16[192,1792]{1,0:T(8,128)(2,1)S(1)} %get-tuple-element.285), channel_id=1, source_target_pairs={{0,8},{8,0},{16,24},{24,16},{1,9},{9,1},{17,25},{25,17},{2,10},{10... | collective-permute-start | bytes 2064392 | tf_op jit(solution)/shard_map/ppermute | solution.py:45
  438.1 25.4 %collective-permute-start.57 = (bf16[96,1920]{1,0:T(8,128)(2,1)}, bf16[96,1920]{1,0:T(8,128)(2,1)S(1)}, u32[]{:S(2)}, u32[]{:S(2)}) collective-permute-start(bf16[96,1920]{1,0:T(8,128)(2,1)} %get-tuple-element.294), channel_id=1, source_target_pairs={{0,2},{2,0},{4,6},{6,4},{1,3},{3,1},{5,7},{7,5},{8,10},{10,8},{12,... | collective-permute-start | bytes 1105928 | tf_op jit(solution)/shard_map/ppermute | solution.py:45
  445.8 17.7 %collective-permute-start.58 = (bf16[96,1920]{1,0:T(8,128)(2,1)}, bf16[96,1920]{1,0:T(8,128)(2,1)S(1)}, u32[]{:S(2)}, u32[]{:S(2)}) collective-permute-start(bf16[96,1920]{1,0:T(8,128)(2,1)} %get-tuple-element.295), channel_id=1, source_target_pairs={{0,4},{2,6},{4,0},{6,2},{1,5},{3,7},{5,1},{7,3},{8,12},{10,14},{12... | collective-permute-start | bytes 1105928 | tf_op jit(solution)/shard_map/ppermute | solution.py:45
  445.8 33.2 %collective-permute-start.59 = (bf16[96,1920]{1,0:T(8,128)(2,1)}, bf16[96,1920]{1,0:T(8,128)(2,1)S(1)}, u32[]{:S(2)}, u32[]{:S(2)}) collective-permute-start(bf16[96,1920]{1,0:T(8,128)(2,1)} %get-tuple-element.296), channel_id=1, source_target_pairs={{0,6},{2,4},{4,2},{6,0},{1,7},{3,5},{5,3},{7,1},{8,14},{10,12},{12... | collective-permute-start | bytes 1105928 | tf_op jit(solution)/shard_map/ppermute | solution.py:45
  447.0 7.5 %collective-permute-start.60 = (f32[128,1536]{1,0:T(8,128)}, f32[128,1536]{1,0:T(8,128)S(1)}, u32[]{:S(2)}, u32[]{:S(2)}) collective-permute-start(f32[128,1536]{1,0:T(8,128)} %get-tuple-element.299), channel_id=1, source_target_pairs={{0,1},{1,0},{2,3},{3,2},{4,5},{5,4},{6,7},{7,6},{8,9},{9,8},{10,11... | collective-permute-start | bytes 2359304 | tf_op jit(solution)/shard_map/ppermute | solution.py:45
  450.0 11.4 %collective-permute-start.62 = (bf16[128,1536]{1,0:T(8,128)(2,1)S(1)}, bf16[128,1536]{1,0:T(8,128)(2,1)S(1)}, u32[]{:S(2)}, u32[]{:S(2)}) collective-permute-start(bf16[128,1536]{1,0:T(8,128)(2,1)S(1)} %pad_maximum_fusion.30), channel_id=1, source_target_pairs={{0,1},{1,0},{2,3},{3,2},{4,5},{5,4},{6,7},{7,6},{8,9},{9,8},{10,11... | collective-permute-start | bytes 1179656 | tf_op jit(solution)/shard_map/ppermute | solution.py:45
  (56 other events, 345.7 us)

commit v5 on v4

--- a/solution.py
+++ b/solution.py
@@ -1,4 +1,5 @@
 import functools
+import math
 
 import jax
 import jax.numpy as jnp
@@ -89,12 +90,21 @@
     return swap(from_y[:half], "seq", 1), swap(from_x[half:], "seq", 2)
 
 
+def near_payload(partial_sum):
+    _, for_x, for_y, for_far = jnp.split(partial_sum, 4, 0)
+    half = for_x.shape[0] // 2
+    return (
+        jnp.concatenate([for_far[half:], for_x[half:]], 0),
+        jnp.concatenate([for_far[:half], for_y[:half]], 0),
+    )
+
+
+def near_swap(payload):
+    return swap(payload[0], "seq", 1), swap(payload[1], "seq", 2)
+
+
 def scatter_near(partial_sum):
-    own, for_x, for_y, for_far = jnp.split(partial_sum, 4, 0)
-    half = own.shape[0] // 2
-    got_x = swap(jnp.concatenate([for_far[half:], for_x[half:]], 0), "seq", 1)
-    got_y = swap(jnp.concatenate([for_far[:half], for_y[:half]], 0), "seq", 2)
-    return got_x, got_y
+    return near_swap(near_payload(partial_sum))
 
 
 def relay(partial_sum, got_x, got_y):
@@ -171,6 +181,7 @@
 
 
 VMEM_BYTES = 56 * 1024 * 1024
+ALONE = ("mlp_norm_back", "attend_back", "project_back",)
 LITTLE = pl.CostEstimate(flops=1, bytes_accessed=1, transcendentals=0)
 
 
@@ -272,7 +283,7 @@
         out_send[...] = out.astype(jnp.bfloat16)
 
 
-def by_tiles(body, count, ins, halves, parts, outs, half_outs, scratch, name):
+def by_tiles(body, count, ins, halves, parts, outs, half_outs, scratch, name, grant):
     tile = min(256, count)
     tiles_each = count // tile
 
@@ -301,7 +312,7 @@
         ],
         scratch_shapes=[pltpu.VMEM(shape, jnp.bfloat16) for shape in scratch]
         + [pltpu.SemaphoreType.DMA((15,))],
-        compiler_params=pltpu.CompilerParams(vmem_limit_bytes=VMEM_BYTES),
+        compiler_params=pltpu.CompilerParams(vmem_limit_bytes=grant * 1024 * 1024),
         cost_estimate=LITTLE,
         name=name,
     )(*ins, *(x for pair in halves for x in pair), *parts)
@@ -324,21 +335,26 @@
         in_specs=[columns, columns, pl.BlockSpec(grads.shape, lambda i: (0, 0))],
         out_specs=pl.BlockSpec((tile, grads.shape[1]), lambda i: (i, 0)),
         out_shape=jax.ShapeDtypeStruct((model_width, grads.shape[1]), jnp.bfloat16),
-        compiler_params=pltpu.CompilerParams(vmem_limit_bytes=VMEM_BYTES),
+        compiler_params=pltpu.CompilerParams(vmem_limit_bytes=24 * 1024 * 1024),
         cost_estimate=LITTLE,
         name="weight_grad",
     )(x_mine, x_other, grads)
 
 
-def call(body, outs, args, scratch=(), name=None, in_specs=None):
+def call(body, outs, args, scratch=(), name=None, in_specs=None, rows_keys=0):
     whole = pl.BlockSpec(memory_space=pltpu.VMEM)
+    held = sum(x.size * x.dtype.itemsize for x in args)
+    held += sum(math.prod(shape) * jnp.dtype(dtype).itemsize for shape, dtype in outs)
+    grant = min(VMEM_BYTES, 2 * held + 48 * rows_keys + 8 * 1024 * 1024)
+    if name in ALONE:
+        grant = VMEM_BYTES
     return pl.pallas_call(
         body,
         in_specs=in_specs or [whole] * len(args),
         out_specs=[whole] * len(outs),
         out_shape=[jax.ShapeDtypeStruct(shape, dtype) for shape, dtype in outs],
         scratch_shapes=list(scratch),
-        compiler_params=pltpu.CompilerParams(vmem_limit_bytes=VMEM_BYTES),
+        compiler_params=pltpu.CompilerParams(vmem_limit_bytes=grant),
         cost_estimate=LITTLE,
         name=name,
     )(*args)
@@ -360,16 +376,27 @@
 
 
 def place_body(groups, ctx_ref, *refs):
-    *parts, out = refs
+    *parts, out, sems = refs
     count = len(parts) // groups
     rows = parts[0].shape[0]
     start = 0
+    copies = []
     for group in range(groups):
         cols = parts[group * count].shape[1]
         for k in range(count):
             here = pl.ds(pl.multiple_of((ctx_ref[0] ^ k) * rows, rows), rows)
-            out[here, start : start + cols] = parts[group * count + k][...]
+            copies.append(
+                pltpu.make_async_copy(
+                    parts[group * count + k],
+                    out.at[here, pl.ds(start, cols)],
+                    sems.at[len(copies)],
+                )
+            )
         start += cols
+    for copy in copies:
+        copy.start()
+    for copy in copies:
+        copy.wait()
 
 
 def place_ctx(*groups):
@@ -384,9 +411,10 @@
         functools.partial(place_body, len(groups)),
         [((count * rows, cols), parts[0].dtype)],
         [ctx.astype(jnp.int32).reshape(1), *parts],
-        name="place",
-        in_specs=[pl.BlockSpec(memory_space=pltpu.SMEM)]
-        + [pl.BlockSpec(memory_space=pltpu.VMEM)] * len(parts),
+        [pltpu.SemaphoreType.DMA((len(parts),))],
+        "place",
+        [pl.BlockSpec(memory_space=pltpu.SMEM)]
+        + [pl.BlockSpec(memory_space=pl.ANY)] * len(parts),
     )[0]
 
 
@@ -561,7 +589,8 @@
 
 
 def chip_sum(own, got):
-    return jnp.split(own + got.astype(jnp.float32), lax.axis_size("ctx"), 0)
+    total = (own + got.astype(jnp.float32)).astype(jnp.bfloat16)
+    return jnp.split(total, lax.axis_size("ctx"), 0)
 
 
 def add_tree(parts):
@@ -632,12 +661,34 @@
     gain_one = relative(gain_attn.astype(jnp.float32))[None]
     gain_two = relative(gain_mlp.astype(jnp.float32))[None]
 
+    rms_attn = lax.rsqrt(jnp.mean(input_rows * input_rows, -1, keepdims=True) + EPSILON)
+    normed_attn = (input_rows * rms_attn * gain_one).astype(jnp.bfloat16)
+    qkv_cols = query_cols + 2 * key_cols
+    bias = jnp.concatenate([b_q, b_k, b_v]).astype(jnp.float32)[None]
+    input_half = own_half(input_rows)
     attn_parts = gather_ctx(side_by_side([w_q, w_k, w_v, w_o]))
     gate_up_pieces = unit_pieces([w_gate, w_up])
     down_pieces = unit_pieces([w_down])
     grad_half = own_half(grad_out)
     attn_shard = place_ctx(attn_parts)
-    attn_shard, gate_up_pieces, down_pieces = together(attn_shard, gate_up_pieces, down_pieces)
+    attn_shard, gate_up_pieces, down_pieces, tables = together(
+        attn_shard,
+        gate_up_pieces,
+        down_pieces,
+        (
+            normed_attn,
+            bias,
+            cosines,
+            signed_sines,
+            query_positions,
+            key_positions,
+            input_half,
+            grad_half,
+            gain_two,
+        ),
+    )
+    normed_attn, bias, cosines, signed_sines, query_positions, key_positions = tables[:6]
+    input_half, grad_half, gain_two = tables[6:]
 
     attn_near = near_seq(attn_shard)
     gate_up_parts = exchange_ctx(gate_up_pieces)
@@ -649,10 +700,6 @@
     attn_far, up_shard = together(attn_far, up_shard)
     up_near = near_seq(up_shard)
 
-    rms_attn = lax.rsqrt(jnp.mean(input_rows * input_rows, -1, keepdims=True) + EPSILON)
-    normed_attn = (input_rows * rms_attn * gain_one).astype(jnp.bfloat16)
-    qkv_cols = query_cols + 2 * key_cols
-    bias = jnp.concatenate([b_q, b_k, b_v]).astype(jnp.float32)[None]
     query, key_value, w_qkv, w_out = call(
         functools.partial(project_body, query_cols, key_cols),
         [
@@ -685,8 +732,8 @@
         [pltpu.VMEM((span_rows, model_width), jnp.float32)],
         "attend",
         [scalar] + [whole] * (4 + ctx_size),
-    )
-    input_half = own_half(input_rows)
+        span_rows * key_positions.size,
+    )
     hidden, rms_mlp, normed_half = call(
         norm_body,
         [half_f32, ((half_rows, 1), jnp.float32), half_bf16],
@@ -715,6 +762,7 @@
         [],
         [(model_width, 2 * width)],
         "gate_up",
+        26,
     )
     grad_parts, gate_up = together(gather_ctx(grad_half), gate_up)
     grad_mine = jnp.concatenate(grad_parts, 0)
@@ -729,27 +777,31 @@
         [model_width, model_width],
         [(model_width, 2 * width), (model_width, width)],
         "mlp_back",
+        42,
     )
     back_got = swap(back_send, "wt", 1)
     out_got = swap(out_send, "wt", 1)
     g_down = weight_grad(grad_mine, grad_other, act)
-    g_normed_pieces = narrow_others(chip_sum(back_mine, back_got))
-    g_normed_pieces, g_down, out_got = together(g_normed_pieces, g_down, out_got)
+    g_normed_pieces = chip_sum(back_mine, back_got)
+    g_normed_pieces, g_down, out_got, g_both = together(
+        g_normed_pieces, g_down, out_got, g_both
+    )
 
     g_normed_parts = exchange_ctx(g_normed_pieces)
     down_got = scatter_near(g_down)
-    down_got, g_both = together(down_got, g_both)
     g_gate_up = weight_grad(normed_mine, normed_other, g_both)
+    down_got, g_gate_up = together(down_got, g_gate_up)
+    gate_up_payload = near_payload(g_gate_up)
     mlp_pieces = chip_sum(out_mine, out_got)
     down_sum = scatter_far(g_down, *down_got).astype(jnp.bfloat16)
-    g_normed_parts, down_sum, g_gate_up, mlp_pieces = together(
-        g_normed_parts, down_sum, g_gate_up, mlp_pieces
+    g_normed_parts, down_sum, gate_up_payload, mlp_pieces = together(
+        g_normed_parts, down_sum, gate_up_payload, mlp_pieces
     )
 
     down_back = lax.all_to_all(
         down_sum.reshape(ctx_size, -1, down_sum.shape[1]), "ctx", 0, 0, tiled=True
     )
-    gate_up_got = scatter_near(g_gate_up)
+    gate_up_got = near_swap(gate_up_payload)
     grad_gain_mlp, branch_mine, g_hidden = call(
         functools.partial(norm_back_body, ctx_size),
         [row_f32, half_bf16, half_f32],
@@ -782,13 +834,14 @@
         [pltpu.VMEM((span_rows, model_width), jnp.bfloat16)],
         "attend_back",
         [scalar] + [whole] * (10 + ctx_size),
+        span_rows * key_positions.size,
     )
     g_blocks, down_back = together(g_blocks, down_back)
     g_key_value_parts, gate_up_got, mlp_pieces = together(
         exchange_ctx(g_blocks), gate_up_got, mlp_pieces
     )
 
-    mlp_parts = exchange_ctx(narrow_others(mlp_pieces))
+    mlp_parts = exchange_ctx(mlp_pieces)
     on_x, on_y = relay(g_gate_up, *gate_up_got)
     last_x, last_y, g_out = together(swap(on_x, "seq", 1), swap(on_y, "seq", 2), g_out)
     out_got = scatter_near(g_out)

time: 494 us -> 468 us (0.947)
  the two profiles are of different devices: /device:TPU:13 before, /device:TPU:0 now
where the time goes in v5:
time: 468 us; the launch traced here: 459 us
  waiting for transfers between devices  179 us (38%)
  starting transfers between devices  94.4 us (20%)
  Pallas kernels  81.4 us (17%)
  local copies, waits for them, and re-layouts  57.6 us (12%)
  other arithmetic  39.1 us (8%)
  between operations  7.47 us (2%)
    ppermute x64, waiting for transfers between devices, swap(): return lax.ppermute(values, axis, [(i, i ^ offset) for i in range(size)])  171 us
    ppermute x64, starting transfers between devices, swap(): return lax.ppermute(values, axis, [(i, i ^ offset) for i in range(size)])  81.9 us
    pallas_call x2, Pallas kernels, by_tiles(): pl.pallas_call(functools.partial(body, tiles_each), grid=(2 * tiles_each,...  34.6 us
    pallas_call x12, Pallas kernels, call(): pl.pallas_call(body, in_specs=in_specs or [whole] * len(args), out_specs=...  33.1 us
    unnamed x205, local copies, waits for them, and re-layouts  30.7 us
    pallas_call x2, Pallas kernels, weight_grad(): pl.pallas_call(weight_tile, grid=(4,), in_specs=[columns, columns, pl.Blo...  13.8 us
  transfers between devices with their start and end apart: 66, of which 31 were waited for; matrix products, arithmetic and copies ran while one was open for 13% of the time, Pallas kernels for 12%

profile of v5, /device:TPU:0, one launch (start us, length us, event | category | flops | bytes accessed | tf_op | source)
XLA Modules:
  0.0 459.3 jit_solution(1667905896570433944)
XLA Ops:
  4.0 3.1 collective-permute-start
  7.1 2.6 collective-permute-start.1
  16.3 2.5 dynamic-slice_bitcast_fusion
  21.4 2.3 pad_dynamic-slice_fusion.12
  30.9 2.8 collective-permute-done.1.refs_2_
  34.4 1.6 collective-permute-start.3
  36.0 1.5 collective-permute-start.4
  37.5 6.5 %collective-permute-start.5 = (bf16[96,2304]{1,0:T(8,128)(2,1)S(1)}, bf16[96,2304]{1,0:T(8,128)(2,1)S(1)}, u32[]{:S(2)}, u32[]{:S(2)}) collective-permute-start(bf16[96,2304]{1,0:T(8,128)(2,1)S(1)} %copy-done.75), channel_id=1, source_target_pairs={{0,2},{2,0},{4,6},{6,4},{1,3},{3,1},{5,7},{7,5},{8,10},{10,8},{12,... | collective-permute-start | bytes 1327112 | tf_op jit(solution)/shard_map/ppermute | solution.py:46
  46.5 13.8 %collective-permute-done.5 = bf16[96,2304]{1,0:T(8,128)(2,1)S(1)} collective-permute-done((bf16[96,2304]{1,0:T(8,128)(2,1)S(1)}, bf16[96,2304]{1,0:T(8,128)(2,1)S(1)}, u32[]{:S(2)}, u32[]{:S(2)}) %collective-permute-start.5) | collective-permute-done | bytes 442400 | tf_op jit(solution)/shard_map/ppermute | solution.py:46
  60.3 16.7 %collective-permute-done.6 = bf16[96,2304]{1,0:T(8,128)(2,1)S(1)} collective-permute-done((bf16[96,2304]{1,0:T(8,128)(2,1)S(1)}, bf16[96,2304]{1,0:T(8,128)(2,1)S(1)}, u32[]{:S(2)}, u32[]{:S(2)}) %collective-permute-start.6) | collective-permute-done | bytes 442400 | tf_op jit(solution)/shard_map/ppermute | solution.py:46
  80.5 6.9 %collective-permute-start.10 = (bf16[96,1152]{1,0:T(8,128)(2,1)S(1)}, bf16[96,1152]{1,0:T(8,128)(2,1)S(1)}, u32[]{:S(2)}, u32[]{:S(2)}) collective-permute-start(bf16[96,1152]{1,0:T(8,128)(2,1)S(1)} %copy-done.84), channel_id=1, source_target_pairs={{0,2},{2,0},{4,6},{6,4},{1,3},{3,1},{5,7},{7,5},{8,10},{10,8},{12,... | collective-permute-start | bytes 663560 | tf_op jit(solution)/shard_map/ppermute | solution.py:46
  91.8 2.3 project.1
  94.1 1.6 copy-done.10
  97.2 6.4 %collective-permute-done.11.refs_6_ = bf16[96,1152]{1,0:T(8,128)(2,1)S(1)} collective-permute-done((bf16[96,1152]{1,0:T(8,128)(2,1)S(1)}, bf16[96,1152]{1,0:T(8,128)(2,1)S(1)}, u32[]{:S(2)}, u32[]{:S(2)}) %collective-permute-start.11) | collective-permute-done | bytes 221216 | tf_op jit(solution)/shard_map/ppermute | solution.py:46
  104.9 2.3 collective-permute-start.13
  111.2 1.5 collective-permute-start.18
  121.4 5.9 %attend.1 = (bf16[256,768]{1,0:T(8,128)(2,1)S(1)}, f32[256,768]{1,0:T(8,128)S(1)}, f32[128,1536]{1,0:T(8,128)S(1)}, f32[128,1536]{1,0:T(8,128)S(1)}) custom-call(s32[1]{0:T(128)} %bitcast.core_ref, bf16[256,768]{1,0:T(8,128)(2,1)S(1)} %copy-done.17, s32[256,1]{1,0:T(8,128)S(1)} %copy.30.query_pos, s32[1,1024]{1,0:T(1,128)S(1)} %bitcast.74, ...), custom_call_target="tpu_custom_call" | custom-call | flops 1 | bytes 1 | tf_op jit(solution)/shard_map/attend/pallas_call | solution.py:351
  127.5 2.3 collective-permute-done.16.got
  130.8 1.5 collective-permute-start.23
  132.9 2.4 collective-permute-start.20
  136.7 12.3 %collective-permute-done.19 = bf16[128,1536]{1,0:T(8,128)(2,1)S(1)} collective-permute-done((bf16[128,1536]{1,0:T(8,128)(2,1)S(1)}, bf16[128,1536]{1,0:T(8,128)(2,1)S(1)}, u32[]{:S(2)}, u32[]{:S(2)}) %collective-permute-start.19) | collective-permute-done | bytes 393248 | tf_op jit(solution)/shard_map/ppermute | solution.py:46
  149.0 13.7 %collective-permute-done.20 = bf16[128,1536]{1,0:T(8,128)(2,1)S(1)} collective-permute-done((bf16[128,1536]{1,0:T(8,128)(2,1)S(1)}, bf16[128,1536]{1,0:T(8,128)(2,1)S(1)}, u32[]{:S(2)}, u32[]{:S(2)}) %collective-permute-start.20) | collective-permute-done | bytes 393248 | tf_op jit(solution)/shard_map/ppermute | solution.py:46
  162.7 8.1 %collective-permute-done.22.refs_4_ = bf16[384,2304]{1,0:T(8,128)(2,1)S(1)} collective-permute-done((bf16[384,2304]{1,0:T(8,128)(2,1)S(1)}, bf16[384,2304]{1,0:T(8,128)(2,1)S(1)}, u32[]{:S(2)}, u32[]{:S(2)}) %collective-permute-start.22) | collective-permute-done | bytes 1769504 | tf_op jit(solution)/shard_map/ppermute | solution.py:46
  172.7 1.6 collective-permute-start.28
  177.0 2.0 collective-permute-start.26
  180.4 23.6 %collective-permute-done.28.refs_6_ = bf16[192,3456]{1,0:T(8,128)(2,1)S(1)} collective-permute-done((bf16[192,3456]{1,0:T(8,128)(2,1)S(1)}, bf16[192,3456]{1,0:T(8,128)(2,1)S(1)}, u32[]{:S(2)}, u32[]{:S(2)}) %collective-permute-start.28) | collective-permute-done | bytes 1327136 | tf_op jit(solution)/shard_map/ppermute | solution.py:46
  204.0 2.4 collective-permute-done.29.refs_7_
  206.4 10.0 %gate_up.1 = f32[1024,2304]{1,0:T(8,128)S(1)} custom-call(bf16[512,1536]{1,0:T(8,128)(2,1)S(1)} %constant_dynamic-update-slice_fusion.1.x_mine, bf16[512,1536]{1,0:T(8,128)(2,1)S(1)} %collective-permute-done.24.x_other, bf16[384,1152]{1,0:T(8,128)(2,1)S(1)} %place.4.refs_0_, bf16[384,1152]{1,0:T(8,128)(2,1)} %collective-permute-done.17.refs_1_, ...), custom_call_target="tpu_custom_call" | custom-call | flops 1 | bytes 1 | tf_op jit(solution)/shard_map/gate_up/pallas_call | solution.py:299
  216.4 3.6 copy-done
  220.2 3.4 collective-permute-done.30.o_other.x_other
  223.6 24.6 %mlp_back.1 = (bf16[1024,2304]{1,0:T(8,128)(2,1)}, bf16[1024,1152]{1,0:T(8,128)(2,1)}, f32[512,1536]{1,0:T(8,128)}, bf16[512,1536]{1,0:T(8,128)(2,1)S(1)}, f32[5...) custom-call(f32[1024,2304]{1,0:T(8,128)} %copy-done, ...), custom_call_target="tpu_custom_call" | custom-call | flops 1 | bytes 1 | tf_op jit(solution)/shard_map/mlp_back/pallas_call | solution.py:299
  248.8 1.7 copy-done.13
  250.5 5.2 %weight_grad.2 = bf16[1536,1152]{1,0:T(8,128)(2,1)S(1)} custom-call(bf16[512,1536]{1,0:T(8,128)(2,1)S(1)} %constant_dynamic-update-slice_fusion.5.o_mine.x_mine, bf16[512,1536]{1,0:T(8,128)(2,1)S(1)} %collective-permute-done.30.o_other.x_other, bf16[1024,1152]{1,0:T(8,128)(2,1)S(1)} %copy-done.13), custom_call_target="tpu_custom_call" | custom-call | flops 1 | bytes 1 | tf_op jit(solution)/shard_map/weight_grad/pallas_call | solution.py:332
  258.1 2.0 collective-permute-start.34
  262.9 8.5 %weight_grad.3 = bf16[1536,2304]{1,0:T(8,128)(2,1)S(1)} custom-call(bf16[512,1536]{1,0:T(8,128)(2,1)S(1)} %constant_dynamic-update-slice_fusion.1.x_mine, bf16[512,1536]{1,0:T(8,128)(2,1)S(1)} %collective-permute-done.24.x_other, bf16[1024,2304]{1,0:T(8,128)(2,1)S(1)} %bitcast.73), custom_call_target="tpu_custom_call" | custom-call | flops 1 | bytes 1 | tf_op jit(solution)/shard_map/weight_grad/pallas_call | solution.py:332
  272.1 1.5 fusion.39
  273.6 9.0 %collective-permute-done.36 = bf16[384,1152]{1,0:T(8,128)(2,1)S(1)} collective-permute-done((bf16[384,1152]{1,0:T(8,128)(2,1)S(1)}, bf16[384,1152]{1,0:T(8,128)(2,1)S(1)}, u32[]{:S(2)}, u32[]{:S(2)}) %collective-permute-start.36) | collective-permute-done | bytes 884768 | tf_op jit(solution)/shard_map/ppermute | solution.py:46
  283.2 1.6 collective-permute-start.38
  287.0 6.5 %collective-permute-done.38 = bf16[192,1152]{1,0:T(8,128)(2,1)S(1)} collective-permute-done((bf16[192,1152]{1,0:T(8,128)(2,1)S(1)}, bf16[192,1152]{1,0:T(8,128)(2,1)S(1)}, u32[]{:S(2)}, u32[]{:S(2)}) %collective-permute-start.38) | collective-permute-done | bytes 442400 | tf_op jit(solution)/shard_map/ppermute | solution.py:46
  297.2 4.0 all-to-all-start
  301.3 3.4 mlp_norm_back.1
  304.6 1.9 collective-permute-done.40.branch_other
  307.3 11.8 %attend_back.1 = (bf16[256,768]{1,0:T(8,128)(2,1)}, bf16[1536,768]{1,0:T(8,128)(2,1)}, f32[256,256]{1,0:T(8,128)}, bf16[256,256]{1,0:T(8,128)(2,1)}, bf16[256,256]{1,0:T(8,128)(2,1)}, /*index=5*/bf16[256,256]{1,0:T(8,128)(2,1)}) custom-call(s32[1]{0:T(128)} %bitcast.core_ref, bf16[128,1536]{1,0:T(8,128)(2,1)} %get-tuple-element.263.branch_mine, ...), custom_call_target="tpu_custom_call" | custom-call | flops 1 | bytes 1 | tf_op jit(solution)/shard_map/attend_back/pallas_call | solution.py:351
  321.3 2.4 collective-permute-start.42
  324.6 2.7 collective-permute-done.41.refs_1_
  327.3 7.1 %collective-permute-done.42.refs_2_ = bf16[256,256]{1,0:T(8,128)(2,1)S(1)} collective-permute-done((bf16[256,256]{1,0:T(8,128)(2,1)}, bf16[256,256]{1,0:T(8,128)(2,1)S(1)}, u32[]{:S(2)}, u32[]{:S(2)}) %collective-permute-start.42) | collective-permute-done | bytes 131104 | tf_op jit(solution)/shard_map/ppermute | solution.py:46
  334.4 3.6 add_convert_fusion.4
  341.9 2.3 collective-permute-start.46
  346.6 5.1 %project_back.1 = (bf16[256,1024]{1,0:T(8,128)(2,1)}, f32[1,1024]{1,0:T(1,128)}, f32[1,1536]{1,0:T(1,128)}, f32[128,1536]{1,0:T(8,128)}, f32[128,1536]{1,0:T(8,128)}) custom-call(s32[1]{0:T(128)} %bitcast.core_ref, bf16[256,768]{1,0:T(8,128)(2,1)} %get-tuple-element.293.query_lin, bf16[1536,1024]{1,0:T(8,128)(2,1)} %copy-done.10, f32[256,128]{1,0:T(8,128)} %copy-done.14, ...), custom_call_target="tpu_custom_call" | custom-call | flops 1 | bytes 1 | tf_op jit(solution)/shard_map/project_back/pallas_call | solution.py:351
  355.9 2.0 collective-permute-done.49
  361.1 1.6 collective-permute-start.52
  362.7 3.3 add_convert_fusion.3
  367.4 6.9 %collective-permute-done.47 = bf16[128,1536]{1,0:T(8,128)(2,1)} collective-permute-done((bf16[128,1536]{1,0:T(8,128)(2,1)}, bf16[128,1536]{1,0:T(8,128)(2,1)}, u32[]{:S(2)}, u32[]{:S(2)}) %collective-permute-start.47) | collective-permute-done | bytes 393248 | tf_op jit(solution)/shard_map/ppermute | solution.py:46
  378.4 8.4 %all-to-all-start.1 = ((bf16[4,96,2304]{2,1,0:T(8,128)(2,1)}), bf16[4,96,2304]{2,1,0:T(8,128)(2,1)}, u32[]{:S(2)}, u32[]{:S(2)}) async-start(bf16[4,96,2304]{2,1,0:T(8,128)(2,1)} %bitcast.76), calls=%async_computation.1 | async-start | bytes 3538944 | tf_op jit(solution)/shard_map/all_to_all | solution.py:894
  386.8 2.0 constant_dynamic-update-slice_fusion.10
  389.4 1.6 constant_dynamic-update-slice_fusion.9
  394.2 2.5 add_convert_fusion.6
  400.6 12.3 %collective-permute-done.56 = bf16[208,1792]{1,0:T(8,128)(2,1)} collective-permute-done((bf16[208,1792]{1,0:T(8,128)(2,1)S(1)}, bf16[208,1792]{1,0:T(8,128)(2,1)}, u32[]{:S(2)}, u32[]{:S(2)}) %collective-permute-start.56) | collective-permute-done | bytes 745504 | tf_op jit(solution)/shard_map/ppermute | solution.py:46
  413.6 2.4 convert_add_fusion
  418.2 7.6 %all-to-all-done.1 = bf16[4,96,2304]{2,1,0:T(8,128)(2,1)} async-done(((bf16[4,96,2304]{2,1,0:T(8,128)(2,1)}), bf16[4,96,2304]{2,1,0:T(8,128)(2,1)}, u32[]{:S(2)}, u32[]{:S(2)}) %all-to-all-start.1) | async-done | bytes 1769504 | tf_op jit(solution)/shard_map/all_to_all | solution.py:894
  427.9 2.3 collective-permute-start.59
  432.3 1.5 slice_bitcast_fusion.3
  442.4 2.2 collective-permute-done.57
  444.6 10.3 %collective-permute-done.58 = bf16[96,1920]{1,0:T(8,128)(2,1)S(1)} collective-permute-done((bf16[96,1920]{1,0:T(8,128)(2,1)}, bf16[96,1920]{1,0:T(8,128)(2,1)S(1)}, u32[]{:S(2)}, u32[]{:S(2)}) %collective-permute-start.58) | collective-permute-done | bytes 368672 | tf_op jit(solution)/shard_map/ppermute | solution.py:46
  (406 shorter events, 113.0 us)
Async XLA Ops:
  4.0 26.9 %collective-permute-start = (bf16[96,1792]{1,0:T(8,128)(2,1)S(1)}, bf16[96,1792]{1,0:T(8,128)(2,1)S(1)}, u32[]{:S(2)}, u32[]{:S(2)}) collective-permute-start(bf16[96,1792]{1,0:T(8,128)(2,1)S(1)} %side_by_side.1.refs_0_), channel_id=1, source_target_pairs={{0,2},{2,0},{4,6},{6,4},{1,3},{3,1},{5,7},{7,5},{8,10},{10,8},{12,... | collective-permute-start | bytes 1032200 | tf_op jit(solution)/shard_map/ppermute | solution.py:46
  7.1 26.6 %collective-permute-start.1 = (bf16[96,1792]{1,0:T(8,128)(2,1)S(1)}, bf16[96,1792]{1,0:T(8,128)(2,1)S(1)}, u32[]{:S(2)}, u32[]{:S(2)}) collective-permute-start(bf16[96,1792]{1,0:T(8,128)(2,1)S(1)} %side_by_side.1.refs_0_), channel_id=1, source_target_pairs={{0,4},{2,6},{4,0},{6,2},{1,5},{3,7},{5,1},{7,3},{8,12},{10,14},{12... | collective-permute-start | bytes 1032200 | tf_op jit(solution)/shard_map/ppermute | solution.py:46
  9.7 24.0 %collective-permute-start.2 = (bf16[96,1792]{1,0:T(8,128)(2,1)S(1)}, bf16[96,1792]{1,0:T(8,128)(2,1)S(1)}, u32[]{:S(2)}, u32[]{:S(2)}) collective-permute-start(bf16[96,1792]{1,0:T(8,128)(2,1)S(1)} %side_by_side.1.refs_0_), channel_id=1, source_target_pairs={{0,6},{2,4},{4,2},{6,0},{1,7},{3,5},{5,3},{7,1},{8,14},{10,12},{12... | collective-permute-start | bytes 1032200 | tf_op jit(solution)/shard_map/ppermute | solution.py:46
  34.4 42.6 %collective-permute-start.3 = (bf16[384,1792]{1,0:T(8,128)(2,1)S(1)}, bf16[384,1792]{1,0:T(8,128)(2,1)S(1)}, u32[]{:S(2)}, u32[]{:S(2)}) collective-permute-start(bf16[384,1792]{1,0:T(8,128)(2,1)S(1)} %place.3.refs_0_), channel_id=1, source_target_pairs={{0,8},{8,0},{16,24},{24,16},{1,9},{9,1},{17,25},{25,17},{2,10},{10... | collective-permute-start | bytes 4128776 | tf_op jit(solution)/shard_map/ppermute | solution.py:46
  36.0 41.0 %collective-permute-start.4 = (bf16[384,1792]{1,0:T(8,128)(2,1)S(1)}, bf16[384,1792]{1,0:T(8,128)(2,1)S(1)}, u32[]{:S(2)}, u32[]{:S(2)}) collective-permute-start(bf16[384,1792]{1,0:T(8,128)(2,1)S(1)} %place.3.refs_0_), channel_id=1, source_target_pairs={{0,16},{8,24},{16,0},{24,8},{1,17},{9,25},{17,1},{25,9},{2,18},{10... | collective-permute-start | bytes 4128776 | tf_op jit(solution)/shard_map/ppermute | solution.py:46
  37.5 22.8 %collective-permute-start.5 = (bf16[96,2304]{1,0:T(8,128)(2,1)S(1)}, bf16[96,2304]{1,0:T(8,128)(2,1)S(1)}, u32[]{:S(2)}, u32[]{:S(2)}) collective-permute-start(bf16[96,2304]{1,0:T(8,128)(2,1)S(1)} %copy-done.75), channel_id=1, source_target_pairs={{0,2},{2,0},{4,6},{6,4},{1,3},{3,1},{5,7},{7,5},{8,10},{10,8},{12,... | collective-permute-start | bytes 1327112 | tf_op jit(solution)/shard_map/ppermute | solution.py:46
  44.0 33.0 %collective-permute-start.6 = (bf16[96,2304]{1,0:T(8,128)(2,1)S(1)}, bf16[96,2304]{1,0:T(8,128)(2,1)S(1)}, u32[]{:S(2)}, u32[]{:S(2)}) collective-permute-start(bf16[96,2304]{1,0:T(8,128)(2,1)S(1)} %copy-done.74), channel_id=1, source_target_pairs={{0,4},{2,6},{4,0},{6,2},{1,5},{3,7},{5,1},{7,3},{8,12},{10,14},{12... | collective-permute-start | bytes 1327112 | tf_op jit(solution)/shard_map/ppermute | solution.py:46
  45.1 31.9 %collective-permute-start.7 = (bf16[96,2304]{1,0:T(8,128)(2,1)S(1)}, bf16[96,2304]{1,0:T(8,128)(2,1)S(1)}, u32[]{:S(2)}, u32[]{:S(2)}) collective-permute-start(bf16[96,2304]{1,0:T(8,128)(2,1)S(1)} %pad_maximum_fusion.28), channel_id=1, source_target_pairs={{0,6},{2,4},{4,2},{6,0},{1,7},{3,5},{5,3},{7,1},{8,14},{10,12},{12... | collective-permute-start | bytes 1327112 | tf_op jit(solution)/shard_map/ppermute | solution.py:46
  77.0 14.7 %collective-permute-start.8 = (bf16[192,1792]{1,0:T(8,128)(2,1)S(1)}, bf16[192,1792]{1,0:T(8,128)(2,1)S(1)}, u32[]{:S(2)}, u32[]{:S(2)}) collective-permute-start(bf16[192,1792]{1,0:T(8,128)(2,1)S(1)} %slice.311), channel_id=1, source_target_pairs={{0,8},{8,0},{16,24},{24,16},{1,9},{9,1},{17,25},{25,17},{2,10},{10... | collective-permute-start | bytes 2064392 | tf_op jit(solution)/shard_map/ppermute | solution.py:46
  77.7 14.1 %collective-permute-start.9 = (bf16[192,1792]{1,0:T(8,128)(2,1)S(1)}, bf16[192,1792]{1,0:T(8,128)(2,1)S(1)}, u32[]{:S(2)}, u32[]{:S(2)}) collective-permute-start(bf16[192,1792]{1,0:T(8,128)(2,1)S(1)} %slice.312), channel_id=1, source_target_pairs={{0,16},{8,24},{16,0},{24,8},{1,17},{9,25},{17,1},{25,9},{2,18},{10... | collective-permute-start | bytes 2064392 | tf_op jit(solution)/shard_map/ppermute | solution.py:46
  80.5 16.0 %collective-permute-start.10 = (bf16[96,1152]{1,0:T(8,128)(2,1)S(1)}, bf16[96,1152]{1,0:T(8,128)(2,1)S(1)}, u32[]{:S(2)}, u32[]{:S(2)}) collective-permute-start(bf16[96,1152]{1,0:T(8,128)(2,1)S(1)} %copy-done.84), channel_id=1, source_target_pairs={{0,2},{2,0},{4,6},{6,4},{1,3},{3,1},{5,7},{7,5},{8,10},{10,8},{12,... | collective-permute-start | bytes 663560 | tf_op jit(solution)/shard_map/ppermute | solution.py:46
  87.4 16.2 %collective-permute-start.11 = (bf16[96,1152]{1,0:T(8,128)(2,1)S(1)}, bf16[96,1152]{1,0:T(8,128)(2,1)S(1)}, u32[]{:S(2)}, u32[]{:S(2)}) collective-permute-start(bf16[96,1152]{1,0:T(8,128)(2,1)S(1)} %copy-done.83), channel_id=1, source_target_pairs={{0,4},{2,6},{4,0},{6,2},{1,5},{3,7},{5,1},{7,3},{8,12},{10,14},{12... | collective-permute-start | bytes 663560 | tf_op jit(solution)/shard_map/ppermute | solution.py:46
  88.4 15.8 %collective-permute-start.12 = (bf16[96,1152]{1,0:T(8,128)(2,1)S(1)}, bf16[96,1152]{1,0:T(8,128)(2,1)S(1)}, u32[]{:S(2)}, u32[]{:S(2)}) collective-permute-start(bf16[96,1152]{1,0:T(8,128)(2,1)S(1)} %copy-done.82), channel_id=1, source_target_pairs={{0,6},{2,4},{4,2},{6,0},{1,7},{3,5},{5,3},{7,1},{8,14},{10,12},{12... | collective-permute-start | bytes 663560 | tf_op jit(solution)/shard_map/ppermute | solution.py:46
  104.9 15.8 %collective-permute-start.13 = (bf16[256,256]{1,0:T(8,128)(2,1)}, bf16[256,256]{1,0:T(8,128)(2,1)S(1)}, u32[]{:S(2)}, u32[]{:S(2)}) collective-permute-start(bf16[256,256]{1,0:T(8,128)(2,1)} %get-tuple-element.209.refs_0_), channel_id=1, source_target_pairs={{0,2},{2,0},{4,6},{6,4},{1,3},{3,1},{5,7},{7,5},{8,10},{10,8},{12,... | collective-permute-start | bytes 393224 | tf_op jit(solution)/shard_map/ppermute | solution.py:46
  107.2 13.5 %collective-permute-start.14 = (bf16[256,256]{1,0:T(8,128)(2,1)}, bf16[256,256]{1,0:T(8,128)(2,1)}, u32[]{:S(2)}, u32[]{:S(2)}) collective-permute-start(bf16[256,256]{1,0:T(8,128)(2,1)} %get-tuple-element.209.refs_0_), channel_id=1, source_target_pairs={{0,4},{2,6},{4,0},{6,2},{1,5},{3,7},{5,1},{7,3},{8,12},{10,14},{12... | collective-permute-start | bytes 393224 | tf_op jit(solution)/shard_map/ppermute | solution.py:46
  108.3 12.5 %collective-permute-start.15 = (bf16[256,256]{1,0:T(8,128)(2,1)}, bf16[256,256]{1,0:T(8,128)(2,1)}, u32[]{:S(2)}, u32[]{:S(2)}) collective-permute-start(bf16[256,256]{1,0:T(8,128)(2,1)} %get-tuple-element.209.refs_0_), channel_id=1, source_target_pairs={{0,6},{2,4},{4,2},{6,0},{1,7},{3,5},{5,3},{7,1},{8,14},{10,12},{12... | collective-permute-start | bytes 393224 | tf_op jit(solution)/shard_map/ppermute | solution.py:46
  109.7 20.3 %collective-permute-start.17 = (bf16[384,1152]{1,0:T(8,128)(2,1)S(1)}, bf16[384,1152]{1,0:T(8,128)(2,1)}, u32[]{:S(2)}, u32[]{:S(2)}) collective-permute-start(bf16[384,1152]{1,0:T(8,128)(2,1)S(1)} %place.4.refs_0_), channel_id=1, source_target_pairs={{0,8},{8,0},{16,24},{24,16},{1,9},{9,1},{17,25},{25,17},{2,10},{10... | collective-permute-start | bytes 2654216 | tf_op jit(solution)/shard_map/ppermute | solution.py:46
  111.2 19.0 %collective-permute-start.18 = (bf16[384,1152]{1,0:T(8,128)(2,1)S(1)}, bf16[384,1152]{1,0:T(8,128)(2,1)}, u32[]{:S(2)}, u32[]{:S(2)}) collective-permute-start(bf16[384,1152]{1,0:T(8,128)(2,1)S(1)} %place.4.refs_0_), channel_id=1, source_target_pairs={{0,16},{8,24},{16,0},{24,8},{1,17},{9,25},{17,1},{25,9},{2,18},{10... | collective-permute-start | bytes 2654216 | tf_op jit(solution)/shard_map/ppermute | solution.py:46
  127.4 2.4 collective-permute-start.16
  130.2 40.5 %collective-permute-start.22 = (bf16[384,2304]{1,0:T(8,128)(2,1)S(1)}, bf16[384,2304]{1,0:T(8,128)(2,1)S(1)}, u32[]{:S(2)}, u32[]{:S(2)}) collective-permute-start(bf16[384,2304]{1,0:T(8,128)(2,1)S(1)} %place.5.refs_3_), channel_id=1, source_target_pairs={{0,8},{8,0},{16,24},{24,16},{1,9},{9,1},{17,25},{25,17},{2,10},{10... | collective-permute-start | bytes 5308424 | tf_op jit(solution)/shard_map/ppermute | solution.py:46
  130.8 40.2 %collective-permute-start.23 = (bf16[384,2304]{1,0:T(8,128)(2,1)S(1)}, bf16[384,2304]{1,0:T(8,128)(2,1)S(1)}, u32[]{:S(2)}, u32[]{:S(2)}) collective-permute-start(bf16[384,2304]{1,0:T(8,128)(2,1)S(1)} %place.5.refs_3_), channel_id=1, source_target_pairs={{0,16},{8,24},{16,0},{24,8},{1,17},{9,25},{17,1},{25,9},{2,18},{10... | collective-permute-start | bytes 5308424 | tf_op jit(solution)/shard_map/ppermute | solution.py:46
  132.3 16.7 %collective-permute-start.19 = (bf16[128,1536]{1,0:T(8,128)(2,1)S(1)}, bf16[128,1536]{1,0:T(8,128)(2,1)S(1)}, u32[]{:S(2)}, u32[]{:S(2)}) collective-permute-start(bf16[128,1536]{1,0:T(8,128)(2,1)S(1)} %get-tuple-element.223), channel_id=1, source_target_pairs={{0,2},{2,0},{4,6},{6,4},{1,3},{3,1},{5,7},{7,5},{8,10},{10,8},{12,... | collective-permute-start | bytes 1179656 | tf_op jit(solution)/shard_map/ppermute | solution.py:46
  132.9 29.8 %collective-permute-start.20 = (bf16[128,1536]{1,0:T(8,128)(2,1)S(1)}, bf16[128,1536]{1,0:T(8,128)(2,1)S(1)}, u32[]{:S(2)}, u32[]{:S(2)}) collective-permute-start(bf16[128,1536]{1,0:T(8,128)(2,1)S(1)} %get-tuple-element.223), channel_id=1, source_target_pairs={{0,4},{2,6},{4,0},{6,2},{1,5},{3,7},{5,1},{7,3},{8,12},{10,14},{12... | collective-permute-start | bytes 1179656 | tf_op jit(solution)/shard_map/ppermute | solution.py:46
  135.2 27.4 %collective-permute-start.21 = (bf16[128,1536]{1,0:T(8,128)(2,1)S(1)}, bf16[128,1536]{1,0:T(8,128)(2,1)S(1)}, u32[]{:S(2)}, u32[]{:S(2)}) collective-permute-start(bf16[128,1536]{1,0:T(8,128)(2,1)S(1)} %get-tuple-element.223), channel_id=1, source_target_pairs={{0,6},{2,4},{4,2},{6,0},{1,7},{3,5},{5,3},{7,1},{8,14},{10,12},{12... | collective-permute-start | bytes 1179656 | tf_op jit(solution)/shard_map/ppermute | solution.py:46
  171.2 4.8 %collective-permute-start.24 = (bf16[512,1536]{1,0:T(8,128)(2,1)S(1)}, bf16[512,1536]{1,0:T(8,128)(2,1)S(1)}, u32[]{:S(2)}, u32[]{:S(2)}) collective-permute-start(bf16[512,1536]{1,0:T(8,128)(2,1)S(1)} %constant_dynamic-update-slice_fusion.1.x_mine), channel_id=1, source_target_pairs={{0,1},{1,0},{2,3},{3,2},{4,5},{5,4},{6,7},{7,6},{8,9},{9,8},{10,11... | collective-permute-start | bytes 4718600 | tf_op jit(solution)/shard_map/ppermute | solution.py:46
  172.7 31.3 %collective-permute-start.28 = (bf16[192,3456]{1,0:T(8,128)(2,1)S(1)}, bf16[192,3456]{1,0:T(8,128)(2,1)S(1)}, u32[]{:S(2)}, u32[]{:S(2)}) collective-permute-start(bf16[192,3456]{1,0:T(8,128)(2,1)S(1)} %pad_maximum_fusion.4), channel_id=1, source_target_pairs={{0,8},{8,0},{16,24},{24,16},{1,9},{9,1},{17,25},{25,17},{2,10},{10... | collective-permute-start | bytes 3981320 | tf_op jit(solution)/shard_map/ppermute | solution.py:46
  175.4 31.0 %collective-permute-start.29 = (bf16[192,3456]{1,0:T(8,128)(2,1)S(1)}, bf16[192,3456]{1,0:T(8,128)(2,1)S(1)}, u32[]{:S(2)}, u32[]{:S(2)}) collective-permute-start(bf16[192,3456]{1,0:T(8,128)(2,1)S(1)} %pad_maximum_fusion.3), channel_id=1, source_target_pairs={{0,16},{8,24},{16,0},{24,8},{1,17},{9,25},{17,1},{25,9},{2,18},{10... | collective-permute-start | bytes 3981320 | tf_op jit(solution)/shard_map/ppermute | solution.py:46
  176.0 44.0 %collective-permute-start.25 = (bf16[128,1536]{1,0:T(8,128)(2,1)S(1)}, bf16[128,1536]{1,0:T(8,128)(2,1)S(1)}, u32[]{:S(2)}, u32[]{:S(2)}) collective-permute-start(bf16[128,1536]{1,0:T(8,128)(2,1)S(1)} %copy-done.49), channel_id=1, source_target_pairs={{0,2},{2,0},{4,6},{6,4},{1,3},{3,1},{5,7},{7,5},{8,10},{10,8},{12,... | collective-permute-start | bytes 1179656 | tf_op jit(solution)/shard_map/ppermute | solution.py:46
  177.0 43.0 %collective-permute-start.26 = (bf16[128,1536]{1,0:T(8,128)(2,1)S(1)}, bf16[128,1536]{1,0:T(8,128)(2,1)S(1)}, u32[]{:S(2)}, u32[]{:S(2)}) collective-permute-start(bf16[128,1536]{1,0:T(8,128)(2,1)S(1)} %copy-done.49), channel_id=1, source_target_pairs={{0,4},{2,6},{4,0},{6,2},{1,5},{3,7},{5,1},{7,3},{8,12},{10,14},{12... | collective-permute-start | bytes 1179656 | tf_op jit(solution)/shard_map/ppermute | solution.py:46
  178.9 41.1 %collective-permute-start.27 = (bf16[128,1536]{1,0:T(8,128)(2,1)S(1)}, bf16[128,1536]{1,0:T(8,128)(2,1)S(1)}, u32[]{:S(2)}, u32[]{:S(2)}) collective-permute-start(bf16[128,1536]{1,0:T(8,128)(2,1)S(1)} %copy-done.49), channel_id=1, source_target_pairs={{0,6},{2,4},{4,2},{6,0},{1,7},{3,5},{5,3},{7,1},{8,14},{10,12},{12... | collective-permute-start | bytes 1179656 | tf_op jit(solution)/shard_map/ppermute | solution.py:46
  220.1 3.5 collective-permute-start.30
  248.2 7.5 %collective-permute-start.31 = (bf16[512,1536]{1,0:T(8,128)(2,1)S(1)}, bf16[512,1536]{1,0:T(8,128)(2,1)S(1)}, u32[]{:S(2)}, u32[]{:S(2)}) collective-permute-start(bf16[512,1536]{1,0:T(8,128)(2,1)S(1)} %get-tuple-element.242), channel_id=1, source_target_pairs={{0,1},{1,0},{2,3},{3,2},{4,5},{5,4},{6,7},{7,6},{8,9},{9,8},{10,11... | collective-permute-start | bytes 4718600 | tf_op jit(solution)/shard_map/ppermute | solution.py:46
  248.4 8.7 %collective-permute-start.32 = (bf16[512,1536]{1,0:T(8,128)(2,1)S(1)}, bf16[512,1536]{1,0:T(8,128)(2,1)S(1)}, u32[]{:S(2)}, u32[]{:S(2)}) collective-permute-start(bf16[512,1536]{1,0:T(8,128)(2,1)S(1)} %get-tuple-element.244), channel_id=1, source_target_pairs={{0,1},{1,0},{2,3},{3,2},{4,5},{5,4},{6,7},{7,6},{8,9},{9,8},{10,11... | collective-permute-start | bytes 4718600 | tf_op jit(solution)/shard_map/ppermute | solution.py:46
  257.1 38.9 %collective-permute-start.33 = (bf16[128,1536]{1,0:T(8,128)(2,1)S(1)}, bf16[128,1536]{1,0:T(8,128)(2,1)S(1)}, u32[]{:S(2)}, u32[]{:S(2)}) collective-permute-start(bf16[128,1536]{1,0:T(8,128)(2,1)S(1)} %get-tuple-element.247), channel_id=1, source_target_pairs={{0,2},{2,0},{4,6},{6,4},{1,3},{3,1},{5,7},{7,5},{8,10},{10,8},{12,... | collective-permute-start | bytes 1179656 | tf_op jit(solution)/shard_map/ppermute | solution.py:46
  258.1 37.9 %collective-permute-start.34 = (bf16[128,1536]{1,0:T(8,128)(2,1)S(1)}, bf16[128,1536]{1,0:T(8,128)(2,1)S(1)}, u32[]{:S(2)}, u32[]{:S(2)}) collective-permute-start(bf16[128,1536]{1,0:T(8,128)(2,1)S(1)} %get-tuple-element.248), channel_id=1, source_target_pairs={{0,4},{2,6},{4,0},{6,2},{1,5},{3,7},{5,1},{7,3},{8,12},{10,14},{12... | collective-permute-start | bytes 1179656 | tf_op jit(solution)/shard_map/ppermute | solution.py:46
  260.0 36.0 %collective-permute-start.35 = (bf16[128,1536]{1,0:T(8,128)(2,1)S(1)}, bf16[128,1536]{1,0:T(8,128)(2,1)S(1)}, u32[]{:S(2)}, u32[]{:S(2)}) collective-permute-start(bf16[128,1536]{1,0:T(8,128)(2,1)S(1)} %get-tuple-element.249), channel_id=1, source_target_pairs={{0,6},{2,4},{4,2},{6,0},{1,7},{3,5},{5,3},{7,1},{8,14},{10,12},{12... | collective-permute-start | bytes 1179656 | tf_op jit(solution)/shard_map/ppermute | solution.py:46
  261.7 20.9 %collective-permute-start.36 = (bf16[384,1152]{1,0:T(8,128)(2,1)S(1)}, bf16[384,1152]{1,0:T(8,128)(2,1)S(1)}, u32[]{:S(2)}, u32[]{:S(2)}) collective-permute-start(bf16[384,1152]{1,0:T(8,128)(2,1)S(1)} %pad_maximum_fusion.5), channel_id=1, source_target_pairs={{0,8},{8,0},{16,24},{24,16},{1,9},{9,1},{17,25},{25,17},{2,10},{10... | collective-permute-start | bytes 2654216 | tf_op jit(solution)/shard_map/ppermute | solution.py:46
  262.4 20.6 %collective-permute-start.37 = (bf16[384,1152]{1,0:T(8,128)(2,1)S(1)}, bf16[384,1152]{1,0:T(8,128)(2,1)S(1)}, u32[]{:S(2)}, u32[]{:S(2)}) collective-permute-start(bf16[384,1152]{1,0:T(8,128)(2,1)S(1)} %pad_maximum_fusion.6), channel_id=1, source_target_pairs={{0,16},{8,24},{16,0},{24,8},{1,17},{9,25},{17,1},{25,9},{2,18},{10... | collective-permute-start | bytes 2654216 | tf_op jit(solution)/shard_map/ppermute | solution.py:46
  283.2 10.2 %collective-permute-start.38 = (bf16[192,1152]{1,0:T(8,128)(2,1)S(1)}, bf16[192,1152]{1,0:T(8,128)(2,1)S(1)}, u32[]{:S(2)}, u32[]{:S(2)}) collective-permute-start(bf16[192,1152]{1,0:T(8,128)(2,1)S(1)} %get-tuple-element.254), channel_id=1, source_target_pairs={{0,8},{8,0},{16,24},{24,16},{1,9},{9,1},{17,25},{25,17},{2,10},{10... | collective-permute-start | bytes 1327112 | tf_op jit(solution)/shard_map/ppermute | solution.py:46
  284.8 9.9 %collective-permute-start.39 = (bf16[192,1152]{1,0:T(8,128)(2,1)S(1)}, bf16[192,1152]{1,0:T(8,128)(2,1)S(1)}, u32[]{:S(2)}, u32[]{:S(2)}) collective-permute-start(bf16[192,1152]{1,0:T(8,128)(2,1)S(1)} %get-tuple-element.255), channel_id=1, source_target_pairs={{0,16},{8,24},{16,0},{24,8},{1,17},{9,25},{17,1},{25,9},{2,18},{10... | collective-permute-start | bytes 1327112 | tf_op jit(solution)/shard_map/ppermute | solution.py:46
  296.0 38.4 %collective-permute-start.44 = (bf16[384,2304]{1,0:T(8,128)(2,1)S(1)}, bf16[384,2304]{1,0:T(8,128)(2,1)}, u32[]{:S(2)}, u32[]{:S(2)}) collective-permute-start(bf16[384,2304]{1,0:T(8,128)(2,1)S(1)} %pad_maximum_fusion), channel_id=1, source_target_pairs={{0,8},{8,0},{16,24},{24,16},{1,9},{9,1},{17,25},{25,17},{2,10},{10... | collective-permute-start | bytes 5308424 | tf_op jit(solution)/shard_map/ppermute | solution.py:46
  296.7 37.7 %collective-permute-start.45 = (bf16[384,2304]{1,0:T(8,128)(2,1)}, bf16[384,2304]{1,0:T(8,128)(2,1)}, u32[]{:S(2)}, u32[]{:S(2)}) collective-permute-start(bf16[384,2304]{1,0:T(8,128)(2,1)} %pad_maximum_fusion.1), channel_id=1, source_target_pairs={{0,16},{8,24},{16,0},{24,8},{1,17},{9,25},{17,1},{25,9},{2,18},{10... | collective-permute-start | bytes 5308424 | tf_op jit(solution)/shard_map/ppermute | solution.py:46
  297.2 23.0 %all-to-all-start = ((bf16[4,96,1152]{2,1,0:T(8,128)(2,1)}), bf16[4,96,1152]{2,1,0:T(8,128)(2,1)S(1)}, u32[]{:S(2)}, u32[]{:S(2)}) async-start(bf16[4,96,1152]{2,1,0:T(8,128)(2,1)} %bitcast.22), calls=%async_computation | async-start | bytes 1769472 | tf_op jit(solution)/shard_map/all_to_all | solution.py:801
  320.2 7.1 %collective-permute-start.41 = (bf16[256,256]{1,0:T(8,128)(2,1)}, bf16[256,256]{1,0:T(8,128)(2,1)S(1)}, u32[]{:S(2)}, u32[]{:S(2)}) collective-permute-start(bf16[256,256]{1,0:T(8,128)(2,1)} %get-tuple-element.272), channel_id=1, source_target_pairs={{0,2},{2,0},{4,6},{6,4},{1,3},{3,1},{5,7},{7,5},{8,10},{10,8},{12,... | collective-permute-start | bytes 393224 | tf_op jit(solution)/shard_map/ppermute | solution.py:46
  321.3 13.1 %collective-permute-start.42 = (bf16[256,256]{1,0:T(8,128)(2,1)}, bf16[256,256]{1,0:T(8,128)(2,1)S(1)}, u32[]{:S(2)}, u32[]{:S(2)}) collective-permute-start(bf16[256,256]{1,0:T(8,128)(2,1)} %get-tuple-element.273), channel_id=1, source_target_pairs={{0,4},{2,6},{4,0},{6,2},{1,5},{3,7},{5,1},{7,3},{8,12},{10,14},{12... | collective-permute-start | bytes 393224 | tf_op jit(solution)/shard_map/ppermute | solution.py:46
  323.6 10.8 %collective-permute-start.43 = (bf16[256,256]{1,0:T(8,128)(2,1)}, bf16[256,256]{1,0:T(8,128)(2,1)S(1)}, u32[]{:S(2)}, u32[]{:S(2)}) collective-permute-start(bf16[256,256]{1,0:T(8,128)(2,1)} %get-tuple-element.274), channel_id=1, source_target_pairs={{0,6},{2,4},{4,2},{6,0},{1,7},{3,5},{5,3},{7,1},{8,14},{10,12},{12... | collective-permute-start | bytes 393224 | tf_op jit(solution)/shard_map/ppermute | solution.py:46
  338.1 19.8 %collective-permute-start.49 = (bf16[192,2304]{1,0:T(8,128)(2,1)}, bf16[192,2304]{1,0:T(8,128)(2,1)}, u32[]{:S(2)}, u32[]{:S(2)}) collective-permute-start(bf16[192,2304]{1,0:T(8,128)(2,1)} %get-tuple-element.287), channel_id=1, source_target_pairs={{0,8},{8,0},{16,24},{24,16},{1,9},{9,1},{17,25},{25,17},{2,10},{10... | collective-permute-start | bytes 2654216 | tf_op jit(solution)/shard_map/ppermute | solution.py:46
  339.5 19.5 %collective-permute-start.50 = (bf16[192,2304]{1,0:T(8,128)(2,1)}, bf16[192,2304]{1,0:T(8,128)(2,1)}, u32[]{:S(2)}, u32[]{:S(2)}) collective-permute-start(bf16[192,2304]{1,0:T(8,128)(2,1)} %get-tuple-element.288), channel_id=1, source_target_pairs={{0,16},{8,24},{16,0},{24,8},{1,17},{9,25},{17,1},{25,9},{2,18},{10... | collective-permute-start | bytes 2654216 | tf_op jit(solution)/shard_map/ppermute | solution.py:46
  341.9 25.5 %collective-permute-start.46 = (bf16[128,1536]{1,0:T(8,128)(2,1)}, bf16[128,1536]{1,0:T(8,128)(2,1)}, u32[]{:S(2)}, u32[]{:S(2)}) collective-permute-start(bf16[128,1536]{1,0:T(8,128)(2,1)} %get-tuple-element.282), channel_id=1, source_target_pairs={{0,2},{2,0},{4,6},{6,4},{1,3},{3,1},{5,7},{7,5},{8,10},{10,8},{12,... | collective-permute-start | bytes 1179656 | tf_op jit(solution)/shard_map/ppermute | solution.py:46
  344.2 30.1 %collective-permute-start.47 = (bf16[128,1536]{1,0:T(8,128)(2,1)}, bf16[128,1536]{1,0:T(8,128)(2,1)}, u32[]{:S(2)}, u32[]{:S(2)}) collective-permute-start(bf16[128,1536]{1,0:T(8,128)(2,1)} %get-tuple-element.283), channel_id=1, source_target_pairs={{0,4},{2,6},{4,0},{6,2},{1,5},{3,7},{5,1},{7,3},{8,12},{10,14},{12... | collective-permute-start | bytes 1179656 | tf_op jit(solution)/shard_map/ppermute | solution.py:46
  345.1 29.2 %collective-permute-start.48 = (bf16[128,1536]{1,0:T(8,128)(2,1)}, bf16[128,1536]{1,0:T(8,128)(2,1)}, u32[]{:S(2)}, u32[]{:S(2)}) collective-permute-start(bf16[128,1536]{1,0:T(8,128)(2,1)} %get-tuple-element.284), channel_id=1, source_target_pairs={{0,6},{2,4},{4,2},{6,0},{1,7},{3,5},{5,3},{7,1},{8,14},{10,12},{12... | collective-permute-start | bytes 1179656 | tf_op jit(solution)/shard_map/ppermute | solution.py:46
  360.3 14.0 %collective-permute-start.51 = (bf16[384,768]{1,0:T(8,128)(2,1)S(1)}, bf16[384,768]{1,0:T(8,128)(2,1)S(1)}, u32[]{:S(2)}, u32[]{:S(2)}) collective-permute-start(bf16[384,768]{1,0:T(8,128)(2,1)S(1)} %pad_maximum_fusion.23), channel_id=1, source_target_pairs={{0,8},{8,0},{16,24},{24,16},{1,9},{9,1},{17,25},{25,17},{2,10},{10... | collective-permute-start | bytes 1769480 | tf_op jit(solution)/shard_map/ppermute | solution.py:46
  361.1 13.2 %collective-permute-start.52 = (bf16[384,768]{1,0:T(8,128)(2,1)S(1)}, bf16[384,768]{1,0:T(8,128)(2,1)S(1)}, u32[]{:S(2)}, u32[]{:S(2)}) collective-permute-start(bf16[384,768]{1,0:T(8,128)(2,1)S(1)} %pad_maximum_fusion.24), channel_id=1, source_target_pairs={{0,16},{8,24},{16,0},{24,8},{1,17},{9,25},{17,1},{25,9},{2,18},{10... | collective-permute-start | bytes 1769480 | tf_op jit(solution)/shard_map/ppermute | solution.py:46
  376.2 14.8 %collective-permute-start.53 = (bf16[384,1024]{1,0:T(8,128)(2,1)}, bf16[384,1024]{1,0:T(8,128)(2,1)}, u32[]{:S(2)}, u32[]{:S(2)}) collective-permute-start(bf16[384,1024]{1,0:T(8,128)(2,1)} %pad_maximum_fusion.18), channel_id=1, source_target_pairs={{0,16},{8,24},{16,0},{24,8},{1,17},{9,25},{17,1},{25,9},{2,18},{10... | collective-permute-start | bytes 2359304 | tf_op jit(solution)/shard_map/ppermute | solution.py:46
  377.7 15.1 %collective-permute-start.54 = (bf16[400,1024]{1,0:T(8,128)(2,1)}, bf16[400,1024]{1,0:T(8,128)(2,1)}, u32[]{:S(2)}, u32[]{:S(2)}) collective-permute-start(bf16[400,1024]{1,0:T(8,128)(2,1)} %pad_maximum_fusion.17), channel_id=1, source_target_pairs={{0,8},{8,0},{16,24},{24,16},{1,9},{9,1},{17,25},{25,17},{2,10},{10... | collective-permute-start | bytes 2457608 | tf_op jit(solution)/shard_map/ppermute | solution.py:46
  378.4 47.4 %all-to-all-start.1 = ((bf16[4,96,2304]{2,1,0:T(8,128)(2,1)}), bf16[4,96,2304]{2,1,0:T(8,128)(2,1)}, u32[]{:S(2)}, u32[]{:S(2)}) async-start(bf16[4,96,2304]{2,1,0:T(8,128)(2,1)} %bitcast.76), calls=%async_computation.1 | async-start | bytes 3538944 | tf_op jit(solution)/shard_map/all_to_all | solution.py:894
  397.6 15.3 %collective-permute-start.56 = (bf16[208,1792]{1,0:T(8,128)(2,1)S(1)}, bf16[208,1792]{1,0:T(8,128)(2,1)}, u32[]{:S(2)}, u32[]{:S(2)}) collective-permute-start(bf16[208,1792]{1,0:T(8,128)(2,1)S(1)} %fusion.4), channel_id=1, source_target_pairs={{0,16},{8,24},{16,0},{24,8},{1,17},{9,25},{17,1},{25,9},{2,18},{10... | collective-permute-start | bytes 2236424 | tf_op jit(solution)/shard_map/ppermute | solution.py:46
  399.0 14.6 %collective-permute-start.55 = (bf16[192,1792]{1,0:T(8,128)(2,1)}, bf16[192,1792]{1,0:T(8,128)(2,1)}, u32[]{:S(2)}, u32[]{:S(2)}) collective-permute-start(bf16[192,1792]{1,0:T(8,128)(2,1)} %get-tuple-element.307), channel_id=1, source_target_pairs={{0,8},{8,0},{16,24},{24,16},{1,9},{9,1},{17,25},{25,17},{2,10},{10... | collective-permute-start | bytes 2064392 | tf_op jit(solution)/shard_map/ppermute | solution.py:46
  425.8 18.8 %collective-permute-start.57 = (bf16[96,1920]{1,0:T(8,128)(2,1)}, bf16[96,1920]{1,0:T(8,128)(2,1)S(1)}, u32[]{:S(2)}, u32[]{:S(2)}) collective-permute-start(bf16[96,1920]{1,0:T(8,128)(2,1)} %get-tuple-element.316), channel_id=1, source_target_pairs={{0,2},{2,0},{4,6},{6,4},{1,3},{3,1},{5,7},{7,5},{8,10},{10,8},{12,... | collective-permute-start | bytes 1105928 | tf_op jit(solution)/shard_map/ppermute | solution.py:46
  426.5 28.4 %collective-permute-start.58 = (bf16[96,1920]{1,0:T(8,128)(2,1)}, bf16[96,1920]{1,0:T(8,128)(2,1)S(1)}, u32[]{:S(2)}, u32[]{:S(2)}) collective-permute-start(bf16[96,1920]{1,0:T(8,128)(2,1)} %get-tuple-element.317), channel_id=1, source_target_pairs={{0,4},{2,6},{4,0},{6,2},{1,5},{3,7},{5,1},{7,3},{8,12},{10,14},{12... | collective-permute-start | bytes 1105928 | tf_op jit(solution)/shard_map/ppermute | solution.py:46
  427.9 27.0 %collective-permute-start.59 = (bf16[96,1920]{1,0:T(8,128)(2,1)}, bf16[96,1920]{1,0:T(8,128)(2,1)S(1)}, u32[]{:S(2)}, u32[]{:S(2)}) collective-permute-start(bf16[96,1920]{1,0:T(8,128)(2,1)} %get-tuple-element.318), channel_id=1, source_target_pairs={{0,6},{2,4},{4,2},{6,0},{1,7},{3,5},{5,3},{7,1},{8,14},{10,12},{12... | collective-permute-start | bytes 1105928 | tf_op jit(solution)/shard_map/ppermute | solution.py:46
  430.2 6.6 %collective-permute-start.60 = (f32[128,1536]{1,0:T(8,128)}, f32[128,1536]{1,0:T(8,128)S(1)}, u32[]{:S(2)}, u32[]{:S(2)}) collective-permute-start(f32[128,1536]{1,0:T(8,128)} %get-tuple-element.321), channel_id=1, source_target_pairs={{0,1},{1,0},{2,3},{3,2},{4,5},{5,4},{6,7},{7,6},{8,9},{9,8},{10,11... | collective-permute-start | bytes 2359304 | tf_op jit(solution)/shard_map/ppermute | solution.py:46
  431.8 8.6 %collective-permute-start.62 = (bf16[128,1536]{1,0:T(8,128)(2,1)S(1)}, bf16[128,1536]{1,0:T(8,128)(2,1)S(1)}, u32[]{:S(2)}, u32[]{:S(2)}) collective-permute-start(bf16[128,1536]{1,0:T(8,128)(2,1)S(1)} %pad_maximum_fusion.30), channel_id=1, source_target_pairs={{0,1},{1,0},{2,3},{3,2},{4,5},{5,4},{6,7},{7,6},{8,9},{9,8},{10,11... | collective-permute-start | bytes 1179656 | tf_op jit(solution)/shard_map/ppermute | solution.py:46
  439.0 2.4 collective-permute-start.61
  (100 other events, 1046.4 us)

commit v6 on v5

--- a/solution.py
+++ b/solution.py
@@ -181,7 +181,7 @@
 
 
 VMEM_BYTES = 56 * 1024 * 1024
-ALONE = ("mlp_norm_back", "attend_back", "project_back",)
+ALONE = ("side_by_side", "mlp_norm_back", "attend_back", "project_back")
 LITTLE = pl.CostEstimate(flops=1, bytes_accessed=1, transcendentals=0)
 
 
@@ -375,47 +375,54 @@
     )[0]
 
 
-def place_body(groups, ctx_ref, *refs):
-    *parts, out, sems = refs
-    count = len(parts) // groups
-    rows = parts[0].shape[0]
-    start = 0
+def place_body(plan, ctx_ref, *refs):
+    count = max(part for part, *_ in plan) + 1
+    parts, outs, sems = refs[:count], refs[count:-1], refs[-1]
     copies = []
-    for group in range(groups):
-        cols = parts[group * count].shape[1]
-        for k in range(count):
-            here = pl.ds(pl.multiple_of((ctx_ref[0] ^ k) * rows, rows), rows)
-            copies.append(
-                pltpu.make_async_copy(
-                    parts[group * count + k],
-                    out.at[here, pl.ds(start, cols)],
-                    sems.at[len(copies)],
-                )
+    for part, k, column, cols, out, start in plan:
+        rows = parts[part].shape[0]
+        first = 0 if k is None else pl.multiple_of((ctx_ref[0] ^ k) * rows, rows)
+        copies.append(
+            pltpu.make_async_copy(
+                parts[part].at[:, pl.ds(column, cols)],
+                outs[out].at[pl.ds(first, rows), pl.ds(start, cols)],
+                sems.at[len(copies)],
             )
-        start += cols
+        )
     for copy in copies:
         copy.start()
     for copy in copies:
         copy.wait()
 
 
-def place_ctx(*groups):
+def place_ctx(parts, spans, beside=None):
     ctx = lax.axis_index("ctx")
-    count, rows = len(groups[0]), groups[0][0].shape[0]
+    count, rows = len(parts), parts[0].shape[0]
     if rows % 16:
         order = [ctx ^ k for k in range(count)]
-        return jnp.concatenate([place_rows(parts, order) for parts in groups], 1)
-    cols = sum(parts[0].shape[1] for parts in groups)
-    parts = [part for group in groups for part in group]
+        placed = [
+            place_rows([part[:, column : column + cols] for part in parts], order)
+            for column, cols in spans
+        ]
+        return placed if beside is None else [jnp.concatenate([beside, placed[0]], 1)]
+    start = 0 if beside is None else beside.shape[1]
+    plan = [
+        (k, k, column, cols, out, start)
+        for out, (column, cols) in enumerate(spans)
+        for k in range(count)
+    ]
+    if beside is not None:
+        plan.append((count, None, 0, start, 0, 0))
+        parts = [*parts, beside]
     return call(
-        functools.partial(place_body, len(groups)),
-        [((count * rows, cols), parts[0].dtype)],
+        functools.partial(place_body, plan),
+        [((count * rows, start + cols), parts[0].dtype) for _, cols in spans],
         [ctx.astype(jnp.int32).reshape(1), *parts],
-        [pltpu.SemaphoreType.DMA((len(parts),))],
+        [pltpu.SemaphoreType.DMA((len(plan),))],
         "place",
         [pl.BlockSpec(memory_space=pltpu.SMEM)]
         + [pl.BlockSpec(memory_space=pl.ANY)] * len(parts),
-    )[0]
+    )
 
 
 def turn(values, cosines, signed_sines):
@@ -670,7 +677,7 @@
     gate_up_pieces = unit_pieces([w_gate, w_up])
     down_pieces = unit_pieces([w_down])
     grad_half = own_half(grad_out)
-    attn_shard = place_ctx(attn_parts)
+    (attn_shard,) = place_ctx(attn_parts, [(0, attn_parts[0].shape[1])])
     attn_shard, gate_up_pieces, down_pieces, tables = together(
         attn_shard,
         gate_up_pieces,
@@ -696,7 +703,7 @@
     attn_far = far_seq(*attn_near)
     down_parts = exchange_ctx(down_pieces)
     width = units_per(units_here)
-    up_shard = place_ctx([part[:, width:] for part in gate_up_parts])
+    up_shard, gate_shard = place_ctx(gate_up_parts, [(width, width), (0, width)])
     attn_far, up_shard = together(attn_far, up_shard)
     up_near = near_seq(up_shard)
 
@@ -715,7 +722,7 @@
     )
     key_value, down_parts = together(key_value, down_parts)
 
-    gate_down_shard = place_ctx([part[:, :width] for part in gate_up_parts], down_parts)
+    (gate_down_shard,) = place_ctx(down_parts, [(0, width)], gate_shard)
     keys_values, gate_down_shard = together(gather_ctx(key_value), gate_down_shard)
     half_f32 = ((half_rows, model_width), jnp.float32)
     half_bf16 = ((half_rows, model_width), jnp.bfloat16)
@@ -887,23 +894,26 @@
     small_rows = -(-small_size // (qkv_cols * 16)) * 16
     small = jnp.pad(small, (0, small_rows * qkv_cols - small_size)).reshape(small_rows, qkv_cols)
 
-    mlp_parts, gate_up_blocks, out_got, g_qkv, small = together(
-        mlp_parts, gate_up_blocks, out_got, g_qkv, small
-    )
+    payload_x, payload_y = near_payload(g_qkv)
+    rows = payload_x.shape[0]
+    half = rows // 2
+    mlp_parts, gate_up_blocks, out_got, g_qkv, small, payload_y = together(
+        mlp_parts, gate_up_blocks, out_got, g_qkv, small, payload_y
+    )
+    payload_x = jnp.concatenate([near_payload(g_qkv)[0], small], 0)
 
     gate_up_back = lax.all_to_all(gate_up_blocks, "ctx", 0, 0, tiled=True)
-    _, for_x, for_y, for_far = jnp.split(g_qkv, 4, 0)
-    rows = for_x.shape[0]
-    half = rows // 2
-    got_x = swap(jnp.concatenate([for_far[half:], for_x[half:], small], 0), "seq", 1)
-    got_y = swap(jnp.concatenate([for_far[:half], for_y[:half]], 0), "seq", 2)
-    attn_got = tuple(jnp.concatenate(pair, 1) for pair in zip((got_x[:rows], got_y), out_got))
+    got_x, got_y = near_swap((payload_x, payload_y))
+    qkv_got = (got_x[:rows], got_y)
     small = add_up([small, got_x[rows:]]).astype(jnp.bfloat16)
-    g_attn = jnp.concatenate([g_qkv, g_out], 1)
-    on_x, on_y = relay(g_attn, *attn_got)
+    on_x, on_y = together(
+        *(jnp.concatenate(pair, 1) for pair in zip(relay(g_qkv, *qkv_got), relay(g_out, *out_got)))
+    )
     last_x = swap(on_x, "seq", 1)
     last_y = swap(with_rows(on_y, small), "seq", 2)
     small = add_up([small, last_y[half:, :qkv_cols]]).astype(jnp.bfloat16)
+    attn_got = tuple(jnp.concatenate(pair, 1) for pair in zip(qkv_got, out_got))
+    g_attn = jnp.concatenate([g_qkv, g_out], 1)
     attn_sum = scatter_end(g_attn, *attn_got, last_x, last_y[:half])
     attn_pieces = row_pieces(attn_sum)
     rows, attn_cols = attn_pieces[0].shape

time: 468 us -> 462 us (0.987)
  local copies, waits for them, and re-layouts: 57.6 us -> 43.5 us
    unnamed x205 -> x184, local copies, waits for them, and re-layouts: 30.7 us -> 22.1 us
    all_to_all x1, waiting for transfers between devices: 7.61 us -> 14.8 us  [on_device(): gate_up_back = lax.all_to_all(gate_up_blocks, 'ctx', 0, 0, tiled=True)]
    ppermute x64, waiting for transfers between devices: 171 us -> 166 us  [swap(): return lax.ppermute(values, axis, [(i, i ^ offset) for i in range(size)])]
  transfers between devices with their start and end apart: 66 -> 66, of which waited for: 31 -> 33; matrix products, arithmetic and copies ran while one was open for 13% -> 12% of each run, Pallas kernels for 12% -> 12%
where the time goes in v6:
time: 462 us; the launch traced here: 454 us
  waiting for transfers between devices  182 us (39%)
  starting transfers between devices  97.4 us (21%)
  Pallas kernels  83.5 us (18%)
  local copies, waits for them, and re-layouts  43.5 us (9%)
  other arithmetic  39.9 us (9%)
  between operations  7.5 us (2%)
    ppermute x64, waiting for transfers between devices, swap(): return lax.ppermute(values, axis, [(i, i ^ offset) for i in range(size)])  166 us
    ppermute x64, starting transfers between devices, swap(): return lax.ppermute(values, axis, [(i, i ^ offset) for i in range(size)])  85 us
    pallas_call x2, Pallas kernels, by_tiles(): pl.pallas_call(functools.partial(body, tiles_each), grid=(2 * tiles_each,...  34.9 us
    pallas_call x12, Pallas kernels, call(): pl.pallas_call(body, in_specs=in_specs or [whole] * len(args), out_specs=...  34.8 us
    unnamed x184, local copies, waits for them, and re-layouts  22.1 us
    all_to_all x1, waiting for transfers between devices, on_device(): gate_up_back = lax.all_to_all(gate_up_blocks, 'ctx', 0, 0, tiled=True)  14.8 us
    pallas_call x2, Pallas kernels, weight_grad(): pl.pallas_call(weight_tile, grid=(4,), in_specs=[columns, columns, pl.Blo...  13.8 us
  transfers between devices with their start and end apart: 66, of which 33 were waited for; matrix products, arithmetic and copies ran while one was open for 12% of the time, Pallas kernels for 12%

profile of v6, /device:TPU:0, one launch (start us, length us, event | category | flops | bytes accessed | tf_op | source)
XLA Modules:
  0.0 453.6 jit_solution(132958651652660543)
XLA Ops:
  0.6 1.8 side_by_side.1.refs_0_
  2.4 3.0 collective-permute-start
  5.4 2.6 collective-permute-start.1
  14.7 2.5 dynamic-slice_bitcast_fusion
  25.3 2.6 constant_dynamic-slice_fusion.16.inputs
  28.9 3.4 collective-permute-done.1.refs_2_
  33.0 1.6 collective-permute-start.3
  34.6 1.5 collective-permute-start.4
  36.1 6.5 %collective-permute-start.5 = (bf16[96,2304]{1,0:T(8,128)(2,1)S(1)}, bf16[96,2304]{1,0:T(8,128)(2,1)S(1)}, u32[]{:S(2)}, u32[]{:S(2)}) collective-permute-start(bf16[96,2304]{1,0:T(8,128)(2,1)S(1)} %copy-done.65), channel_id=1, source_target_pairs={{0,2},{2,0},{4,6},{6,4},{1,3},{3,1},{5,7},{7,5},{8,10},{10,8},{12,... | collective-permute-start | bytes 1327112 | tf_op jit(solution)/shard_map/ppermute | solution.py:46
  45.1 13.9 %collective-permute-done.5.refs_1_ = bf16[96,2304]{1,0:T(8,128)(2,1)S(1)} collective-permute-done((bf16[96,2304]{1,0:T(8,128)(2,1)S(1)}, bf16[96,2304]{1,0:T(8,128)(2,1)S(1)}, u32[]{:S(2)}, u32[]{:S(2)}) %collective-permute-start.5) | collective-permute-done | bytes 442400 | tf_op jit(solution)/shard_map/ppermute | solution.py:46
  59.0 16.7 %collective-permute-done.6.refs_2_ = bf16[96,2304]{1,0:T(8,128)(2,1)S(1)} collective-permute-done((bf16[96,2304]{1,0:T(8,128)(2,1)S(1)}, bf16[96,2304]{1,0:T(8,128)(2,1)S(1)}, u32[]{:S(2)}, u32[]{:S(2)}) %collective-permute-start.6) | collective-permute-done | bytes 442400 | tf_op jit(solution)/shard_map/ppermute | solution.py:46
  76.9 6.9 %collective-permute-start.10 = (bf16[96,1152]{1,0:T(8,128)(2,1)S(1)}, bf16[96,1152]{1,0:T(8,128)(2,1)S(1)}, u32[]{:S(2)}, u32[]{:S(2)}) collective-permute-start(bf16[96,1152]{1,0:T(8,128)(2,1)S(1)} %copy-done.74), channel_id=1, source_target_pairs={{0,2},{2,0},{4,6},{6,4},{1,3},{3,1},{5,7},{7,5},{8,10},{10,8},{12,... | collective-permute-start | bytes 663560 | tf_op jit(solution)/shard_map/ppermute | solution.py:46
  88.5 2.3 project.1
  90.7 1.6 copy-done.10
  93.9 6.2 %collective-permute-done.11.refs_2_ = bf16[96,1152]{1,0:T(8,128)(2,1)S(1)} collective-permute-done((bf16[96,1152]{1,0:T(8,128)(2,1)S(1)}, bf16[96,1152]{1,0:T(8,128)(2,1)S(1)}, u32[]{:S(2)}, u32[]{:S(2)}) %collective-permute-start.11) | collective-permute-done | bytes 221216 | tf_op jit(solution)/shard_map/ppermute | solution.py:46
  101.4 2.8 collective-permute-start.13
  115.3 5.9 %attend.1 = (bf16[256,768]{1,0:T(8,128)(2,1)S(1)}, f32[256,768]{1,0:T(8,128)S(1)}, f32[128,1536]{1,0:T(8,128)S(1)}, f32[128,1536]{1,0:T(8,128)S(1)}) custom-call(s32[1]{0:T(128)} %bitcast.core_ref, bf16[256,768]{1,0:T(8,128)(2,1)S(1)} %copy-done.17, s32[256,1]{1,0:T(8,128)S(1)} %copy.30.query_pos, s32[1,1024]{1,0:T(1,128)S(1)} %bitcast.74, ...), custom_call_target="tpu_custom_call" | custom-call | flops 1 | bytes 1 | tf_op jit(solution)/shard_map/attend/pallas_call | solution.py:351
  121.3 2.3 collective-permute-done.16.got
  123.9 1.6 collective-permute-done.17.refs_1_
  127.4 1.5 collective-permute-start.23
  129.5 2.4 collective-permute-start.20
  133.3 11.5 %collective-permute-done.19 = bf16[128,1536]{1,0:T(8,128)(2,1)S(1)} collective-permute-done((bf16[128,1536]{1,0:T(8,128)(2,1)S(1)}, bf16[128,1536]{1,0:T(8,128)(2,1)S(1)}, u32[]{:S(2)}, u32[]{:S(2)}) %collective-permute-start.19) | collective-permute-done | bytes 393248 | tf_op jit(solution)/shard_map/ppermute | solution.py:46
  144.8 14.5 %collective-permute-done.20 = bf16[128,1536]{1,0:T(8,128)(2,1)S(1)} collective-permute-done((bf16[128,1536]{1,0:T(8,128)(2,1)S(1)}, bf16[128,1536]{1,0:T(8,128)(2,1)S(1)}, u32[]{:S(2)}, u32[]{:S(2)}) %collective-permute-start.20) | collective-permute-done | bytes 393248 | tf_op jit(solution)/shard_map/ppermute | solution.py:46
  159.3 5.4 %collective-permute-done.22.refs_4_ = bf16[384,2304]{1,0:T(8,128)(2,1)S(1)} collective-permute-done((bf16[384,2304]{1,0:T(8,128)(2,1)S(1)}, bf16[384,2304]{1,0:T(8,128)(2,1)S(1)}, u32[]{:S(2)}, u32[]{:S(2)}) %collective-permute-start.22) | collective-permute-done | bytes 1769504 | tf_op jit(solution)/shard_map/ppermute | solution.py:46
  169.6 2.0 collective-permute-start.25
  174.0 24.6 %collective-permute-done.28.refs_6_ = bf16[192,3456]{1,0:T(8,128)(2,1)S(1)} collective-permute-done((bf16[192,3456]{1,0:T(8,128)(2,1)S(1)}, bf16[192,3456]{1,0:T(8,128)(2,1)S(1)}, u32[]{:S(2)}, u32[]{:S(2)}) %collective-permute-start.28) | collective-permute-done | bytes 1327136 | tf_op jit(solution)/shard_map/ppermute | solution.py:46
  199.2 9.9 %gate_up.1 = f32[1024,2304]{1,0:T(8,128)S(1)} custom-call(bf16[512,1536]{1,0:T(8,128)(2,1)S(1)} %constant_dynamic-update-slice_fusion.1.x_mine, bf16[512,1536]{1,0:T(8,128)(2,1)S(1)} %collective-permute-done.24.x_other, bf16[384,1152]{1,0:T(8,128)(2,1)} %get-tuple-element.228.refs_0_, bf16[384,1152]{1,0:T(8,128)(2,1)S(1)} %collective-permute-done.17.refs_1_, ...), custom_call_target="tpu_custom_call" | custom-call | flops 1 | bytes 1 | tf_op jit(solution)/shard_map/gate_up/pallas_call | solution.py:299
  209.2 3.6 copy-done
  213.0 3.4 collective-permute-done.30.o_other.x_other
  216.4 25.0 %mlp_back.1 = (bf16[1024,2304]{1,0:T(8,128)(2,1)}, bf16[1024,1152]{1,0:T(8,128)(2,1)}, f32[512,1536]{1,0:T(8,128)}, bf16[512,1536]{1,0:T(8,128)(2,1)}, f32[512,1...) custom-call(f32[1024,2304]{1,0:T(8,128)} %copy-done, bf16[512,1536]{1,0:T(8,128)(2,1)S(1)} %constant_dynamic-update-slice_fusion.5.o_mine.x_mine, ...), custom_call_target="tpu_custom_call" | custom-call | flops 1 | bytes 1 | tf_op jit(solution)/shard_map/mlp_back/pallas_call | solution.py:299
  241.9 1.7 copy-done.13
  243.6 5.2 %weight_grad.2 = bf16[1536,1152]{1,0:T(8,128)(2,1)S(1)} custom-call(bf16[512,1536]{1,0:T(8,128)(2,1)S(1)} %constant_dynamic-update-slice_fusion.5.o_mine.x_mine, bf16[512,1536]{1,0:T(8,128)(2,1)S(1)} %collective-permute-done.30.o_other.x_other, bf16[1024,1152]{1,0:T(8,128)(2,1)S(1)} %copy-done.13), custom_call_target="tpu_custom_call" | custom-call | flops 1 | bytes 1 | tf_op jit(solution)/shard_map/weight_grad/pallas_call | solution.py:332
  250.2 1.8 collective-permute-start.33
  256.3 1.6 collective-permute-start.37
  257.9 8.5 %weight_grad.3 = bf16[1536,2304]{1,0:T(8,128)(2,1)S(1)} custom-call(bf16[512,1536]{1,0:T(8,128)(2,1)S(1)} %constant_dynamic-update-slice_fusion.1.x_mine, bf16[512,1536]{1,0:T(8,128)(2,1)S(1)} %collective-permute-done.24.x_other, bf16[1024,2304]{1,0:T(8,128)(2,1)S(1)} %bitcast.73), custom_call_target="tpu_custom_call" | custom-call | flops 1 | bytes 1 | tf_op jit(solution)/shard_map/weight_grad/pallas_call | solution.py:332
  267.0 1.6 fusion.39
  268.6 7.2 %collective-permute-done.36 = bf16[384,1152]{1,0:T(8,128)(2,1)S(1)} collective-permute-done((bf16[384,1152]{1,0:T(8,128)(2,1)S(1)}, bf16[384,1152]{1,0:T(8,128)(2,1)S(1)}, u32[]{:S(2)}, u32[]{:S(2)}) %collective-permute-start.36) | collective-permute-done | bytes 884768 | tf_op jit(solution)/shard_map/ppermute | solution.py:46
  281.2 6.7 %collective-permute-done.38 = bf16[192,1152]{1,0:T(8,128)(2,1)S(1)} collective-permute-done((bf16[192,1152]{1,0:T(8,128)(2,1)S(1)}, bf16[192,1152]{1,0:T(8,128)(2,1)S(1)}, u32[]{:S(2)}, u32[]{:S(2)}) %collective-permute-start.38) | collective-permute-done | bytes 442400 | tf_op jit(solution)/shard_map/ppermute | solution.py:46
  289.4 1.7 collective-permute-start.44
  291.0 1.5 collective-permute-start.45
  292.6 4.0 all-to-all-start
  296.6 3.4 mlp_norm_back.1
  300.0 1.9 collective-permute-done.40.branch_other
  302.7 11.8 %attend_back.1 = (bf16[256,768]{1,0:T(8,128)(2,1)}, bf16[1536,768]{1,0:T(8,128)(2,1)}, f32[256,256]{1,0:T(8,128)}, bf16[256,256]{1,0:T(8,128)(2,1)}, bf16[256,256]{1,0:T(8,128)(2,1)}, /*index=5*/bf16[256,256]{1,0:T(8,128)(2,1)}) custom-call(s32[1]{0:T(128)} %bitcast.core_ref, bf16[128,1536]{1,0:T(8,128)(2,1)} %get-tuple-element.272.branch_mine, ...), custom_call_target="tpu_custom_call" | custom-call | flops 1 | bytes 1 | tf_op jit(solution)/shard_map/attend_back/pallas_call | solution.py:351
  316.6 2.4 collective-permute-start.42
  320.9 1.9 collective-permute-done.41.refs_1_
  322.9 6.9 %collective-permute-done.42.refs_2_ = bf16[256,256]{1,0:T(8,128)(2,1)S(1)} collective-permute-done((bf16[256,256]{1,0:T(8,128)(2,1)}, bf16[256,256]{1,0:T(8,128)(2,1)S(1)}, u32[]{:S(2)}, u32[]{:S(2)}) %collective-permute-start.42) | collective-permute-done | bytes 131104 | tf_op jit(solution)/shard_map/ppermute | solution.py:46
  329.8 3.7 add_convert_fusion.4
  335.0 2.1 collective-permute-start.46
  339.5 5.1 %project_back.1 = (bf16[256,1024]{1,0:T(8,128)(2,1)}, f32[1,1024]{1,0:T(1,128)}, f32[1,1536]{1,0:T(1,128)}, f32[128,1536]{1,0:T(8,128)}, f32[128,1536]{1,0:T(8,128)}) custom-call(s32[1]{0:T(128)} %bitcast.core_ref, bf16[256,768]{1,0:T(8,128)(2,1)} %get-tuple-element.302.query_lin, bf16[1536,1024]{1,0:T(8,128)(2,1)} %copy-done.10, f32[256,128]{1,0:T(8,128)} %copy-done.14, ...), custom_call_target="tpu_custom_call" | custom-call | flops 1 | bytes 1 | tf_op jit(solution)/shard_map/project_back/pallas_call | solution.py:351
  349.8 3.5 collective-permute-done.49
  355.8 3.3 add_convert_fusion.3
  360.5 6.7 %collective-permute-done.47 = bf16[128,1536]{1,0:T(8,128)(2,1)} collective-permute-done((bf16[128,1536]{1,0:T(8,128)(2,1)}, bf16[128,1536]{1,0:T(8,128)(2,1)}, u32[]{:S(2)}, u32[]{:S(2)}) %collective-permute-start.47) | collective-permute-done | bytes 393248 | tf_op jit(solution)/shard_map/ppermute | solution.py:46
  369.9 1.5 collective-permute-start.53
  371.4 2.1 add_convert_fusion.13
  373.4 8.4 %all-to-all-start.1 = ((bf16[4,96,2304]{2,1,0:T(8,128)(2,1)}), bf16[4,96,2304]{2,1,0:T(8,128)(2,1)}, u32[]{:S(2)}, u32[]{:S(2)}) async-start(bf16[4,96,2304]{2,1,0:T(8,128)(2,1)} %bitcast.76), calls=%async_computation.1 | async-start | bytes 3538944 | tf_op jit(solution)/shard_map/all_to_all | solution.py:905
  381.8 2.2 collective-permute-done.53
  393.9 7.5 %collective-permute-done.56 = bf16[208,1792]{1,0:T(8,128)(2,1)} collective-permute-done((bf16[208,1792]{1,0:T(8,128)(2,1)}, bf16[208,1792]{1,0:T(8,128)(2,1)}, u32[]{:S(2)}, u32[]{:S(2)}) %collective-permute-start.56) | collective-permute-done | bytes 745504 | tf_op jit(solution)/shard_map/ppermute | solution.py:46
  402.2 1.7 convert_add_fusion
  406.0 14.8 %all-to-all-done.1 = bf16[4,96,2304]{2,1,0:T(8,128)(2,1)} async-done(((bf16[4,96,2304]{2,1,0:T(8,128)(2,1)}), bf16[4,96,2304]{2,1,0:T(8,128)(2,1)}, u32[]{:S(2)}, u32[]{:S(2)}) %all-to-all-start.1) | async-done | bytes 1769504 | tf_op jit(solution)/shard_map/all_to_all | solution.py:905
  420.8 1.9 collective-permute-start.58
  422.8 2.5 collective-permute-start.59
  427.3 1.5 slice_bitcast_fusion.3
  438.0 11.2 %collective-permute-done.58 = bf16[96,1920]{1,0:T(8,128)(2,1)S(1)} collective-permute-done((bf16[96,1920]{1,0:T(8,128)(2,1)}, bf16[96,1920]{1,0:T(8,128)(2,1)S(1)}, u32[]{:S(2)}, u32[]{:S(2)}) %collective-permute-start.58) | collective-permute-done | bytes 368672 | tf_op jit(solution)/shard_map/ppermute | solution.py:46
  (384 shorter events, 107.5 us)
Async XLA Ops:
  2.4 26.4 %collective-permute-start = (bf16[96,1792]{1,0:T(8,128)(2,1)}, bf16[96,1792]{1,0:T(8,128)(2,1)S(1)}, u32[]{:S(2)}, u32[]{:S(2)}) collective-permute-start(bf16[96,1792]{1,0:T(8,128)(2,1)} %side_by_side.1.refs_0_), channel_id=1, source_target_pairs={{0,2},{2,0},{4,6},{6,4},{1,3},{3,1},{5,7},{7,5},{8,10},{10,8},{12,... | collective-permute-start | bytes 1032200 | tf_op jit(solution)/shard_map/ppermute | solution.py:46
  5.4 26.8 %collective-permute-start.1 = (bf16[96,1792]{1,0:T(8,128)(2,1)}, bf16[96,1792]{1,0:T(8,128)(2,1)S(1)}, u32[]{:S(2)}, u32[]{:S(2)}) collective-permute-start(bf16[96,1792]{1,0:T(8,128)(2,1)} %side_by_side.1.refs_0_), channel_id=1, source_target_pairs={{0,4},{2,6},{4,0},{6,2},{1,5},{3,7},{5,1},{7,3},{8,12},{10,14},{12... | collective-permute-start | bytes 1032200 | tf_op jit(solution)/shard_map/ppermute | solution.py:46
  8.0 24.3 %collective-permute-start.2 = (bf16[96,1792]{1,0:T(8,128)(2,1)}, bf16[96,1792]{1,0:T(8,128)(2,1)S(1)}, u32[]{:S(2)}, u32[]{:S(2)}) collective-permute-start(bf16[96,1792]{1,0:T(8,128)(2,1)} %side_by_side.1.refs_0_), channel_id=1, source_target_pairs={{0,6},{2,4},{4,2},{6,0},{1,7},{3,5},{5,3},{7,1},{8,14},{10,12},{12... | collective-permute-start | bytes 1032200 | tf_op jit(solution)/shard_map/ppermute | solution.py:46
  33.0 42.6 %collective-permute-start.3 = (bf16[384,1792]{1,0:T(8,128)(2,1)S(1)}, bf16[384,1792]{1,0:T(8,128)(2,1)S(1)}, u32[]{:S(2)}, u32[]{:S(2)}) collective-permute-start(bf16[384,1792]{1,0:T(8,128)(2,1)S(1)} %place.3.refs_0_), channel_id=1, source_target_pairs={{0,8},{8,0},{16,24},{24,16},{1,9},{9,1},{17,25},{25,17},{2,10},{10... | collective-permute-start | bytes 4128776 | tf_op jit(solution)/shard_map/ppermute | solution.py:46
  34.6 41.0 %collective-permute-start.4 = (bf16[384,1792]{1,0:T(8,128)(2,1)S(1)}, bf16[384,1792]{1,0:T(8,128)(2,1)S(1)}, u32[]{:S(2)}, u32[]{:S(2)}) collective-permute-start(bf16[384,1792]{1,0:T(8,128)(2,1)S(1)} %place.3.refs_0_), channel_id=1, source_target_pairs={{0,16},{8,24},{16,0},{24,8},{1,17},{9,25},{17,1},{25,9},{2,18},{10... | collective-permute-start | bytes 4128776 | tf_op jit(solution)/shard_map/ppermute | solution.py:46
  36.1 22.8 %collective-permute-start.5 = (bf16[96,2304]{1,0:T(8,128)(2,1)S(1)}, bf16[96,2304]{1,0:T(8,128)(2,1)S(1)}, u32[]{:S(2)}, u32[]{:S(2)}) collective-permute-start(bf16[96,2304]{1,0:T(8,128)(2,1)S(1)} %copy-done.65), channel_id=1, source_target_pairs={{0,2},{2,0},{4,6},{6,4},{1,3},{3,1},{5,7},{7,5},{8,10},{10,8},{12,... | collective-permute-start | bytes 1327112 | tf_op jit(solution)/shard_map/ppermute | solution.py:46
  42.6 33.0 %collective-permute-start.6 = (bf16[96,2304]{1,0:T(8,128)(2,1)S(1)}, bf16[96,2304]{1,0:T(8,128)(2,1)S(1)}, u32[]{:S(2)}, u32[]{:S(2)}) collective-permute-start(bf16[96,2304]{1,0:T(8,128)(2,1)S(1)} %copy-done.64), channel_id=1, source_target_pairs={{0,4},{2,6},{4,0},{6,2},{1,5},{3,7},{5,1},{7,3},{8,12},{10,14},{12... | collective-permute-start | bytes 1327112 | tf_op jit(solution)/shard_map/ppermute | solution.py:46
  43.7 31.9 %collective-permute-start.7 = (bf16[96,2304]{1,0:T(8,128)(2,1)S(1)}, bf16[96,2304]{1,0:T(8,128)(2,1)S(1)}, u32[]{:S(2)}, u32[]{:S(2)}) collective-permute-start(bf16[96,2304]{1,0:T(8,128)(2,1)S(1)} %pad_maximum_fusion.31), channel_id=1, source_target_pairs={{0,6},{2,4},{4,2},{6,0},{1,7},{3,5},{5,3},{7,1},{8,14},{10,12},{12... | collective-permute-start | bytes 1327112 | tf_op jit(solution)/shard_map/ppermute | solution.py:46
  75.7 12.8 %collective-permute-start.8 = (bf16[192,1792]{1,0:T(8,128)(2,1)S(1)}, bf16[192,1792]{1,0:T(8,128)(2,1)S(1)}, u32[]{:S(2)}, u32[]{:S(2)}) collective-permute-start(bf16[192,1792]{1,0:T(8,128)(2,1)S(1)} %slice.302), channel_id=1, source_target_pairs={{0,8},{8,0},{16,24},{24,16},{1,9},{9,1},{17,25},{25,17},{2,10},{10... | collective-permute-start | bytes 2064392 | tf_op jit(solution)/shard_map/ppermute | solution.py:46
  76.3 12.1 %collective-permute-start.9 = (bf16[192,1792]{1,0:T(8,128)(2,1)S(1)}, bf16[192,1792]{1,0:T(8,128)(2,1)S(1)}, u32[]{:S(2)}, u32[]{:S(2)}) collective-permute-start(bf16[192,1792]{1,0:T(8,128)(2,1)S(1)} %slice.303), channel_id=1, source_target_pairs={{0,16},{8,24},{16,0},{24,8},{1,17},{9,25},{17,1},{25,9},{2,18},{10... | collective-permute-start | bytes 2064392 | tf_op jit(solution)/shard_map/ppermute | solution.py:46
  76.9 16.2 %collective-permute-start.10 = (bf16[96,1152]{1,0:T(8,128)(2,1)S(1)}, bf16[96,1152]{1,0:T(8,128)(2,1)S(1)}, u32[]{:S(2)}, u32[]{:S(2)}) collective-permute-start(bf16[96,1152]{1,0:T(8,128)(2,1)S(1)} %copy-done.74), channel_id=1, source_target_pairs={{0,2},{2,0},{4,6},{6,4},{1,3},{3,1},{5,7},{7,5},{8,10},{10,8},{12,... | collective-permute-start | bytes 663560 | tf_op jit(solution)/shard_map/ppermute | solution.py:46
  83.8 16.2 %collective-permute-start.11 = (bf16[96,1152]{1,0:T(8,128)(2,1)S(1)}, bf16[96,1152]{1,0:T(8,128)(2,1)S(1)}, u32[]{:S(2)}, u32[]{:S(2)}) collective-permute-start(bf16[96,1152]{1,0:T(8,128)(2,1)S(1)} %copy-done.73), channel_id=1, source_target_pairs={{0,4},{2,6},{4,0},{6,2},{1,5},{3,7},{5,1},{7,3},{8,12},{10,14},{12... | collective-permute-start | bytes 663560 | tf_op jit(solution)/shard_map/ppermute | solution.py:46
  84.9 15.9 %collective-permute-start.12 = (bf16[96,1152]{1,0:T(8,128)(2,1)S(1)}, bf16[96,1152]{1,0:T(8,128)(2,1)S(1)}, u32[]{:S(2)}, u32[]{:S(2)}) collective-permute-start(bf16[96,1152]{1,0:T(8,128)(2,1)S(1)} %copy-done.72), channel_id=1, source_target_pairs={{0,6},{2,4},{4,2},{6,0},{1,7},{3,5},{5,3},{7,1},{8,14},{10,12},{12... | collective-permute-start | bytes 663560 | tf_op jit(solution)/shard_map/ppermute | solution.py:46
  101.4 13.1 %collective-permute-start.13 = (bf16[256,256]{1,0:T(8,128)(2,1)}, bf16[256,256]{1,0:T(8,128)(2,1)S(1)}, u32[]{:S(2)}, u32[]{:S(2)}) collective-permute-start(bf16[256,256]{1,0:T(8,128)(2,1)} %get-tuple-element.218.refs_0_), channel_id=1, source_target_pairs={{0,2},{2,0},{4,6},{6,4},{1,3},{3,1},{5,7},{7,5},{8,10},{10,8},{12,... | collective-permute-start | bytes 393224 | tf_op jit(solution)/shard_map/ppermute | solution.py:46
  104.2 10.8 %collective-permute-start.14 = (bf16[256,256]{1,0:T(8,128)(2,1)}, bf16[256,256]{1,0:T(8,128)(2,1)}, u32[]{:S(2)}, u32[]{:S(2)}) collective-permute-start(bf16[256,256]{1,0:T(8,128)(2,1)} %get-tuple-element.218.refs_0_), channel_id=1, source_target_pairs={{0,4},{2,6},{4,0},{6,2},{1,5},{3,7},{5,1},{7,3},{8,12},{10,14},{12... | collective-permute-start | bytes 393224 | tf_op jit(solution)/shard_map/ppermute | solution.py:46
  105.2 9.8 %collective-permute-start.15 = (bf16[256,256]{1,0:T(8,128)(2,1)}, bf16[256,256]{1,0:T(8,128)(2,1)}, u32[]{:S(2)}, u32[]{:S(2)}) collective-permute-start(bf16[256,256]{1,0:T(8,128)(2,1)} %get-tuple-element.218.refs_0_), channel_id=1, source_target_pairs={{0,6},{2,4},{4,2},{6,0},{1,7},{3,5},{5,3},{7,1},{8,14},{10,12},{12... | collective-permute-start | bytes 393224 | tf_op jit(solution)/shard_map/ppermute | solution.py:46
  106.6 18.9 %collective-permute-start.17 = (bf16[384,1152]{1,0:T(8,128)(2,1)}, bf16[384,1152]{1,0:T(8,128)(2,1)S(1)}, u32[]{:S(2)}, u32[]{:S(2)}) collective-permute-start(bf16[384,1152]{1,0:T(8,128)(2,1)} %get-tuple-element.228.refs_0_), channel_id=1, source_target_pairs={{0,8},{8,0},{16,24},{24,16},{1,9},{9,1},{17,25},{25,17},{2,10},{10... | collective-permute-start | bytes 2654216 | tf_op jit(solution)/shard_map/ppermute | solution.py:46
  108.1 18.7 %collective-permute-start.18 = (bf16[384,1152]{1,0:T(8,128)(2,1)}, bf16[384,1152]{1,0:T(8,128)(2,1)}, u32[]{:S(2)}, u32[]{:S(2)}) collective-permute-start(bf16[384,1152]{1,0:T(8,128)(2,1)} %get-tuple-element.228.refs_0_), channel_id=1, source_target_pairs={{0,16},{8,24},{16,0},{24,8},{1,17},{9,25},{17,1},{25,9},{2,18},{10... | collective-permute-start | bytes 2654216 | tf_op jit(solution)/shard_map/ppermute | solution.py:46
  121.2 2.4 collective-permute-start.16
  126.8 37.8 %collective-permute-start.22 = (bf16[384,2304]{1,0:T(8,128)(2,1)S(1)}, bf16[384,2304]{1,0:T(8,128)(2,1)S(1)}, u32[]{:S(2)}, u32[]{:S(2)}) collective-permute-start(bf16[384,2304]{1,0:T(8,128)(2,1)S(1)} %place.5.refs_3_), channel_id=1, source_target_pairs={{0,8},{8,0},{16,24},{24,16},{1,9},{9,1},{17,25},{25,17},{2,10},{10... | collective-permute-start | bytes 5308424 | tf_op jit(solution)/shard_map/ppermute | solution.py:46
  127.4 38.3 %collective-permute-start.23 = (bf16[384,2304]{1,0:T(8,128)(2,1)S(1)}, bf16[384,2304]{1,0:T(8,128)(2,1)S(1)}, u32[]{:S(2)}, u32[]{:S(2)}) collective-permute-start(bf16[384,2304]{1,0:T(8,128)(2,1)S(1)} %place.5.refs_3_), channel_id=1, source_target_pairs={{0,16},{8,24},{16,0},{24,8},{1,17},{9,25},{17,1},{25,9},{2,18},{10... | collective-permute-start | bytes 5308424 | tf_op jit(solution)/shard_map/ppermute | solution.py:46
  128.9 15.9 %collective-permute-start.19 = (bf16[128,1536]{1,0:T(8,128)(2,1)S(1)}, bf16[128,1536]{1,0:T(8,128)(2,1)S(1)}, u32[]{:S(2)}, u32[]{:S(2)}) collective-permute-start(bf16[128,1536]{1,0:T(8,128)(2,1)S(1)} %get-tuple-element.232), channel_id=1, source_target_pairs={{0,2},{2,0},{4,6},{6,4},{1,3},{3,1},{5,7},{7,5},{8,10},{10,8},{12,... | collective-permute-start | bytes 1179656 | tf_op jit(solution)/shard_map/ppermute | solution.py:46
  129.5 29.8 %collective-permute-start.20 = (bf16[128,1536]{1,0:T(8,128)(2,1)S(1)}, bf16[128,1536]{1,0:T(8,128)(2,1)S(1)}, u32[]{:S(2)}, u32[]{:S(2)}) collective-permute-start(bf16[128,1536]{1,0:T(8,128)(2,1)S(1)} %get-tuple-element.232), channel_id=1, source_target_pairs={{0,4},{2,6},{4,0},{6,2},{1,5},{3,7},{5,1},{7,3},{8,12},{10,14},{12... | collective-permute-start | bytes 1179656 | tf_op jit(solution)/shard_map/ppermute | solution.py:46
  131.8 27.4 %collective-permute-start.21 = (bf16[128,1536]{1,0:T(8,128)(2,1)S(1)}, bf16[128,1536]{1,0:T(8,128)(2,1)S(1)}, u32[]{:S(2)}, u32[]{:S(2)}) collective-permute-start(bf16[128,1536]{1,0:T(8,128)(2,1)S(1)} %get-tuple-element.232), channel_id=1, source_target_pairs={{0,6},{2,4},{4,2},{6,0},{1,7},{3,5},{5,3},{7,1},{8,14},{10,12},{12... | collective-permute-start | bytes 1179656 | tf_op jit(solution)/shard_map/ppermute | solution.py:46
  165.8 3.8 collective-permute-start.24
  167.4 31.3 %collective-permute-start.28 = (bf16[192,3456]{1,0:T(8,128)(2,1)S(1)}, bf16[192,3456]{1,0:T(8,128)(2,1)S(1)}, u32[]{:S(2)}, u32[]{:S(2)}) collective-permute-start(bf16[192,3456]{1,0:T(8,128)(2,1)S(1)} %pad_maximum_fusion.4), channel_id=1, source_target_pairs={{0,8},{8,0},{16,24},{24,16},{1,9},{9,1},{17,25},{25,17},{2,10},{10... | collective-permute-start | bytes 3981320 | tf_op jit(solution)/shard_map/ppermute | solution.py:46
  168.2 31.0 %collective-permute-start.29 = (bf16[192,3456]{1,0:T(8,128)(2,1)S(1)}, bf16[192,3456]{1,0:T(8,128)(2,1)S(1)}, u32[]{:S(2)}, u32[]{:S(2)}) collective-permute-start(bf16[192,3456]{1,0:T(8,128)(2,1)S(1)} %pad_maximum_fusion.3), channel_id=1, source_target_pairs={{0,16},{8,24},{16,0},{24,8},{1,17},{9,25},{17,1},{25,9},{2,18},{10... | collective-permute-start | bytes 3981320 | tf_op jit(solution)/shard_map/ppermute | solution.py:46
  169.6 43.1 %collective-permute-start.25 = (bf16[128,1536]{1,0:T(8,128)(2,1)S(1)}, bf16[128,1536]{1,0:T(8,128)(2,1)S(1)}, u32[]{:S(2)}, u32[]{:S(2)}) collective-permute-start(bf16[128,1536]{1,0:T(8,128)(2,1)S(1)} %copy-done.44), channel_id=1, source_target_pairs={{0,2},{2,0},{4,6},{6,4},{1,3},{3,1},{5,7},{7,5},{8,10},{10,8},{12,... | collective-permute-start | bytes 1179656 | tf_op jit(solution)/shard_map/ppermute | solution.py:46
  171.6 41.2 %collective-permute-start.26 = (bf16[128,1536]{1,0:T(8,128)(2,1)S(1)}, bf16[128,1536]{1,0:T(8,128)(2,1)S(1)}, u32[]{:S(2)}, u32[]{:S(2)}) collective-permute-start(bf16[128,1536]{1,0:T(8,128)(2,1)S(1)} %copy-done.44), channel_id=1, source_target_pairs={{0,4},{2,6},{4,0},{6,2},{1,5},{3,7},{5,1},{7,3},{8,12},{10,14},{12... | collective-permute-start | bytes 1179656 | tf_op jit(solution)/shard_map/ppermute | solution.py:46
  172.6 40.2 %collective-permute-start.27 = (bf16[128,1536]{1,0:T(8,128)(2,1)S(1)}, bf16[128,1536]{1,0:T(8,128)(2,1)S(1)}, u32[]{:S(2)}, u32[]{:S(2)}) collective-permute-start(bf16[128,1536]{1,0:T(8,128)(2,1)S(1)} %copy-done.44), channel_id=1, source_target_pairs={{0,6},{2,4},{4,2},{6,0},{1,7},{3,5},{5,3},{7,1},{8,14},{10,12},{12... | collective-permute-start | bytes 1179656 | tf_op jit(solution)/shard_map/ppermute | solution.py:46
  212.9 3.5 collective-permute-start.30
  241.4 7.5 %collective-permute-start.31 = (bf16[512,1536]{1,0:T(8,128)(2,1)}, bf16[512,1536]{1,0:T(8,128)(2,1)S(1)}, u32[]{:S(2)}, u32[]{:S(2)}) collective-permute-start(bf16[512,1536]{1,0:T(8,128)(2,1)} %get-tuple-element.251), channel_id=1, source_target_pairs={{0,1},{1,0},{2,3},{3,2},{4,5},{5,4},{6,7},{7,6},{8,9},{9,8},{10,11... | collective-permute-start | bytes 4718600 | tf_op jit(solution)/shard_map/ppermute | solution.py:46
  241.6 8.7 %collective-permute-start.32 = (bf16[512,1536]{1,0:T(8,128)(2,1)S(1)}, bf16[512,1536]{1,0:T(8,128)(2,1)S(1)}, u32[]{:S(2)}, u32[]{:S(2)}) collective-permute-start(bf16[512,1536]{1,0:T(8,128)(2,1)S(1)} %get-tuple-element.253), channel_id=1, source_target_pairs={{0,1},{1,0},{2,3},{3,2},{4,5},{5,4},{6,7},{7,6},{8,9},{9,8},{10,11... | collective-permute-start | bytes 4718600 | tf_op jit(solution)/shard_map/ppermute | solution.py:46
  250.2 39.1 %collective-permute-start.33 = (bf16[128,1536]{1,0:T(8,128)(2,1)S(1)}, bf16[128,1536]{1,0:T(8,128)(2,1)S(1)}, u32[]{:S(2)}, u32[]{:S(2)}) collective-permute-start(bf16[128,1536]{1,0:T(8,128)(2,1)S(1)} %get-tuple-element.256), channel_id=1, source_target_pairs={{0,2},{2,0},{4,6},{6,4},{1,3},{3,1},{5,7},{7,5},{8,10},{10,8},{12,... | collective-permute-start | bytes 1179656 | tf_op jit(solution)/shard_map/ppermute | solution.py:46
  252.0 37.4 %collective-permute-start.34 = (bf16[128,1536]{1,0:T(8,128)(2,1)S(1)}, bf16[128,1536]{1,0:T(8,128)(2,1)S(1)}, u32[]{:S(2)}, u32[]{:S(2)}) collective-permute-start(bf16[128,1536]{1,0:T(8,128)(2,1)S(1)} %get-tuple-element.257), channel_id=1, source_target_pairs={{0,4},{2,6},{4,0},{6,2},{1,5},{3,7},{5,1},{7,3},{8,12},{10,14},{12... | collective-permute-start | bytes 1179656 | tf_op jit(solution)/shard_map/ppermute | solution.py:46
  253.1 36.2 %collective-permute-start.35 = (bf16[128,1536]{1,0:T(8,128)(2,1)S(1)}, bf16[128,1536]{1,0:T(8,128)(2,1)S(1)}, u32[]{:S(2)}, u32[]{:S(2)}) collective-permute-start(bf16[128,1536]{1,0:T(8,128)(2,1)S(1)} %get-tuple-element.258), channel_id=1, source_target_pairs={{0,6},{2,4},{4,2},{6,0},{1,7},{3,5},{5,3},{7,1},{8,14},{10,12},{12... | collective-permute-start | bytes 1179656 | tf_op jit(solution)/shard_map/ppermute | solution.py:46
  254.8 21.0 %collective-permute-start.36 = (bf16[384,1152]{1,0:T(8,128)(2,1)S(1)}, bf16[384,1152]{1,0:T(8,128)(2,1)S(1)}, u32[]{:S(2)}, u32[]{:S(2)}) collective-permute-start(bf16[384,1152]{1,0:T(8,128)(2,1)S(1)} %pad_maximum_fusion.5), channel_id=1, source_target_pairs={{0,8},{8,0},{16,24},{24,16},{1,9},{9,1},{17,25},{25,17},{2,10},{10... | collective-permute-start | bytes 2654216 | tf_op jit(solution)/shard_map/ppermute | solution.py:46
  256.3 20.9 %collective-permute-start.37 = (bf16[384,1152]{1,0:T(8,128)(2,1)S(1)}, bf16[384,1152]{1,0:T(8,128)(2,1)S(1)}, u32[]{:S(2)}, u32[]{:S(2)}) collective-permute-start(bf16[384,1152]{1,0:T(8,128)(2,1)S(1)} %pad_maximum_fusion.6), channel_id=1, source_target_pairs={{0,16},{8,24},{16,0},{24,8},{1,17},{9,25},{17,1},{25,9},{2,18},{10... | collective-permute-start | bytes 2654216 | tf_op jit(solution)/shard_map/ppermute | solution.py:46
  277.4 10.5 %collective-permute-start.38 = (bf16[192,1152]{1,0:T(8,128)(2,1)S(1)}, bf16[192,1152]{1,0:T(8,128)(2,1)S(1)}, u32[]{:S(2)}, u32[]{:S(2)}) collective-permute-start(bf16[192,1152]{1,0:T(8,128)(2,1)S(1)} %get-tuple-element.263), channel_id=1, source_target_pairs={{0,8},{8,0},{16,24},{24,16},{1,9},{9,1},{17,25},{25,17},{2,10},{10... | collective-permute-start | bytes 1327112 | tf_op jit(solution)/shard_map/ppermute | solution.py:46
  278.0 10.0 %collective-permute-start.39 = (bf16[192,1152]{1,0:T(8,128)(2,1)S(1)}, bf16[192,1152]{1,0:T(8,128)(2,1)S(1)}, u32[]{:S(2)}, u32[]{:S(2)}) collective-permute-start(bf16[192,1152]{1,0:T(8,128)(2,1)S(1)} %get-tuple-element.264), channel_id=1, source_target_pairs={{0,16},{8,24},{16,0},{24,8},{1,17},{9,25},{17,1},{25,9},{2,18},{10... | collective-permute-start | bytes 1327112 | tf_op jit(solution)/shard_map/ppermute | solution.py:46
  289.4 40.4 %collective-permute-start.44 = (bf16[384,2304]{1,0:T(8,128)(2,1)S(1)}, bf16[384,2304]{1,0:T(8,128)(2,1)}, u32[]{:S(2)}, u32[]{:S(2)}) collective-permute-start(bf16[384,2304]{1,0:T(8,128)(2,1)S(1)} %pad_maximum_fusion), channel_id=1, source_target_pairs={{0,8},{8,0},{16,24},{24,16},{1,9},{9,1},{17,25},{25,17},{2,10},{10... | collective-permute-start | bytes 5308424 | tf_op jit(solution)/shard_map/ppermute | solution.py:46
  291.0 38.7 %collective-permute-start.45 = (bf16[384,2304]{1,0:T(8,128)(2,1)}, bf16[384,2304]{1,0:T(8,128)(2,1)}, u32[]{:S(2)}, u32[]{:S(2)}) collective-permute-start(bf16[384,2304]{1,0:T(8,128)(2,1)} %pad_maximum_fusion.1), channel_id=1, source_target_pairs={{0,16},{8,24},{16,0},{24,8},{1,17},{9,25},{17,1},{25,9},{2,18},{10... | collective-permute-start | bytes 5308424 | tf_op jit(solution)/shard_map/ppermute | solution.py:46
  292.6 23.2 %all-to-all-start = ((bf16[4,96,1152]{2,1,0:T(8,128)(2,1)}), bf16[4,96,1152]{2,1,0:T(8,128)(2,1)S(1)}, u32[]{:S(2)}, u32[]{:S(2)}) async-start(bf16[4,96,1152]{2,1,0:T(8,128)(2,1)} %bitcast.22), calls=%async_computation | async-start | bytes 1769472 | tf_op jit(solution)/shard_map/all_to_all | solution.py:808
  315.7 7.1 %collective-permute-start.41 = (bf16[256,256]{1,0:T(8,128)(2,1)}, bf16[256,256]{1,0:T(8,128)(2,1)S(1)}, u32[]{:S(2)}, u32[]{:S(2)}) collective-permute-start(bf16[256,256]{1,0:T(8,128)(2,1)} %get-tuple-element.281), channel_id=1, source_target_pairs={{0,2},{2,0},{4,6},{6,4},{1,3},{3,1},{5,7},{7,5},{8,10},{10,8},{12,... | collective-permute-start | bytes 393224 | tf_op jit(solution)/shard_map/ppermute | solution.py:46
  316.6 13.1 %collective-permute-start.42 = (bf16[256,256]{1,0:T(8,128)(2,1)}, bf16[256,256]{1,0:T(8,128)(2,1)S(1)}, u32[]{:S(2)}, u32[]{:S(2)}) collective-permute-start(bf16[256,256]{1,0:T(8,128)(2,1)} %get-tuple-element.282), channel_id=1, source_target_pairs={{0,4},{2,6},{4,0},{6,2},{1,5},{3,7},{5,1},{7,3},{8,12},{10,14},{12... | collective-permute-start | bytes 393224 | tf_op jit(solution)/shard_map/ppermute | solution.py:46
  319.0 10.8 %collective-permute-start.43 = (bf16[256,256]{1,0:T(8,128)(2,1)}, bf16[256,256]{1,0:T(8,128)(2,1)S(1)}, u32[]{:S(2)}, u32[]{:S(2)}) collective-permute-start(bf16[256,256]{1,0:T(8,128)(2,1)} %get-tuple-element.283), channel_id=1, source_target_pairs={{0,6},{2,4},{4,2},{6,0},{1,7},{3,5},{5,3},{7,1},{8,14},{10,12},{12... | collective-permute-start | bytes 393224 | tf_op jit(solution)/shard_map/ppermute | solution.py:46
  333.4 19.8 %collective-permute-start.49 = (bf16[192,2304]{1,0:T(8,128)(2,1)}, bf16[192,2304]{1,0:T(8,128)(2,1)}, u32[]{:S(2)}, u32[]{:S(2)}) collective-permute-start(bf16[192,2304]{1,0:T(8,128)(2,1)} %get-tuple-element.296), channel_id=1, source_target_pairs={{0,8},{8,0},{16,24},{24,16},{1,9},{9,1},{17,25},{25,17},{2,10},{10... | collective-permute-start | bytes 2654216 | tf_op jit(solution)/shard_map/ppermute | solution.py:46
  334.2 19.5 %collective-permute-start.50 = (bf16[192,2304]{1,0:T(8,128)(2,1)}, bf16[192,2304]{1,0:T(8,128)(2,1)}, u32[]{:S(2)}, u32[]{:S(2)}) collective-permute-start(bf16[192,2304]{1,0:T(8,128)(2,1)} %get-tuple-element.297), channel_id=1, source_target_pairs={{0,16},{8,24},{16,0},{24,8},{1,17},{9,25},{17,1},{25,9},{2,18},{10... | collective-permute-start | bytes 2654216 | tf_op jit(solution)/shard_map/ppermute | solution.py:46
  335.0 25.5 %collective-permute-start.46 = (bf16[128,1536]{1,0:T(8,128)(2,1)}, bf16[128,1536]{1,0:T(8,128)(2,1)}, u32[]{:S(2)}, u32[]{:S(2)}) collective-permute-start(bf16[128,1536]{1,0:T(8,128)(2,1)} %get-tuple-element.291), channel_id=1, source_target_pairs={{0,2},{2,0},{4,6},{6,4},{1,3},{3,1},{5,7},{7,5},{8,10},{10,8},{12,... | collective-permute-start | bytes 1179656 | tf_op jit(solution)/shard_map/ppermute | solution.py:46
  337.1 30.1 %collective-permute-start.47 = (bf16[128,1536]{1,0:T(8,128)(2,1)}, bf16[128,1536]{1,0:T(8,128)(2,1)}, u32[]{:S(2)}, u32[]{:S(2)}) collective-permute-start(bf16[128,1536]{1,0:T(8,128)(2,1)} %get-tuple-element.292), channel_id=1, source_target_pairs={{0,4},{2,6},{4,0},{6,2},{1,5},{3,7},{5,1},{7,3},{8,12},{10,14},{12... | collective-permute-start | bytes 1179656 | tf_op jit(solution)/shard_map/ppermute | solution.py:46
  338.0 29.2 %collective-permute-start.48 = (bf16[128,1536]{1,0:T(8,128)(2,1)S(1)}, bf16[128,1536]{1,0:T(8,128)(2,1)}, u32[]{:S(2)}, u32[]{:S(2)}) collective-permute-start(bf16[128,1536]{1,0:T(8,128)(2,1)S(1)} %get-tuple-element.293), channel_id=1, source_target_pairs={{0,6},{2,4},{4,2},{6,0},{1,7},{3,5},{5,3},{7,1},{8,14},{10,12},{12... | collective-permute-start | bytes 1179656 | tf_op jit(solution)/shard_map/ppermute | solution.py:46
  353.8 13.4 %collective-permute-start.51 = (bf16[384,768]{1,0:T(8,128)(2,1)S(1)}, bf16[384,768]{1,0:T(8,128)(2,1)S(1)}, u32[]{:S(2)}, u32[]{:S(2)}) collective-permute-start(bf16[384,768]{1,0:T(8,128)(2,1)S(1)} %pad_maximum_fusion.26), channel_id=1, source_target_pairs={{0,8},{8,0},{16,24},{24,16},{1,9},{9,1},{17,25},{25,17},{2,10},{10... | collective-permute-start | bytes 1769480 | tf_op jit(solution)/shard_map/ppermute | solution.py:46
  355.3 11.9 %collective-permute-start.52 = (bf16[384,768]{1,0:T(8,128)(2,1)S(1)}, bf16[384,768]{1,0:T(8,128)(2,1)S(1)}, u32[]{:S(2)}, u32[]{:S(2)}) collective-permute-start(bf16[384,768]{1,0:T(8,128)(2,1)S(1)} %pad_maximum_fusion.27), channel_id=1, source_target_pairs={{0,16},{8,24},{16,0},{24,8},{1,17},{9,25},{17,1},{25,9},{2,18},{10... | collective-permute-start | bytes 1769480 | tf_op jit(solution)/shard_map/ppermute | solution.py:46
  368.5 15.6 %collective-permute-start.54 = (bf16[400,1024]{1,0:T(8,128)(2,1)}, bf16[400,1024]{1,0:T(8,128)(2,1)}, u32[]{:S(2)}, u32[]{:S(2)}) collective-permute-start(bf16[400,1024]{1,0:T(8,128)(2,1)} %pad_maximum_fusion.17), channel_id=1, source_target_pairs={{0,8},{8,0},{16,24},{24,16},{1,9},{9,1},{17,25},{25,17},{2,10},{10... | collective-permute-start | bytes 2457608 | tf_op jit(solution)/shard_map/ppermute | solution.py:46
  369.9 14.1 %collective-permute-start.53 = (bf16[384,1024]{1,0:T(8,128)(2,1)}, bf16[384,1024]{1,0:T(8,128)(2,1)}, u32[]{:S(2)}, u32[]{:S(2)}) collective-permute-start(bf16[384,1024]{1,0:T(8,128)(2,1)} %pad_maximum_fusion.18), channel_id=1, source_target_pairs={{0,16},{8,24},{16,0},{24,8},{1,17},{9,25},{17,1},{25,9},{2,18},{10... | collective-permute-start | bytes 2359304 | tf_op jit(solution)/shard_map/ppermute | solution.py:46
  373.4 47.4 %all-to-all-start.1 = ((bf16[4,96,2304]{2,1,0:T(8,128)(2,1)}), bf16[4,96,2304]{2,1,0:T(8,128)(2,1)}, u32[]{:S(2)}, u32[]{:S(2)}) async-start(bf16[4,96,2304]{2,1,0:T(8,128)(2,1)} %bitcast.76), calls=%async_computation.1 | async-start | bytes 3538944 | tf_op jit(solution)/shard_map/all_to_all | solution.py:905
  388.2 13.2 %collective-permute-start.56 = (bf16[208,1792]{1,0:T(8,128)(2,1)}, bf16[208,1792]{1,0:T(8,128)(2,1)}, u32[]{:S(2)}, u32[]{:S(2)}) collective-permute-start(bf16[208,1792]{1,0:T(8,128)(2,1)} %fusion.4), channel_id=1, source_target_pairs={{0,16},{8,24},{16,0},{24,8},{1,17},{9,25},{17,1},{25,9},{2,18},{10... | collective-permute-start | bytes 2236424 | tf_op jit(solution)/shard_map/ppermute | solution.py:46
  389.7 12.5 %collective-permute-start.55 = (bf16[192,1792]{1,0:T(8,128)(2,1)}, bf16[192,1792]{1,0:T(8,128)(2,1)S(1)}, u32[]{:S(2)}, u32[]{:S(2)}) collective-permute-start(bf16[192,1792]{1,0:T(8,128)(2,1)} %pad_maximum_fusion.21), channel_id=1, source_target_pairs={{0,8},{8,0},{16,24},{24,16},{1,9},{9,1},{17,25},{25,17},{2,10},{10... | collective-permute-start | bytes 2064392 | tf_op jit(solution)/shard_map/ppermute | solution.py:46
  420.8 17.2 %collective-permute-start.57 = (bf16[96,1920]{1,0:T(8,128)(2,1)}, bf16[96,1920]{1,0:T(8,128)(2,1)S(1)}, u32[]{:S(2)}, u32[]{:S(2)}) collective-permute-start(bf16[96,1920]{1,0:T(8,128)(2,1)} %get-tuple-element.330), channel_id=1, source_target_pairs={{0,2},{2,0},{4,6},{6,4},{1,3},{3,1},{5,7},{7,5},{8,10},{10,8},{12,... | collective-permute-start | bytes 1105928 | tf_op jit(solution)/shard_map/ppermute | solution.py:46
  420.8 28.4 %collective-permute-start.58 = (bf16[96,1920]{1,0:T(8,128)(2,1)}, bf16[96,1920]{1,0:T(8,128)(2,1)S(1)}, u32[]{:S(2)}, u32[]{:S(2)}) collective-permute-start(bf16[96,1920]{1,0:T(8,128)(2,1)} %get-tuple-element.331), channel_id=1, source_target_pairs={{0,4},{2,6},{4,0},{6,2},{1,5},{3,7},{5,1},{7,3},{8,12},{10,14},{12... | collective-permute-start | bytes 1105928 | tf_op jit(solution)/shard_map/ppermute | solution.py:46
  422.8 26.5 %collective-permute-start.59 = (bf16[96,1920]{1,0:T(8,128)(2,1)}, bf16[96,1920]{1,0:T(8,128)(2,1)S(1)}, u32[]{:S(2)}, u32[]{:S(2)}) collective-permute-start(bf16[96,1920]{1,0:T(8,128)(2,1)} %get-tuple-element.332), channel_id=1, source_target_pairs={{0,6},{2,4},{4,2},{6,0},{1,7},{3,5},{5,3},{7,1},{8,14},{10,12},{12... | collective-permute-start | bytes 1105928 | tf_op jit(solution)/shard_map/ppermute | solution.py:46
  425.2 6.6 %collective-permute-start.60 = (f32[128,1536]{1,0:T(8,128)}, f32[128,1536]{1,0:T(8,128)S(1)}, u32[]{:S(2)}, u32[]{:S(2)}) collective-permute-start(f32[128,1536]{1,0:T(8,128)} %get-tuple-element.335), channel_id=1, source_target_pairs={{0,1},{1,0},{2,3},{3,2},{4,5},{5,4},{6,7},{7,6},{8,9},{9,8},{10,11... | collective-permute-start | bytes 2359304 | tf_op jit(solution)/shard_map/ppermute | solution.py:46
  426.8 8.6 %collective-permute-start.62 = (bf16[128,1536]{1,0:T(8,128)(2,1)S(1)}, bf16[128,1536]{1,0:T(8,128)(2,1)S(1)}, u32[]{:S(2)}, u32[]{:S(2)}) collective-permute-start(bf16[128,1536]{1,0:T(8,128)(2,1)S(1)} %pad_maximum_fusion.33), channel_id=1, source_target_pairs={{0,1},{1,0},{2,3},{3,2},{4,5},{5,4},{6,7},{7,6},{8,9},{9,8},{10,11... | collective-permute-start | bytes 1179656 | tf_op jit(solution)/shard_map/ppermute | solution.py:46
  434.0 2.4 collective-permute-start.61
  (90 other events, 1213.1 us)

commit v7 on v6

--- a/solution.py
+++ b/solution.py
@@ -235,7 +235,7 @@
         wait_all(copies)
 
     rows = jnp.where(step < tiles_each, x_mine[...], x_other[...])
-    gate_up[...] = matmul(rows, gu[...])
+    gate_up[...] = matmul(rows, gu[...]).astype(gate_up.dtype)
 
 
 def backward_tile(tiles_each, gate_up, o_mine, o_other, *refs):
@@ -256,7 +256,8 @@
 
     grads = jnp.where(own, o_mine[...], o_other[...])
     g_act = matmul(grads, down[...])
-    gate, up = gate_up[:, :width], gate_up[:, width:]
+    gate = gate_up[:, :width].astype(jnp.float32)
+    up = gate_up[:, width:].astype(jnp.float32)
     sigmoid_gate = 1.0 / (1.0 + jnp.exp(-gate))
     silu_gate = gate * sigmoid_gate
     act_ref[...] = (silu_gate * up).astype(jnp.bfloat16)
@@ -327,15 +328,15 @@
 
 def weight_grad(x_mine, x_other, grads):
     count, model_width = x_mine.shape
-    tile = model_width // 4
+    tile = model_width // 3
     columns = pl.BlockSpec((count, tile), lambda i: (0, i))
     return pl.pallas_call(
         weight_tile,
-        grid=(4,),
+        grid=(3,),
         in_specs=[columns, columns, pl.BlockSpec(grads.shape, lambda i: (0, 0))],
         out_specs=pl.BlockSpec((tile, grads.shape[1]), lambda i: (i, 0)),
         out_shape=jax.ShapeDtypeStruct((model_width, grads.shape[1]), jnp.bfloat16),
-        compiler_params=pltpu.CompilerParams(vmem_limit_bytes=24 * 1024 * 1024),
+        compiler_params=pltpu.CompilerParams(vmem_limit_bytes=28 * 1024 * 1024),
         cost_estimate=LITTLE,
         name="weight_grad",
     )(x_mine, x_other, grads)
@@ -765,11 +766,11 @@
         [],
         [(normed_mine, normed_other)],
         mlp_parts,
-        [(2 * width, jnp.float32)],
+        [(2 * width, jnp.bfloat16)],
         [],
         [(model_width, 2 * width)],
         "gate_up",
-        26,
+        22,
     )
     grad_parts, gate_up = together(gather_ctx(grad_half), gate_up)
     grad_mine = jnp.concatenate(grad_parts, 0)
@@ -784,7 +785,7 @@
         [model_width, model_width],
         [(model_width, 2 * width), (model_width, width)],
         "mlp_back",
-        42,
+        39,
     )
     back_got = swap(back_send, "wt", 1)
     out_got = swap(out_send, "wt", 1)

time: 462 us -> 460 us (level)
    unnamed x184 -> x180, local copies, waits for them, and re-layouts: 22.1 us -> 20.7 us
  transfers between devices with their start and end apart: 66 -> 66, of which waited for: 33 -> 32; matrix products, arithmetic and copies ran while one was open for 12% -> 12% of each run, Pallas kernels for 12% -> 12%
where the time goes in v7:
time: 460 us; the launch traced here: 451 us
  waiting for transfers between devices  182 us (40%)
  starting transfers between devices  97.3 us (21%)
  Pallas kernels  81.9 us (18%)
  local copies, waits for them, and re-layouts  42.1 us (9%)
  other arithmetic  39.7 us (9%)
  between operations  7.49 us (2%)
    ppermute x64, waiting for transfers between devices, swap(): return lax.ppermute(values, axis, [(i, i ^ offset) for i in range(size)])  166 us
    ppermute x64, starting transfers between devices, swap(): return lax.ppermute(values, axis, [(i, i ^ offset) for i in range(size)])  85 us
    pallas_call x12, Pallas kernels, call(): pl.pallas_call(body, in_specs=in_specs or [whole] * len(args), out_specs=...  34.8 us
    pallas_call x2, Pallas kernels, by_tiles(): pl.pallas_call(functools.partial(body, tiles_each), grid=(2 * tiles_each,...  33.9 us
    unnamed x180, local copies, waits for them, and re-layouts  20.7 us
    all_to_all x1, waiting for transfers between devices, on_device(): gate_up_back = lax.all_to_all(gate_up_blocks, 'ctx', 0, 0, tiled=True)  14.7 us
    pallas_call x2, Pallas kernels, weight_grad(): pl.pallas_call(weight_tile, grid=(3,), in_specs=[columns, columns, pl.Blo...  13.2 us
  transfers between devices with their start and end apart: 66, of which 32 were waited for; matrix products, arithmetic and copies ran while one was open for 12% of the time, Pallas kernels for 12%

profile of v7, /device:TPU:0, one launch (start us, length us, event | category | flops | bytes accessed | tf_op | source)
XLA Modules:
  0.0 450.7 jit_solution(10271261508283189909)
XLA Ops:
  0.6 1.8 side_by_side.1.refs_0_
  2.4 3.0 collective-permute-start
  5.4 2.6 collective-permute-start.1
  14.7 2.5 dynamic-slice_bitcast_fusion
  25.4 2.6 constant_dynamic-slice_fusion.16.inputs
  28.9 3.4 collective-permute-done.1.refs_2_
  33.0 1.6 collective-permute-start.3
  34.6 1.5 collective-permute-start.4
  36.1 6.5 %collective-permute-start.5 = (bf16[96,2304]{1,0:T(8,128)(2,1)S(1)}, bf16[96,2304]{1,0:T(8,128)(2,1)S(1)}, u32[]{:S(2)}, u32[]{:S(2)}) collective-permute-start(bf16[96,2304]{1,0:T(8,128)(2,1)S(1)} %copy-done.63), channel_id=1, source_target_pairs={{0,2},{2,0},{4,6},{6,4},{1,3},{3,1},{5,7},{7,5},{8,10},{10,8},{12,... | collective-permute-start | bytes 1327112 | tf_op jit(solution)/shard_map/ppermute | solution.py:46
  45.1 13.9 %collective-permute-done.5.refs_1_ = bf16[96,2304]{1,0:T(8,128)(2,1)S(1)} collective-permute-done((bf16[96,2304]{1,0:T(8,128)(2,1)S(1)}, bf16[96,2304]{1,0:T(8,128)(2,1)S(1)}, u32[]{:S(2)}, u32[]{:S(2)}) %collective-permute-start.5) | collective-permute-done | bytes 442400 | tf_op jit(solution)/shard_map/ppermute | solution.py:46
  59.0 16.7 %collective-permute-done.6.refs_2_ = bf16[96,2304]{1,0:T(8,128)(2,1)S(1)} collective-permute-done((bf16[96,2304]{1,0:T(8,128)(2,1)S(1)}, bf16[96,2304]{1,0:T(8,128)(2,1)S(1)}, u32[]{:S(2)}, u32[]{:S(2)}) %collective-permute-start.6) | collective-permute-done | bytes 442400 | tf_op jit(solution)/shard_map/ppermute | solution.py:46
  76.9 6.9 %collective-permute-start.10 = (bf16[96,1152]{1,0:T(8,128)(2,1)S(1)}, bf16[96,1152]{1,0:T(8,128)(2,1)S(1)}, u32[]{:S(2)}, u32[]{:S(2)}) collective-permute-start(bf16[96,1152]{1,0:T(8,128)(2,1)S(1)} %copy-done.72), channel_id=1, source_target_pairs={{0,2},{2,0},{4,6},{6,4},{1,3},{3,1},{5,7},{7,5},{8,10},{10,8},{12,... | collective-permute-start | bytes 663560 | tf_op jit(solution)/shard_map/ppermute | solution.py:46
  88.5 2.3 project.1
  90.8 1.7 copy-done.8
  93.9 6.1 %collective-permute-done.11.refs_2_ = bf16[96,1152]{1,0:T(8,128)(2,1)S(1)} collective-permute-done((bf16[96,1152]{1,0:T(8,128)(2,1)S(1)}, bf16[96,1152]{1,0:T(8,128)(2,1)S(1)}, u32[]{:S(2)}, u32[]{:S(2)}) %collective-permute-start.11) | collective-permute-done | bytes 221216 | tf_op jit(solution)/shard_map/ppermute | solution.py:46
  101.4 2.9 collective-permute-start.13
  115.3 5.9 %attend.1 = (bf16[256,768]{1,0:T(8,128)(2,1)S(1)}, f32[256,768]{1,0:T(8,128)S(1)}, f32[128,1536]{1,0:T(8,128)S(1)}, f32[128,1536]{1,0:T(8,128)S(1)}) custom-call(s32[1]{0:T(128)} %bitcast.core_ref, bf16[256,768]{1,0:T(8,128)(2,1)S(1)} %copy-done.15, s32[256,1]{1,0:T(8,128)S(1)} %copy.30.query_pos, s32[1,1024]{1,0:T(1,128)S(1)} %bitcast.74, ...), custom_call_target="tpu_custom_call" | custom-call | flops 1 | bytes 1 | tf_op jit(solution)/shard_map/attend/pallas_call | solution.py:352
  121.3 2.3 collective-permute-done.16.got
  123.9 1.6 collective-permute-done.17.refs_1_
  127.4 1.5 collective-permute-start.23
  129.5 2.4 collective-permute-start.20
  133.3 11.5 %collective-permute-done.19 = bf16[128,1536]{1,0:T(8,128)(2,1)S(1)} collective-permute-done((bf16[128,1536]{1,0:T(8,128)(2,1)S(1)}, bf16[128,1536]{1,0:T(8,128)(2,1)S(1)}, u32[]{:S(2)}, u32[]{:S(2)}) %collective-permute-start.19) | collective-permute-done | bytes 393248 | tf_op jit(solution)/shard_map/ppermute | solution.py:46
  144.8 14.5 %collective-permute-done.20 = bf16[128,1536]{1,0:T(8,128)(2,1)S(1)} collective-permute-done((bf16[128,1536]{1,0:T(8,128)(2,1)S(1)}, bf16[128,1536]{1,0:T(8,128)(2,1)S(1)}, u32[]{:S(2)}, u32[]{:S(2)}) %collective-permute-start.20) | collective-permute-done | bytes 393248 | tf_op jit(solution)/shard_map/ppermute | solution.py:46
  159.3 5.4 %collective-permute-done.22.refs_4_ = bf16[384,2304]{1,0:T(8,128)(2,1)S(1)} collective-permute-done((bf16[384,2304]{1,0:T(8,128)(2,1)S(1)}, bf16[384,2304]{1,0:T(8,128)(2,1)S(1)}, u32[]{:S(2)}, u32[]{:S(2)}) %collective-permute-start.22) | collective-permute-done | bytes 1769504 | tf_op jit(solution)/shard_map/ppermute | solution.py:46
  169.6 2.0 collective-permute-start.25
  174.0 24.6 %collective-permute-done.28.refs_6_ = bf16[192,3456]{1,0:T(8,128)(2,1)S(1)} collective-permute-done((bf16[192,3456]{1,0:T(8,128)(2,1)S(1)}, bf16[192,3456]{1,0:T(8,128)(2,1)S(1)}, u32[]{:S(2)}, u32[]{:S(2)}) %collective-permute-start.28) | collective-permute-done | bytes 1327136 | tf_op jit(solution)/shard_map/ppermute | solution.py:46
  199.2 9.9 %gate_up.1 = bf16[1024,2304]{1,0:T(8,128)(2,1)S(1)} custom-call(bf16[512,1536]{1,0:T(8,128)(2,1)S(1)} %constant_dynamic-update-slice_fusion.1.x_mine, bf16[512,1536]{1,0:T(8,128)(2,1)S(1)} %collective-permute-done.24.x_other, bf16[384,1152]{1,0:T(8,128)(2,1)} %get-tuple-element.228.refs_0_, bf16[384,1152]{1,0:T(8,128)(2,1)S(1)} %collective-permute-done.17.refs_1_, ...), custom_call_target="tpu_custom_call" | custom-call | flops 1 | bytes 1 | tf_op jit(solution)/shard_map/gate_up/pallas_call | solution.py:300
  209.1 2.1 copy-done.1
  211.5 3.4 collective-permute-done.30.o_other.x_other
  214.9 24.0 %mlp_back.1 = (bf16[1024,2304]{1,0:T(8,128)(2,1)}, bf16[1024,1152]{1,0:T(8,128)(2,1)}, f32[512,1536]{1,0:T(8,128)}, bf16[512,1536]{1,0:T(8,128)(2,1)S(1)}, f32[5...) custom-call(bf16[1024,2304]{1,0:T(8,128)(2,1)} %copy-done.1, ...), custom_call_target="tpu_custom_call" | custom-call | flops 1 | bytes 1 | tf_op jit(solution)/shard_map/mlp_back/pallas_call | solution.py:300
  239.5 1.7 copy-done.11
  241.1 5.0 %weight_grad.2 = bf16[1536,1152]{1,0:T(8,128)(2,1)S(1)} custom-call(bf16[512,1536]{1,0:T(8,128)(2,1)S(1)} %constant_dynamic-update-slice_fusion.5.o_mine.x_mine, bf16[512,1536]{1,0:T(8,128)(2,1)S(1)} %collective-permute-done.30.o_other.x_other, bf16[1024,1152]{1,0:T(8,128)(2,1)S(1)} %copy-done.11), custom_call_target="tpu_custom_call" | custom-call | flops 1 | bytes 1 | tf_op jit(solution)/shard_map/weight_grad/pallas_call | solution.py:333
  247.5 1.8 collective-permute-start.33
  253.5 1.6 collective-permute-start.37
  255.1 8.2 %weight_grad.3 = bf16[1536,2304]{1,0:T(8,128)(2,1)S(1)} custom-call(bf16[512,1536]{1,0:T(8,128)(2,1)S(1)} %constant_dynamic-update-slice_fusion.1.x_mine, bf16[512,1536]{1,0:T(8,128)(2,1)S(1)} %collective-permute-done.24.x_other, bf16[1024,2304]{1,0:T(8,128)(2,1)S(1)} %bitcast.73), custom_call_target="tpu_custom_call" | custom-call | flops 1 | bytes 1 | tf_op jit(solution)/shard_map/weight_grad/pallas_call | solution.py:333
  263.8 1.6 fusion.39
  265.4 7.6 %collective-permute-done.36 = bf16[384,1152]{1,0:T(8,128)(2,1)S(1)} collective-permute-done((bf16[384,1152]{1,0:T(8,128)(2,1)S(1)}, bf16[384,1152]{1,0:T(8,128)(2,1)S(1)}, u32[]{:S(2)}, u32[]{:S(2)}) %collective-permute-start.36) | collective-permute-done | bytes 884768 | tf_op jit(solution)/shard_map/ppermute | solution.py:46
  278.4 6.7 %collective-permute-done.38 = bf16[192,1152]{1,0:T(8,128)(2,1)S(1)} collective-permute-done((bf16[192,1152]{1,0:T(8,128)(2,1)S(1)}, bf16[192,1152]{1,0:T(8,128)(2,1)S(1)}, u32[]{:S(2)}, u32[]{:S(2)}) %collective-permute-start.38) | collective-permute-done | bytes 442400 | tf_op jit(solution)/shard_map/ppermute | solution.py:46
  286.6 1.7 collective-permute-start.44
  288.3 1.5 collective-permute-start.45
  289.8 4.0 all-to-all-start
  293.8 3.4 mlp_norm_back.1
  297.2 1.9 collective-permute-done.40.branch_other
  299.9 11.8 %attend_back.1 = (bf16[256,768]{1,0:T(8,128)(2,1)}, bf16[1536,768]{1,0:T(8,128)(2,1)}, f32[256,256]{1,0:T(8,128)}, bf16[256,256]{1,0:T(8,128)(2,1)}, bf16[256,256]{1,0:T(8,128)(2,1)}, /*index=5*/bf16[256,256]{1,0:T(8,128)(2,1)}) custom-call(s32[1]{0:T(128)} %bitcast.core_ref, bf16[128,1536]{1,0:T(8,128)(2,1)} %get-tuple-element.272.branch_mine, ...), custom_call_target="tpu_custom_call" | custom-call | flops 1 | bytes 1 | tf_op jit(solution)/shard_map/attend_back/pallas_call | solution.py:352
  313.8 2.4 collective-permute-start.42
  318.2 1.9 collective-permute-done.41.refs_1_
  320.1 6.8 %collective-permute-done.42.refs_2_ = bf16[256,256]{1,0:T(8,128)(2,1)S(1)} collective-permute-done((bf16[256,256]{1,0:T(8,128)(2,1)}, bf16[256,256]{1,0:T(8,128)(2,1)S(1)}, u32[]{:S(2)}, u32[]{:S(2)}) %collective-permute-start.42) | collective-permute-done | bytes 131104 | tf_op jit(solution)/shard_map/ppermute | solution.py:46
  327.0 3.7 add_convert_fusion.4
  332.2 2.1 collective-permute-start.46
  336.7 5.1 %project_back.1 = (bf16[256,1024]{1,0:T(8,128)(2,1)}, f32[1,1024]{1,0:T(1,128)}, f32[1,1536]{1,0:T(1,128)}, f32[128,1536]{1,0:T(8,128)}, f32[128,1536]{1,0:T(8,128)}) custom-call(s32[1]{0:T(128)} %bitcast.core_ref, bf16[256,768]{1,0:T(8,128)(2,1)} %get-tuple-element.302.query_lin, bf16[1536,1024]{1,0:T(8,128)(2,1)} %copy-done.8, f32[256,128]{1,0:T(8,128)} %copy-done.12, ...), custom_call_target="tpu_custom_call" | custom-call | flops 1 | bytes 1 | tf_op jit(solution)/shard_map/project_back/pallas_call | solution.py:352
  347.0 3.5 collective-permute-done.49
  353.0 3.3 add_convert_fusion.3
  357.7 6.7 %collective-permute-done.47 = bf16[128,1536]{1,0:T(8,128)(2,1)} collective-permute-done((bf16[128,1536]{1,0:T(8,128)(2,1)}, bf16[128,1536]{1,0:T(8,128)(2,1)}, u32[]{:S(2)}, u32[]{:S(2)}) %collective-permute-start.47) | collective-permute-done | bytes 393248 | tf_op jit(solution)/shard_map/ppermute | solution.py:46
  367.1 1.5 collective-permute-start.53
  368.6 2.1 add_convert_fusion.13
  370.7 8.3 %all-to-all-start.1 = ((bf16[4,96,2304]{2,1,0:T(8,128)(2,1)}), bf16[4,96,2304]{2,1,0:T(8,128)(2,1)}, u32[]{:S(2)}, u32[]{:S(2)}) async-start(bf16[4,96,2304]{2,1,0:T(8,128)(2,1)} %bitcast.76), calls=%async_computation.1 | async-start | bytes 3538944 | tf_op jit(solution)/shard_map/all_to_all | solution.py:906
  379.0 2.2 collective-permute-done.53
  391.0 7.5 %collective-permute-done.56 = bf16[208,1792]{1,0:T(8,128)(2,1)} collective-permute-done((bf16[208,1792]{1,0:T(8,128)(2,1)}, bf16[208,1792]{1,0:T(8,128)(2,1)}, u32[]{:S(2)}, u32[]{:S(2)}) %collective-permute-start.56) | collective-permute-done | bytes 745504 | tf_op jit(solution)/shard_map/ppermute | solution.py:46
  399.3 1.7 convert_add_fusion
  403.2 14.7 %all-to-all-done.1 = bf16[4,96,2304]{2,1,0:T(8,128)(2,1)} async-done(((bf16[4,96,2304]{2,1,0:T(8,128)(2,1)}), bf16[4,96,2304]{2,1,0:T(8,128)(2,1)}, u32[]{:S(2)}, u32[]{:S(2)}) %all-to-all-start.1) | async-done | bytes 1769504 | tf_op jit(solution)/shard_map/all_to_all | solution.py:906
  417.9 2.0 collective-permute-start.58
  420.0 2.3 collective-permute-start.59
  424.5 1.5 slice_bitcast_fusion.3
  435.2 11.1 %collective-permute-done.58 = bf16[96,1920]{1,0:T(8,128)(2,1)S(1)} collective-permute-done((bf16[96,1920]{1,0:T(8,128)(2,1)}, bf16[96,1920]{1,0:T(8,128)(2,1)S(1)}, u32[]{:S(2)}, u32[]{:S(2)}) %collective-permute-start.58) | collective-permute-done | bytes 368672 | tf_op jit(solution)/shard_map/ppermute | solution.py:46
  (380 shorter events, 107.3 us)
Async XLA Ops:
  2.4 26.4 %collective-permute-start = (bf16[96,1792]{1,0:T(8,128)(2,1)}, bf16[96,1792]{1,0:T(8,128)(2,1)S(1)}, u32[]{:S(2)}, u32[]{:S(2)}) collective-permute-start(bf16[96,1792]{1,0:T(8,128)(2,1)} %side_by_side.1.refs_0_), channel_id=1, source_target_pairs={{0,2},{2,0},{4,6},{6,4},{1,3},{3,1},{5,7},{7,5},{8,10},{10,8},{12,... | collective-permute-start | bytes 1032200 | tf_op jit(solution)/shard_map/ppermute | solution.py:46
  5.4 26.8 %collective-permute-start.1 = (bf16[96,1792]{1,0:T(8,128)(2,1)}, bf16[96,1792]{1,0:T(8,128)(2,1)S(1)}, u32[]{:S(2)}, u32[]{:S(2)}) collective-permute-start(bf16[96,1792]{1,0:T(8,128)(2,1)} %side_by_side.1.refs_0_), channel_id=1, source_target_pairs={{0,4},{2,6},{4,0},{6,2},{1,5},{3,7},{5,1},{7,3},{8,12},{10,14},{12... | collective-permute-start | bytes 1032200 | tf_op jit(solution)/shard_map/ppermute | solution.py:46
  8.0 24.3 %collective-permute-start.2 = (bf16[96,1792]{1,0:T(8,128)(2,1)}, bf16[96,1792]{1,0:T(8,128)(2,1)S(1)}, u32[]{:S(2)}, u32[]{:S(2)}) collective-permute-start(bf16[96,1792]{1,0:T(8,128)(2,1)} %side_by_side.1.refs_0_), channel_id=1, source_target_pairs={{0,6},{2,4},{4,2},{6,0},{1,7},{3,5},{5,3},{7,1},{8,14},{10,12},{12... | collective-permute-start | bytes 1032200 | tf_op jit(solution)/shard_map/ppermute | solution.py:46
  33.0 42.6 %collective-permute-start.3 = (bf16[384,1792]{1,0:T(8,128)(2,1)S(1)}, bf16[384,1792]{1,0:T(8,128)(2,1)S(1)}, u32[]{:S(2)}, u32[]{:S(2)}) collective-permute-start(bf16[384,1792]{1,0:T(8,128)(2,1)S(1)} %place.3.refs_0_), channel_id=1, source_target_pairs={{0,8},{8,0},{16,24},{24,16},{1,9},{9,1},{17,25},{25,17},{2,10},{10... | collective-permute-start | bytes 4128776 | tf_op jit(solution)/shard_map/ppermute | solution.py:46
  34.6 41.0 %collective-permute-start.4 = (bf16[384,1792]{1,0:T(8,128)(2,1)S(1)}, bf16[384,1792]{1,0:T(8,128)(2,1)S(1)}, u32[]{:S(2)}, u32[]{:S(2)}) collective-permute-start(bf16[384,1792]{1,0:T(8,128)(2,1)S(1)} %place.3.refs_0_), channel_id=1, source_target_pairs={{0,16},{8,24},{16,0},{24,8},{1,17},{9,25},{17,1},{25,9},{2,18},{10... | collective-permute-start | bytes 4128776 | tf_op jit(solution)/shard_map/ppermute | solution.py:46
  36.1 22.8 %collective-permute-start.5 = (bf16[96,2304]{1,0:T(8,128)(2,1)S(1)}, bf16[96,2304]{1,0:T(8,128)(2,1)S(1)}, u32[]{:S(2)}, u32[]{:S(2)}) collective-permute-start(bf16[96,2304]{1,0:T(8,128)(2,1)S(1)} %copy-done.63), channel_id=1, source_target_pairs={{0,2},{2,0},{4,6},{6,4},{1,3},{3,1},{5,7},{7,5},{8,10},{10,8},{12,... | collective-permute-start | bytes 1327112 | tf_op jit(solution)/shard_map/ppermute | solution.py:46
  42.6 33.0 %collective-permute-start.6 = (bf16[96,2304]{1,0:T(8,128)(2,1)S(1)}, bf16[96,2304]{1,0:T(8,128)(2,1)S(1)}, u32[]{:S(2)}, u32[]{:S(2)}) collective-permute-start(bf16[96,2304]{1,0:T(8,128)(2,1)S(1)} %copy-done.62), channel_id=1, source_target_pairs={{0,4},{2,6},{4,0},{6,2},{1,5},{3,7},{5,1},{7,3},{8,12},{10,14},{12... | collective-permute-start | bytes 1327112 | tf_op jit(solution)/shard_map/ppermute | solution.py:46
  43.7 31.9 %collective-permute-start.7 = (bf16[96,2304]{1,0:T(8,128)(2,1)S(1)}, bf16[96,2304]{1,0:T(8,128)(2,1)S(1)}, u32[]{:S(2)}, u32[]{:S(2)}) collective-permute-start(bf16[96,2304]{1,0:T(8,128)(2,1)S(1)} %pad_maximum_fusion.31), channel_id=1, source_target_pairs={{0,6},{2,4},{4,2},{6,0},{1,7},{3,5},{5,3},{7,1},{8,14},{10,12},{12... | collective-permute-start | bytes 1327112 | tf_op jit(solution)/shard_map/ppermute | solution.py:46
  75.7 12.8 %collective-permute-start.8 = (bf16[192,1792]{1,0:T(8,128)(2,1)S(1)}, bf16[192,1792]{1,0:T(8,128)(2,1)S(1)}, u32[]{:S(2)}, u32[]{:S(2)}) collective-permute-start(bf16[192,1792]{1,0:T(8,128)(2,1)S(1)} %slice.302), channel_id=1, source_target_pairs={{0,8},{8,0},{16,24},{24,16},{1,9},{9,1},{17,25},{25,17},{2,10},{10... | collective-permute-start | bytes 2064392 | tf_op jit(solution)/shard_map/ppermute | solution.py:46
  76.3 12.1 %collective-permute-start.9 = (bf16[192,1792]{1,0:T(8,128)(2,1)S(1)}, bf16[192,1792]{1,0:T(8,128)(2,1)S(1)}, u32[]{:S(2)}, u32[]{:S(2)}) collective-permute-start(bf16[192,1792]{1,0:T(8,128)(2,1)S(1)} %slice.303), channel_id=1, source_target_pairs={{0,16},{8,24},{16,0},{24,8},{1,17},{9,25},{17,1},{25,9},{2,18},{10... | collective-permute-start | bytes 2064392 | tf_op jit(solution)/shard_map/ppermute | solution.py:46
  76.9 16.3 %collective-permute-start.10 = (bf16[96,1152]{1,0:T(8,128)(2,1)S(1)}, bf16[96,1152]{1,0:T(8,128)(2,1)S(1)}, u32[]{:S(2)}, u32[]{:S(2)}) collective-permute-start(bf16[96,1152]{1,0:T(8,128)(2,1)S(1)} %copy-done.72), channel_id=1, source_target_pairs={{0,2},{2,0},{4,6},{6,4},{1,3},{3,1},{5,7},{7,5},{8,10},{10,8},{12,... | collective-permute-start | bytes 663560 | tf_op jit(solution)/shard_map/ppermute | solution.py:46
  83.8 16.2 %collective-permute-start.11 = (bf16[96,1152]{1,0:T(8,128)(2,1)S(1)}, bf16[96,1152]{1,0:T(8,128)(2,1)S(1)}, u32[]{:S(2)}, u32[]{:S(2)}) collective-permute-start(bf16[96,1152]{1,0:T(8,128)(2,1)S(1)} %copy-done.71), channel_id=1, source_target_pairs={{0,4},{2,6},{4,0},{6,2},{1,5},{3,7},{5,1},{7,3},{8,12},{10,14},{12... | collective-permute-start | bytes 663560 | tf_op jit(solution)/shard_map/ppermute | solution.py:46
  84.9 15.9 %collective-permute-start.12 = (bf16[96,1152]{1,0:T(8,128)(2,1)S(1)}, bf16[96,1152]{1,0:T(8,128)(2,1)S(1)}, u32[]{:S(2)}, u32[]{:S(2)}) collective-permute-start(bf16[96,1152]{1,0:T(8,128)(2,1)S(1)} %copy-done.70), channel_id=1, source_target_pairs={{0,6},{2,4},{4,2},{6,0},{1,7},{3,5},{5,3},{7,1},{8,14},{10,12},{12... | collective-permute-start | bytes 663560 | tf_op jit(solution)/shard_map/ppermute | solution.py:46
  101.4 13.1 %collective-permute-start.13 = (bf16[256,256]{1,0:T(8,128)(2,1)}, bf16[256,256]{1,0:T(8,128)(2,1)S(1)}, u32[]{:S(2)}, u32[]{:S(2)}) collective-permute-start(bf16[256,256]{1,0:T(8,128)(2,1)} %get-tuple-element.218.refs_0_), channel_id=1, source_target_pairs={{0,2},{2,0},{4,6},{6,4},{1,3},{3,1},{5,7},{7,5},{8,10},{10,8},{12,... | collective-permute-start | bytes 393224 | tf_op jit(solution)/shard_map/ppermute | solution.py:46
  104.3 10.8 %collective-permute-start.14 = (bf16[256,256]{1,0:T(8,128)(2,1)}, bf16[256,256]{1,0:T(8,128)(2,1)}, u32[]{:S(2)}, u32[]{:S(2)}) collective-permute-start(bf16[256,256]{1,0:T(8,128)(2,1)} %get-tuple-element.218.refs_0_), channel_id=1, source_target_pairs={{0,4},{2,6},{4,0},{6,2},{1,5},{3,7},{5,1},{7,3},{8,12},{10,14},{12... | collective-permute-start | bytes 393224 | tf_op jit(solution)/shard_map/ppermute | solution.py:46
  105.2 9.8 %collective-permute-start.15 = (bf16[256,256]{1,0:T(8,128)(2,1)}, bf16[256,256]{1,0:T(8,128)(2,1)}, u32[]{:S(2)}, u32[]{:S(2)}) collective-permute-start(bf16[256,256]{1,0:T(8,128)(2,1)} %get-tuple-element.218.refs_0_), channel_id=1, source_target_pairs={{0,6},{2,4},{4,2},{6,0},{1,7},{3,5},{5,3},{7,1},{8,14},{10,12},{12... | collective-permute-start | bytes 393224 | tf_op jit(solution)/shard_map/ppermute | solution.py:46
  106.7 18.8 %collective-permute-start.17 = (bf16[384,1152]{1,0:T(8,128)(2,1)}, bf16[384,1152]{1,0:T(8,128)(2,1)S(1)}, u32[]{:S(2)}, u32[]{:S(2)}) collective-permute-start(bf16[384,1152]{1,0:T(8,128)(2,1)} %get-tuple-element.228.refs_0_), channel_id=1, source_target_pairs={{0,8},{8,0},{16,24},{24,16},{1,9},{9,1},{17,25},{25,17},{2,10},{10... | collective-permute-start | bytes 2654216 | tf_op jit(solution)/shard_map/ppermute | solution.py:46
  108.2 18.6 %collective-permute-start.18 = (bf16[384,1152]{1,0:T(8,128)(2,1)}, bf16[384,1152]{1,0:T(8,128)(2,1)}, u32[]{:S(2)}, u32[]{:S(2)}) collective-permute-start(bf16[384,1152]{1,0:T(8,128)(2,1)} %get-tuple-element.228.refs_0_), channel_id=1, source_target_pairs={{0,16},{8,24},{16,0},{24,8},{1,17},{9,25},{17,1},{25,9},{2,18},{10... | collective-permute-start | bytes 2654216 | tf_op jit(solution)/shard_map/ppermute | solution.py:46
  121.2 2.4 collective-permute-start.16
  126.8 37.8 %collective-permute-start.22 = (bf16[384,2304]{1,0:T(8,128)(2,1)S(1)}, bf16[384,2304]{1,0:T(8,128)(2,1)S(1)}, u32[]{:S(2)}, u32[]{:S(2)}) collective-permute-start(bf16[384,2304]{1,0:T(8,128)(2,1)S(1)} %place.5.refs_3_), channel_id=1, source_target_pairs={{0,8},{8,0},{16,24},{24,16},{1,9},{9,1},{17,25},{25,17},{2,10},{10... | collective-permute-start | bytes 5308424 | tf_op jit(solution)/shard_map/ppermute | solution.py:46
  127.4 38.3 %collective-permute-start.23 = (bf16[384,2304]{1,0:T(8,128)(2,1)S(1)}, bf16[384,2304]{1,0:T(8,128)(2,1)S(1)}, u32[]{:S(2)}, u32[]{:S(2)}) collective-permute-start(bf16[384,2304]{1,0:T(8,128)(2,1)S(1)} %place.5.refs_3_), channel_id=1, source_target_pairs={{0,16},{8,24},{16,0},{24,8},{1,17},{9,25},{17,1},{25,9},{2,18},{10... | collective-permute-start | bytes 5308424 | tf_op jit(solution)/shard_map/ppermute | solution.py:46
  128.9 15.9 %collective-permute-start.19 = (bf16[128,1536]{1,0:T(8,128)(2,1)S(1)}, bf16[128,1536]{1,0:T(8,128)(2,1)S(1)}, u32[]{:S(2)}, u32[]{:S(2)}) collective-permute-start(bf16[128,1536]{1,0:T(8,128)(2,1)S(1)} %get-tuple-element.232), channel_id=1, source_target_pairs={{0,2},{2,0},{4,6},{6,4},{1,3},{3,1},{5,7},{7,5},{8,10},{10,8},{12,... | collective-permute-start | bytes 1179656 | tf_op jit(solution)/shard_map/ppermute | solution.py:46
  129.5 29.8 %collective-permute-start.20 = (bf16[128,1536]{1,0:T(8,128)(2,1)S(1)}, bf16[128,1536]{1,0:T(8,128)(2,1)S(1)}, u32[]{:S(2)}, u32[]{:S(2)}) collective-permute-start(bf16[128,1536]{1,0:T(8,128)(2,1)S(1)} %get-tuple-element.232), channel_id=1, source_target_pairs={{0,4},{2,6},{4,0},{6,2},{1,5},{3,7},{5,1},{7,3},{8,12},{10,14},{12... | collective-permute-start | bytes 1179656 | tf_op jit(solution)/shard_map/ppermute | solution.py:46
  131.8 27.4 %collective-permute-start.21 = (bf16[128,1536]{1,0:T(8,128)(2,1)S(1)}, bf16[128,1536]{1,0:T(8,128)(2,1)S(1)}, u32[]{:S(2)}, u32[]{:S(2)}) collective-permute-start(bf16[128,1536]{1,0:T(8,128)(2,1)S(1)} %get-tuple-element.232), channel_id=1, source_target_pairs={{0,6},{2,4},{4,2},{6,0},{1,7},{3,5},{5,3},{7,1},{8,14},{10,12},{12... | collective-permute-start | bytes 1179656 | tf_op jit(solution)/shard_map/ppermute | solution.py:46
  165.8 3.8 collective-permute-start.24
  167.4 31.3 %collective-permute-start.28 = (bf16[192,3456]{1,0:T(8,128)(2,1)S(1)}, bf16[192,3456]{1,0:T(8,128)(2,1)S(1)}, u32[]{:S(2)}, u32[]{:S(2)}) collective-permute-start(bf16[192,3456]{1,0:T(8,128)(2,1)S(1)} %pad_maximum_fusion.4), channel_id=1, source_target_pairs={{0,8},{8,0},{16,24},{24,16},{1,9},{9,1},{17,25},{25,17},{2,10},{10... | collective-permute-start | bytes 3981320 | tf_op jit(solution)/shard_map/ppermute | solution.py:46
  168.2 31.0 %collective-permute-start.29 = (bf16[192,3456]{1,0:T(8,128)(2,1)S(1)}, bf16[192,3456]{1,0:T(8,128)(2,1)S(1)}, u32[]{:S(2)}, u32[]{:S(2)}) collective-permute-start(bf16[192,3456]{1,0:T(8,128)(2,1)S(1)} %pad_maximum_fusion.3), channel_id=1, source_target_pairs={{0,16},{8,24},{16,0},{24,8},{1,17},{9,25},{17,1},{25,9},{2,18},{10... | collective-permute-start | bytes 3981320 | tf_op jit(solution)/shard_map/ppermute | solution.py:46
  169.6 41.7 %collective-permute-start.25 = (bf16[128,1536]{1,0:T(8,128)(2,1)S(1)}, bf16[128,1536]{1,0:T(8,128)(2,1)S(1)}, u32[]{:S(2)}, u32[]{:S(2)}) collective-permute-start(bf16[128,1536]{1,0:T(8,128)(2,1)S(1)} %copy-done.42), channel_id=1, source_target_pairs={{0,2},{2,0},{4,6},{6,4},{1,3},{3,1},{5,7},{7,5},{8,10},{10,8},{12,... | collective-permute-start | bytes 1179656 | tf_op jit(solution)/shard_map/ppermute | solution.py:46
  171.6 39.7 %collective-permute-start.26 = (bf16[128,1536]{1,0:T(8,128)(2,1)S(1)}, bf16[128,1536]{1,0:T(8,128)(2,1)S(1)}, u32[]{:S(2)}, u32[]{:S(2)}) collective-permute-start(bf16[128,1536]{1,0:T(8,128)(2,1)S(1)} %copy-done.42), channel_id=1, source_target_pairs={{0,4},{2,6},{4,0},{6,2},{1,5},{3,7},{5,1},{7,3},{8,12},{10,14},{12... | collective-permute-start | bytes 1179656 | tf_op jit(solution)/shard_map/ppermute | solution.py:46
  172.6 38.7 %collective-permute-start.27 = (bf16[128,1536]{1,0:T(8,128)(2,1)S(1)}, bf16[128,1536]{1,0:T(8,128)(2,1)S(1)}, u32[]{:S(2)}, u32[]{:S(2)}) collective-permute-start(bf16[128,1536]{1,0:T(8,128)(2,1)S(1)} %copy-done.42), channel_id=1, source_target_pairs={{0,6},{2,4},{4,2},{6,0},{1,7},{3,5},{5,3},{7,1},{8,14},{10,12},{12... | collective-permute-start | bytes 1179656 | tf_op jit(solution)/shard_map/ppermute | solution.py:46
  211.4 3.5 collective-permute-start.30
  238.9 7.2 %collective-permute-start.31 = (bf16[512,1536]{1,0:T(8,128)(2,1)S(1)}, bf16[512,1536]{1,0:T(8,128)(2,1)S(1)}, u32[]{:S(2)}, u32[]{:S(2)}) collective-permute-start(bf16[512,1536]{1,0:T(8,128)(2,1)S(1)} %get-tuple-element.251), channel_id=1, source_target_pairs={{0,1},{1,0},{2,3},{3,2},{4,5},{5,4},{6,7},{7,6},{8,9},{9,8},{10,11... | collective-permute-start | bytes 4718600 | tf_op jit(solution)/shard_map/ppermute | solution.py:46
  239.1 8.4 %collective-permute-start.32 = (bf16[512,1536]{1,0:T(8,128)(2,1)S(1)}, bf16[512,1536]{1,0:T(8,128)(2,1)S(1)}, u32[]{:S(2)}, u32[]{:S(2)}) collective-permute-start(bf16[512,1536]{1,0:T(8,128)(2,1)S(1)} %get-tuple-element.253), channel_id=1, source_target_pairs={{0,1},{1,0},{2,3},{3,2},{4,5},{5,4},{6,7},{7,6},{8,9},{9,8},{10,11... | collective-permute-start | bytes 4718600 | tf_op jit(solution)/shard_map/ppermute | solution.py:46
  247.5 39.1 %collective-permute-start.33 = (bf16[128,1536]{1,0:T(8,128)(2,1)S(1)}, bf16[128,1536]{1,0:T(8,128)(2,1)S(1)}, u32[]{:S(2)}, u32[]{:S(2)}) collective-permute-start(bf16[128,1536]{1,0:T(8,128)(2,1)S(1)} %get-tuple-element.256), channel_id=1, source_target_pairs={{0,2},{2,0},{4,6},{6,4},{1,3},{3,1},{5,7},{7,5},{8,10},{10,8},{12,... | collective-permute-start | bytes 1179656 | tf_op jit(solution)/shard_map/ppermute | solution.py:46
  249.2 37.3 %collective-permute-start.34 = (bf16[128,1536]{1,0:T(8,128)(2,1)S(1)}, bf16[128,1536]{1,0:T(8,128)(2,1)S(1)}, u32[]{:S(2)}, u32[]{:S(2)}) collective-permute-start(bf16[128,1536]{1,0:T(8,128)(2,1)S(1)} %get-tuple-element.257), channel_id=1, source_target_pairs={{0,4},{2,6},{4,0},{6,2},{1,5},{3,7},{5,1},{7,3},{8,12},{10,14},{12... | collective-permute-start | bytes 1179656 | tf_op jit(solution)/shard_map/ppermute | solution.py:46
  250.4 36.2 %collective-permute-start.35 = (bf16[128,1536]{1,0:T(8,128)(2,1)S(1)}, bf16[128,1536]{1,0:T(8,128)(2,1)S(1)}, u32[]{:S(2)}, u32[]{:S(2)}) collective-permute-start(bf16[128,1536]{1,0:T(8,128)(2,1)S(1)} %get-tuple-element.258), channel_id=1, source_target_pairs={{0,6},{2,4},{4,2},{6,0},{1,7},{3,5},{5,3},{7,1},{8,14},{10,12},{12... | collective-permute-start | bytes 1179656 | tf_op jit(solution)/shard_map/ppermute | solution.py:46
  252.1 21.0 %collective-permute-start.36 = (bf16[384,1152]{1,0:T(8,128)(2,1)S(1)}, bf16[384,1152]{1,0:T(8,128)(2,1)S(1)}, u32[]{:S(2)}, u32[]{:S(2)}) collective-permute-start(bf16[384,1152]{1,0:T(8,128)(2,1)S(1)} %pad_maximum_fusion.5), channel_id=1, source_target_pairs={{0,8},{8,0},{16,24},{24,16},{1,9},{9,1},{17,25},{25,17},{2,10},{10... | collective-permute-start | bytes 2654216 | tf_op jit(solution)/shard_map/ppermute | solution.py:46
  253.5 20.9 %collective-permute-start.37 = (bf16[384,1152]{1,0:T(8,128)(2,1)S(1)}, bf16[384,1152]{1,0:T(8,128)(2,1)S(1)}, u32[]{:S(2)}, u32[]{:S(2)}) collective-permute-start(bf16[384,1152]{1,0:T(8,128)(2,1)S(1)} %pad_maximum_fusion.6), channel_id=1, source_target_pairs={{0,16},{8,24},{16,0},{24,8},{1,17},{9,25},{17,1},{25,9},{2,18},{10... | collective-permute-start | bytes 2654216 | tf_op jit(solution)/shard_map/ppermute | solution.py:46
  274.6 10.5 %collective-permute-start.38 = (bf16[192,1152]{1,0:T(8,128)(2,1)S(1)}, bf16[192,1152]{1,0:T(8,128)(2,1)S(1)}, u32[]{:S(2)}, u32[]{:S(2)}) collective-permute-start(bf16[192,1152]{1,0:T(8,128)(2,1)S(1)} %get-tuple-element.263), channel_id=1, source_target_pairs={{0,8},{8,0},{16,24},{24,16},{1,9},{9,1},{17,25},{25,17},{2,10},{10... | collective-permute-start | bytes 1327112 | tf_op jit(solution)/shard_map/ppermute | solution.py:46
  275.2 10.0 %collective-permute-start.39 = (bf16[192,1152]{1,0:T(8,128)(2,1)S(1)}, bf16[192,1152]{1,0:T(8,128)(2,1)S(1)}, u32[]{:S(2)}, u32[]{:S(2)}) collective-permute-start(bf16[192,1152]{1,0:T(8,128)(2,1)S(1)} %get-tuple-element.264), channel_id=1, source_target_pairs={{0,16},{8,24},{16,0},{24,8},{1,17},{9,25},{17,1},{25,9},{2,18},{10... | collective-permute-start | bytes 1327112 | tf_op jit(solution)/shard_map/ppermute | solution.py:46
  286.6 40.3 %collective-permute-start.44 = (bf16[384,2304]{1,0:T(8,128)(2,1)S(1)}, bf16[384,2304]{1,0:T(8,128)(2,1)}, u32[]{:S(2)}, u32[]{:S(2)}) collective-permute-start(bf16[384,2304]{1,0:T(8,128)(2,1)S(1)} %pad_maximum_fusion), channel_id=1, source_target_pairs={{0,8},{8,0},{16,24},{24,16},{1,9},{9,1},{17,25},{25,17},{2,10},{10... | collective-permute-start | bytes 5308424 | tf_op jit(solution)/shard_map/ppermute | solution.py:46
  288.3 38.7 %collective-permute-start.45 = (bf16[384,2304]{1,0:T(8,128)(2,1)}, bf16[384,2304]{1,0:T(8,128)(2,1)}, u32[]{:S(2)}, u32[]{:S(2)}) collective-permute-start(bf16[384,2304]{1,0:T(8,128)(2,1)} %pad_maximum_fusion.1), channel_id=1, source_target_pairs={{0,16},{8,24},{16,0},{24,8},{1,17},{9,25},{17,1},{25,9},{2,18},{10... | collective-permute-start | bytes 5308424 | tf_op jit(solution)/shard_map/ppermute | solution.py:46
  289.8 23.2 %all-to-all-start = ((bf16[4,96,1152]{2,1,0:T(8,128)(2,1)}), bf16[4,96,1152]{2,1,0:T(8,128)(2,1)S(1)}, u32[]{:S(2)}, u32[]{:S(2)}) async-start(bf16[4,96,1152]{2,1,0:T(8,128)(2,1)} %bitcast.22), calls=%async_computation | async-start | bytes 1769472 | tf_op jit(solution)/shard_map/all_to_all | solution.py:809
  313.0 7.1 %collective-permute-start.41 = (bf16[256,256]{1,0:T(8,128)(2,1)}, bf16[256,256]{1,0:T(8,128)(2,1)S(1)}, u32[]{:S(2)}, u32[]{:S(2)}) collective-permute-start(bf16[256,256]{1,0:T(8,128)(2,1)} %get-tuple-element.281), channel_id=1, source_target_pairs={{0,2},{2,0},{4,6},{6,4},{1,3},{3,1},{5,7},{7,5},{8,10},{10,8},{12,... | collective-permute-start | bytes 393224 | tf_op jit(solution)/shard_map/ppermute | solution.py:46
  313.8 13.1 %collective-permute-start.42 = (bf16[256,256]{1,0:T(8,128)(2,1)}, bf16[256,256]{1,0:T(8,128)(2,1)S(1)}, u32[]{:S(2)}, u32[]{:S(2)}) collective-permute-start(bf16[256,256]{1,0:T(8,128)(2,1)} %get-tuple-element.282), channel_id=1, source_target_pairs={{0,4},{2,6},{4,0},{6,2},{1,5},{3,7},{5,1},{7,3},{8,12},{10,14},{12... | collective-permute-start | bytes 393224 | tf_op jit(solution)/shard_map/ppermute | solution.py:46
  316.2 10.8 %collective-permute-start.43 = (bf16[256,256]{1,0:T(8,128)(2,1)}, bf16[256,256]{1,0:T(8,128)(2,1)S(1)}, u32[]{:S(2)}, u32[]{:S(2)}) collective-permute-start(bf16[256,256]{1,0:T(8,128)(2,1)} %get-tuple-element.283), channel_id=1, source_target_pairs={{0,6},{2,4},{4,2},{6,0},{1,7},{3,5},{5,3},{7,1},{8,14},{10,12},{12... | collective-permute-start | bytes 393224 | tf_op jit(solution)/shard_map/ppermute | solution.py:46
  330.6 19.8 %collective-permute-start.49 = (bf16[192,2304]{1,0:T(8,128)(2,1)}, bf16[192,2304]{1,0:T(8,128)(2,1)}, u32[]{:S(2)}, u32[]{:S(2)}) collective-permute-start(bf16[192,2304]{1,0:T(8,128)(2,1)} %get-tuple-element.296), channel_id=1, source_target_pairs={{0,8},{8,0},{16,24},{24,16},{1,9},{9,1},{17,25},{25,17},{2,10},{10... | collective-permute-start | bytes 2654216 | tf_op jit(solution)/shard_map/ppermute | solution.py:46
  331.4 19.5 %collective-permute-start.50 = (bf16[192,2304]{1,0:T(8,128)(2,1)}, bf16[192,2304]{1,0:T(8,128)(2,1)}, u32[]{:S(2)}, u32[]{:S(2)}) collective-permute-start(bf16[192,2304]{1,0:T(8,128)(2,1)} %get-tuple-element.297), channel_id=1, source_target_pairs={{0,16},{8,24},{16,0},{24,8},{1,17},{9,25},{17,1},{25,9},{2,18},{10... | collective-permute-start | bytes 2654216 | tf_op jit(solution)/shard_map/ppermute | solution.py:46
  332.2 25.5 %collective-permute-start.46 = (bf16[128,1536]{1,0:T(8,128)(2,1)}, bf16[128,1536]{1,0:T(8,128)(2,1)}, u32[]{:S(2)}, u32[]{:S(2)}) collective-permute-start(bf16[128,1536]{1,0:T(8,128)(2,1)} %get-tuple-element.291), channel_id=1, source_target_pairs={{0,2},{2,0},{4,6},{6,4},{1,3},{3,1},{5,7},{7,5},{8,10},{10,8},{12,... | collective-permute-start | bytes 1179656 | tf_op jit(solution)/shard_map/ppermute | solution.py:46
  334.2 30.1 %collective-permute-start.47 = (bf16[128,1536]{1,0:T(8,128)(2,1)}, bf16[128,1536]{1,0:T(8,128)(2,1)}, u32[]{:S(2)}, u32[]{:S(2)}) collective-permute-start(bf16[128,1536]{1,0:T(8,128)(2,1)} %get-tuple-element.292), channel_id=1, source_target_pairs={{0,4},{2,6},{4,0},{6,2},{1,5},{3,7},{5,1},{7,3},{8,12},{10,14},{12... | collective-permute-start | bytes 1179656 | tf_op jit(solution)/shard_map/ppermute | solution.py:46
  335.2 29.2 %collective-permute-start.48 = (bf16[128,1536]{1,0:T(8,128)(2,1)S(1)}, bf16[128,1536]{1,0:T(8,128)(2,1)}, u32[]{:S(2)}, u32[]{:S(2)}) collective-permute-start(bf16[128,1536]{1,0:T(8,128)(2,1)S(1)} %get-tuple-element.293), channel_id=1, source_target_pairs={{0,6},{2,4},{4,2},{6,0},{1,7},{3,5},{5,3},{7,1},{8,14},{10,12},{12... | collective-permute-start | bytes 1179656 | tf_op jit(solution)/shard_map/ppermute | solution.py:46
  351.0 13.4 %collective-permute-start.51 = (bf16[384,768]{1,0:T(8,128)(2,1)S(1)}, bf16[384,768]{1,0:T(8,128)(2,1)S(1)}, u32[]{:S(2)}, u32[]{:S(2)}) collective-permute-start(bf16[384,768]{1,0:T(8,128)(2,1)S(1)} %pad_maximum_fusion.26), channel_id=1, source_target_pairs={{0,8},{8,0},{16,24},{24,16},{1,9},{9,1},{17,25},{25,17},{2,10},{10... | collective-permute-start | bytes 1769480 | tf_op jit(solution)/shard_map/ppermute | solution.py:46
  352.4 11.9 %collective-permute-start.52 = (bf16[384,768]{1,0:T(8,128)(2,1)S(1)}, bf16[384,768]{1,0:T(8,128)(2,1)S(1)}, u32[]{:S(2)}, u32[]{:S(2)}) collective-permute-start(bf16[384,768]{1,0:T(8,128)(2,1)S(1)} %pad_maximum_fusion.27), channel_id=1, source_target_pairs={{0,16},{8,24},{16,0},{24,8},{1,17},{9,25},{17,1},{25,9},{2,18},{10... | collective-permute-start | bytes 1769480 | tf_op jit(solution)/shard_map/ppermute | solution.py:46
  365.7 15.5 %collective-permute-start.54 = (bf16[400,1024]{1,0:T(8,128)(2,1)}, bf16[400,1024]{1,0:T(8,128)(2,1)}, u32[]{:S(2)}, u32[]{:S(2)}) collective-permute-start(bf16[400,1024]{1,0:T(8,128)(2,1)} %pad_maximum_fusion.17), channel_id=1, source_target_pairs={{0,8},{8,0},{16,24},{24,16},{1,9},{9,1},{17,25},{25,17},{2,10},{10... | collective-permute-start | bytes 2457608 | tf_op jit(solution)/shard_map/ppermute | solution.py:46
  367.1 14.2 %collective-permute-start.53 = (bf16[384,1024]{1,0:T(8,128)(2,1)}, bf16[384,1024]{1,0:T(8,128)(2,1)}, u32[]{:S(2)}, u32[]{:S(2)}) collective-permute-start(bf16[384,1024]{1,0:T(8,128)(2,1)} %pad_maximum_fusion.18), channel_id=1, source_target_pairs={{0,16},{8,24},{16,0},{24,8},{1,17},{9,25},{17,1},{25,9},{2,18},{10... | collective-permute-start | bytes 2359304 | tf_op jit(solution)/shard_map/ppermute | solution.py:46
  370.7 47.3 %all-to-all-start.1 = ((bf16[4,96,2304]{2,1,0:T(8,128)(2,1)}), bf16[4,96,2304]{2,1,0:T(8,128)(2,1)}, u32[]{:S(2)}, u32[]{:S(2)}) async-start(bf16[4,96,2304]{2,1,0:T(8,128)(2,1)} %bitcast.76), calls=%async_computation.1 | async-start | bytes 3538944 | tf_op jit(solution)/shard_map/all_to_all | solution.py:906
  385.4 13.1 %collective-permute-start.56 = (bf16[208,1792]{1,0:T(8,128)(2,1)}, bf16[208,1792]{1,0:T(8,128)(2,1)}, u32[]{:S(2)}, u32[]{:S(2)}) collective-permute-start(bf16[208,1792]{1,0:T(8,128)(2,1)} %fusion.4), channel_id=1, source_target_pairs={{0,16},{8,24},{16,0},{24,8},{1,17},{9,25},{17,1},{25,9},{2,18},{10... | collective-permute-start | bytes 2236424 | tf_op jit(solution)/shard_map/ppermute | solution.py:46
  386.8 12.5 %collective-permute-start.55 = (bf16[192,1792]{1,0:T(8,128)(2,1)}, bf16[192,1792]{1,0:T(8,128)(2,1)S(1)}, u32[]{:S(2)}, u32[]{:S(2)}) collective-permute-start(bf16[192,1792]{1,0:T(8,128)(2,1)} %pad_maximum_fusion.21), channel_id=1, source_target_pairs={{0,8},{8,0},{16,24},{24,16},{1,9},{9,1},{17,25},{25,17},{2,10},{10... | collective-permute-start | bytes 2064392 | tf_op jit(solution)/shard_map/ppermute | solution.py:46
  417.9 17.3 %collective-permute-start.57 = (bf16[96,1920]{1,0:T(8,128)(2,1)}, bf16[96,1920]{1,0:T(8,128)(2,1)S(1)}, u32[]{:S(2)}, u32[]{:S(2)}) collective-permute-start(bf16[96,1920]{1,0:T(8,128)(2,1)} %get-tuple-element.330), channel_id=1, source_target_pairs={{0,2},{2,0},{4,6},{6,4},{1,3},{3,1},{5,7},{7,5},{8,10},{10,8},{12,... | collective-permute-start | bytes 1105928 | tf_op jit(solution)/shard_map/ppermute | solution.py:46
  417.9 28.4 %collective-permute-start.58 = (bf16[96,1920]{1,0:T(8,128)(2,1)}, bf16[96,1920]{1,0:T(8,128)(2,1)S(1)}, u32[]{:S(2)}, u32[]{:S(2)}) collective-permute-start(bf16[96,1920]{1,0:T(8,128)(2,1)} %get-tuple-element.331), channel_id=1, source_target_pairs={{0,4},{2,6},{4,0},{6,2},{1,5},{3,7},{5,1},{7,3},{8,12},{10,14},{12... | collective-permute-start | bytes 1105928 | tf_op jit(solution)/shard_map/ppermute | solution.py:46
  420.0 26.3 %collective-permute-start.59 = (bf16[96,1920]{1,0:T(8,128)(2,1)}, bf16[96,1920]{1,0:T(8,128)(2,1)S(1)}, u32[]{:S(2)}, u32[]{:S(2)}) collective-permute-start(bf16[96,1920]{1,0:T(8,128)(2,1)} %get-tuple-element.332), channel_id=1, source_target_pairs={{0,6},{2,4},{4,2},{6,0},{1,7},{3,5},{5,3},{7,1},{8,14},{10,12},{12... | collective-permute-start | bytes 1105928 | tf_op jit(solution)/shard_map/ppermute | solution.py:46
  422.3 6.6 %collective-permute-start.60 = (f32[128,1536]{1,0:T(8,128)}, f32[128,1536]{1,0:T(8,128)S(1)}, u32[]{:S(2)}, u32[]{:S(2)}) collective-permute-start(f32[128,1536]{1,0:T(8,128)} %get-tuple-element.335), channel_id=1, source_target_pairs={{0,1},{1,0},{2,3},{3,2},{4,5},{5,4},{6,7},{7,6},{8,9},{9,8},{10,11... | collective-permute-start | bytes 2359304 | tf_op jit(solution)/shard_map/ppermute | solution.py:46
  423.9 8.6 %collective-permute-start.62 = (bf16[128,1536]{1,0:T(8,128)(2,1)S(1)}, bf16[128,1536]{1,0:T(8,128)(2,1)S(1)}, u32[]{:S(2)}, u32[]{:S(2)}) collective-permute-start(bf16[128,1536]{1,0:T(8,128)(2,1)S(1)} %pad_maximum_fusion.33), channel_id=1, source_target_pairs={{0,1},{1,0},{2,3},{3,2},{4,5},{5,4},{6,7},{7,6},{8,9},{9,8},{10,11... | collective-permute-start | bytes 1179656 | tf_op jit(solution)/shard_map/ppermute | solution.py:46
  431.1 2.4 collective-permute-start.61
  (88 other events, 1091.8 us)

commit v8 on v7

--- a/solution.py
+++ b/solution.py
@@ -251,8 +251,8 @@
     def _():
         first = stack_copies(down_target, sems)
         start_all(first)
+        wait_all(first)
         start_all(stack_copies(gate_up_copies(parts, gu, sems), sems, 5))
-        wait_all(first)
 
     grads = jnp.where(own, o_mine[...], o_other[...])
     g_act = matmul(grads, down[...])

time: 460 us -> 460 us (level)
  transfers between devices with their start and end apart: 66 -> 66, of which waited for: 32 -> 33; matrix products, arithmetic and copies ran while one was open for 12% -> 12% of each run, Pallas kernels for 12% -> 12%
where the time goes in v8:
time: 460 us; the launch traced here: 451 us
  waiting for transfers between devices  182 us (40%)
  starting transfers between devices  97.3 us (21%)
  Pallas kernels  82.2 us (18%)
  local copies, waits for them, and re-layouts  42.1 us (9%)
  other arithmetic  39.7 us (9%)
  between operations  7.49 us (2%)
    ppermute x64, waiting for transfers between devices, swap(): return lax.ppermute(values, axis, [(i, i ^ offset) for i in range(size)])  166 us
    ppermute x64, starting transfers between devices, swap(): return lax.ppermute(values, axis, [(i, i ^ offset) for i in range(size)])  85 us
    pallas_call x12, Pallas kernels, call(): pl.pallas_call(body, in_specs=in_specs or [whole] * len(args), out_specs=...  34.8 us
    pallas_call x2, Pallas kernels, by_tiles(): pl.pallas_call(functools.partial(body, tiles_each), grid=(2 * tiles_each,...  34.2 us
    unnamed x180, local copies, waits for them, and re-layouts  20.7 us
    all_to_all x1, waiting for transfers between devices, on_device(): gate_up_back = lax.all_to_all(gate_up_blocks, 'ctx', 0, 0, tiled=True)  14.7 us
    pallas_call x2, Pallas kernels, weight_grad(): pl.pallas_call(weight_tile, grid=(3,), in_specs=[columns, columns, pl.Blo...  13.2 us
  transfers between devices with their start and end apart: 66, of which 33 were waited for; matrix products, arithmetic and copies ran while one was open for 12% of the time, Pallas kernels for 12%

profile of v8, /device:TPU:0, one launch (start us, length us, event | category | flops | bytes accessed | tf_op | source)
XLA Modules:
  0.0 451.0 jit_solution(13730571049371403583)
XLA Ops:
  0.6 1.8 side_by_side.1.refs_0_
  2.4 3.0 collective-permute-start
  5.4 2.6 collective-permute-start.1
  14.7 2.5 dynamic-slice_bitcast_fusion
  25.4 2.6 constant_dynamic-slice_fusion.16.inputs
  28.9 3.4 collective-permute-done.1.refs_2_
  33.0 1.6 collective-permute-start.3
  34.6 1.5 collective-permute-start.4
  36.1 6.5 %collective-permute-start.5 = (bf16[96,2304]{1,0:T(8,128)(2,1)S(1)}, bf16[96,2304]{1,0:T(8,128)(2,1)S(1)}, u32[]{:S(2)}, u32[]{:S(2)}) collective-permute-start(bf16[96,2304]{1,0:T(8,128)(2,1)S(1)} %copy-done.63), channel_id=1, source_target_pairs={{0,2},{2,0},{4,6},{6,4},{1,3},{3,1},{5,7},{7,5},{8,10},{10,8},{12,... | collective-permute-start | bytes 1327112 | tf_op jit(solution)/shard_map/ppermute | solution.py:46
  45.1 13.9 %collective-permute-done.5.refs_1_ = bf16[96,2304]{1,0:T(8,128)(2,1)S(1)} collective-permute-done((bf16[96,2304]{1,0:T(8,128)(2,1)S(1)}, bf16[96,2304]{1,0:T(8,128)(2,1)S(1)}, u32[]{:S(2)}, u32[]{:S(2)}) %collective-permute-start.5) | collective-permute-done | bytes 442400 | tf_op jit(solution)/shard_map/ppermute | solution.py:46
  59.0 16.7 %collective-permute-done.6.refs_2_ = bf16[96,2304]{1,0:T(8,128)(2,1)S(1)} collective-permute-done((bf16[96,2304]{1,0:T(8,128)(2,1)S(1)}, bf16[96,2304]{1,0:T(8,128)(2,1)S(1)}, u32[]{:S(2)}, u32[]{:S(2)}) %collective-permute-start.6) | collective-permute-done | bytes 442400 | tf_op jit(solution)/shard_map/ppermute | solution.py:46
  76.9 6.9 %collective-permute-start.10 = (bf16[96,1152]{1,0:T(8,128)(2,1)S(1)}, bf16[96,1152]{1,0:T(8,128)(2,1)S(1)}, u32[]{:S(2)}, u32[]{:S(2)}) collective-permute-start(bf16[96,1152]{1,0:T(8,128)(2,1)S(1)} %copy-done.72), channel_id=1, source_target_pairs={{0,2},{2,0},{4,6},{6,4},{1,3},{3,1},{5,7},{7,5},{8,10},{10,8},{12,... | collective-permute-start | bytes 663560 | tf_op jit(solution)/shard_map/ppermute | solution.py:46
  88.5 2.3 project.1
  90.8 1.7 copy-done.8
  93.9 6.1 %collective-permute-done.11.refs_2_ = bf16[96,1152]{1,0:T(8,128)(2,1)S(1)} collective-permute-done((bf16[96,1152]{1,0:T(8,128)(2,1)S(1)}, bf16[96,1152]{1,0:T(8,128)(2,1)S(1)}, u32[]{:S(2)}, u32[]{:S(2)}) %collective-permute-start.11) | collective-permute-done | bytes 221216 | tf_op jit(solution)/shard_map/ppermute | solution.py:46
  101.4 2.9 collective-permute-start.13
  115.3 5.9 %attend.1 = (bf16[256,768]{1,0:T(8,128)(2,1)S(1)}, f32[256,768]{1,0:T(8,128)S(1)}, f32[128,1536]{1,0:T(8,128)S(1)}, f32[128,1536]{1,0:T(8,128)S(1)}) custom-call(s32[1]{0:T(128)} %bitcast.core_ref, bf16[256,768]{1,0:T(8,128)(2,1)S(1)} %copy-done.15, s32[256,1]{1,0:T(8,128)S(1)} %copy.30.query_pos, s32[1,1024]{1,0:T(1,128)S(1)} %bitcast.74, ...), custom_call_target="tpu_custom_call" | custom-call | flops 1 | bytes 1 | tf_op jit(solution)/shard_map/attend/pallas_call | solution.py:352
  121.3 2.3 collective-permute-done.16.got
  123.9 1.6 collective-permute-done.17.refs_1_
  127.4 1.5 collective-permute-start.23
  129.5 2.4 collective-permute-start.20
  133.3 11.5 %collective-permute-done.19 = bf16[128,1536]{1,0:T(8,128)(2,1)S(1)} collective-permute-done((bf16[128,1536]{1,0:T(8,128)(2,1)S(1)}, bf16[128,1536]{1,0:T(8,128)(2,1)S(1)}, u32[]{:S(2)}, u32[]{:S(2)}) %collective-permute-start.19) | collective-permute-done | bytes 393248 | tf_op jit(solution)/shard_map/ppermute | solution.py:46
  144.8 14.5 %collective-permute-done.20 = bf16[128,1536]{1,0:T(8,128)(2,1)S(1)} collective-permute-done((bf16[128,1536]{1,0:T(8,128)(2,1)S(1)}, bf16[128,1536]{1,0:T(8,128)(2,1)S(1)}, u32[]{:S(2)}, u32[]{:S(2)}) %collective-permute-start.20) | collective-permute-done | bytes 393248 | tf_op jit(solution)/shard_map/ppermute | solution.py:46
  159.3 5.4 %collective-permute-done.22.refs_4_ = bf16[384,2304]{1,0:T(8,128)(2,1)S(1)} collective-permute-done((bf16[384,2304]{1,0:T(8,128)(2,1)S(1)}, bf16[384,2304]{1,0:T(8,128)(2,1)S(1)}, u32[]{:S(2)}, u32[]{:S(2)}) %collective-permute-start.22) | collective-permute-done | bytes 1769504 | tf_op jit(solution)/shard_map/ppermute | solution.py:46
  169.6 2.0 collective-permute-start.25
  174.0 24.6 %collective-permute-done.28.refs_6_ = bf16[192,3456]{1,0:T(8,128)(2,1)S(1)} collective-permute-done((bf16[192,3456]{1,0:T(8,128)(2,1)S(1)}, bf16[192,3456]{1,0:T(8,128)(2,1)S(1)}, u32[]{:S(2)}, u32[]{:S(2)}) %collective-permute-start.28) | collective-permute-done | bytes 1327136 | tf_op jit(solution)/shard_map/ppermute | solution.py:46
  199.2 9.9 %gate_up.1 = bf16[1024,2304]{1,0:T(8,128)(2,1)S(1)} custom-call(bf16[512,1536]{1,0:T(8,128)(2,1)S(1)} %constant_dynamic-update-slice_fusion.1.x_mine, bf16[512,1536]{1,0:T(8,128)(2,1)S(1)} %collective-permute-done.24.x_other, bf16[384,1152]{1,0:T(8,128)(2,1)} %get-tuple-element.228.refs_0_, bf16[384,1152]{1,0:T(8,128)(2,1)S(1)} %collective-permute-done.17.refs_1_, ...), custom_call_target="tpu_custom_call" | custom-call | flops 1 | bytes 1 | tf_op jit(solution)/shard_map/gate_up/pallas_call | solution.py:300
  209.1 2.1 copy-done.1
  211.5 3.4 collective-permute-done.30.o_other.x_other
  214.9 24.3 %mlp_back.1 = (bf16[1024,2304]{1,0:T(8,128)(2,1)}, bf16[1024,1152]{1,0:T(8,128)(2,1)}, f32[512,1536]{1,0:T(8,128)}, bf16[512,1536]{1,0:T(8,128)(2,1)S(1)}, f32[5...) custom-call(bf16[1024,2304]{1,0:T(8,128)(2,1)} %copy-done.1, ...), custom_call_target="tpu_custom_call" | custom-call | flops 1 | bytes 1 | tf_op jit(solution)/shard_map/mlp_back/pallas_call | solution.py:300
  239.8 1.7 copy-done.11
  241.5 4.9 %weight_grad.2 = bf16[1536,1152]{1,0:T(8,128)(2,1)S(1)} custom-call(bf16[512,1536]{1,0:T(8,128)(2,1)S(1)} %constant_dynamic-update-slice_fusion.5.o_mine.x_mine, bf16[512,1536]{1,0:T(8,128)(2,1)S(1)} %collective-permute-done.30.o_other.x_other, bf16[1024,1152]{1,0:T(8,128)(2,1)S(1)} %copy-done.11), custom_call_target="tpu_custom_call" | custom-call | flops 1 | bytes 1 | tf_op jit(solution)/shard_map/weight_grad/pallas_call | solution.py:333
  247.8 1.8 collective-permute-start.33
  253.9 1.6 collective-permute-start.37
  255.5 8.2 %weight_grad.3 = bf16[1536,2304]{1,0:T(8,128)(2,1)S(1)} custom-call(bf16[512,1536]{1,0:T(8,128)(2,1)S(1)} %constant_dynamic-update-slice_fusion.1.x_mine, bf16[512,1536]{1,0:T(8,128)(2,1)S(1)} %collective-permute-done.24.x_other, bf16[1024,2304]{1,0:T(8,128)(2,1)S(1)} %bitcast.73), custom_call_target="tpu_custom_call" | custom-call | flops 1 | bytes 1 | tf_op jit(solution)/shard_map/weight_grad/pallas_call | solution.py:333
  264.2 1.6 fusion.39
  265.8 7.6 %collective-permute-done.36 = bf16[384,1152]{1,0:T(8,128)(2,1)S(1)} collective-permute-done((bf16[384,1152]{1,0:T(8,128)(2,1)S(1)}, bf16[384,1152]{1,0:T(8,128)(2,1)S(1)}, u32[]{:S(2)}, u32[]{:S(2)}) %collective-permute-start.36) | collective-permute-done | bytes 884768 | tf_op jit(solution)/shard_map/ppermute | solution.py:46
  278.8 6.7 %collective-permute-done.38 = bf16[192,1152]{1,0:T(8,128)(2,1)S(1)} collective-permute-done((bf16[192,1152]{1,0:T(8,128)(2,1)S(1)}, bf16[192,1152]{1,0:T(8,128)(2,1)S(1)}, u32[]{:S(2)}, u32[]{:S(2)}) %collective-permute-start.38) | collective-permute-done | bytes 442400 | tf_op jit(solution)/shard_map/ppermute | solution.py:46
  287.0 1.7 collective-permute-start.44
  288.6 1.5 collective-permute-start.45
  290.2 4.0 all-to-all-start
  294.2 3.4 mlp_norm_back.1
  297.6 1.9 collective-permute-done.40.branch_other
  300.3 11.8 %attend_back.1 = (bf16[256,768]{1,0:T(8,128)(2,1)}, bf16[1536,768]{1,0:T(8,128)(2,1)}, f32[256,256]{1,0:T(8,128)}, bf16[256,256]{1,0:T(8,128)(2,1)}, bf16[256,256]{1,0:T(8,128)(2,1)}, /*index=5*/bf16[256,256]{1,0:T(8,128)(2,1)}) custom-call(s32[1]{0:T(128)} %bitcast.core_ref, bf16[128,1536]{1,0:T(8,128)(2,1)} %get-tuple-element.272.branch_mine, ...), custom_call_target="tpu_custom_call" | custom-call | flops 1 | bytes 1 | tf_op jit(solution)/shard_map/attend_back/pallas_call | solution.py:352
  314.2 2.4 collective-permute-start.42
  318.5 1.9 collective-permute-done.41.refs_1_
  320.5 6.8 %collective-permute-done.42.refs_2_ = bf16[256,256]{1,0:T(8,128)(2,1)S(1)} collective-permute-done((bf16[256,256]{1,0:T(8,128)(2,1)}, bf16[256,256]{1,0:T(8,128)(2,1)S(1)}, u32[]{:S(2)}, u32[]{:S(2)}) %collective-permute-start.42) | collective-permute-done | bytes 131104 | tf_op jit(solution)/shard_map/ppermute | solution.py:46
  327.3 3.7 add_convert_fusion.4
  332.6 2.1 collective-permute-start.46
  337.1 5.1 %project_back.1 = (bf16[256,1024]{1,0:T(8,128)(2,1)}, f32[1,1024]{1,0:T(1,128)}, f32[1,1536]{1,0:T(1,128)}, f32[128,1536]{1,0:T(8,128)}, f32[128,1536]{1,0:T(8,128)}) custom-call(s32[1]{0:T(128)} %bitcast.core_ref, bf16[256,768]{1,0:T(8,128)(2,1)} %get-tuple-element.302.query_lin, bf16[1536,1024]{1,0:T(8,128)(2,1)} %copy-done.8, f32[256,128]{1,0:T(8,128)} %copy-done.12, ...), custom_call_target="tpu_custom_call" | custom-call | flops 1 | bytes 1 | tf_op jit(solution)/shard_map/project_back/pallas_call | solution.py:352
  347.4 3.5 collective-permute-done.49
  353.4 3.3 add_convert_fusion.3
  358.0 6.7 %collective-permute-done.47 = bf16[128,1536]{1,0:T(8,128)(2,1)} collective-permute-done((bf16[128,1536]{1,0:T(8,128)(2,1)}, bf16[128,1536]{1,0:T(8,128)(2,1)}, u32[]{:S(2)}, u32[]{:S(2)}) %collective-permute-start.47) | collective-permute-done | bytes 393248 | tf_op jit(solution)/shard_map/ppermute | solution.py:46
  367.5 1.5 collective-permute-start.53
  369.0 2.1 add_convert_fusion.13
  371.1 8.3 %all-to-all-start.1 = ((bf16[4,96,2304]{2,1,0:T(8,128)(2,1)}), bf16[4,96,2304]{2,1,0:T(8,128)(2,1)}, u32[]{:S(2)}, u32[]{:S(2)}) async-start(bf16[4,96,2304]{2,1,0:T(8,128)(2,1)} %bitcast.76), calls=%async_computation.1 | async-start | bytes 3538944 | tf_op jit(solution)/shard_map/all_to_all | solution.py:906
  379.4 2.2 collective-permute-done.53
  391.3 7.5 %collective-permute-done.56 = bf16[208,1792]{1,0:T(8,128)(2,1)} collective-permute-done((bf16[208,1792]{1,0:T(8,128)(2,1)}, bf16[208,1792]{1,0:T(8,128)(2,1)}, u32[]{:S(2)}, u32[]{:S(2)}) %collective-permute-start.56) | collective-permute-done | bytes 745504 | tf_op jit(solution)/shard_map/ppermute | solution.py:46
  399.7 1.7 convert_add_fusion
  403.6 14.7 %all-to-all-done.1 = bf16[4,96,2304]{2,1,0:T(8,128)(2,1)} async-done(((bf16[4,96,2304]{2,1,0:T(8,128)(2,1)}), bf16[4,96,2304]{2,1,0:T(8,128)(2,1)}, u32[]{:S(2)}, u32[]{:S(2)}) %all-to-all-start.1) | async-done | bytes 1769504 | tf_op jit(solution)/shard_map/all_to_all | solution.py:906
  418.3 2.1 collective-permute-start.58
  420.4 2.3 collective-permute-start.59
  424.8 1.5 slice_bitcast_fusion.3
  435.6 11.0 %collective-permute-done.58 = bf16[96,1920]{1,0:T(8,128)(2,1)S(1)} collective-permute-done((bf16[96,1920]{1,0:T(8,128)(2,1)}, bf16[96,1920]{1,0:T(8,128)(2,1)S(1)}, u32[]{:S(2)}, u32[]{:S(2)}) %collective-permute-start.58) | collective-permute-done | bytes 368672 | tf_op jit(solution)/shard_map/ppermute | solution.py:46
  (380 shorter events, 107.5 us)
Async XLA Ops:
  2.4 26.4 %collective-permute-start = (bf16[96,1792]{1,0:T(8,128)(2,1)}, bf16[96,1792]{1,0:T(8,128)(2,1)S(1)}, u32[]{:S(2)}, u32[]{:S(2)}) collective-permute-start(bf16[96,1792]{1,0:T(8,128)(2,1)} %side_by_side.1.refs_0_), channel_id=1, source_target_pairs={{0,2},{2,0},{4,6},{6,4},{1,3},{3,1},{5,7},{7,5},{8,10},{10,8},{12,... | collective-permute-start | bytes 1032200 | tf_op jit(solution)/shard_map/ppermute | solution.py:46
  5.4 26.8 %collective-permute-start.1 = (bf16[96,1792]{1,0:T(8,128)(2,1)}, bf16[96,1792]{1,0:T(8,128)(2,1)S(1)}, u32[]{:S(2)}, u32[]{:S(2)}) collective-permute-start(bf16[96,1792]{1,0:T(8,128)(2,1)} %side_by_side.1.refs_0_), channel_id=1, source_target_pairs={{0,4},{2,6},{4,0},{6,2},{1,5},{3,7},{5,1},{7,3},{8,12},{10,14},{12... | collective-permute-start | bytes 1032200 | tf_op jit(solution)/shard_map/ppermute | solution.py:46
  8.0 24.3 %collective-permute-start.2 = (bf16[96,1792]{1,0:T(8,128)(2,1)}, bf16[96,1792]{1,0:T(8,128)(2,1)S(1)}, u32[]{:S(2)}, u32[]{:S(2)}) collective-permute-start(bf16[96,1792]{1,0:T(8,128)(2,1)} %side_by_side.1.refs_0_), channel_id=1, source_target_pairs={{0,6},{2,4},{4,2},{6,0},{1,7},{3,5},{5,3},{7,1},{8,14},{10,12},{12... | collective-permute-start | bytes 1032200 | tf_op jit(solution)/shard_map/ppermute | solution.py:46
  33.0 42.6 %collective-permute-start.3 = (bf16[384,1792]{1,0:T(8,128)(2,1)S(1)}, bf16[384,1792]{1,0:T(8,128)(2,1)S(1)}, u32[]{:S(2)}, u32[]{:S(2)}) collective-permute-start(bf16[384,1792]{1,0:T(8,128)(2,1)S(1)} %place.3.refs_0_), channel_id=1, source_target_pairs={{0,8},{8,0},{16,24},{24,16},{1,9},{9,1},{17,25},{25,17},{2,10},{10... | collective-permute-start | bytes 4128776 | tf_op jit(solution)/shard_map/ppermute | solution.py:46
  34.6 41.0 %collective-permute-start.4 = (bf16[384,1792]{1,0:T(8,128)(2,1)S(1)}, bf16[384,1792]{1,0:T(8,128)(2,1)S(1)}, u32[]{:S(2)}, u32[]{:S(2)}) collective-permute-start(bf16[384,1792]{1,0:T(8,128)(2,1)S(1)} %place.3.refs_0_), channel_id=1, source_target_pairs={{0,16},{8,24},{16,0},{24,8},{1,17},{9,25},{17,1},{25,9},{2,18},{10... | collective-permute-start | bytes 4128776 | tf_op jit(solution)/shard_map/ppermute | solution.py:46
  36.1 22.8 %collective-permute-start.5 = (bf16[96,2304]{1,0:T(8,128)(2,1)S(1)}, bf16[96,2304]{1,0:T(8,128)(2,1)S(1)}, u32[]{:S(2)}, u32[]{:S(2)}) collective-permute-start(bf16[96,2304]{1,0:T(8,128)(2,1)S(1)} %copy-done.63), channel_id=1, source_target_pairs={{0,2},{2,0},{4,6},{6,4},{1,3},{3,1},{5,7},{7,5},{8,10},{10,8},{12,... | collective-permute-start | bytes 1327112 | tf_op jit(solution)/shard_map/ppermute | solution.py:46
  42.6 33.0 %collective-permute-start.6 = (bf16[96,2304]{1,0:T(8,128)(2,1)S(1)}, bf16[96,2304]{1,0:T(8,128)(2,1)S(1)}, u32[]{:S(2)}, u32[]{:S(2)}) collective-permute-start(bf16[96,2304]{1,0:T(8,128)(2,1)S(1)} %copy-done.62), channel_id=1, source_target_pairs={{0,4},{2,6},{4,0},{6,2},{1,5},{3,7},{5,1},{7,3},{8,12},{10,14},{12... | collective-permute-start | bytes 1327112 | tf_op jit(solution)/shard_map/ppermute | solution.py:46
  43.7 31.9 %collective-permute-start.7 = (bf16[96,2304]{1,0:T(8,128)(2,1)S(1)}, bf16[96,2304]{1,0:T(8,128)(2,1)S(1)}, u32[]{:S(2)}, u32[]{:S(2)}) collective-permute-start(bf16[96,2304]{1,0:T(8,128)(2,1)S(1)} %pad_maximum_fusion.31), channel_id=1, source_target_pairs={{0,6},{2,4},{4,2},{6,0},{1,7},{3,5},{5,3},{7,1},{8,14},{10,12},{12... | collective-permute-start | bytes 1327112 | tf_op jit(solution)/shard_map/ppermute | solution.py:46
  75.7 12.8 %collective-permute-start.8 = (bf16[192,1792]{1,0:T(8,128)(2,1)S(1)}, bf16[192,1792]{1,0:T(8,128)(2,1)S(1)}, u32[]{:S(2)}, u32[]{:S(2)}) collective-permute-start(bf16[192,1792]{1,0:T(8,128)(2,1)S(1)} %slice.302), channel_id=1, source_target_pairs={{0,8},{8,0},{16,24},{24,16},{1,9},{9,1},{17,25},{25,17},{2,10},{10... | collective-permute-start | bytes 2064392 | tf_op jit(solution)/shard_map/ppermute | solution.py:46
  76.3 12.1 %collective-permute-start.9 = (bf16[192,1792]{1,0:T(8,128)(2,1)S(1)}, bf16[192,1792]{1,0:T(8,128)(2,1)S(1)}, u32[]{:S(2)}, u32[]{:S(2)}) collective-permute-start(bf16[192,1792]{1,0:T(8,128)(2,1)S(1)} %slice.303), channel_id=1, source_target_pairs={{0,16},{8,24},{16,0},{24,8},{1,17},{9,25},{17,1},{25,9},{2,18},{10... | collective-permute-start | bytes 2064392 | tf_op jit(solution)/shard_map/ppermute | solution.py:46
  76.9 16.3 %collective-permute-start.10 = (bf16[96,1152]{1,0:T(8,128)(2,1)S(1)}, bf16[96,1152]{1,0:T(8,128)(2,1)S(1)}, u32[]{:S(2)}, u32[]{:S(2)}) collective-permute-start(bf16[96,1152]{1,0:T(8,128)(2,1)S(1)} %copy-done.72), channel_id=1, source_target_pairs={{0,2},{2,0},{4,6},{6,4},{1,3},{3,1},{5,7},{7,5},{8,10},{10,8},{12,... | collective-permute-start | bytes 663560 | tf_op jit(solution)/shard_map/ppermute | solution.py:46
  83.8 16.2 %collective-permute-start.11 = (bf16[96,1152]{1,0:T(8,128)(2,1)S(1)}, bf16[96,1152]{1,0:T(8,128)(2,1)S(1)}, u32[]{:S(2)}, u32[]{:S(2)}) collective-permute-start(bf16[96,1152]{1,0:T(8,128)(2,1)S(1)} %copy-done.71), channel_id=1, source_target_pairs={{0,4},{2,6},{4,0},{6,2},{1,5},{3,7},{5,1},{7,3},{8,12},{10,14},{12... | collective-permute-start | bytes 663560 | tf_op jit(solution)/shard_map/ppermute | solution.py:46
  84.9 15.9 %collective-permute-start.12 = (bf16[96,1152]{1,0:T(8,128)(2,1)S(1)}, bf16[96,1152]{1,0:T(8,128)(2,1)S(1)}, u32[]{:S(2)}, u32[]{:S(2)}) collective-permute-start(bf16[96,1152]{1,0:T(8,128)(2,1)S(1)} %copy-done.70), channel_id=1, source_target_pairs={{0,6},{2,4},{4,2},{6,0},{1,7},{3,5},{5,3},{7,1},{8,14},{10,12},{12... | collective-permute-start | bytes 663560 | tf_op jit(solution)/shard_map/ppermute | solution.py:46
  101.4 13.1 %collective-permute-start.13 = (bf16[256,256]{1,0:T(8,128)(2,1)}, bf16[256,256]{1,0:T(8,128)(2,1)S(1)}, u32[]{:S(2)}, u32[]{:S(2)}) collective-permute-start(bf16[256,256]{1,0:T(8,128)(2,1)} %get-tuple-element.218.refs_0_), channel_id=1, source_target_pairs={{0,2},{2,0},{4,6},{6,4},{1,3},{3,1},{5,7},{7,5},{8,10},{10,8},{12,... | collective-permute-start | bytes 393224 | tf_op jit(solution)/shard_map/ppermute | solution.py:46
  104.3 10.8 %collective-permute-start.14 = (bf16[256,256]{1,0:T(8,128)(2,1)}, bf16[256,256]{1,0:T(8,128)(2,1)}, u32[]{:S(2)}, u32[]{:S(2)}) collective-permute-start(bf16[256,256]{1,0:T(8,128)(2,1)} %get-tuple-element.218.refs_0_), channel_id=1, source_target_pairs={{0,4},{2,6},{4,0},{6,2},{1,5},{3,7},{5,1},{7,3},{8,12},{10,14},{12... | collective-permute-start | bytes 393224 | tf_op jit(solution)/shard_map/ppermute | solution.py:46
  105.2 9.8 %collective-permute-start.15 = (bf16[256,256]{1,0:T(8,128)(2,1)}, bf16[256,256]{1,0:T(8,128)(2,1)}, u32[]{:S(2)}, u32[]{:S(2)}) collective-permute-start(bf16[256,256]{1,0:T(8,128)(2,1)} %get-tuple-element.218.refs_0_), channel_id=1, source_target_pairs={{0,6},{2,4},{4,2},{6,0},{1,7},{3,5},{5,3},{7,1},{8,14},{10,12},{12... | collective-permute-start | bytes 393224 | tf_op jit(solution)/shard_map/ppermute | solution.py:46
  106.7 18.8 %collective-permute-start.17 = (bf16[384,1152]{1,0:T(8,128)(2,1)}, bf16[384,1152]{1,0:T(8,128)(2,1)S(1)}, u32[]{:S(2)}, u32[]{:S(2)}) collective-permute-start(bf16[384,1152]{1,0:T(8,128)(2,1)} %get-tuple-element.228.refs_0_), channel_id=1, source_target_pairs={{0,8},{8,0},{16,24},{24,16},{1,9},{9,1},{17,25},{25,17},{2,10},{10... | collective-permute-start | bytes 2654216 | tf_op jit(solution)/shard_map/ppermute | solution.py:46
  108.2 18.6 %collective-permute-start.18 = (bf16[384,1152]{1,0:T(8,128)(2,1)}, bf16[384,1152]{1,0:T(8,128)(2,1)}, u32[]{:S(2)}, u32[]{:S(2)}) collective-permute-start(bf16[384,1152]{1,0:T(8,128)(2,1)} %get-tuple-element.228.refs_0_), channel_id=1, source_target_pairs={{0,16},{8,24},{16,0},{24,8},{1,17},{9,25},{17,1},{25,9},{2,18},{10... | collective-permute-start | bytes 2654216 | tf_op jit(solution)/shard_map/ppermute | solution.py:46
  121.2 2.4 collective-permute-start.16
  126.8 37.8 %collective-permute-start.22 = (bf16[384,2304]{1,0:T(8,128)(2,1)S(1)}, bf16[384,2304]{1,0:T(8,128)(2,1)S(1)}, u32[]{:S(2)}, u32[]{:S(2)}) collective-permute-start(bf16[384,2304]{1,0:T(8,128)(2,1)S(1)} %place.5.refs_3_), channel_id=1, source_target_pairs={{0,8},{8,0},{16,24},{24,16},{1,9},{9,1},{17,25},{25,17},{2,10},{10... | collective-permute-start | bytes 5308424 | tf_op jit(solution)/shard_map/ppermute | solution.py:46
  127.4 38.3 %collective-permute-start.23 = (bf16[384,2304]{1,0:T(8,128)(2,1)S(1)}, bf16[384,2304]{1,0:T(8,128)(2,1)S(1)}, u32[]{:S(2)}, u32[]{:S(2)}) collective-permute-start(bf16[384,2304]{1,0:T(8,128)(2,1)S(1)} %place.5.refs_3_), channel_id=1, source_target_pairs={{0,16},{8,24},{16,0},{24,8},{1,17},{9,25},{17,1},{25,9},{2,18},{10... | collective-permute-start | bytes 5308424 | tf_op jit(solution)/shard_map/ppermute | solution.py:46
  128.9 15.9 %collective-permute-start.19 = (bf16[128,1536]{1,0:T(8,128)(2,1)S(1)}, bf16[128,1536]{1,0:T(8,128)(2,1)S(1)}, u32[]{:S(2)}, u32[]{:S(2)}) collective-permute-start(bf16[128,1536]{1,0:T(8,128)(2,1)S(1)} %get-tuple-element.232), channel_id=1, source_target_pairs={{0,2},{2,0},{4,6},{6,4},{1,3},{3,1},{5,7},{7,5},{8,10},{10,8},{12,... | collective-permute-start | bytes 1179656 | tf_op jit(solution)/shard_map/ppermute | solution.py:46
  129.5 29.8 %collective-permute-start.20 = (bf16[128,1536]{1,0:T(8,128)(2,1)S(1)}, bf16[128,1536]{1,0:T(8,128)(2,1)S(1)}, u32[]{:S(2)}, u32[]{:S(2)}) collective-permute-start(bf16[128,1536]{1,0:T(8,128)(2,1)S(1)} %get-tuple-element.232), channel_id=1, source_target_pairs={{0,4},{2,6},{4,0},{6,2},{1,5},{3,7},{5,1},{7,3},{8,12},{10,14},{12... | collective-permute-start | bytes 1179656 | tf_op jit(solution)/shard_map/ppermute | solution.py:46
  131.8 27.4 %collective-permute-start.21 = (bf16[128,1536]{1,0:T(8,128)(2,1)S(1)}, bf16[128,1536]{1,0:T(8,128)(2,1)S(1)}, u32[]{:S(2)}, u32[]{:S(2)}) collective-permute-start(bf16[128,1536]{1,0:T(8,128)(2,1)S(1)} %get-tuple-element.232), channel_id=1, source_target_pairs={{0,6},{2,4},{4,2},{6,0},{1,7},{3,5},{5,3},{7,1},{8,14},{10,12},{12... | collective-permute-start | bytes 1179656 | tf_op jit(solution)/shard_map/ppermute | solution.py:46
  165.8 3.8 collective-permute-start.24
  167.4 31.3 %collective-permute-start.28 = (bf16[192,3456]{1,0:T(8,128)(2,1)S(1)}, bf16[192,3456]{1,0:T(8,128)(2,1)S(1)}, u32[]{:S(2)}, u32[]{:S(2)}) collective-permute-start(bf16[192,3456]{1,0:T(8,128)(2,1)S(1)} %pad_maximum_fusion.4), channel_id=1, source_target_pairs={{0,8},{8,0},{16,24},{24,16},{1,9},{9,1},{17,25},{25,17},{2,10},{10... | collective-permute-start | bytes 3981320 | tf_op jit(solution)/shard_map/ppermute | solution.py:46
  168.2 31.0 %collective-permute-start.29 = (bf16[192,3456]{1,0:T(8,128)(2,1)S(1)}, bf16[192,3456]{1,0:T(8,128)(2,1)S(1)}, u32[]{:S(2)}, u32[]{:S(2)}) collective-permute-start(bf16[192,3456]{1,0:T(8,128)(2,1)S(1)} %pad_maximum_fusion.3), channel_id=1, source_target_pairs={{0,16},{8,24},{16,0},{24,8},{1,17},{9,25},{17,1},{25,9},{2,18},{10... | collective-permute-start | bytes 3981320 | tf_op jit(solution)/shard_map/ppermute | solution.py:46
  169.6 41.7 %collective-permute-start.25 = (bf16[128,1536]{1,0:T(8,128)(2,1)S(1)}, bf16[128,1536]{1,0:T(8,128)(2,1)S(1)}, u32[]{:S(2)}, u32[]{:S(2)}) collective-permute-start(bf16[128,1536]{1,0:T(8,128)(2,1)S(1)} %copy-done.42), channel_id=1, source_target_pairs={{0,2},{2,0},{4,6},{6,4},{1,3},{3,1},{5,7},{7,5},{8,10},{10,8},{12,... | collective-permute-start | bytes 1179656 | tf_op jit(solution)/shard_map/ppermute | solution.py:46
  171.6 39.7 %collective-permute-start.26 = (bf16[128,1536]{1,0:T(8,128)(2,1)S(1)}, bf16[128,1536]{1,0:T(8,128)(2,1)S(1)}, u32[]{:S(2)}, u32[]{:S(2)}) collective-permute-start(bf16[128,1536]{1,0:T(8,128)(2,1)S(1)} %copy-done.42), channel_id=1, source_target_pairs={{0,4},{2,6},{4,0},{6,2},{1,5},{3,7},{5,1},{7,3},{8,12},{10,14},{12... | collective-permute-start | bytes 1179656 | tf_op jit(solution)/shard_map/ppermute | solution.py:46
  172.6 38.7 %collective-permute-start.27 = (bf16[128,1536]{1,0:T(8,128)(2,1)S(1)}, bf16[128,1536]{1,0:T(8,128)(2,1)S(1)}, u32[]{:S(2)}, u32[]{:S(2)}) collective-permute-start(bf16[128,1536]{1,0:T(8,128)(2,1)S(1)} %copy-done.42), channel_id=1, source_target_pairs={{0,6},{2,4},{4,2},{6,0},{1,7},{3,5},{5,3},{7,1},{8,14},{10,12},{12... | collective-permute-start | bytes 1179656 | tf_op jit(solution)/shard_map/ppermute | solution.py:46
  211.4 3.5 collective-permute-start.30
  239.3 7.2 %collective-permute-start.31 = (bf16[512,1536]{1,0:T(8,128)(2,1)S(1)}, bf16[512,1536]{1,0:T(8,128)(2,1)S(1)}, u32[]{:S(2)}, u32[]{:S(2)}) collective-permute-start(bf16[512,1536]{1,0:T(8,128)(2,1)S(1)} %get-tuple-element.251), channel_id=1, source_target_pairs={{0,1},{1,0},{2,3},{3,2},{4,5},{5,4},{6,7},{7,6},{8,9},{9,8},{10,11... | collective-permute-start | bytes 4718600 | tf_op jit(solution)/shard_map/ppermute | solution.py:46
  239.5 8.4 %collective-permute-start.32 = (bf16[512,1536]{1,0:T(8,128)(2,1)S(1)}, bf16[512,1536]{1,0:T(8,128)(2,1)S(1)}, u32[]{:S(2)}, u32[]{:S(2)}) collective-permute-start(bf16[512,1536]{1,0:T(8,128)(2,1)S(1)} %get-tuple-element.253), channel_id=1, source_target_pairs={{0,1},{1,0},{2,3},{3,2},{4,5},{5,4},{6,7},{7,6},{8,9},{9,8},{10,11... | collective-permute-start | bytes 4718600 | tf_op jit(solution)/shard_map/ppermute | solution.py:46
  247.8 39.1 %collective-permute-start.33 = (bf16[128,1536]{1,0:T(8,128)(2,1)S(1)}, bf16[128,1536]{1,0:T(8,128)(2,1)S(1)}, u32[]{:S(2)}, u32[]{:S(2)}) collective-permute-start(bf16[128,1536]{1,0:T(8,128)(2,1)S(1)} %get-tuple-element.256), channel_id=1, source_target_pairs={{0,2},{2,0},{4,6},{6,4},{1,3},{3,1},{5,7},{7,5},{8,10},{10,8},{12,... | collective-permute-start | bytes 1179656 | tf_op jit(solution)/shard_map/ppermute | solution.py:46
  249.6 37.4 %collective-permute-start.34 = (bf16[128,1536]{1,0:T(8,128)(2,1)S(1)}, bf16[128,1536]{1,0:T(8,128)(2,1)S(1)}, u32[]{:S(2)}, u32[]{:S(2)}) collective-permute-start(bf16[128,1536]{1,0:T(8,128)(2,1)S(1)} %get-tuple-element.257), channel_id=1, source_target_pairs={{0,4},{2,6},{4,0},{6,2},{1,5},{3,7},{5,1},{7,3},{8,12},{10,14},{12... | collective-permute-start | bytes 1179656 | tf_op jit(solution)/shard_map/ppermute | solution.py:46
  250.7 36.2 %collective-permute-start.35 = (bf16[128,1536]{1,0:T(8,128)(2,1)S(1)}, bf16[128,1536]{1,0:T(8,128)(2,1)S(1)}, u32[]{:S(2)}, u32[]{:S(2)}) collective-permute-start(bf16[128,1536]{1,0:T(8,128)(2,1)S(1)} %get-tuple-element.258), channel_id=1, source_target_pairs={{0,6},{2,4},{4,2},{6,0},{1,7},{3,5},{5,3},{7,1},{8,14},{10,12},{12... | collective-permute-start | bytes 1179656 | tf_op jit(solution)/shard_map/ppermute | solution.py:46
  252.4 21.0 %collective-permute-start.36 = (bf16[384,1152]{1,0:T(8,128)(2,1)S(1)}, bf16[384,1152]{1,0:T(8,128)(2,1)S(1)}, u32[]{:S(2)}, u32[]{:S(2)}) collective-permute-start(bf16[384,1152]{1,0:T(8,128)(2,1)S(1)} %pad_maximum_fusion.5), channel_id=1, source_target_pairs={{0,8},{8,0},{16,24},{24,16},{1,9},{9,1},{17,25},{25,17},{2,10},{10... | collective-permute-start | bytes 2654216 | tf_op jit(solution)/shard_map/ppermute | solution.py:46
  253.9 20.9 %collective-permute-start.37 = (bf16[384,1152]{1,0:T(8,128)(2,1)S(1)}, bf16[384,1152]{1,0:T(8,128)(2,1)S(1)}, u32[]{:S(2)}, u32[]{:S(2)}) collective-permute-start(bf16[384,1152]{1,0:T(8,128)(2,1)S(1)} %pad_maximum_fusion.6), channel_id=1, source_target_pairs={{0,16},{8,24},{16,0},{24,8},{1,17},{9,25},{17,1},{25,9},{2,18},{10... | collective-permute-start | bytes 2654216 | tf_op jit(solution)/shard_map/ppermute | solution.py:46
  275.0 10.5 %collective-permute-start.38 = (bf16[192,1152]{1,0:T(8,128)(2,1)S(1)}, bf16[192,1152]{1,0:T(8,128)(2,1)S(1)}, u32[]{:S(2)}, u32[]{:S(2)}) collective-permute-start(bf16[192,1152]{1,0:T(8,128)(2,1)S(1)} %get-tuple-element.263), channel_id=1, source_target_pairs={{0,8},{8,0},{16,24},{24,16},{1,9},{9,1},{17,25},{25,17},{2,10},{10... | collective-permute-start | bytes 1327112 | tf_op jit(solution)/shard_map/ppermute | solution.py:46
  275.6 10.0 %collective-permute-start.39 = (bf16[192,1152]{1,0:T(8,128)(2,1)S(1)}, bf16[192,1152]{1,0:T(8,128)(2,1)S(1)}, u32[]{:S(2)}, u32[]{:S(2)}) collective-permute-start(bf16[192,1152]{1,0:T(8,128)(2,1)S(1)} %get-tuple-element.264), channel_id=1, source_target_pairs={{0,16},{8,24},{16,0},{24,8},{1,17},{9,25},{17,1},{25,9},{2,18},{10... | collective-permute-start | bytes 1327112 | tf_op jit(solution)/shard_map/ppermute | solution.py:46
  287.0 40.3 %collective-permute-start.44 = (bf16[384,2304]{1,0:T(8,128)(2,1)S(1)}, bf16[384,2304]{1,0:T(8,128)(2,1)}, u32[]{:S(2)}, u32[]{:S(2)}) collective-permute-start(bf16[384,2304]{1,0:T(8,128)(2,1)S(1)} %pad_maximum_fusion), channel_id=1, source_target_pairs={{0,8},{8,0},{16,24},{24,16},{1,9},{9,1},{17,25},{25,17},{2,10},{10... | collective-permute-start | bytes 5308424 | tf_op jit(solution)/shard_map/ppermute | solution.py:46
  288.6 38.7 %collective-permute-start.45 = (bf16[384,2304]{1,0:T(8,128)(2,1)}, bf16[384,2304]{1,0:T(8,128)(2,1)}, u32[]{:S(2)}, u32[]{:S(2)}) collective-permute-start(bf16[384,2304]{1,0:T(8,128)(2,1)} %pad_maximum_fusion.1), channel_id=1, source_target_pairs={{0,16},{8,24},{16,0},{24,8},{1,17},{9,25},{17,1},{25,9},{2,18},{10... | collective-permute-start | bytes 5308424 | tf_op jit(solution)/shard_map/ppermute | solution.py:46
  290.2 23.2 %all-to-all-start = ((bf16[4,96,1152]{2,1,0:T(8,128)(2,1)}), bf16[4,96,1152]{2,1,0:T(8,128)(2,1)S(1)}, u32[]{:S(2)}, u32[]{:S(2)}) async-start(bf16[4,96,1152]{2,1,0:T(8,128)(2,1)} %bitcast.22), calls=%async_computation | async-start | bytes 1769472 | tf_op jit(solution)/shard_map/all_to_all | solution.py:809
  313.4 7.1 %collective-permute-start.41 = (bf16[256,256]{1,0:T(8,128)(2,1)}, bf16[256,256]{1,0:T(8,128)(2,1)S(1)}, u32[]{:S(2)}, u32[]{:S(2)}) collective-permute-start(bf16[256,256]{1,0:T(8,128)(2,1)} %get-tuple-element.281), channel_id=1, source_target_pairs={{0,2},{2,0},{4,6},{6,4},{1,3},{3,1},{5,7},{7,5},{8,10},{10,8},{12,... | collective-permute-start | bytes 393224 | tf_op jit(solution)/shard_map/ppermute | solution.py:46
  314.2 13.1 %collective-permute-start.42 = (bf16[256,256]{1,0:T(8,128)(2,1)}, bf16[256,256]{1,0:T(8,128)(2,1)S(1)}, u32[]{:S(2)}, u32[]{:S(2)}) collective-permute-start(bf16[256,256]{1,0:T(8,128)(2,1)} %get-tuple-element.282), channel_id=1, source_target_pairs={{0,4},{2,6},{4,0},{6,2},{1,5},{3,7},{5,1},{7,3},{8,12},{10,14},{12... | collective-permute-start | bytes 393224 | tf_op jit(solution)/shard_map/ppermute | solution.py:46
  316.6 10.8 %collective-permute-start.43 = (bf16[256,256]{1,0:T(8,128)(2,1)}, bf16[256,256]{1,0:T(8,128)(2,1)S(1)}, u32[]{:S(2)}, u32[]{:S(2)}) collective-permute-start(bf16[256,256]{1,0:T(8,128)(2,1)} %get-tuple-element.283), channel_id=1, source_target_pairs={{0,6},{2,4},{4,2},{6,0},{1,7},{3,5},{5,3},{7,1},{8,14},{10,12},{12... | collective-permute-start | bytes 393224 | tf_op jit(solution)/shard_map/ppermute | solution.py:46
  331.0 19.8 %collective-permute-start.49 = (bf16[192,2304]{1,0:T(8,128)(2,1)}, bf16[192,2304]{1,0:T(8,128)(2,1)}, u32[]{:S(2)}, u32[]{:S(2)}) collective-permute-start(bf16[192,2304]{1,0:T(8,128)(2,1)} %get-tuple-element.296), channel_id=1, source_target_pairs={{0,8},{8,0},{16,24},{24,16},{1,9},{9,1},{17,25},{25,17},{2,10},{10... | collective-permute-start | bytes 2654216 | tf_op jit(solution)/shard_map/ppermute | solution.py:46
  331.8 19.5 %collective-permute-start.50 = (bf16[192,2304]{1,0:T(8,128)(2,1)}, bf16[192,2304]{1,0:T(8,128)(2,1)}, u32[]{:S(2)}, u32[]{:S(2)}) collective-permute-start(bf16[192,2304]{1,0:T(8,128)(2,1)} %get-tuple-element.297), channel_id=1, source_target_pairs={{0,16},{8,24},{16,0},{24,8},{1,17},{9,25},{17,1},{25,9},{2,18},{10... | collective-permute-start | bytes 2654216 | tf_op jit(solution)/shard_map/ppermute | solution.py:46
  332.6 25.5 %collective-permute-start.46 = (bf16[128,1536]{1,0:T(8,128)(2,1)}, bf16[128,1536]{1,0:T(8,128)(2,1)}, u32[]{:S(2)}, u32[]{:S(2)}) collective-permute-start(bf16[128,1536]{1,0:T(8,128)(2,1)} %get-tuple-element.291), channel_id=1, source_target_pairs={{0,2},{2,0},{4,6},{6,4},{1,3},{3,1},{5,7},{7,5},{8,10},{10,8},{12,... | collective-permute-start | bytes 1179656 | tf_op jit(solution)/shard_map/ppermute | solution.py:46
  334.6 30.1 %collective-permute-start.47 = (bf16[128,1536]{1,0:T(8,128)(2,1)}, bf16[128,1536]{1,0:T(8,128)(2,1)}, u32[]{:S(2)}, u32[]{:S(2)}) collective-permute-start(bf16[128,1536]{1,0:T(8,128)(2,1)} %get-tuple-element.292), channel_id=1, source_target_pairs={{0,4},{2,6},{4,0},{6,2},{1,5},{3,7},{5,1},{7,3},{8,12},{10,14},{12... | collective-permute-start | bytes 1179656 | tf_op jit(solution)/shard_map/ppermute | solution.py:46
  335.6 29.2 %collective-permute-start.48 = (bf16[128,1536]{1,0:T(8,128)(2,1)S(1)}, bf16[128,1536]{1,0:T(8,128)(2,1)}, u32[]{:S(2)}, u32[]{:S(2)}) collective-permute-start(bf16[128,1536]{1,0:T(8,128)(2,1)S(1)} %get-tuple-element.293), channel_id=1, source_target_pairs={{0,6},{2,4},{4,2},{6,0},{1,7},{3,5},{5,3},{7,1},{8,14},{10,12},{12... | collective-permute-start | bytes 1179656 | tf_op jit(solution)/shard_map/ppermute | solution.py:46
  351.4 13.3 %collective-permute-start.51 = (bf16[384,768]{1,0:T(8,128)(2,1)S(1)}, bf16[384,768]{1,0:T(8,128)(2,1)S(1)}, u32[]{:S(2)}, u32[]{:S(2)}) collective-permute-start(bf16[384,768]{1,0:T(8,128)(2,1)S(1)} %pad_maximum_fusion.26), channel_id=1, source_target_pairs={{0,8},{8,0},{16,24},{24,16},{1,9},{9,1},{17,25},{25,17},{2,10},{10... | collective-permute-start | bytes 1769480 | tf_op jit(solution)/shard_map/ppermute | solution.py:46
  352.8 11.9 %collective-permute-start.52 = (bf16[384,768]{1,0:T(8,128)(2,1)S(1)}, bf16[384,768]{1,0:T(8,128)(2,1)S(1)}, u32[]{:S(2)}, u32[]{:S(2)}) collective-permute-start(bf16[384,768]{1,0:T(8,128)(2,1)S(1)} %pad_maximum_fusion.27), channel_id=1, source_target_pairs={{0,16},{8,24},{16,0},{24,8},{1,17},{9,25},{17,1},{25,9},{2,18},{10... | collective-permute-start | bytes 1769480 | tf_op jit(solution)/shard_map/ppermute | solution.py:46
  366.1 15.5 %collective-permute-start.54 = (bf16[400,1024]{1,0:T(8,128)(2,1)}, bf16[400,1024]{1,0:T(8,128)(2,1)}, u32[]{:S(2)}, u32[]{:S(2)}) collective-permute-start(bf16[400,1024]{1,0:T(8,128)(2,1)} %pad_maximum_fusion.17), channel_id=1, source_target_pairs={{0,8},{8,0},{16,24},{24,16},{1,9},{9,1},{17,25},{25,17},{2,10},{10... | collective-permute-start | bytes 2457608 | tf_op jit(solution)/shard_map/ppermute | solution.py:46
  367.5 14.1 %collective-permute-start.53 = (bf16[384,1024]{1,0:T(8,128)(2,1)}, bf16[384,1024]{1,0:T(8,128)(2,1)}, u32[]{:S(2)}, u32[]{:S(2)}) collective-permute-start(bf16[384,1024]{1,0:T(8,128)(2,1)} %pad_maximum_fusion.18), channel_id=1, source_target_pairs={{0,16},{8,24},{16,0},{24,8},{1,17},{9,25},{17,1},{25,9},{2,18},{10... | collective-permute-start | bytes 2359304 | tf_op jit(solution)/shard_map/ppermute | solution.py:46
  371.1 47.3 %all-to-all-start.1 = ((bf16[4,96,2304]{2,1,0:T(8,128)(2,1)}), bf16[4,96,2304]{2,1,0:T(8,128)(2,1)}, u32[]{:S(2)}, u32[]{:S(2)}) async-start(bf16[4,96,2304]{2,1,0:T(8,128)(2,1)} %bitcast.76), calls=%async_computation.1 | async-start | bytes 3538944 | tf_op jit(solution)/shard_map/all_to_all | solution.py:906
  385.7 13.1 %collective-permute-start.56 = (bf16[208,1792]{1,0:T(8,128)(2,1)}, bf16[208,1792]{1,0:T(8,128)(2,1)}, u32[]{:S(2)}, u32[]{:S(2)}) collective-permute-start(bf16[208,1792]{1,0:T(8,128)(2,1)} %fusion.4), channel_id=1, source_target_pairs={{0,16},{8,24},{16,0},{24,8},{1,17},{9,25},{17,1},{25,9},{2,18},{10... | collective-permute-start | bytes 2236424 | tf_op jit(solution)/shard_map/ppermute | solution.py:46
  387.2 12.5 %collective-permute-start.55 = (bf16[192,1792]{1,0:T(8,128)(2,1)}, bf16[192,1792]{1,0:T(8,128)(2,1)S(1)}, u32[]{:S(2)}, u32[]{:S(2)}) collective-permute-start(bf16[192,1792]{1,0:T(8,128)(2,1)} %pad_maximum_fusion.21), channel_id=1, source_target_pairs={{0,8},{8,0},{16,24},{24,16},{1,9},{9,1},{17,25},{25,17},{2,10},{10... | collective-permute-start | bytes 2064392 | tf_op jit(solution)/shard_map/ppermute | solution.py:46
  418.3 17.3 %collective-permute-start.57 = (bf16[96,1920]{1,0:T(8,128)(2,1)}, bf16[96,1920]{1,0:T(8,128)(2,1)S(1)}, u32[]{:S(2)}, u32[]{:S(2)}) collective-permute-start(bf16[96,1920]{1,0:T(8,128)(2,1)} %get-tuple-element.330), channel_id=1, source_target_pairs={{0,2},{2,0},{4,6},{6,4},{1,3},{3,1},{5,7},{7,5},{8,10},{10,8},{12,... | collective-permute-start | bytes 1105928 | tf_op jit(solution)/shard_map/ppermute | solution.py:46
  418.3 28.4 %collective-permute-start.58 = (bf16[96,1920]{1,0:T(8,128)(2,1)}, bf16[96,1920]{1,0:T(8,128)(2,1)S(1)}, u32[]{:S(2)}, u32[]{:S(2)}) collective-permute-start(bf16[96,1920]{1,0:T(8,128)(2,1)} %get-tuple-element.331), channel_id=1, source_target_pairs={{0,4},{2,6},{4,0},{6,2},{1,5},{3,7},{5,1},{7,3},{8,12},{10,14},{12... | collective-permute-start | bytes 1105928 | tf_op jit(solution)/shard_map/ppermute | solution.py:46
  420.4 26.3 %collective-permute-start.59 = (bf16[96,1920]{1,0:T(8,128)(2,1)}, bf16[96,1920]{1,0:T(8,128)(2,1)S(1)}, u32[]{:S(2)}, u32[]{:S(2)}) collective-permute-start(bf16[96,1920]{1,0:T(8,128)(2,1)} %get-tuple-element.332), channel_id=1, source_target_pairs={{0,6},{2,4},{4,2},{6,0},{1,7},{3,5},{5,3},{7,1},{8,14},{10,12},{12... | collective-permute-start | bytes 1105928 | tf_op jit(solution)/shard_map/ppermute | solution.py:46
  422.7 6.6 %collective-permute-start.60 = (f32[128,1536]{1,0:T(8,128)}, f32[128,1536]{1,0:T(8,128)S(1)}, u32[]{:S(2)}, u32[]{:S(2)}) collective-permute-start(f32[128,1536]{1,0:T(8,128)} %get-tuple-element.335), channel_id=1, source_target_pairs={{0,1},{1,0},{2,3},{3,2},{4,5},{5,4},{6,7},{7,6},{8,9},{9,8},{10,11... | collective-permute-start | bytes 2359304 | tf_op jit(solution)/shard_map/ppermute | solution.py:46
  424.3 8.6 %collective-permute-start.62 = (bf16[128,1536]{1,0:T(8,128)(2,1)S(1)}, bf16[128,1536]{1,0:T(8,128)(2,1)S(1)}, u32[]{:S(2)}, u32[]{:S(2)}) collective-permute-start(bf16[128,1536]{1,0:T(8,128)(2,1)S(1)} %pad_maximum_fusion.33), channel_id=1, source_target_pairs={{0,1},{1,0},{2,3},{3,2},{4,5},{5,4},{6,7},{7,6},{8,9},{9,8},{10,11... | collective-permute-start | bytes 1179656 | tf_op jit(solution)/shard_map/ppermute | solution.py:46
  431.5 2.4 collective-permute-start.61
  (88 other events, 1091.8 us)
